TPU v7x, 32 devices: a whole 2x2x4 slice. The times are simulated.
32 devices in a mesh: dp: 4 (over y, x), row: 4 (over z), col: 2 (over core).
Axes of the slice: x: 2, y: 2, z: 4, core: 2. Of those that a mesh axis runs over, the one named last changes fastest.
Arguments:
- activations: bfloat16 [4096, 2048], P(('dp', 'col'), 'row'), may hold values from -6 to 6
- per_layer: bfloat16 [4096, 256], P(('dp', 'row'), 'col'), may hold values from -6 to 6
- cotangent: bfloat16 [4096, 2048], P(('dp', 'col'), 'row'), may hold values from -6 to 6
- lengths: int32 [4], replicated, may hold values from 1 to 1024, 2560 in all
- starts: int32 [4, 2], replicated, may hold values from 0 to 768, as said below
- w_query: float32 [2048, 2048], P('row', ('col', 'dp')), may hold values from -0.125 to 0.125
- m_query: float32 [2048, 2048], P('row', ('col', 'dp')), may hold values from -0.0007324219 to 0.0007324219
- v_query: float32 [2048, 2048], P('row', ('col', 'dp')), may hold values from 1.609199e-08 to 6.436796e-08
- key_value_weight: float32 [2048, 1024], P('row', 'dp'), may hold values from -0.125 to 0.125
- key_value_first_moment: float32 [2048, 1024], P('row', 'dp'), may hold values from -0.0007324219 to 0.0007324219
- key_value_second_moment: float32 [2048, 1024], P('row', 'dp'), may hold values from 1.609199e-08 to 6.436796e-08
- w_attend: float32 [2048, 2048], P('col', ('row', 'dp')), may hold values from -0.125 to 0.125
- m_attend: float32 [2048, 2048], P('col', ('row', 'dp')), may hold values from -0.0007324219 to 0.0007324219
- v_attend: float32 [2048, 2048], P('col', ('row', 'dp')), may hold values from 1.609199e-08 to 6.436796e-08
- w_gateup: float32 [2, 2048, 8192], P(None, 'row', ('col', 'dp')), may hold values from -0.125 to 0.125
- m_gateup: float32 [2, 2048, 8192], P(None, 'row', ('col', 'dp')), may hold values from -0.0007324219 to 0.0007324219
- v_gateup: float32 [2, 2048, 8192], P(None, 'row', ('col', 'dp')), may hold values from 1.609199e-08 to 6.436796e-08
- w_down: float32 [8192, 2048], P('col', ('row', 'dp')), may hold values from -0.0625 to 0.0625
- m_down: float32 [8192, 2048], P('col', ('row', 'dp')), may hold values from -0.0007324219 to 0.0007324219
- v_down: float32 [8192, 2048], P('col', ('row', 'dp')), may hold values from 1.609199e-08 to 6.436796e-08
- w_left: float32 [2048, 64], P('row', ('col', 'dp')), may hold values from -0.125 to 0.125
- m_left: float32 [2048, 64], P('row', ('col', 'dp')), may hold values from -0.0007324219 to 0.0007324219
- v_left: float32 [2048, 64], P('row', ('col', 'dp')), may hold values from 1.609199e-08 to 6.436796e-08
- w_right: float32 [64, 2048], P('col', ('row', 'dp')), may hold values from -0.75 to 0.75
- m_right: float32 [64, 2048], P('col', ('row', 'dp')), may hold values from -0.0007324219 to 0.0007324219
- v_right: float32 [64, 2048], P('col', ('row', 'dp')), may hold values from 1.609199e-08 to 6.436796e-08
- w_pergate: float32 [2048, 256], P('row', ('col', 'dp')), may hold values from -0.125 to 0.125
- m_pergate: float32 [2048, 256], P('row', ('col', 'dp')), may hold values from -0.0007324219 to 0.0007324219
- v_pergate: float32 [2048, 256], P('row', ('col', 'dp')), may hold values from 1.609199e-08 to 6.436796e-08
- w_perproj: float32 [256, 2048], P('col', ('row', 'dp')), may hold values from -0.375 to 0.375
- m_perproj: float32 [256, 2048], P('col', ('row', 'dp')), may hold values from -0.0007324219 to 0.0007324219
- v_perproj: float32 [256, 2048], P('col', ('row', 'dp')), may hold values from 1.609199e-08 to 6.436796e-08
- w_gains: float32 [6, 2048], P(None, 'row')
- m_gains: float32 [6, 2048], P(None, 'row'), may hold values from -0.0007324219 to 0.0007324219
- v_gains: float32 [6, 2048], P(None, 'row'), may hold values from 3.218398e-08 to 1.2873592e-07
- w_heads: float32 [9, 256], replicated
- m_heads: float32 [9, 256], replicated, may hold values from -0.0029296875 to 0.0029296875
- v_heads: float32 [9, 256], replicated, may hold values from 2.5747184e-07 to 1.0298874e-06
Outputs:
- result: bfloat16 [4096, 2048], P(('dp', 'col'), 'row')
- grad_input: bfloat16 [4096, 2048], P(('dp', 'col'), 'row')
- grad_norm: float32 [], replicated
- clip_factors: float32 [8], replicated
- mom_query: float32 [2048, 2048], P('row', ('col', 'dp'))
- sec_query: float32 [2048, 2048], P('row', ('col', 'dp'))
- new_query: float32 [2048, 2048], P('row', ('col', 'dp'))
- mom_keyval: float32 [2048, 1024], P('row', 'dp')
- sec_keyval: float32 [2048, 1024], P('row', 'dp')
- new_keyval: float32 [2048, 1024], P('row', 'dp')
- mom_attend: float32 [2048, 2048], P('col', ('row', 'dp'))
- sec_attend: float32 [2048, 2048], P('col', ('row', 'dp'))
- new_attend: float32 [2048, 2048], P('col', ('row', 'dp'))
- mom_gateup: float32 [2, 2048, 8192], P(None, 'row', ('col', 'dp'))
- sec_gateup: float32 [2, 2048, 8192], P(None, 'row', ('col', 'dp'))
- new_gateup: float32 [2, 2048, 8192], P(None, 'row', ('col', 'dp'))
- mom_down: float32 [8192, 2048], P('col', ('row', 'dp'))
- sec_down: float32 [8192, 2048], P('col', ('row', 'dp'))
- new_down: float32 [8192, 2048], P('col', ('row', 'dp'))
- mom_left: float32 [2048, 64], P('row', ('col', 'dp'))
- sec_left: float32 [2048, 64], P('row', ('col', 'dp'))
- new_left: float32 [2048, 64], P('row', ('col', 'dp'))
- mom_right: float32 [64, 2048], P('col', ('row', 'dp'))
- sec_right: float32 [64, 2048], P('col', ('row', 'dp'))
- new_right: float32 [64, 2048], P('col', ('row', 'dp'))
- mom_pergate: float32 [2048, 256], P('row', ('col', 'dp'))
- sec_pergate: float32 [2048, 256], P('row', ('col', 'dp'))
- new_pergate: float32 [2048, 256], P('row', ('col', 'dp'))
- mom_perproj: float32 [256, 2048], P('col', ('row', 'dp'))
- sec_perproj: float32 [256, 2048], P('col', ('row', 'dp'))
- new_perproj: float32 [256, 2048], P('col', ('row', 'dp'))
- mom_gains: float32 [6, 2048], P(None, 'row')
- sec_gains: float32 [6, 2048], P(None, 'row')
- new_gains: float32 [6, 2048], P(None, 'row')
- mom_heads: float32 [9, 256], replicated
- sec_heads: float32 [9, 256], replicated
- new_heads: float32 [9, 256], replicated
Inputs may be any that keep to these rules, and one draw needn't show every extreme that they name: Tokens of sequence s from lengths[s] on are padding; one sequence uses all 1024 tokens. Piece k of sequence s covers starts[s, k] to starts[s, k] + 255 and starts between k * 512 and (k + 1) * 512 - 256.
All inputs are finite; a program needn't handle non-finite values.
Results may differ from a plain program's by a relative error of at most 0.02.
The roundings to bfloat16 on the way count: a program that leaves them out, or rounds other values in their place, can miss the bound.
Values may be sent and summed in bfloat16 or wider, within the bound.
A program may use at most 384 MiB of HBM per device.

v0:
```python
import jax
import jax.numpy as jnp
from jax import lax
from jax.sharding import PartitionSpec as P

MODEL_WIDTH = 2048
QUERY_HEADS = 8
KEY_VALUE_HEADS = 2
HEAD_WIDTH = 256
FF = 8192
RANK = 64
PLD = 256
IMG = 256
STEP = 10


EPS = 1e-06
ROPE_BASE = 1000000.0
BETA_ONE = 0.5
BETA_TWO = 0.5
ADAM_EPS = 1e-08
DECAY = 0.01
CLIP = 1.0
LOGIT_CAP = 4.0
GAIN_RATE = 0.6
HEAD_RATE = 0.1
HALF_ROOT = 0.7071067811865476
NEGATIVE = -1e30


def joined(part, axis, combine):
    gathered = jax.tree.map(lambda a: lax.all_gather(a, axis), part)

    def take(source):
        return jax.tree.map(lambda a: lax.dynamic_index_in_dim(a, source, 0, False), gathered)

    return lax.fori_loop(
        1, lax.axis_size(axis), lambda source, state: combine(state, take(source)), take(0)
    )


def row_total(values_in):
    return lax.psum(values_in, "row")


def spread_col(values_in):
    return lax.all_gather(values_in, "col", axis=0, tiled=True)


def reduce_row(values_in):
    return lax.psum_scatter(values_in, "row", scatter_dimension=0, tiled=True)


def spread_row(values_in):
    return lax.all_gather(values_in, "row", axis=0, tiled=True)


def reduce_col(values_in):
    return lax.psum_scatter(values_in, "col", scatter_dimension=0, tiled=True)


def grads_col(values_in):
    return lax.all_gather(values_in, "col", axis=0, tiled=True)


def grads_row(values_in):
    return lax.all_gather(values_in, "row", axis=0, tiled=True)


def inner_rows(left_mat, right_mat):
    return lax.dot_general(
        left_mat, right_mat, (((0,), (0,)), ((), ())), preferred_element_type=jnp.float32
    )


def against(grad_mat, weight_mat):
    return lax.dot_general(
        grad_mat, weight_mat, (((1,), (1,)), ((), ())), preferred_element_type=jnp.float32
    )


def flat_dot(left_mat, right_mat):
    return jnp.dot(left_mat, right_mat, preferred_element_type=jnp.float32)


def norm_forward(values_in, gain_vec):
    total_sq = row_total(jnp.sum(values_in * values_in, axis=-1, keepdims=True))
    norm_scale = lax.rsqrt(total_sq / MODEL_WIDTH + EPS)
    return (values_in * norm_scale * gain_vec, norm_scale)


def norm_backward(values_in, norm_scale, gain_vec, grad_out):
    weighted = grad_out * gain_vec
    inner_sum = row_total(jnp.sum(weighted * values_in, axis=-1, keepdims=True))
    grad_in = norm_scale * weighted - values_in * (norm_scale * norm_scale * norm_scale) * (
        inner_sum / MODEL_WIDTH
    )
    return (grad_in, jnp.sum(grad_out * values_in * norm_scale, axis=0))


def norm_rows(values_in, gain_vec):
    return (
        values_in
        * lax.rsqrt(jnp.mean(values_in * values_in, axis=-1, keepdims=True) + EPS)
        * gain_vec
    )


def rope_tables(places, feat_width):
    half_width = feat_width // 2
    powers = jnp.arange(half_width, dtype=jnp.int32).astype(jnp.float32) * (2.0 / feat_width)
    frequency = jnp.power(jnp.float32(ROPE_BASE), -powers)
    angles = places.astype(jnp.float32)[:, None] * frequency[None, :]
    return (jnp.cos(angles), jnp.sin(angles))


def rotate(values_in, cos_tab, sin_tab):
    half_width = values_in.shape[-1] // 2
    part_one = values_in[..., :half_width]
    part_two = values_in[..., half_width:]
    cos_row = cos_tab[:, None, :]
    sin_row = sin_tab[:, None, :]
    return jnp.concatenate(
        [part_one * cos_row - part_two * sin_row, part_two * cos_row + part_one * sin_row], axis=-1
    )


def query_form(unscaled_rows, gain_rows, cos_tab, sin_tab):
    shaped = unscaled_rows.reshape(unscaled_rows.shape[0], gain_rows.shape[0], HEAD_WIDTH)
    return rotate(norm_rows(shaped, gain_rows[None]), cos_tab, sin_tab)


def key_form(unscaled_rows, gain_vec, cos_tab, sin_tab):
    count_of_rows = unscaled_rows.shape[0]
    key_rows = unscaled_rows[:, : KEY_VALUE_HEADS * HEAD_WIDTH].reshape(
        count_of_rows, KEY_VALUE_HEADS, HEAD_WIDTH
    )
    value_rows = unscaled_rows[:, KEY_VALUE_HEADS * HEAD_WIDTH :].reshape(
        count_of_rows, KEY_VALUE_HEADS, HEAD_WIDTH
    )
    key_rows = rotate(norm_rows(key_rows, gain_vec), cos_tab, sin_tab)
    value_rows = norm_rows(value_rows, 1.0)
    return jnp.concatenate(
        [
            key_rows.reshape(count_of_rows, KEY_VALUE_HEADS * HEAD_WIDTH),
            value_rows.reshape(count_of_rows, KEY_VALUE_HEADS * HEAD_WIDTH),
        ],
        axis=1,
    )


def piece_of(places, starts):
    inside = (places[:, None] >= starts[None, :]) & (places[:, None] < starts[None, :] + IMG)
    labels = jnp.arange(1, starts.shape[0] + 1, dtype=jnp.int32)
    return jnp.sum(jnp.where(inside, labels[None, :], 0), axis=1) - 1


def visible(query_places, key_places, query_pieces, key_pieces, length):
    causal = key_places[None, :] <= query_places[:, None]
    same_piece = (query_pieces[:, None] == key_pieces[None, :]) & (query_pieces[:, None] >= 0)
    return (key_places[None, :] < length) & (causal | same_piece)


def block_mask(own_places, key_places, key_pieces, length, starts):
    return visible(own_places, key_places, piece_of(own_places, starts), key_pieces, length)


def attention_forward(queries, key_sel, value_sel, own_places, key_places, length, starts):
    count_of_rows, head_count = (queries.shape[0], queries.shape[1])
    block_size = min(512, count_of_rows)
    key_pieces = piece_of(key_places, starts)
    stacked = queries.reshape(count_of_rows // block_size, block_size, head_count, HEAD_WIDTH)

    def one_block(element):
        block_rows, block_at = element
        allowed = block_mask(own_places, key_places, key_pieces, length, starts)
        scores = jnp.einsum("qhd,khd->hqk", block_rows, key_sel, preferred_element_type=jnp.float32)
        masked = jnp.where(allowed[None], scores, NEGATIVE)
        peak_row = jnp.max(masked, axis=-1, keepdims=True)
        raw_weights = jnp.where(allowed[None], jnp.exp(masked - peak_row), 0.0)
        total_row = jnp.sum(raw_weights, axis=-1, keepdims=True)
        attn_probs = (raw_weights / total_row).astype(jnp.bfloat16)
        outputs = jnp.einsum(
            "hqk,khd->qhd", attn_probs, value_sel, preferred_element_type=jnp.float32
        )
        return (outputs, peak_row[..., 0], total_row[..., 0])

    return lax.map(one_block, (stacked, jnp.arange(count_of_rows // block_size, dtype=jnp.int32)))


def attention_backward(
    queries,
    key_sel,
    value_sel,
    grad_attended,
    block_peaks,
    block_totals,
    own_places,
    key_places,
    length,
    starts,
):
    count_of_rows, head_count = (queries.shape[0], queries.shape[1])
    block_size = min(512, count_of_rows)
    block_count = count_of_rows // block_size
    key_pieces = piece_of(key_places, starts)
    stacked = queries.reshape(block_count, block_size, head_count, HEAD_WIDTH)
    grad_stacked = grad_attended.reshape(block_count, block_size, head_count, HEAD_WIDTH)

    def one_block(carry, element):
        dk_sum, dv_sum = carry
        block_rows, grad_rows, peak_row, total_row, block_at = element
        allowed = block_mask(own_places, key_places, key_pieces, length, starts)
        scores = jnp.einsum("qhd,khd->hqk", block_rows, key_sel, preferred_element_type=jnp.float32)
        masked = jnp.where(allowed[None], scores, NEGATIVE)
        raw_weights = jnp.where(allowed[None], jnp.exp(masked - peak_row[..., None]), 0.0)
        attn_probs = raw_weights / total_row[..., None]
        probs_low = attn_probs.astype(jnp.bfloat16)
        grad_probs = jnp.einsum(
            "qhd,khd->hqk", grad_rows, value_sel, preferred_element_type=jnp.float32
        )
        delta_row = jnp.sum(attn_probs * grad_probs, axis=-1, keepdims=True)
        grad_scores = (attn_probs * (grad_probs - delta_row)).astype(jnp.bfloat16)
        grad_query = jnp.einsum(
            "hqk,khd->qhd", grad_scores, key_sel, preferred_element_type=jnp.float32
        )
        dk_sum = dk_sum + jnp.einsum(
            "hqk,qhd->khd", grad_scores, block_rows, preferred_element_type=jnp.float32
        )
        dv_sum = dv_sum + jnp.einsum(
            "hqk,qhd->khd", probs_low, grad_rows, preferred_element_type=jnp.float32
        )
        return ((dk_sum, dv_sum), grad_query)

    zero_keys = jnp.zeros(key_sel.shape, jnp.float32)
    (dk_sum, dv_sum), grad_query = lax.scan(
        one_block,
        (zero_keys, zero_keys),
        (
            stacked,
            grad_stacked,
            block_peaks,
            block_totals,
            jnp.arange(block_count, dtype=jnp.int32),
        ),
    )
    return (grad_query.reshape(count_of_rows, head_count, HEAD_WIDTH), dk_sum, dv_sum)


def adamw_step(weight, moment_one, moment_two, gradient, rate, decay):
    moment_one = BETA_ONE * moment_one + (1.0 - BETA_ONE) * gradient
    moment_two = BETA_TWO * moment_two + (1.0 - BETA_TWO) * gradient * gradient
    mean_step = moment_one / (1.0 - BETA_ONE**STEP)
    spread = moment_two / (1.0 - BETA_TWO**STEP)
    return (
        moment_one,
        moment_two,
        weight - rate * (mean_step / (jnp.sqrt(spread) + ADAM_EPS) + decay * weight),
    )


def per_device(
    activations,
    per_layer,
    cotangent,
    lengths,
    starts,
    w_query,
    m_query,
    v_query,
    key_value_weight,
    key_value_first_moment,
    key_value_second_moment,
    w_attend,
    m_attend,
    v_attend,
    w_gateup,
    m_gateup,
    v_gateup,
    w_down,
    m_down,
    v_down,
    w_left,
    m_left,
    v_left,
    w_right,
    m_right,
    v_right,
    w_pergate,
    m_pergate,
    v_pergate,
    w_perproj,
    m_perproj,
    v_perproj,
    w_gains,
    m_gains,
    v_gains,
    w_heads,
    m_heads,
    v_heads,
):
    row_devs = lax.axis_size("row")
    col_devs = lax.axis_size("col")
    data_devs = lax.axis_size("dp")
    row_place = lax.axis_index("row")
    column_place = lax.axis_index("col")
    data_at = lax.axis_index("dp")
    bf16 = jnp.bfloat16
    single_float = jnp.float32
    query_b, keyval_b, attend_b, gateup_b, down_b, left_b, right_b, pergate_b, perproj_b = (
        lax.all_gather(w_query.astype(bf16), "dp", axis=1, tiled=True),
        lax.all_gather(key_value_weight.astype(bf16), "dp", axis=1, tiled=True),
        lax.all_gather(w_attend.astype(bf16), "dp", axis=1, tiled=True),
        lax.all_gather(w_gateup.astype(bf16), "dp", axis=2, tiled=True),
        lax.all_gather(w_down.astype(bf16), "dp", axis=1, tiled=True),
        lax.all_gather(w_left.astype(bf16), "dp", axis=1, tiled=True),
        lax.all_gather(w_right.astype(bf16), "dp", axis=1, tiled=True),
        lax.all_gather(w_pergate.astype(bf16), "dp", axis=1, tiled=True),
        lax.all_gather(w_perproj.astype(bf16), "dp", axis=1, tiled=True),
    )
    inputs = activations.astype(single_float)
    tok_a, width_a = inputs.shape
    grouped_rows = tok_a * col_devs
    token_batch = grouped_rows // row_devs
    q_cols = query_b.shape[1]
    l_cols = left_b.shape[1]
    kv_cols = keyval_b.shape[1]
    ff_here = gateup_b.shape[2]
    local_heads = q_cols // HEAD_WIDTH
    length = lax.dynamic_index_in_dim(lengths, data_at, 0, keepdims=False)
    piece_starts = lax.dynamic_index_in_dim(starts, data_at, 0, keepdims=False)
    own_places = row_place * token_batch + jnp.arange(token_batch, dtype=jnp.int32)
    all_places = jnp.arange(grouped_rows, dtype=jnp.int32)
    own_cos, own_sin = rope_tables(own_places, HEAD_WIDTH)
    query_gains = lax.dynamic_slice_in_dim(w_heads, column_place * local_heads, local_heads, 0)
    key_gain = w_heads[QUERY_HEADS]
    hidden, scale_in = norm_forward(inputs, w_gains[0])
    hidden_b = hidden.astype(bf16)
    spread_h = spread_col(hidden_b)
    type_one = reduce_row(flat_dot(spread_h, jnp.concatenate([query_b, left_b], axis=1)))
    key_raw_all = lax.psum(flat_dot(spread_h, keyval_b), "row")
    all_cos, all_sin = rope_tables(all_places, HEAD_WIDTH)
    key_value_whole = key_form(key_raw_all, key_gain, all_cos, all_sin).astype(bf16)
    key_raw = lax.dynamic_slice_in_dim(key_raw_all, row_place * token_batch, token_batch, 0)
    query_raw = type_one[:, :q_cols]
    middle_b = type_one[:, q_cols : q_cols + l_cols].astype(bf16)
    queries = query_form(query_raw, query_gains, own_cos, own_sin).astype(bf16)
    key_value_heads = (column_place * local_heads + jnp.arange(local_heads, dtype=jnp.int32)) // (
        QUERY_HEADS // KEY_VALUE_HEADS
    )
    every_key = key_value_whole[:, : KEY_VALUE_HEADS * HEAD_WIDTH].reshape(
        grouped_rows, KEY_VALUE_HEADS, HEAD_WIDTH
    )
    every_value = key_value_whole[:, KEY_VALUE_HEADS * HEAD_WIDTH :].reshape(
        grouped_rows, KEY_VALUE_HEADS, HEAD_WIDTH
    )
    key_sel = jnp.take(every_key, key_value_heads, axis=1)
    value_sel = jnp.take(every_value, key_value_heads, axis=1)
    attended, block_peaks, block_totals = attention_forward(
        queries, key_sel, value_sel, own_places, all_places, length, piece_starts
    )
    attended_b = attended.reshape(token_batch, q_cols).astype(bf16)
    joined_b = jnp.concatenate([attended_b, middle_b], axis=1)
    spread_j = spread_row(joined_b)
    type_two = reduce_col(
        jnp.concatenate(
            [flat_dot(spread_j[:, :q_cols], attend_b), flat_dot(spread_j[:, q_cols:], right_b)],
            axis=1,
        )
    )
    projected = type_two[:, :width_a]
    right_raw = type_two[:, width_a:]
    right_n, scale_r = norm_forward(right_raw, w_gains[1])
    laurel = hidden + right_n
    proj_n, scale_p = norm_forward(projected, w_gains[2])
    gated_sum = inputs + proj_n
    mixture = (gated_sum + laurel) * HALF_ROOT
    ffn_n, scale_f = norm_forward(mixture, w_gains[3])
    ffn_b = ffn_n.astype(bf16)
    spread_f = spread_col(ffn_b)
    gateup_pair = jnp.concatenate([gateup_b[0], gateup_b[1]], axis=1)
    gate_up = reduce_row(flat_dot(spread_f, gateup_pair))
    gate_raw = gate_up[:, :ff_here]
    up_raw = gate_up[:, ff_here:]
    act_b = (jax.nn.gelu(gate_raw, approximate=True) * up_raw).astype(bf16)
    spread_a = spread_row(act_b)
    down_raw = reduce_col(flat_dot(spread_a, down_b))
    down_n, scale_d = norm_forward(down_raw, w_gains[4])
    block_out = mixture + down_n
    out_b = block_out.astype(bf16)
    spread_o = spread_col(out_b)
    pgate = reduce_row(flat_dot(spread_o, pergate_b))
    extras = per_layer.astype(single_float)
    pact_b = (jax.nn.gelu(pgate, approximate=True) * extras).astype(bf16)
    spread_p = spread_row(pact_b)
    perproj = reduce_col(flat_dot(spread_p, perproj_b))
    perproj_n, scale_pp = norm_forward(perproj, w_gains[5])
    result = (block_out + perproj_n).astype(bf16)
    upstream = cotangent.astype(single_float)
    gain_grads = [None, None, None, None, None, None]
    d_perproj, gain_grads[5] = norm_backward(perproj, scale_pp, w_gains[5], upstream)
    grads_five = grads_col(d_perproj.astype(bf16))
    dw_perproj = inner_rows(spread_p, grads_five)
    d_pact = reduce_row(against(grads_five, perproj_b))
    gelu_out, pullback = jax.vjp(lambda v: jax.nn.gelu(v, approximate=True), pgate)
    (d_pgate,) = pullback(d_pact * extras)
    grads_four = grads_row(d_pgate.astype(bf16))
    dw_pergate = inner_rows(spread_o, grads_four)
    d_out = upstream + reduce_col(against(grads_four, pergate_b))
    d_down, gain_grads[4] = norm_backward(down_raw, scale_d, w_gains[4], d_out)
    grads_three = grads_col(d_down.astype(bf16))
    dw_down = inner_rows(spread_a, grads_three)
    d_act = reduce_row(against(grads_three, down_b))
    act_out, pullback = jax.vjp(lambda a, b: jax.nn.gelu(a, approximate=True) * b, gate_raw, up_raw)
    d_gate, d_up = pullback(d_act)
    local_two = jnp.concatenate([d_gate, d_up], axis=1).astype(bf16)
    grads_two = grads_row(local_two)
    dw_gateup = jnp.stack(
        [inner_rows(spread_f, grads_two[:, :ff_here]), inner_rows(spread_f, grads_two[:, ff_here:])]
    )
    d_ffn = reduce_col(
        against(grads_two[:, :ff_here], gateup_b[0]) + against(grads_two[:, ff_here:], gateup_b[1])
    )
    d_mix_norm, gain_grads[3] = norm_backward(mixture, scale_f, w_gains[3], d_ffn)
    d_half = (d_out + d_mix_norm) * HALF_ROOT
    d_proj, gain_grads[2] = norm_backward(projected, scale_p, w_gains[2], d_half)
    d_right, gain_grads[1] = norm_backward(right_raw, scale_r, w_gains[1], d_half)
    grads_one = grads_col(jnp.concatenate([d_proj, d_right], axis=1).astype(bf16))
    dw_attend = inner_rows(spread_j[:, :q_cols], grads_one[:, :width_a])
    dw_right = inner_rows(spread_j[:, q_cols:], grads_one[:, width_a:])
    d_joined = reduce_row(
        jnp.concatenate(
            [against(grads_one[:, :width_a], attend_b), against(grads_one[:, width_a:], right_b)],
            axis=1,
        )
    )
    d_attended = d_joined[:, :q_cols].astype(bf16).reshape(token_batch, local_heads, HEAD_WIDTH)
    d_middle = d_joined[:, q_cols:]
    d_queries, d_key_sel, d_value_sel = attention_backward(
        queries,
        key_sel,
        value_sel,
        d_attended,
        block_peaks,
        block_totals,
        own_places,
        all_places,
        length,
        piece_starts,
    )
    single_hot_mask = (
        key_value_heads[:, None] == jnp.arange(KEY_VALUE_HEADS, dtype=jnp.int32)[None, :]
    ).astype(single_float)
    key_gradient = jnp.sum(d_key_sel[:, :, None, :] * single_hot_mask[None, :, :, None], axis=1)
    value_gradient = jnp.sum(d_value_sel[:, :, None, :] * single_hot_mask[None, :, :, None], axis=1)
    key_gradient, value_gradient = lax.psum((key_gradient, value_gradient), ("row", "col"))
    local_key_gradient = lax.dynamic_slice_in_dim(
        key_gradient, row_place * token_batch, token_batch, 0
    ).reshape(token_batch, KEY_VALUE_HEADS * HEAD_WIDTH)
    local_value_gradient = lax.dynamic_slice_in_dim(
        value_gradient, row_place * token_batch, token_batch, 0
    ).reshape(token_batch, KEY_VALUE_HEADS * HEAD_WIDTH)
    query_out, pullback = jax.vjp(
        lambda r, g: query_form(r, g, own_cos, own_sin), query_raw, query_gains
    )
    d_query_raw, dg_query = pullback(d_queries)
    key_tile = jnp.broadcast_to(key_gain, (token_batch, 1, HEAD_WIDTH))
    key_out, pullback = jax.vjp(lambda r, g: key_form(r, g, own_cos, own_sin), key_raw, key_tile)
    d_key_raw, dg_key_rows = pullback(
        jnp.concatenate([local_key_gradient, local_value_gradient], axis=1)
    )
    slice_rows = token_batch // col_devs
    dg_key = jnp.sum(
        lax.dynamic_slice_in_dim(dg_key_rows, column_place * slice_rows, slice_rows, 0), axis=(0, 1)
    )
    grads_zero = grads_row(jnp.concatenate([d_query_raw, d_middle, d_key_raw], axis=1).astype(bf16))
    dw_query = inner_rows(spread_h, grads_zero[:, :q_cols])
    dw_left = inner_rows(spread_h, grads_zero[:, q_cols : q_cols + l_cols])
    key_grad_rows = grads_zero[:, q_cols + l_cols :]
    dw_keyval = inner_rows(spread_h, key_grad_rows)
    slab_width = kv_cols // col_devs
    d_hidden = reduce_col(
        against(grads_zero[:, :q_cols], query_b)
        + against(grads_zero[:, q_cols : q_cols + l_cols], left_b)
        + against(
            lax.dynamic_slice_in_dim(key_grad_rows, column_place * slab_width, slab_width, 1),
            lax.dynamic_slice_in_dim(keyval_b, column_place * slab_width, slab_width, 1),
        )
    )
    d_in, gain_grads[0] = norm_backward(inputs, scale_in, w_gains[0], d_hidden + d_half)
    grad_input = (d_half + d_in).astype(bf16)
    g_query, g_keyval, g_attend, g_gateup, g_down, g_left, g_right, g_pergate, g_perproj = (
        lax.psum_scatter(dw_query, "dp", scatter_dimension=1, tiled=True),
        lax.psum_scatter(dw_keyval, "dp", scatter_dimension=1, tiled=True),
        lax.psum_scatter(dw_attend, "dp", scatter_dimension=1, tiled=True),
        lax.psum_scatter(dw_gateup, "dp", scatter_dimension=2, tiled=True),
        lax.psum_scatter(dw_down, "dp", scatter_dimension=1, tiled=True),
        lax.psum_scatter(dw_left, "dp", scatter_dimension=1, tiled=True),
        lax.psum_scatter(dw_right, "dp", scatter_dimension=1, tiled=True),
        lax.psum_scatter(dw_pergate, "dp", scatter_dimension=1, tiled=True),
        lax.psum_scatter(dw_perproj, "dp", scatter_dimension=1, tiled=True),
    )
    gain_full = lax.dynamic_update_slice_in_dim(
        jnp.zeros((6, MODEL_WIDTH), single_float), jnp.stack(gain_grads), row_place * width_a, 1
    )
    head_full = lax.dynamic_update_slice_in_dim(
        jnp.zeros((QUERY_HEADS + 1, HEAD_WIDTH), single_float),
        dg_query,
        column_place * local_heads,
        0,
    )
    head_full = head_full.at[QUERY_HEADS].add(dg_key)
    logit_here = lax.dynamic_update_slice_in_dim(
        jnp.full((QUERY_HEADS,), NEGATIVE, single_float),
        jnp.max(block_peaks, axis=(0, 2)),
        column_place * local_heads,
        0,
    )

    def combine(left_part, right_part):
        return (
            left_part[0] + right_part[0],
            left_part[1] + right_part[1],
            jnp.maximum(left_part[2], right_part[2]),
        )

    gain_sum, head_sum, logit_top = joined(
        (gain_full, head_full, logit_here), ("dp", "row", "col"), combine
    )
    g_gains = lax.dynamic_slice_in_dim(gain_sum, row_place * width_a, width_a, 1)
    lead_device = (column_place == 0) & (data_at == 0)
    solo_device = lead_device & (row_place == 0)
    squares = jnp.float32(0.0)
    for gradient in (g_query, g_attend, g_gateup, g_down, g_left, g_right, g_pergate, g_perproj):
        squares = squares + jnp.sum(gradient * gradient)
    squares = squares + jnp.where(column_place == 0, jnp.sum(g_keyval * g_keyval), 0.0)
    squares = squares + jnp.where(lead_device, jnp.sum(g_gains * g_gains), 0.0)
    squares = squares + jnp.where(solo_device, jnp.sum(head_sum * head_sum), 0.0)
    grad_norm = jnp.sqrt(lax.psum(squares, ("dp", "row", "col")))
    clip_scale = CLIP / jnp.maximum(grad_norm, CLIP)
    scale_factors = LOGIT_CAP / jnp.maximum(logit_top, LOGIT_CAP)
    weights = (
        w_query,
        key_value_weight,
        w_attend,
        w_gateup,
        w_down,
        w_left,
        w_right,
        w_pergate,
        w_perproj,
        w_gains,
        w_heads,
    )
    moments = (
        m_query,
        key_value_first_moment,
        m_attend,
        m_gateup,
        m_down,
        m_left,
        m_right,
        m_pergate,
        m_perproj,
        m_gains,
        m_heads,
    )
    seconds = (
        v_query,
        key_value_second_moment,
        v_attend,
        v_gateup,
        v_down,
        v_left,
        v_right,
        v_pergate,
        v_perproj,
        v_gains,
        v_heads,
    )
    gradients = (
        g_query,
        g_keyval,
        g_attend,
        g_gateup,
        g_down,
        g_left,
        g_right,
        g_pergate,
        g_perproj,
        g_gains,
        head_sum,
    )
    step_rates = (
        MODEL_WIDTH ** (-0.5),
        MODEL_WIDTH ** (-0.5),
        (QUERY_HEADS * HEAD_WIDTH) ** (-0.5),
        MODEL_WIDTH ** (-0.5),
        FF ** (-0.5),
        MODEL_WIDTH ** (-0.5),
        RANK ** (-0.5),
        MODEL_WIDTH ** (-0.5),
        PLD ** (-0.5),
        GAIN_RATE,
        HEAD_RATE,
    )
    decays = (DECAY, DECAY, DECAY, DECAY, DECAY, DECAY, DECAY, DECAY, DECAY, 0.0, 0.0)
    updated = [
        adamw_step(
            weights[k], moments[k], seconds[k], gradients[k] * clip_scale, step_rates[k], decays[k]
        )
        for k in range(11)
    ]
    head_scale = jnp.sqrt(scale_factors)
    q_width = w_query.shape[1]
    q_head = (
        (column_place * data_devs + data_at) * q_width + jnp.arange(q_width, dtype=jnp.int32)
    ) // HEAD_WIDTH
    q_factor = jnp.sum(
        jnp.where(
            q_head[:, None] == jnp.arange(QUERY_HEADS, dtype=jnp.int32)[None, :],
            head_scale[None, :],
            0.0,
        ),
        axis=1,
    )
    new_query = updated[0][2] * q_factor[None, :]
    kv_width = key_value_weight.shape[1]
    key_value_index = data_at * kv_width + jnp.arange(kv_width, dtype=jnp.int32)
    key_value_scale = jnp.sqrt(
        jnp.min(scale_factors.reshape(KEY_VALUE_HEADS, QUERY_HEADS // KEY_VALUE_HEADS), axis=1)
    )
    key_value_choice = jnp.sum(
        jnp.where(
            (key_value_index // HEAD_WIDTH)[:, None]
            == jnp.arange(KEY_VALUE_HEADS, dtype=jnp.int32)[None, :],
            key_value_scale[None, :],
            0.0,
        ),
        axis=1,
    )
    key_value_factor = jnp.where(
        key_value_index < KEY_VALUE_HEADS * HEAD_WIDTH, key_value_choice, 1.0
    )
    new_keyval = updated[1][2] * key_value_factor[None, :]
    return (
        result,
        grad_input,
        grad_norm,
        scale_factors,
        updated[0][0],
        updated[0][1],
        new_query,
        updated[1][0],
        updated[1][1],
        new_keyval,
        updated[2][0],
        updated[2][1],
        updated[2][2],
        updated[3][0],
        updated[3][1],
        updated[3][2],
        updated[4][0],
        updated[4][1],
        updated[4][2],
        updated[5][0],
        updated[5][1],
        updated[5][2],
        updated[6][0],
        updated[6][1],
        updated[6][2],
        updated[7][0],
        updated[7][1],
        updated[7][2],
        updated[8][0],
        updated[8][1],
        updated[8][2],
        updated[9][0],
        updated[9][1],
        updated[9][2],
        updated[10][0],
        updated[10][1],
        updated[10][2],
    )


def solution(mesh):
    placed = (
        P(("dp", "col"), "row"),
        P(("dp", "row"), "col"),
        P(("dp", "col"), "row"),
        P(),
        P(),
        P("row", ("col", "dp")),
        P("row", ("col", "dp")),
        P("row", ("col", "dp")),
        P("row", "dp"),
        P("row", "dp"),
        P("row", "dp"),
        P("col", ("row", "dp")),
        P("col", ("row", "dp")),
        P("col", ("row", "dp")),
        P(None, "row", ("col", "dp")),
        P(None, "row", ("col", "dp")),
        P(None, "row", ("col", "dp")),
        P("col", ("row", "dp")),
        P("col", ("row", "dp")),
        P("col", ("row", "dp")),
        P("row", ("col", "dp")),
        P("row", ("col", "dp")),
        P("row", ("col", "dp")),
        P("col", ("row", "dp")),
        P("col", ("row", "dp")),
        P("col", ("row", "dp")),
        P("row", ("col", "dp")),
        P("row", ("col", "dp")),
        P("row", ("col", "dp")),
        P("col", ("row", "dp")),
        P("col", ("row", "dp")),
        P("col", ("row", "dp")),
        P(None, "row"),
        P(None, "row"),
        P(None, "row"),
        P(),
        P(),
        P(),
    )
    return jax.shard_map(
        per_device,
        mesh=mesh,
        in_specs=placed,
        out_specs=(
            P(("dp", "col"), "row"),
            P(("dp", "col"), "row"),
            P(),
            P(),
            P("row", ("col", "dp")),
            P("row", ("col", "dp")),
            P("row", ("col", "dp")),
            P("row", "dp"),
            P("row", "dp"),
            P("row", "dp"),
            P("col", ("row", "dp")),
            P("col", ("row", "dp")),
            P("col", ("row", "dp")),
            P(None, "row", ("col", "dp")),
            P(None, "row", ("col", "dp")),
            P(None, "row", ("col", "dp")),
            P("col", ("row", "dp")),
            P("col", ("row", "dp")),
            P("col", ("row", "dp")),
            P("row", ("col", "dp")),
            P("row", ("col", "dp")),
            P("row", ("col", "dp")),
            P("col", ("row", "dp")),
            P("col", ("row", "dp")),
            P("col", ("row", "dp")),
            P("row", ("col", "dp")),
            P("row", ("col", "dp")),
            P("row", ("col", "dp")),
            P("col", ("row", "dp")),
            P("col", ("row", "dp")),
            P("col", ("row", "dp")),
            P(None, "row"),
            P(None, "row"),
            P(None, "row"),
            P(),
            P(),
            P(),
        ),
        check_vma=False,
    )
```

profile of v0, /device:TPU:0, one launch (start us, length us, event | category | flops | bytes accessed | tf_op | source)
XLA Modules:
  0.0 3130.1 jit_solution(6356260707500685288)
XLA Ops:
  9.7 13.4 psum.112
  32.1 30.1 all-gather.20.cloned.1.call-done
  75.5 15.7 all-gather.22.cloned.1.call-done
  103.6 145.4 %all-reduce.14.cloned.1.call-done = f32[1024,1024]{1,0:T(8,128)} async-done(((f32[1024,1024]{1,0:T(8,128)}), f32[1024,1024]{1,0:T(8,128)}) %all-reduce.14.cloned.1.call-update) | async-done | bytes 4194320 | tf_op jit(solution)/shard_map/psum | solution.py:341
  276.2 53.0 %reduce-scatter.21.cloned.1.call-done = f32[256,1056]{0,1:T(8,128)} async-done(((f32[1024,1056]{0,1:T(8,128)}), f32[256,1056]{0,1:T(8,128)}) %reduce-scatter.21.cloned.1.call-update) | async-done | bytes 1081360 | tf_op jit(solution)/shard_map/reduce_scatter | solution.py:51
  349.6 39.1 %all-gather.24.cloned.1.call-done = bf16[1024,1056]{0,1:T(8,128)(2,1)} async-done(((bf16[256,1056]{0,1:T(8,128)(2,1)}), bf16[1024,1056]{0,1:T(8,128)(2,1)}) %all-gather.24.cloned.1.call-update) | async-done | bytes 2162704 | tf_op jit(solution)/shard_map/all_gather | solution.py:55
  391.3 24.7 all-gather.26.cloned.1.call-done
  435.8 12.1 all-reduce.9
  450.5 8.4 psum.116
  459.9 65.5 %all-gather.30.cloned.1.call-done = bf16[2,512,4096]{2,1,0:T(8,128)(2,1)} async-done(((bf16[2,512,1024]{2,1,0:T(8,128)(2,1)}), bf16[2,512,4096]{2,1,0:T(8,128)(2,1)}) %all-gather.30.cloned.1.call-update) | async-done | bytes 8388624 | tf_op jit(solution)/shard_map/all_gather | solution.py:314
  536.4 19.0 fusion.3
  558.1 550.7 %reduce-scatter.25.cloned.1.call-done = f32[256,8192]{1,0:T(8,128)} async-done(((f32[1024,8192]{1,0:T(8,128)}), f32[256,8192]{1,0:T(8,128)}) %reduce-scatter.25.cloned.1.call-update) | async-done | bytes 8388624 | tf_op jit(solution)/shard_map/reduce_scatter | solution.py:51
  1114.0 50.5 %all-gather.34.cloned.1.call-done = bf16[4096,512]{1,0:T(8,128)(2,1)} async-done(((bf16[4096,128]{1,0:T(8,128)(2,1)}), bf16[4096,512]{1,0:T(8,128)(2,1)}) %all-gather.34.cloned.1.call-update) | async-done | bytes 4194320 | tf_op jit(solution)/shard_map/all_gather | solution.py:315
  1164.5 151.9 %all-gather.32.cloned.1.call-done = bf16[1024,4096]{1,0:T(8,128)(2,1)} async-done(((bf16[256,4096]{1,0:T(8,128)(2,1)}), bf16[1024,4096]{1,0:T(8,128)(2,1)}) %all-gather.32.cloned.1.call-update) | async-done | bytes 8388624 | tf_op jit(solution)/shard_map/all_gather | solution.py:55
  1316.4 10.4 fusion.168
  1336.2 11.9 psum.117
  1350.5 8.6 all_gather.97
  1361.7 8.4 all_gather.99
  1370.1 13.2 reduce-scatter.29.cloned.1.call-done
  1384.3 14.1 all_gather.98
  1409.5 12.0 psum.118
  1423.1 8.4 psum.119
  1433.8 8.7 all-gather.38.cloned.1.call-done
  1445.1 23.2 reduce-scatter.33.cloned.1.call-done
  1469.3 14.2 all_gather.101
  1495.4 11.9 psum.120
  1517.8 12.8 fusion.173
  1530.7 281.6 %reduce-scatter.37.cloned.1.call-done = f32[256,4096]{1,0:T(8,128)} async-done(((f32[1024,4096]{1,0:T(8,128)}), f32[256,4096]{1,0:T(8,128)}) %reduce-scatter.37.cloned.1.call-update) | async-done | bytes 4194320 | tf_op jit(solution)/shard_map/reduce_scatter | solution.py:51
  1821.3 287.4 %all-gather.42.cloned.1.call-done = bf16[1024,8192]{1,0:T(8,128)(2,1)} async-done(((bf16[256,8192]{1,0:T(8,128)(2,1)}), bf16[1024,8192]{1,0:T(8,128)(2,1)}) %all-gather.42.cloned.1.call-update) | async-done | bytes 16777232 | tf_op jit(solution)/shard_map/all_gather | solution.py:67
  2136.6 11.9 psum.121
  2163.8 10.3 all-gather.44.cloned.1.call-done
  2181.2 79.7 %reduce-scatter.41.cloned.1.call-done = f32[256,1056]{0,1:T(8,128)} async-done(((f32[1024,1056]{0,1:T(8,128)}), f32[256,1056]{0,1:T(8,128)}) %reduce-scatter.41.cloned.1.call-update) | async-done | bytes 1081360 | tf_op jit(solution)/shard_map/reduce_scatter | solution.py:51
  2308.5 84.9 %all-reduce.18.cloned.1.call-done = (f32[1024,2,256]{2,0,1:T(8,128)}, f32[1024,2,256]{2,0,1:T(8,128)}) async-done(((f32[1024,2,256]{2,0,1:T(8,128)}, f32[1024,2,256]{2,0,1:T(8,128)}), (f32[1024,2,256]{2,0,1:T(8,128)}, f32[1024,2,256]{2,0,1:T(8,128)})) %all-reduce.18.cloned.1.call-update) | async-done | bytes 4194320 | tf_op jit(solution)/shard_map/psum | solution.py:456
  2399.9 81.6 %all-gather.46.cloned.1.call-done = bf16[1024,2080]{0,1:T(8,128)(2,1)} async-done(((bf16[256,2080]{0,1:T(8,128)(2,1)}), bf16[1024,2080]{0,1:T(8,128)(2,1)}) %all-gather.46.cloned.1.call-update) | async-done | bytes 4259856 | tf_op jit(solution)/shard_map/all_gather | solution.py:67
  2491.4 12.2 fusion.174
  2547.4 37.7 %all-gather = f32[32,1,8]{2,1,0:T(1,128)S(1)} all-gather(f32[1,1,8]{2,1,0:T(1,128)S(1)} %dynamic_update_slice.24), channel_id=1, replica_groups=mesh['dp'=4,'row'=4,'col'=2] {'dp','row','col'}, dimensions={0}, use_global_device_ids=true | all-gather | bytes 1056 | tf_op jit(solution)/shard_map/all_gather | solution.py:32
  2589.1 53.6 %reduce-scatter.51.cloned.1.call-done = f32[4096,128]{1,0:T(8,128)} async-done(((f32[4096,512]{1,0:T(8,128)}), f32[4096,128]{1,0:T(8,128)}) %reduce-scatter.51.cloned.1.call-update) | async-done | bytes 2097168 | tf_op jit(solution)/shard_map/reduce_scatter | solution.py:497
  2645.4 24.1 reduce-scatter.53.cloned.1.call-done
  2670.8 37.7 %reduce-scatter.47.cloned.1.call-done = f32[1024,128]{1,0:T(8,128)} async-done(((f32[1024,512]{1,0:T(8,128)}), f32[1024,128]{1,0:T(8,128)}) %reduce-scatter.47.cloned.1.call-update) | async-done | bytes 524304 | tf_op jit(solution)/shard_map/reduce_scatter | solution.py:495
  2710.6 42.7 %all_gather.110 = f32[32,9,256]{2,1,0:T(8,128)S(1)} all-gather(f32[1,9,256]{2,1,0:T(8,128)S(1)} %scatter-add.4), channel_id=1, replica_groups=mesh['dp'=4,'row'=4,'col'=2] {'dp','row','col'}, dimensions={0}, use_global_device_ids=true | all-gather | bytes 304128 | tf_op jit(solution)/shard_map/all_gather | solution.py:32
  2754.9 11.7 psum.126
  2768.1 24.4 reduce-scatter.59.cloned.1.call-done
  2794.9 36.2 %reduce-scatter.45.cloned.1.call-done = f32[512,256]{1,0:T(8,128)} async-done(((f32[512,1024]{1,0:T(8,128)}), f32[512,256]{1,0:T(8,128)}) %reduce-scatter.45.cloned.1.call-update) | async-done | bytes 524304 | tf_op jit(solution)/shard_map/reduce_scatter | solution.py:493
  2834.2 57.4 %all-gather.48.cloned.1.call-done = f32[32,6,2048]{2,1,0:T(8,128)} async-done(((f32[1,6,2048]{2,1,0:T(8,128)}), f32[32,6,2048]{2,1,0:T(8,128)}) %all-gather.48.cloned.1.call-update) | async-done | bytes 1572880 | tf_op jit(solution)/shard_map/all_gather | solution.py:32
  2892.4 50.2 %while.13 = (s32[]{:T(128)}, f32[6,2048]{1,0:T(8,128)S(1)}, f32[9,256]{1,0:T(8,128)S(1)}, f32[8]{0:T(128)S(1)}, f32[32,6,2048]{2,1,0:T(8,128)}, /*index=5*/f32[3...) while((s32[]{:T(128)}, f32[6,2048]{1,0:T(8,128)S(1)}, ...), condition=%wide.region_83.85_spmd, body=%wide.region_82.84_spmd.sunk | while | flops 14605 | bytes 175355 | solution.py:37
  2945.5 102.0 %reduce-scatter.49.cloned.1.call-done = f32[2,512,1024]{2,1,0:T(8,128)} async-done(((f32[2,512,4096]{2,1,0:T(8,128)}), f32[2,512,1024]{2,1,0:T(8,128)}) %reduce-scatter.49.cloned.1.call-update) | async-done | bytes 4194320 | tf_op jit(solution)/shard_map/reduce_scatter | solution.py:496
  3055.4 39.5 %psum.127 = f32[]{:T(128)} all-reduce(f32[]{:T(128)S(6)} %add.660), channel_id=1, replica_groups=mesh['dp'=4,'row'=4,'col'=2] {'dp','row','col'}, use_global_device_ids=true, to_apply=%region_86.88 | all-reduce | flops 1 | bytes 8 | tf_op jit(solution)/shard_map/psum | solution.py:539
  3098.4 10.9 multiply_subtract_fusion
  (631 shorter events, 438.1 us)
Async XLA Ops:
  7.2 24.8 all-gather.18.cloned.1.call-start
  8.2 439.7 %copy-start.85 = (f32[1,512]{1,0:T(1,128)}, f32[1,512]{1,0:T(1,128)S(1)}, u32[]{:S(2)}) copy-start(f32[1,512]{1,0:T(1,128)S(1)} %get-tuple-element.725) | copy-start | bytes 6148
  9.5 438.4 %copy-start.1 = (bf16[512,512]{0,1:T(8,128)(2,1)}, bf16[512,512]{0,1:T(8,128)(2,1)S(1)}, u32[]{:S(2)}) copy-start(bf16[512,512]{0,1:T(8,128)(2,1)S(1)} %copy.303) | copy-start | bytes 1572868
  23.7 424.2 %copy-start.87 = (f32[512,1]{0,1:T(1,128)}, f32[512,1]{0,1:T(1,128)S(1)}, u32[]{:S(2)}) copy-start(f32[512,1]{0,1:T(1,128)S(1)} %get-tuple-element.686) | copy-start | bytes 6148
  24.7 37.5 %all-gather.20.cloned.1.call-start = ((), (), s32[]{:S(2)}) async-start(), calls=%async_computation.21 | async-start | bytes 1310720 | tf_op jit(solution)/shard_map/all_gather | solution.py:312
  26.5 64.7 %all-gather.22.cloned.1.call-start = ((), (), s32[]{:S(2)}) async-start(), calls=%async_computation.23 | async-start | bytes 1310720 | tf_op jit(solution)/shard_map/all_gather | solution.py:311
  27.3 221.6 %all-reduce.14.cloned.1.call-start = ((), (), s32[]{:S(2)}) async-start(), calls=%async_computation.22 | async-start | bytes 8388608 | tf_op jit(solution)/shard_map/psum | solution.py:341
  67.0 262.2 %reduce-scatter.21.cloned.1.call-start = ((), (), s32[]{:S(2)}) async-start(), calls=%async_computation.24 | async-start | bytes 5406720 | tf_op jit(solution)/shard_map/reduce_scatter | solution.py:51
  95.8 292.9 %all-gather.24.cloned.1.call-start = ((), (), s32[]{:S(2)}) async-start(), calls=%async_computation.25 | async-start | bytes 2703360 | tf_op jit(solution)/shard_map/all_gather | solution.py:55
  340.7 75.3 %all-gather.26.cloned.1.call-start = ((), (), s32[]{:S(2)}) async-start(), calls=%async_computation.26 | async-start | bytes 1310720 | tf_op jit(solution)/shard_map/all_gather | solution.py:313
  341.5 92.5 %reduce-scatter.23.cloned.1.call-start = ((), (), s32[]{:S(2)}) async-start(), calls=%async_computation.27 | async-start | bytes 6291456 | tf_op jit(solution)/shard_map/reduce_scatter | solution.py:59
  421.8 103.6 %all-gather.30.cloned.1.call-start = ((), (), s32[]{:S(2)}) async-start(), calls=%async_computation.29 | async-start | bytes 10485760 | tf_op jit(solution)/shard_map/all_gather | solution.py:314
  425.8 110.7 %all-gather.28.cloned.1.call-start = ((), (), s32[]{:S(2)}) async-start(), calls=%async_computation.28 | async-start | bytes 1572864 | tf_op jit(solution)/shard_map/all_gather | solution.py:47
  459.8 649.0 %reduce-scatter.25.cloned.1.call-start = ((), (), s32[]{:S(2)}) async-start(), calls=%async_computation.30 | async-start | bytes 41943040 | tf_op jit(solution)/shard_map/reduce_scatter | solution.py:51
  555.4 609.1 %all-gather.34.cloned.1.call-start = ((), (), s32[]{:S(2)}) async-start(), calls=%async_computation.32 | async-start | bytes 5242880 | tf_op jit(solution)/shard_map/all_gather | solution.py:315
  558.1 758.3 %all-gather.32.cloned.1.call-start = ((), (), s32[]{:S(2)}) async-start(), calls=%async_computation.31 | async-start | bytes 10485760 | tf_op jit(solution)/shard_map/all_gather | solution.py:55
  1114.0 220.9 %reduce-scatter.27.cloned.1.call-start = ((), (), s32[]{:S(2)}) async-start(), calls=%async_computation.33 | async-start | bytes 3145728 | tf_op jit(solution)/shard_map/reduce_scatter | solution.py:59
  1326.9 32.2 %all-gather.36.cloned.1.call-start = ((), (), s32[]{:S(2)}) async-start(), calls=%async_computation.34 | async-start | bytes 1572864 | tf_op jit(solution)/shard_map/all_gather | solution.py:47
  1350.4 32.9 %reduce-scatter.29.cloned.1.call-start = ((), (), s32[]{:S(2)}) async-start(), calls=%async_computation.35 | async-start | bytes 655360 | tf_op jit(solution)/shard_map/reduce_scatter | solution.py:51
  1361.6 46.5 %reduce-scatter.31.cloned.1.call-start = ((), (), s32[]{:S(2)}) async-start(), calls=%async_computation.36 | async-start | bytes 3145728 | tf_op jit(solution)/shard_map/reduce_scatter | solution.py:59
  1400.2 42.3 %all-gather.38.cloned.1.call-start = ((), (), s32[]{:S(2)}) async-start(), calls=%async_computation.37 | async-start | bytes 1572864 | tf_op jit(solution)/shard_map/all_gather | solution.py:63
  1433.7 34.6 %reduce-scatter.33.cloned.1.call-start = ((), (), s32[]{:S(2)}) async-start(), calls=%async_computation.38 | async-start | bytes 655360 | tf_op jit(solution)/shard_map/reduce_scatter | solution.py:51
  1445.0 48.1 %reduce-scatter.35.cloned.1.call-start = ((), (), s32[]{:S(2)}) async-start(), calls=%async_computation.39 | async-start | bytes 3145728 | tf_op jit(solution)/shard_map/reduce_scatter | solution.py:59
  1485.3 32.5 %all-gather.40.cloned.1.call-start = ((), (), s32[]{:S(2)}) async-start(), calls=%async_computation.40 | async-start | bytes 1572864 | tf_op jit(solution)/shard_map/all_gather | solution.py:63
  1510.4 301.8 %reduce-scatter.37.cloned.1.call-start = ((), (), s32[]{:S(2)}) async-start(), calls=%async_computation.41 | async-start | bytes 20971520 | tf_op jit(solution)/shard_map/reduce_scatter | solution.py:51
  1530.6 578.1 %all-gather.42.cloned.1.call-start = ((), (), s32[]{:S(2)}) async-start(), calls=%async_computation.42 | async-start | bytes 20971520 | tf_op jit(solution)/shard_map/all_gather | solution.py:67
  1821.0 313.3 %reduce-scatter.39.cloned.1.call-start = ((), (), s32[]{:S(2)}) async-start(), calls=%async_computation.43 | async-start | bytes 3145728 | tf_op jit(solution)/shard_map/reduce_scatter | solution.py:59
  2126.4 47.6 %all-gather.44.cloned.1.call-start = ((), (), s32[]{:S(2)}) async-start(), calls=%async_computation.44 | async-start | bytes 3145728 | tf_op jit(solution)/shard_map/all_gather | solution.py:63
  2163.8 97.1 %reduce-scatter.41.cloned.1.call-start = ((), (), s32[]{:S(2)}) async-start(), calls=%async_computation.45 | async-start | bytes 5406720 | tf_op jit(solution)/shard_map/reduce_scatter | solution.py:51
  2180.7 212.8 %all-reduce.18.cloned.1.call-start = ((), (), s32[]{:S(2)}) async-start(), calls=%async_computation.58 | async-start | bytes 8388608 | tf_op jit(solution)/shard_map/psum | solution.py:456
  2295.9 185.6 %all-gather.46.cloned.1.call-start = ((), (), s32[]{:S(2)}) async-start(), calls=%async_computation.46 | async-start | bytes 5324800 | tf_op jit(solution)/shard_map/all_gather | solution.py:67
  2399.7 123.0 %reduce-scatter.43.cloned.1.call-start = ((), (), s32[]{:S(2)}) async-start(), calls=%async_computation.47 | async-start | bytes 3145728 | tf_op jit(solution)/shard_map/reduce_scatter | solution.py:59
  2488.8 96.4 %reduce-scatter.57.cloned.1.call-start = ((), (), s32[]{:S(2)}) async-start(), calls=%async_computation.54 | async-start | bytes 327680 | tf_op jit(solution)/shard_map/reduce_scatter | solution.py:501
  2490.0 96.5 %reduce-scatter.55.cloned.1.call-start = ((), (), s32[]{:S(2)}) async-start(), calls=%async_computation.53 | async-start | bytes 327680 | tf_op jit(solution)/shard_map/reduce_scatter | solution.py:500
  2491.3 151.4 %reduce-scatter.51.cloned.1.call-start = ((), (), s32[]{:S(2)}) async-start(), calls=%async_computation.51 | async-start | bytes 10485760 | tf_op jit(solution)/shard_map/reduce_scatter | solution.py:497
  2503.6 165.9 %reduce-scatter.53.cloned.1.call-start = ((), (), s32[]{:S(2)}) async-start(), calls=%async_computation.52 | async-start | bytes 81920 | tf_op jit(solution)/shard_map/reduce_scatter | solution.py:499
  2507.1 201.5 %reduce-scatter.47.cloned.1.call-start = ((), (), s32[]{:S(2)}) async-start(), calls=%async_computation.49 | async-start | bytes 2621440 | tf_op jit(solution)/shard_map/reduce_scatter | solution.py:495
  2511.7 241.9 %all-reduce.16.cloned.1.call-start = ((), (), s32[]{:S(2)}) async-start(), calls=%async_computation.57 | async-start | bytes 131072
  2513.7 278.8 %reduce-scatter.59.cloned.1.call-start = ((), (), s32[]{:S(2)}) async-start(), calls=%async_computation.55 | async-start | bytes 2621440 | tf_op jit(solution)/shard_map/reduce_scatter | solution.py:494
  2518.0 313.1 %reduce-scatter.45.cloned.1.call-start = ((), (), s32[]{:S(2)}) async-start(), calls=%async_computation.48 | async-start | bytes 2621440 | tf_op jit(solution)/shard_map/reduce_scatter | solution.py:493
  2522.4 369.2 %all-gather.48.cloned.1.call-start = ((), (), s32[]{:S(2)}) async-start(), calls=%async_computation.56 | async-start | bytes 2162688 | tf_op jit(solution)/shard_map/all_gather | solution.py:32
  2525.2 522.3 %reduce-scatter.49.cloned.1.call-start = ((), (), s32[]{:S(2)}) async-start(), calls=%async_computation.50 | async-start | bytes 20971520 | tf_op jit(solution)/shard_map/reduce_scatter | solution.py:496
  2767.0 329.3 %copy-start.92 = (f32[9,256]{1,0:T(8,128)S(1)}, f32[9,256]{1,0:T(8,128)}, u32[]{:S(2)}) copy-start(f32[9,256]{1,0:T(8,128)} %param.79) | copy-start | bytes 27652
  2767.0 329.3 %copy-start.95 = (f32[9,256]{1,0:T(8,128)S(1)}, f32[9,256]{1,0:T(8,128)}, u32[]{:S(2)}) copy-start(f32[9,256]{1,0:T(8,128)} %param.81) | copy-start | bytes 27652
  2767.0 329.9 %copy-start.36 = (f32[1024,128]{1,0:T(8,128)S(1)}, f32[1024,128]{1,0:T(8,128)}, u32[]{:S(2)}) copy-start(f32[1024,128]{1,0:T(8,128)} %param.55) | copy-start | bytes 1572868
  2767.0 329.9 %copy-start.42 = (f32[1024,128]{1,0:T(8,128)S(1)}, f32[1024,128]{1,0:T(8,128)}, u32[]{:S(2)}) copy-start(f32[1024,128]{1,0:T(8,128)} %reduce-scatter.47.cloned.1.call-done) | copy-start | bytes 1572868
  2767.0 329.9 %copy-start.55 = (f32[1024,128]{1,0:T(8,128)S(1)}, f32[1024,128]{1,0:T(8,128)}, u32[]{:S(2)}) copy-start(f32[1024,128]{1,0:T(8,128)} %param.57) | copy-start | bytes 1572868
  2767.1 329.9 %copy-start.56 = (f32[1024,128]{1,0:T(8,128)S(1)}, f32[1024,128]{1,0:T(8,128)}, u32[]{:S(2)}) copy-start(f32[1024,128]{1,0:T(8,128)} %param.56) | copy-start | bytes 1572868
  (109 other events, 4400.7 us)
Sparse Core Ops, SparseCore 0:
  24.8 7.2 all-gather.17
  34.5 27.6 all-gather.19
  64.6 26.5 all-gather.21
  94.0 154.9 all-reduce.13
  251.3 77.8 reduce-scatter.20
  340.8 47.7 all-gather.23
  391.2 24.7 all-gather.25
  422.0 12.0 reduce-scatter.22
  436.5 88.8 all-gather.29
  527.4 9.0 all-gather.27
  555.5 553.2 reduce-scatter.24
  1111.2 53.2 all-gather.33
  1166.7 149.6 all-gather.31
  1327.0 7.8 reduce-scatter.26
  1350.5 7.1 all-gather.35
  1361.7 21.5 reduce-scatter.28
  1400.3 7.7 reduce-scatter.30
  1433.9 8.6 all-gather.37
  1445.5 22.8 reduce-scatter.32
  1485.4 7.6 reduce-scatter.34
  1510.6 7.1 all-gather.39
  1530.7 281.4 reduce-scatter.36
  1821.2 287.4 all-gather.41
  2126.6 7.7 reduce-scatter.38
  2163.9 10.1 all-gather.43
  2180.8 80.0 reduce-scatter.40
  2296.0 97.3 all-reduce.17
  2399.8 81.6 all-gather.45
  2488.9 7.7 reduce-scatter.42
  2500.1 25.2 reduce-scatter.56
  2528.8 24.0 reduce-scatter.54
  2556.2 86.4 reduce-scatter.50
  2645.8 23.6 reduce-scatter.52
  2673.3 35.2 reduce-scatter.46
  2712.0 41.5 all-reduce.15
  2757.2 35.1 reduce-scatter.58
  2795.9 35.1 reduce-scatter.44
  2835.1 56.4 all-gather.47
  2894.8 152.6 reduce-scatter.48
where the time goes:
time: 3140 us; the launch traced here: 3130 us
  waiting for transfers between devices  2390 us (76%)
  blocking collectives  291 us (9%)
  other arithmetic  207 us (7%)
  matrix products  155 us (5%)
  local copies, waits for them, and re-layouts  57.5 us (2%)
    reduce_scatter x6, waiting for transfers between devices, reduce_row(): return lax.psum_scatter(values_in, 'row', scatter_dimension=0, tiled=True)  1000 us
    all_gather x2, waiting for transfers between devices, grads_row(): return lax.all_gather(values_in, 'row', axis=0, tiled=True)  369 us
    all_gather x2, waiting for transfers between devices, spread_row(): return lax.all_gather(values_in, 'row', axis=0, tiled=True)  191 us
    psum x1, waiting for transfers between devices, per_device(): key_raw_all = lax.psum(flat_dot(spread_h, keyval_b), 'row')  145 us
    psum x10, blocking collectives, row_total(): return lax.psum(values_in, 'row')  110 us
    reduce_scatter x1, waiting for transfers between devices, per_device(): lax.psum_scatter(dw_gateup, 'dp', scatter_dimension=2, tiled=True)  102 us
    psum x1, waiting for transfers between devices, per_device(): lax.psum((key_gradient, value_gradient), ('row', 'col'))  84.9 us
    all_gather x2, blocking collectives, joined(): gathered = jax.tree.map(lambda a: lax.all_gather(a, axis), part)  80.5 us
  transfers between devices with their start and end apart: 39, of which 35 were waited for; matrix products, arithmetic and copies ran while one was open for 7% of the time, Pallas kernels for 0%

commit v1 on v0

--- a/solution.py
+++ b/solution.py
@@ -1,6 +1,8 @@
 import jax
 import jax.numpy as jnp
 from jax import lax
+from jax.experimental import pallas as pl
+from jax.experimental.pallas import tpu as pltpu
 from jax.sharding import PartitionSpec as P
 
 MODEL_WIDTH = 2048
@@ -256,6 +258,1012 @@
         moment_one,
         moment_two,
         weight - rate * (mean_step / (jnp.sqrt(spread) + ADAM_EPS) + decay * weight),
+    )
+
+
+MESH = pl.DeviceIdType.MESH
+LOW = jnp.bfloat16
+FULL = jnp.float32
+
+
+def cost(micros, flops=0):
+    return pl.CostEstimate(
+        flops=flops, bytes_accessed=int(micros * 3.0e6), transcendentals=0
+    )
+
+
+def params(ident, mebibytes=48):
+    return pltpu.CompilerParams(
+        collective_id=ident, has_side_effects=True, vmem_limit_bytes=mebibytes * 2**20
+    )
+
+
+def push(source, target, send, recv, device):
+    return pltpu.make_async_remote_copy(
+        source, target, send, recv, device_id=device, device_id_type=MESH
+    )
+
+
+def greet_line(me, count, column, core):
+    barrier = pltpu.get_barrier_semaphore()
+
+    @pl.when(me > 0)
+    def _():
+        pl.semaphore_signal(barrier, inc=1, device_id={"row": me - 1}, device_id_type=MESH)
+
+    @pl.when(me < count - 1)
+    def _():
+        pl.semaphore_signal(barrier, inc=1, device_id={"row": me + 1}, device_id_type=MESH)
+
+    if core:
+        pl.semaphore_signal(barrier, inc=1, device_id={"col": 1 - column}, device_id_type=MESH)
+
+    ends = (me == 0) | (me == count - 1)
+
+    @pl.when(ends)
+    def _():
+        pl.semaphore_wait(barrier, 1 + int(core))
+
+    @pl.when(jnp.logical_not(ends))
+    def _():
+        pl.semaphore_wait(barrier, 2 + int(core))
+
+
+def line_gather(block, ident, core, micros):
+    count = lax.axis_size("row")
+
+    def kernel(x_ref, o_ref, send_l, send_r, send_c, recv_l, recv_r, recv_c, local):
+        me = lax.axis_index("row")
+        column = lax.axis_index("col")
+
+        def slot(source):
+            return o_ref.at[column, source] if core else o_ref.at[source]
+
+        def other(source):
+            return o_ref.at[1 - column, source]
+
+        def to_left(source, k):
+            origin = x_ref if k == 0 else slot(source)
+            return push(origin, slot(source), send_l.at[k], recv_r.at[k], {"row": me - 1})
+
+        def to_right(source, k):
+            origin = x_ref if k == 0 else slot(source)
+            return push(origin, slot(source), send_r.at[k], recv_l.at[k], {"row": me + 1})
+
+        def to_core(source, k):
+            origin = x_ref if k == 0 else slot(source)
+            return push(origin, slot(source), send_c.at[k], recv_c.at[k], {"col": 1 - column})
+
+        def from_core(source, k):
+            return push(other(source), other(source), send_c.at[k], recv_c.at[k], {"col": 1 - column})
+
+        greet_line(me, count, column, core)
+
+        @pl.when(me > 0)
+        def _():
+            to_left(me, 0).start()
+
+        @pl.when(me < count - 1)
+        def _():
+            to_right(me, 0).start()
+
+        if core:
+            to_core(me, 0).start()
+        own = pltpu.make_async_copy(x_ref, slot(me), local)
+        own.start()
+        for k in range(1, count):
+
+            @pl.when(me - k >= 0)
+            def _():
+                push(slot(me - k), slot(me - k), send_r.at[k], recv_l.at[k - 1], {"row": me - 1}).wait_recv()
+
+                @pl.when(me < count - 1)
+                def _():
+                    to_right(me - k, k).start()
+
+                if core:
+                    to_core(me - k, k).start()
+
+            @pl.when(me + k < count)
+            def _():
+                push(slot(me + k), slot(me + k), send_l.at[k], recv_r.at[k - 1], {"row": me + 1}).wait_recv()
+
+                @pl.when(me > 0)
+                def _():
+                    to_left(me + k, k).start()
+
+                if core:
+                    to_core(me + k, count - 1 + k).start()
+
+        own.wait()
+
+        @pl.when(me > 0)
+        def _():
+            to_left(me, 0).wait_send()
+
+        @pl.when(me < count - 1)
+        def _():
+            to_right(me, 0).wait_send()
+
+        if core:
+            to_core(me, 0).wait_send()
+            from_core(me, 0).wait_recv()
+        for k in range(1, count):
+
+            @pl.when(me - k >= 0)
+            def _():
+                @pl.when(me < count - 1)
+                def _():
+                    to_right(me - k, k).wait_send()
+
+                if core:
+                    to_core(me - k, k).wait_send()
+                    from_core(me - k, k).wait_recv()
+
+            @pl.when(me + k < count)
+            def _():
+                @pl.when(me > 0)
+                def _():
+                    to_left(me + k, k).wait_send()
+
+                if core:
+                    to_core(me + k, count - 1 + k).wait_send()
+                    from_core(me + k, count - 1 + k).wait_recv()
+
+    shape = ((2, count) if core else (count,)) + block.shape
+    dma = pltpu.SemaphoreType.DMA
+    return pl.pallas_call(
+        kernel,
+        out_shape=jax.ShapeDtypeStruct(shape, block.dtype),
+        in_specs=[pl.BlockSpec(memory_space=pl.ANY)],
+        out_specs=pl.BlockSpec(memory_space=pl.ANY),
+        scratch_shapes=[
+            dma((count,)),
+            dma((count,)),
+            dma((2 * count,)),
+            dma((count,)),
+            dma((count,)),
+            dma((2 * count,)),
+            dma,
+        ],
+        compiler_params=params(ident),
+        cost_estimate=cost(micros),
+    )(block)
+
+
+def line_reduce(parts, ident, core, micros):
+    count = lax.axis_size("row")
+    high, wide = parts.shape[-2:]
+    chunk = min(high, max(16, 65536 // wide))
+
+    def kernel(x_ref, o_ref, c_buf, l_buf, r_buf, s_buf, send_l, send_r, send_c, recv_l, recv_r, recv_c):
+        me = lax.axis_index("row")
+        column = lax.axis_index("col")
+
+        def mine(q):
+            return x_ref.at[column, q] if core else x_ref.at[q]
+
+        def core_copy(q):
+            return push(x_ref.at[1 - column, q], c_buf.at[q], send_c.at[q], recv_c.at[q], {"col": 1 - column})
+
+        def left_copy(q):
+            return push(s_buf.at[q], l_buf.at[q], send_l.at[q], recv_l.at[q], {"row": me - 1})
+
+        def right_copy(q):
+            return push(s_buf.at[q], r_buf.at[q], send_r.at[q], recv_r.at[q], {"row": me + 1})
+
+        def left_arrival(q):
+            return push(s_buf.at[q], l_buf.at[q], send_l.at[q], recv_l.at[q], {"row": me + 1})
+
+        def right_arrival(q):
+            return push(s_buf.at[q], r_buf.at[q], send_r.at[q], recv_r.at[q], {"row": me - 1})
+
+        def added(target, terms):
+            @pl.loop(0, high // chunk)
+            def _(at):
+                rows = pl.ds(pl.multiple_of(at * chunk, chunk), chunk)
+                total = terms[0][rows].astype(FULL)
+                for term in terms[1:]:
+                    total = total + term[rows].astype(FULL)
+                target[rows] = total.astype(target.dtype)
+
+        def base(q):
+            return [mine(q)] + ([c_buf.at[q]] if core else [])
+
+        greet_line(me, count, column, core)
+        if core:
+            for q in range(count):
+                core_copy(q).start()
+
+        def leftward(q):
+            @pl.when(me > q)
+            def _():
+                if core:
+                    core_copy(q).wait_recv()
+
+                @pl.when(me < count - 1)
+                def _():
+                    left_arrival(q).wait_recv()
+                    added(s_buf.at[q], base(q) + [l_buf.at[q]])
+
+                @pl.when(me == count - 1)
+                def _():
+                    added(s_buf.at[q], base(q))
+
+                left_copy(q).start()
+
+        def rightward(q):
+            @pl.when(me < q)
+            def _():
+                if core:
+                    core_copy(q).wait_recv()
+
+                @pl.when(me > 0)
+                def _():
+                    right_arrival(q).wait_recv()
+                    added(s_buf.at[q], base(q) + [r_buf.at[q]])
+
+                @pl.when(me == 0)
+                def _():
+                    added(s_buf.at[q], base(q))
+
+                right_copy(q).start()
+
+        for j in range(count - 1):
+
+            @pl.when(me < count // 2)
+            def _():
+                rightward(count - 1 - j)
+
+            leftward(j)
+
+            @pl.when(me >= count // 2)
+            def _():
+                rightward(count - 1 - j)
+
+        if core:
+            core_copy(me).wait_recv()
+
+        @pl.when(me < count - 1)
+        def _():
+            left_arrival(me).wait_recv()
+
+        @pl.when(me > 0)
+        def _():
+            right_arrival(me).wait_recv()
+
+        @pl.when(me == 0)
+        def _():
+            added(o_ref, base(me) + [l_buf.at[me]])
+
+        @pl.when(me == count - 1)
+        def _():
+            added(o_ref, base(me) + [r_buf.at[me]])
+
+        @pl.when((me > 0) & (me < count - 1))
+        def _():
+            added(o_ref, base(me) + [l_buf.at[me], r_buf.at[me]])
+
+        for q in range(count):
+            if core:
+                core_copy(q).wait_send()
+
+            @pl.when(me > q)
+            def _():
+                left_copy(q).wait_send()
+
+            @pl.when(me < q)
+            def _():
+                right_copy(q).wait_send()
+
+    dma = pltpu.SemaphoreType.DMA
+    slots = (count, high, wide)
+    vmem = pl.BlockSpec(memory_space=pltpu.VMEM)
+    return pl.pallas_call(
+        kernel,
+        out_shape=jax.ShapeDtypeStruct((high, wide), FULL),
+        in_specs=[vmem],
+        out_specs=vmem,
+        scratch_shapes=[
+            pltpu.VMEM(slots if core else (1, 16, 128), parts.dtype),
+            pltpu.VMEM(slots, parts.dtype),
+            pltpu.VMEM(slots, parts.dtype),
+            pltpu.VMEM(slots, parts.dtype),
+        ]
+        + [dma((count,))] * 6,
+        compiler_params=params(ident),
+        cost_estimate=cost(micros),
+    )(parts)
+
+
+def core_gather(block, ident):
+    def kernel(x_ref, o_ref, send, recv, local):
+        column = lax.axis_index("col")
+        barrier = pltpu.get_barrier_semaphore()
+        pl.semaphore_signal(barrier, inc=1, device_id={"col": 1 - column}, device_id_type=MESH)
+        pl.semaphore_wait(barrier, 1)
+        copy = push(x_ref, o_ref.at[column], send, recv, {"col": 1 - column})
+        copy.start()
+        own = pltpu.make_async_copy(x_ref, o_ref.at[column], local)
+        own.start()
+        own.wait()
+        copy.wait_send()
+        push(x_ref, o_ref.at[1 - column], send, recv, {"col": 1 - column}).wait_recv()
+
+    dma = pltpu.SemaphoreType.DMA
+    return pl.pallas_call(
+        kernel,
+        out_shape=jax.ShapeDtypeStruct((2,) + block.shape, block.dtype),
+        in_specs=[pl.BlockSpec(memory_space=pl.ANY)],
+        out_specs=pl.BlockSpec(memory_space=pl.ANY),
+        scratch_shapes=[dma, dma, dma],
+        compiler_params=params(ident),
+        cost_estimate=cost(6),
+    )(block)
+
+
+def core_reduce(parts, ident):
+    def kernel(x_ref, o_ref, buf, send, recv):
+        column = lax.axis_index("col")
+        barrier = pltpu.get_barrier_semaphore()
+        pl.semaphore_signal(barrier, inc=1, device_id={"col": 1 - column}, device_id_type=MESH)
+        pl.semaphore_wait(barrier, 1)
+        copy = push(x_ref.at[1 - column], buf, send, recv, {"col": 1 - column})
+        copy.start()
+        copy.wait()
+
+        @pl.loop(0, o_ref.shape[0] // 64)
+        def _(at):
+            rows = pl.ds(pl.multiple_of(at * 64, 64), 64)
+            o_ref[rows] = x_ref[column, rows].astype(FULL) + buf[rows].astype(FULL)
+
+    dma = pltpu.SemaphoreType.DMA
+    vmem = pl.BlockSpec(memory_space=pltpu.VMEM)
+    return pl.pallas_call(
+        kernel,
+        out_shape=jax.ShapeDtypeStruct(parts.shape[1:], FULL),
+        in_specs=[vmem],
+        out_specs=vmem,
+        scratch_shapes=[pltpu.VMEM(parts.shape[1:], parts.dtype), dma, dma],
+        compiler_params=params(ident),
+        cost_estimate=cost(6),
+    )(parts)
+
+
+def small_total(values_in, axes, max_rows, ident):
+    sizes = [lax.axis_size(axis) for axis in axes]
+    high = values_in.shape[0]
+
+    def kernel(x_ref, o_ref, *scratch):
+        slots, sends, recvs = (scratch[k :: 3] for k in range(3))
+        barrier = pltpu.get_barrier_semaphore()
+        spots = [lax.axis_index(axis) for axis in axes]
+        for axis, size, me in zip(axes, sizes, spots):
+            for k in range(1, size):
+                pl.semaphore_signal(
+                    barrier, inc=1, device_id={axis: lax.rem(me + k, size)}, device_id_type=MESH
+                )
+        pl.semaphore_wait(barrier, sum(sizes) - len(sizes))
+        for at, (axis, size, me) in enumerate(zip(axes, sizes, spots)):
+            buf, send, recv = slots[at], sends[at], recvs[at]
+            buf[me] = x_ref[...] if at == 0 else o_ref[...]
+            for k in range(1, size):
+                push(buf.at[me], buf.at[me], send.at[k], recv.at[k], {axis: lax.rem(me + k, size)}).start()
+            for k in range(1, size):
+                origin = lax.rem(me + size - k, size)
+                push(buf.at[origin], buf.at[origin], send.at[k], recv.at[k], {axis: origin}).wait()
+            total = buf[0]
+            for k in range(1, size):
+                total = total + buf[k]
+            o_ref[...] = total
+            if max_rows:
+                top = buf[0, high - max_rows :]
+                for k in range(1, size):
+                    top = jnp.maximum(top, buf[k, high - max_rows :])
+                o_ref[high - max_rows :] = top
+
+    dma = pltpu.SemaphoreType.DMA
+    vmem = pl.BlockSpec(memory_space=pltpu.VMEM)
+    scratch = []
+    for size in sizes:
+        scratch += [pltpu.VMEM((size,) + values_in.shape, FULL), dma((size,)), dma((size,))]
+    return pl.pallas_call(
+        kernel,
+        out_shape=jax.ShapeDtypeStruct(values_in.shape, FULL),
+        in_specs=[vmem],
+        out_specs=vmem,
+        scratch_shapes=scratch,
+        compiler_params=params(ident, 16),
+        cost_estimate=cost(4 * len(sizes)),
+    )(values_in)
+
+
+def allowed_block(at, high, width, spans):
+    key_places = lax.broadcasted_iota(jnp.int32, (high, width), 1)
+    query_places = at * high + lax.broadcasted_iota(jnp.int32, (high, width), 0)
+    seen = key_places <= query_places
+    for piece in range(spans.shape[0] - 1):
+        start = spans[piece + 1]
+        both = (
+            (key_places >= start)
+            & (key_places < start + IMG)
+            & (query_places >= start)
+            & (query_places < start + IMG)
+        )
+        seen = seen | both
+    return seen & (key_places < spans[0])
+
+
+def softmax_block(block_rows, keys, allowed):
+    scores = against(block_rows, keys)
+    masked = jnp.where(allowed, scores, NEGATIVE)
+    peak_row = jnp.max(masked, axis=-1, keepdims=True)
+    raw_weights = jnp.where(allowed, jnp.exp(masked - peak_row), 0.0)
+    return raw_weights / jnp.sum(raw_weights, axis=-1, keepdims=True), peak_row
+
+
+def head_forward(queries, keys, values, spans):
+    rows = queries.shape[0]
+    step = min(256, rows)
+
+    def kernel(spans_ref, q_ref, k_ref, v_ref, o_ref, top_ref):
+        top_ref[...] = jnp.full(top_ref.shape, NEGATIVE, FULL)
+
+        @pl.loop(0, rows // step)
+        def _(at):
+            here = pl.ds(pl.multiple_of(at * step, step), step)
+            allowed = allowed_block(at, step, keys.shape[0], spans_ref)
+            probs, peak_row = softmax_block(q_ref[here], k_ref[...], allowed)
+            o_ref[here] = flat_dot(probs.astype(LOW), v_ref[...]).astype(LOW)
+            top_ref[...] = jnp.maximum(top_ref[...], jnp.max(peak_row))
+
+    vmem = pl.BlockSpec(memory_space=pltpu.VMEM)
+    return pl.pallas_call(
+        kernel,
+        out_shape=(
+            jax.ShapeDtypeStruct(queries.shape, LOW),
+            jax.ShapeDtypeStruct((8, 128), FULL),
+        ),
+        in_specs=[pl.BlockSpec(memory_space=pltpu.SMEM), vmem, vmem, vmem],
+        out_specs=(vmem, vmem),
+        compiler_params=pltpu.CompilerParams(vmem_limit_bytes=48 * 2**20),
+        cost_estimate=cost(10),
+    )(spans, queries, keys, values)
+
+
+def head_backward(queries, keys, values, grads, spans):
+    rows = queries.shape[0]
+    step = min(256, rows)
+
+    def kernel(spans_ref, q_ref, k_ref, v_ref, g_ref, dq_ref, dk_ref, dv_ref):
+        dk_ref[...] = jnp.zeros(dk_ref.shape, FULL)
+        dv_ref[...] = jnp.zeros(dv_ref.shape, FULL)
+
+        @pl.loop(0, rows // step)
+        def _(at):
+            here = pl.ds(pl.multiple_of(at * step, step), step)
+            allowed = allowed_block(at, step, keys.shape[0], spans_ref)
+            block_rows, grad_rows = q_ref[here], g_ref[here]
+            probs, _ = softmax_block(block_rows, k_ref[...], allowed)
+            grad_probs = against(grad_rows, v_ref[...])
+            delta_row = jnp.sum(probs * grad_probs, axis=-1, keepdims=True)
+            grad_scores = (probs * (grad_probs - delta_row)).astype(LOW)
+            dq_ref[here] = flat_dot(grad_scores, k_ref[...])
+            dk_ref[...] += inner_rows(grad_scores, block_rows)
+            dv_ref[...] += inner_rows(probs.astype(LOW), grad_rows)
+
+    vmem = pl.BlockSpec(memory_space=pltpu.VMEM)
+    return pl.pallas_call(
+        kernel,
+        out_shape=(jax.ShapeDtypeStruct(queries.shape, FULL),)
+        + (jax.ShapeDtypeStruct(keys.shape, FULL),) * 2,
+        in_specs=[pl.BlockSpec(memory_space=pltpu.SMEM)] + [vmem] * 4,
+        out_specs=(vmem, vmem, vmem),
+        compiler_params=pltpu.CompilerParams(vmem_limit_bytes=48 * 2**20),
+        cost_estimate=cost(20),
+    )(spans, queries, keys, values, grads)
+
+
+def whole_norm(values_in, gain_vec):
+    scale = lax.rsqrt(jnp.mean(values_in * values_in, axis=-1, keepdims=True) + EPS)
+    return values_in * scale * gain_vec, scale
+
+
+def whole_norm_backward(values_in, scale, gain_vec, grad_out):
+    weighted = grad_out * gain_vec
+    inner = jnp.mean(weighted * values_in, axis=-1, keepdims=True)
+    return (
+        scale * weighted - values_in * (scale * scale * scale) * inner,
+        jnp.sum(grad_out * values_in * scale, axis=0),
+    )
+
+
+def turn(values_in, cos_tab, sin_tab):
+    half_width = values_in.shape[-1] // 2
+    one, two = values_in[:, :half_width], values_in[:, half_width:]
+    return jnp.concatenate(
+        [one * cos_tab - two * sin_tab, two * cos_tab + one * sin_tab], axis=1
+    )
+
+
+def turn_back(values_in, cos_tab, sin_tab):
+    return turn(values_in, cos_tab, -sin_tab)
+
+
+def swap_row(values_in, split, concat, tiled=True):
+    return lax.all_to_all(values_in, "row", split, concat, tiled=tiled)
+
+
+def line_device(
+    activations,
+    per_layer,
+    cotangent,
+    lengths,
+    starts,
+    w_query,
+    m_query,
+    v_query,
+    key_value_weight,
+    key_value_first_moment,
+    key_value_second_moment,
+    w_attend,
+    m_attend,
+    v_attend,
+    w_gateup,
+    m_gateup,
+    v_gateup,
+    w_down,
+    m_down,
+    v_down,
+    w_left,
+    m_left,
+    v_left,
+    w_right,
+    m_right,
+    v_right,
+    w_pergate,
+    m_pergate,
+    v_pergate,
+    w_perproj,
+    m_perproj,
+    v_perproj,
+    w_gains,
+    m_gains,
+    v_gains,
+    w_heads,
+    m_heads,
+    v_heads,
+):
+    rows_n = lax.axis_size("row")
+    cols_n = lax.axis_size("col")
+    data_n = lax.axis_size("dp")
+    me = lax.axis_index("row")
+    column = lax.axis_index("col")
+    data_at = lax.axis_index("dp")
+    half_tok, width_a = activations.shape
+    tokens = half_tok * cols_n
+    share = half_tok // rows_n
+    quarter = tokens // rows_n
+    width = width_a * rows_n
+
+    heads_here = data_n
+    qkv = lax.all_gather(
+        jnp.concatenate([w_query, key_value_weight], axis=1).astype(LOW), "dp", axis=0
+    )
+    query_w = qkv[:, :, : w_query.shape[1]]
+    kv_w = qkv[:, :, w_query.shape[1] :]
+    key_w = lax.dynamic_index_in_dim(kv_w, column, 0, False)
+    value_w = lax.dynamic_index_in_dim(kv_w, KEY_VALUE_HEADS + column, 0, False)
+    attend_cols = w_attend.shape[1]
+    attend_w = swap_row(
+        w_attend.astype(LOW).reshape(rows_n, -1, attend_cols), 0, 1, False
+    )
+    attend_w = lax.all_gather(attend_w, "dp", axis=2).reshape(-1, width)
+    gateup_w = swap_row(w_gateup.astype(LOW), 2, 1)
+    ff_part = gateup_w.shape[2]
+    gateup_w = lax.all_gather(gateup_w, "dp", axis=2, tiled=True)
+    down_w = swap_row(
+        w_down.astype(LOW).reshape(data_n, rows_n, ff_part, w_down.shape[1]), 1, 2, False
+    )
+    down_w = lax.all_gather(
+        down_w.reshape(data_n * ff_part, rows_n, w_down.shape[1]), "dp", axis=2
+    ).reshape(data_n * ff_part, width)
+    smalls = (w_left, w_right, w_pergate, w_perproj)
+    flat = jnp.concatenate([w.astype(LOW).reshape(-1) for w in smalls]).reshape(-1, 128)
+    flat = lax.all_gather(lax.all_gather(lax.all_gather(flat, "dp"), "row"), "col")
+    flat = flat.reshape(cols_n, rows_n, data_n, -1)
+    cuts = []
+    start = 0
+    for w in smalls:
+        cuts.append(flat[..., start : start + w.size].reshape((cols_n, rows_n, data_n) + w.shape))
+        start += w.size
+    left_w = cuts[0].transpose(1, 3, 0, 2, 4).reshape(width, -1)
+    right_w = cuts[1].transpose(0, 3, 1, 2, 4).reshape(-1, width)
+    pergate_w = cuts[2].transpose(1, 3, 0, 2, 4).reshape(width, -1)
+    perproj_w = cuts[3].transpose(0, 3, 1, 2, 4).reshape(-1, width)
+
+    inputs = swap_row(activations, 0, 1).astype(FULL)
+    upstream = swap_row(cotangent, 0, 1).astype(FULL)
+    extras = lax.all_gather(lax.all_gather(per_layer, "row"), "col", axis=2)
+    extras = extras.reshape(tokens, -1)
+    token_at = column * half_tok + me * share
+    extras = lax.dynamic_slice_in_dim(extras, token_at, share, 0).astype(FULL)
+    length = lax.dynamic_index_in_dim(lengths, data_at, 0, keepdims=True)
+    piece_starts = lax.dynamic_index_in_dim(starts, data_at, 0, keepdims=False)
+    spans = jnp.concatenate([length, piece_starts])
+    gains_here = lax.dynamic_slice_in_dim(w_gains, 0, 1, 0)[0]
+    gains = lax.all_gather(w_gains, "row", axis=1, tiled=True)
+
+    acts = activations.astype(FULL)
+    sums = jnp.sum(acts * acts, axis=1)
+    sums = small_total(sums.reshape(-1, 128), ("row",), 0, 1).reshape(-1, 1)
+    scale_here = lax.rsqrt(sums / MODEL_WIDTH + EPS)
+    hidden_here = (acts * scale_here * gains_here).astype(LOW)
+    spread_h = core_gather(hidden_here, 2).reshape(tokens, width_a)
+
+    raw_q = [flat_dot(spread_h, query_w[k]).astype(LOW) for k in range(heads_here)]
+    raw_k = flat_dot(spread_h, key_w).astype(LOW).reshape(rows_n, quarter, HEAD_WIDTH)
+    raw_v = flat_dot(spread_h, value_w).astype(LOW).reshape(rows_n, quarter, HEAD_WIDTH)
+    qkv_parts = jnp.concatenate([jnp.stack(raw_q), raw_k, raw_v], axis=1)
+    qkv_raw = line_reduce(qkv_parts, 3, False, 55)
+    query_raw = qkv_raw[:tokens]
+    key_raw = qkv_raw[tokens : tokens + quarter]
+    value_raw = qkv_raw[tokens + quarter :]
+    query_gain = lax.dynamic_index_in_dim(w_heads, column * rows_n + me, 0, True)
+    key_gain = w_heads[QUERY_HEADS :]
+    all_cos, all_sin = rope_tables(jnp.arange(tokens, dtype=jnp.int32), HEAD_WIDTH)
+    own_cos = lax.dynamic_slice_in_dim(all_cos, me * quarter, quarter, 0)
+    own_sin = lax.dynamic_slice_in_dim(all_sin, me * quarter, quarter, 0)
+    query_n, query_scale = whole_norm(query_raw, query_gain)
+    queries = turn(query_n, all_cos, all_sin).astype(LOW)
+    key_n, key_scale = whole_norm(key_raw, key_gain)
+    value_n, value_scale = whole_norm(value_raw, 1.0)
+    kv_here = jnp.concatenate([turn(key_n, own_cos, own_sin), value_n], axis=0).astype(LOW)
+    kv_all = line_gather(kv_here, 4, False, 20)
+    keys = kv_all[:, :quarter].reshape(tokens, HEAD_WIDTH)
+    values = kv_all[:, quarter:].reshape(tokens, HEAD_WIDTH)
+    attended, top = head_forward(queries, keys, values, spans)
+
+    def shares(parts):
+        return parts.astype(LOW).reshape(cols_n, rows_n, share, width)
+
+    hidden, _ = whole_norm(inputs, gains[0])
+    hidden_low = hidden.astype(LOW)
+    middle = flat_dot(hidden_low, left_w).astype(LOW)
+    right_raw = flat_dot(middle, right_w)
+    right_n, scale_r = whole_norm(right_raw, gains[1])
+    projected = line_reduce(shares(flat_dot(attended, attend_w)), 5, True, 45)
+    proj_n, scale_p = whole_norm(projected, gains[2])
+    mixture = ((inputs + proj_n) + (hidden + right_n)) * HALF_ROOT
+    ffn_n, scale_f = whole_norm(mixture, gains[3])
+    spread_f = line_gather(ffn_n.astype(LOW), 6, True, 40).reshape(tokens, width)
+    gate_raw = flat_dot(spread_f, gateup_w[0])
+    up_raw = flat_dot(spread_f, gateup_w[1])
+    act = (jax.nn.gelu(gate_raw, approximate=True) * up_raw).astype(LOW)
+    down_raw = line_reduce(shares(flat_dot(act, down_w)), 7, True, 45)
+    down_n, scale_d = whole_norm(down_raw, gains[4])
+    block_out = mixture + down_n
+    out_low = block_out.astype(LOW)
+    pgate = flat_dot(out_low, pergate_w)
+    pact = (jax.nn.gelu(pgate, approximate=True) * extras).astype(LOW)
+    perproj = flat_dot(pact, perproj_w)
+    perproj_n, scale_pp = whole_norm(perproj, gains[5])
+    result = swap_row((block_out + perproj_n).astype(LOW), 1, 0)
+
+    gain_grads = [None] * 6
+    d_perproj, gain_grads[5] = whole_norm_backward(perproj, scale_pp, gains[5], upstream)
+    d_perproj = d_perproj.astype(LOW)
+    dw_perproj = inner_rows(pact, d_perproj)
+    d_pact = against(d_perproj, perproj_w)
+    _, pullback = jax.vjp(lambda v: jax.nn.gelu(v, approximate=True), pgate)
+    (d_pgate,) = pullback(d_pact * extras)
+    d_pgate = d_pgate.astype(LOW)
+    dw_pergate = inner_rows(out_low, d_pgate)
+    d_out = upstream + against(d_pgate, pergate_w)
+    d_down, gain_grads[4] = whole_norm_backward(down_raw, scale_d, gains[4], d_out)
+    spread_d = line_gather(d_down.astype(LOW), 8, True, 40).reshape(tokens, width)
+    d_act = against(spread_d, down_w)
+    _, pullback = jax.vjp(
+        lambda a, b: jax.nn.gelu(a, approximate=True) * b, gate_raw, up_raw
+    )
+    d_gate, d_up = pullback(d_act)
+    d_gate, d_up = d_gate.astype(LOW), d_up.astype(LOW)
+    d_ffn = against(d_gate, gateup_w[0]) + against(d_up, gateup_w[1])
+    d_ffn = line_reduce(shares(d_ffn), 9, True, 45)
+    dw_down = inner_rows(act, spread_d).astype(LOW)
+    dw_gateup = jnp.stack(
+        [inner_rows(spread_f, d_gate).astype(LOW), inner_rows(spread_f, d_up).astype(LOW)]
+    )
+    d_mix, gain_grads[3] = whole_norm_backward(mixture, scale_f, gains[3], d_ffn)
+    d_half = (d_out + d_mix) * HALF_ROOT
+    d_proj, gain_grads[2] = whole_norm_backward(projected, scale_p, gains[2], d_half)
+    spread_p = line_gather(d_proj.astype(LOW), 10, True, 40).reshape(tokens, width)
+    d_right, gain_grads[1] = whole_norm_backward(right_raw, scale_r, gains[1], d_half)
+    d_right = d_right.astype(LOW)
+    dw_right = inner_rows(middle, d_right)
+    d_middle = against(d_right, right_w).astype(LOW)
+    dw_left = inner_rows(hidden_low, d_middle)
+    d_hidden_share = d_half + against(d_middle, left_w)
+    both = jnp.stack([d_half, d_hidden_share]).astype(LOW)
+    both = swap_row(both, 2, 1)
+    d_attended = against(spread_p, attend_w).astype(LOW)
+    dw_attend = inner_rows(attended, spread_p).astype(LOW)
+    d_queries, d_keys, d_values = head_backward(queries, keys, values, d_attended, spans)
+    kv_parts = jnp.concatenate(
+        [
+            d_keys.astype(LOW).reshape(rows_n, quarter, HEAD_WIDTH),
+            d_values.astype(LOW).reshape(rows_n, quarter, HEAD_WIDTH),
+        ],
+        axis=1,
+    )
+    d_kv = line_reduce(kv_parts, 11, False, 20)
+    d_q_raw, dg_query = whole_norm_backward(
+        query_raw, query_scale, query_gain, turn_back(d_queries, all_cos, all_sin)
+    )
+    d_k_raw, dg_key = whole_norm_backward(
+        key_raw, key_scale, key_gain, turn_back(d_kv[:quarter], own_cos, own_sin)
+    )
+    d_v_raw, _ = whole_norm_backward(value_raw, value_scale, 1.0, d_kv[quarter:])
+    d_raw = jnp.concatenate([d_q_raw, d_k_raw, d_v_raw], axis=0).astype(LOW)
+    spread_q = line_gather(d_raw, 12, False, 55)
+    d_q_all = spread_q[:, :tokens]
+    d_k_all = spread_q[:, tokens : tokens + quarter].reshape(tokens, HEAD_WIDTH)
+    d_v_all = spread_q[:, tokens + quarter :].reshape(tokens, HEAD_WIDTH)
+    d_hidden = against(d_k_all, key_w) + against(d_v_all, value_w)
+    for k in range(heads_here):
+        d_hidden = d_hidden + against(d_q_all[k], query_w[k])
+    d_hidden = core_reduce(d_hidden.astype(LOW).reshape(cols_n, half_tok, width_a), 13)
+    d_hidden = d_hidden + both[1].astype(FULL)
+    weighted = d_hidden * gains_here
+    inner = jnp.sum(weighted * acts, axis=1)
+    inner = small_total(inner.reshape(-1, 128), ("row",), 0, 14).reshape(-1, 1) / MODEL_WIDTH
+    grad_input = (
+        both[0].astype(FULL)
+        + scale_here * weighted
+        - acts * (scale_here * scale_here * scale_here) * inner
+    ).astype(LOW)
+    gain_zero = jnp.sum(d_hidden * acts * scale_here, axis=0)
+
+    dw_query = jnp.stack([inner_rows(spread_h, d_q_all[k]) for k in range(heads_here)])
+    dw_key = inner_rows(spread_h, d_k_all)
+    dw_value = inner_rows(spread_h, d_v_all)
+    zero = jnp.zeros_like(dw_key)
+    first = column == 0
+    dw_kv = jnp.stack(
+        [
+            jnp.where(first, dw_key, zero),
+            jnp.where(first, zero, dw_key),
+            jnp.where(first, dw_value, zero),
+            jnp.where(first, zero, dw_value),
+        ]
+    )
+    g_qkv = lax.psum_scatter(
+        jnp.concatenate([dw_query, dw_kv], axis=2).astype(LOW), "dp", scatter_dimension=0
+    ).astype(FULL)
+    g_query = g_qkv[:, : w_query.shape[1]]
+    g_keyval = g_qkv[:, w_query.shape[1] :]
+    g_keyval = g_keyval + lax.ppermute(g_keyval, "col", [(0, 1), (1, 0)])
+    g_attend = lax.psum_scatter(
+        dw_attend.reshape(HEAD_WIDTH, rows_n, data_n, attend_cols), "dp", scatter_dimension=2
+    )
+    g_attend = swap_row(g_attend, 1, 0, False).reshape(w_attend.shape).astype(FULL)
+    g_gateup = lax.psum_scatter(dw_gateup, "dp", scatter_dimension=2, tiled=True)
+    g_gateup = swap_row(g_gateup, 1, 2).astype(FULL)
+    g_down = lax.psum_scatter(
+        dw_down.reshape(data_n * ff_part, rows_n, data_n, w_down.shape[1]),
+        "dp",
+        scatter_dimension=2,
+    )
+    g_down = swap_row(g_down.reshape(data_n, ff_part, rows_n, w_down.shape[1]), 2, 1, False)
+    g_down = g_down.reshape(w_down.shape).astype(FULL)
+
+    def to_shards(grad, rows_first):
+        if rows_first:
+            cut = grad.reshape(rows_n, width_a, cols_n, data_n, -1).transpose(2, 0, 3, 1, 4)
+        else:
+            cut = grad.reshape(cols_n, -1, rows_n, data_n, width_a // data_n).transpose(0, 2, 3, 1, 4)
+        return cut.astype(LOW).reshape(cols_n, rows_n, data_n, -1)
+
+    flat_grads = jnp.concatenate(
+        [
+            to_shards(dw_left, True),
+            to_shards(dw_right, False),
+            to_shards(dw_pergate, True),
+            to_shards(dw_perproj, False),
+        ],
+        axis=3,
+    ).reshape(cols_n, rows_n, data_n, -1, 128)
+    flat_grads = lax.psum_scatter(flat_grads, "col", scatter_dimension=0)
+    flat_grads = lax.psum_scatter(flat_grads, "row", scatter_dimension=0)
+    flat_grads = lax.psum_scatter(flat_grads, "dp", scatter_dimension=0).astype(FULL).reshape(-1)
+    small_grads = []
+    start = 0
+    for w in smalls:
+        small_grads.append(flat_grads[start : start + w.size].reshape(w.shape))
+        start += w.size
+    g_left, g_right, g_pergate, g_perproj = small_grads
+
+    gain_full = jnp.stack(
+        [
+            lax.dynamic_update_slice_in_dim(
+                jnp.zeros((width,), FULL), gain_zero, me * width_a, 0
+            )
+        ]
+        + gain_grads[1:]
+    )
+    head_full = lax.dynamic_update_slice_in_dim(
+        jnp.zeros((QUERY_HEADS + 1, HEAD_WIDTH), FULL), dg_query[None], column * rows_n + me, 0
+    )
+    head_full = head_full.at[QUERY_HEADS].add(dg_key)
+    logit_row = lax.dynamic_update_slice_in_dim(
+        jnp.full((128,), NEGATIVE, FULL), top[0, :1], column * rows_n + me, 0
+    )
+    gain_rows = gain_full.size // 128
+    head_rows = head_full.size // 128
+    pad_rows = -(gain_rows + head_rows) % 8
+    small = jnp.concatenate(
+        [
+            gain_full.reshape(-1, 128),
+            head_full.reshape(-1, 128),
+            jnp.zeros((pad_rows, 128), FULL),
+            jnp.broadcast_to(logit_row[None], (8, 128)),
+        ]
+    )
+    small = small_total(small, ("col", "row", "dp"), 8, 15)
+    gain_sum = small[:gain_rows].reshape(6, width)
+    head_sum = small[gain_rows : gain_rows + head_rows].reshape(QUERY_HEADS + 1, HEAD_WIDTH)
+    logit_top = small[-1, :QUERY_HEADS]
+    g_gains = lax.dynamic_slice_in_dim(gain_sum, me * width_a, width_a, 1)
+    squares = jnp.where(first, jnp.sum(g_keyval * g_keyval), 0.0)
+    for gradient in (g_query, g_attend, g_gateup, g_down, g_left, g_right, g_pergate, g_perproj):
+        squares = squares + jnp.sum(gradient * gradient)
+    squares = small_total(jnp.broadcast_to(squares, (8, 128)), ("col", "row", "dp"), 0, 16)[0, 0]
+    squares = squares + jnp.sum(gain_sum * gain_sum) + jnp.sum(head_sum * head_sum)
+    grad_norm = jnp.sqrt(squares)
+    clip_scale = CLIP / jnp.maximum(grad_norm, CLIP)
+    scale_factors = LOGIT_CAP / jnp.maximum(logit_top, LOGIT_CAP)
+    weights = (
+        w_query,
+        key_value_weight,
+        w_attend,
+        w_gateup,
+        w_down,
+        w_left,
+        w_right,
+        w_pergate,
+        w_perproj,
+        w_gains,
+        w_heads,
+    )
+    moments = (
+        m_query,
+        key_value_first_moment,
+        m_attend,
+        m_gateup,
+        m_down,
+        m_left,
+        m_right,
+        m_pergate,
+        m_perproj,
+        m_gains,
+        m_heads,
+    )
+    seconds = (
+        v_query,
+        key_value_second_moment,
+        v_attend,
+        v_gateup,
+        v_down,
+        v_left,
+        v_right,
+        v_pergate,
+        v_perproj,
+        v_gains,
+        v_heads,
+    )
+    gradients = (
+        g_query,
+        g_keyval,
+        g_attend,
+        g_gateup,
+        g_down,
+        g_left,
+        g_right,
+        g_pergate,
+        g_perproj,
+        g_gains,
+        head_sum,
+    )
+    step_rates = (
+        MODEL_WIDTH ** (-0.5),
+        MODEL_WIDTH ** (-0.5),
+        (QUERY_HEADS * HEAD_WIDTH) ** (-0.5),
+        MODEL_WIDTH ** (-0.5),
+        FF ** (-0.5),
+        MODEL_WIDTH ** (-0.5),
+        RANK ** (-0.5),
+        MODEL_WIDTH ** (-0.5),
+        PLD ** (-0.5),
+        GAIN_RATE,
+        HEAD_RATE,
+    )
+    decays = (DECAY, DECAY, DECAY, DECAY, DECAY, DECAY, DECAY, DECAY, DECAY, 0.0, 0.0)
+    updated = [
+        adamw_step(
+            weights[k], moments[k], seconds[k], gradients[k] * clip_scale, step_rates[k], decays[k]
+        )
+        for k in range(11)
+    ]
+    head_scale = jnp.sqrt(scale_factors)
+    q_width = w_query.shape[1]
+    q_head = (
+        (column * data_n + data_at) * q_width + jnp.arange(q_width, dtype=jnp.int32)
+    ) // HEAD_WIDTH
+    q_factor = jnp.sum(
+        jnp.where(
+            q_head[:, None] == jnp.arange(QUERY_HEADS, dtype=jnp.int32)[None, :],
+            head_scale[None, :],
+            0.0,
+        ),
+        axis=1,
+    )
+    new_query = updated[0][2] * q_factor[None, :]
+    kv_width = key_value_weight.shape[1]
+    key_value_index = data_at * kv_width + jnp.arange(kv_width, dtype=jnp.int32)
+    key_value_scale = jnp.sqrt(
+        jnp.min(scale_factors.reshape(KEY_VALUE_HEADS, QUERY_HEADS // KEY_VALUE_HEADS), axis=1)
+    )
+    key_value_choice = jnp.sum(
+        jnp.where(
+            (key_value_index // HEAD_WIDTH)[:, None]
+            == jnp.arange(KEY_VALUE_HEADS, dtype=jnp.int32)[None, :],
+            key_value_scale[None, :],
+            0.0,
+        ),
+        axis=1,
+    )
+    key_value_factor = jnp.where(
+        key_value_index < KEY_VALUE_HEADS * HEAD_WIDTH, key_value_choice, 1.0
+    )
+    new_keyval = updated[1][2] * key_value_factor[None, :]
+    return (
+        result,
+        grad_input,
+        grad_norm,
+        scale_factors,
+        updated[0][0],
+        updated[0][1],
+        new_query,
+        updated[1][0],
+        updated[1][1],
+        new_keyval,
+        updated[2][0],
+        updated[2][1],
+        updated[2][2],
+        updated[3][0],
+        updated[3][1],
+        updated[3][2],
+        updated[4][0],
+        updated[4][1],
+        updated[4][2],
+        updated[5][0],
+        updated[5][1],
+        updated[5][2],
+        updated[6][0],
+        updated[6][1],
+        updated[6][2],
+        updated[7][0],
+        updated[7][1],
+        updated[7][2],
+        updated[8][0],
+        updated[8][1],
+        updated[8][2],
+        updated[9][0],
+        updated[9][1],
+        updated[9][2],
+        updated[10][0],
+        updated[10][1],
+        updated[10][2],
     )
 
 
@@ -725,8 +1733,13 @@
         P(),
         P(),
     )
+    fits = (
+        mesh.shape["col"] == KEY_VALUE_HEADS
+        and mesh.shape["row"] * KEY_VALUE_HEADS == QUERY_HEADS
+        and mesh.shape["dp"] == mesh.shape["row"]
+    )
     return jax.shard_map(
-        per_device,
+        line_device if fits else per_device,
         mesh=mesh,
         in_specs=placed,
         out_specs=(

time: 3140 us -> 1160 us (0.37)
  waiting for transfers between devices: 2390 us -> 73.8 us
  Pallas kernels: 0 us -> 500 us
  blocking collectives: 291 us -> 132 us
  local copies, waits for them, and re-layouts: 57.5 us -> 175 us
  other arithmetic: 207 us -> 94.7 us
  matrix products: 155 us -> 113 us
  starting transfers between devices: 2.8 us -> 35.4 us
    reduce_scatter x20 -> x3, waiting for transfers between devices: 1320 us -> 0.02 us  [the longest x1 0.02 us: line_device(): flat_grads = lax.psum_scatter(flat_grads, 'col', scatter_dimension=0)]
    all_gather x16 -> x6, waiting for transfers between devices: 839 us -> 17.7 us  [the longest x1 17.7 us: line_device(): lax.all_gather(lax.all_gather(flat, 'dp'), 'row')]
    pallas_call x0 -> x18, Pallas kernels: none -> 500 us  [the longest x5 203 us: line_gather(): pl.pallas_call(kernel, out_shape=jax.ShapeDtypeStruct(shape, block.dtype)...]
    psum x2 -> x0, waiting for transfers between devices: 230 us -> none  [the longest x1 145 us: per_device(): key_raw_all = lax.psum(flat_dot(spread_h, keyval_b), 'row')]
    psum x11 -> x0, blocking collectives: 150 us -> none  [the longest x10 110 us: row_total(): return lax.psum(values_in, 'row')]
    all_gather x8 -> x4, blocking collectives: 142 us -> 89.2 us  [the longest x1 53.3 us: line_device(): gains = lax.all_gather(w_gains, 'row', axis=1, tiled=True)]
    add x64 -> x2, other arithmetic: 49.3 us -> 0.23 us  [the longest x1 0.22 us: line_device(): block_out = mixture + down_n]
    reshape x6 -> x21, local copies, waits for them, and re-layouts: 6.44 us -> 52.4 us  [the longest x4 13.8 us: to_shards(): return cut.astype(LOW).reshape(cols_n, rows_n, data_n, -1)]
  transfers between devices with their start and end apart: 39 -> 22, of which waited for: 35 -> 6; matrix products, arithmetic and copies ran while one was open for 7% -> 22% of each run, Pallas kernels for 0% -> 28%
where the time goes in v1:
time: 1160 us; the launch traced here: 1150 us
  Pallas kernels  500 us (43%)
  local copies, waits for them, and re-layouts  175 us (15%)
  blocking collectives  132 us (11%)
  matrix products  113 us (10%)
  other arithmetic  94.7 us (8%)
  waiting for transfers between devices  73.8 us (6%)
  starting transfers between devices  35.4 us (3%)
  between operations  25.6 us (2%)
    pallas_call x5, Pallas kernels, line_gather(): pl.pallas_call(kernel, out_shape=jax.ShapeDtypeStruct(shape, block.dtype)...  203 us
    pallas_call x5, Pallas kernels, line_reduce(): pl.pallas_call(kernel, out_shape=jax.ShapeDtypeStruct((high, wide), FULL)...  200 us
    pallas_call x4, Pallas kernels, small_total(): pl.pallas_call(kernel, out_shape=jax.ShapeDtypeStruct(values_in.shape, FU...  73.4 us
    all_gather x1, blocking collectives, line_device(): gains = lax.all_gather(w_gains, 'row', axis=1, tiled=True)  53.3 us
    dot_general x14, matrix products, against(): lax.dot_general(grad_mat, weight_mat, (((1,), (1,)), ((), ())), preferred...  52 us
    unnamed x266, local copies, waits for them, and re-layouts  43.6 us
    all_to_all x2, blocking collectives, swap_row(): return lax.all_to_all(values_in, 'row', split, concat, tiled=tiled)  43 us
    all_to_all x8, waiting for transfers between devices, swap_row(): return lax.all_to_all(values_in, 'row', split, concat, tiled=tiled)  38.2 us
  transfers between devices with their start and end apart: 22, of which 6 were waited for; matrix products, arithmetic and copies ran while one was open for 22% of the time, Pallas kernels for 28%

profile of v1, /device:TPU:0, one launch (start us, length us, event | category | flops | bytes accessed | tf_op | source)
XLA Modules:
  0.0 1149.8 jit_solution(6244054898783954122)
XLA Ops:
  11.2 11.4 all_gather.46
  23.7 13.7 %all_to_all.135 = bf16[4,256,1,128]{3,1,2,0:T(8,128)(2,1)} all-to-all(bf16[4,256,1,128]{3,1,2,0:T(8,128)(2,1)S(1)} %bitcast.438), channel_id=1, replica_groups=mesh['dp'=4,'row'=4,'col'=2] {'row'}, dimensions={0} | all-to-all | bytes 524288 | tf_op jit(solution)/shard_map/all_to_all | solution.py:794
  39.6 17.7 %all-gather.20.cloned.1.call-done = bf16[16,320,128]{2,1,0:T(8,128)(2,1)} async-done(((bf16[4,320,128]{2,1,0:T(8,128)(2,1)}), bf16[16,320,128]{2,1,0:T(8,128)(2,1)}) %all-gather.20.cloned.1.call-update) | async-done | bytes 1310736 | tf_op jit(solution)/shard_map/all_gather | solution.py:873
  57.6 29.4 %all_to_all.136 = bf16[4,4,256,1,128]{4,2,0,3,1:T(8,128)(2,1)} all-to-all(bf16[4,4,256,1,128]{4,2,0,3,1:T(8,128)(2,1)S(1)} %copy.424), channel_id=1, replica_groups=mesh['dp'=4,'row'=4,'col'=2] {'row'}, dimensions={1} | all-to-all | bytes 2097152 | tf_op jit(solution)/shard_map/all_to_all | solution.py:794
  90.5 7.0 copy.421
  97.5 7.1 all-to-all-done
  108.3 53.3 %all_gather.45 = f32[6,2048]{1,0:T(8,128)S(1)} all-gather(f32[6,512]{1,0:T(8,128)S(1)} %copy-done.62), channel_id=1, replica_groups=mesh['dp'=4,'row'=4,'col'=2] {'row'}, dimensions={1}, use_global_device_ids=true | all-gather | bytes 61440 | tf_op jit(solution)/shard_map/all_gather | solution.py:895
  163.7 5.5 shard_map.645
  177.3 22.2 %all-gather.3 = bf16[1024,128]{1,0:T(8,128)(2,1)S(1)} all-gather(bf16[256,128]{1,0:T(8,128)(2,1)} %param.41), channel_id=5, replica_groups=mesh['dp'=4,'row'=4,'col'=2] {'row'}, dimensions={0}, use_global_device_ids=true | all-gather | bytes 327680 | tf_op jit(solution)/shard_map/all_gather | solution.py:887
  225.0 56.8 %shard_map.647 = f32[1536,256]{1,0:T(8,128)S(1)} custom-call(bf16[4,1536,256]{2,1,0:T(8,128)(2,1)S(1)} %pad_maximum_fusion.1.x_ref), custom_call_target="tpu_custom_call" | custom-call | bytes 165000000 | tf_op jit(solution)/shard_map/pallas_call | solution.py:562
  287.6 20.0 %shard_map.648 = bf16[4,512,256]{2,1,0:T(8,128)(2,1)S(1)} custom-call(bf16[512,256]{1,0:T(8,128)(2,1)S(1)} %pad_maximum_fusion.9.x_ref), custom_call_target="tpu_custom_call" | custom-call | bytes 60000000 | tf_op jit(solution)/shard_map/pallas_call | solution.py:415
  307.8 8.6 shard_map.649
  317.8 40.2 %shard_map.650 = f32[128,2048]{1,0:T(8,128)S(1)} custom-call(bf16[2,4,128,2048]{3,2,1,0:T(8,128)(2,1)S(1)} %bitcast.379), custom_call_target="tpu_custom_call" | custom-call | bytes 135000000 | tf_op jit(solution)/shard_map/pallas_call | solution.py:562
  376.3 5.8 reshape.651
  390.5 42.0 %shard_map.651 = bf16[2,4,128,2048]{3,2,1,0:T(8,128)(2,1)S(1)} custom-call(bf16[128,2048]{1,0:T(8,128)(2,1)S(1)} %multiply_convert_fusion.2.x_ref), custom_call_target="tpu_custom_call" | custom-call | bytes 120000000 | tf_op jit(solution)/shard_map/pallas_call | solution.py:415
  443.0 6.2 copy.425
  449.2 7.6 fusion.10
  456.9 6.7 multiply_convert_fusion.1
  468.5 41.3 %shard_map.652 = f32[128,2048]{1,0:T(8,128)S(1)} custom-call(bf16[2,4,128,2048]{3,2,1,0:T(8,128)(2,1)S(1)} %bitcast.385), custom_call_target="tpu_custom_call" | custom-call | bytes 135000000 | tf_op jit(solution)/shard_map/pallas_call | solution.py:562
  517.5 43.5 %shard_map.653 = bf16[2,4,128,2048]{3,2,1,0:T(8,128)(2,1)S(1)} custom-call(bf16[128,2048]{1,0:T(8,128)(2,1)S(1)} %subtract_convert_fusion.3.x_ref), custom_call_target="tpu_custom_call" | custom-call | bytes 120000000 | tf_op jit(solution)/shard_map/pallas_call | solution.py:415
  561.1 11.1 multiply_convert_fusion
  572.3 10.6 fusion.9
  582.8 8.3 add_convert_fusion
  591.1 40.7 %shard_map.654 = f32[128,2048]{1,0:T(8,128)S(1)} custom-call(bf16[2,4,128,2048]{3,2,1,0:T(8,128)(2,1)S(1)} %bitcast.384), custom_call_target="tpu_custom_call" | custom-call | bytes 135000000 | tf_op jit(solution)/shard_map/pallas_call | solution.py:562
  636.0 44.2 %shard_map.655 = bf16[2,4,128,2048]{3,2,1,0:T(8,128)(2,1)S(1)} custom-call(bf16[128,2048]{1,0:T(8,128)(2,1)S(1)} %get-tuple-element.414.x_ref), custom_call_target="tpu_custom_call" | custom-call | bytes 120000000 | tf_op jit(solution)/shard_map/pallas_call | solution.py:415
  685.6 9.4 convolution_convert_fusion.1
  695.0 7.7 reshape.673
  702.7 5.3 copy.435
  721.6 6.5 reshape.676
  732.4 6.1 reshape.674
  744.9 10.2 convert_bitcast_fusion
  755.1 6.2 convert_bitcast_fusion.1
  761.2 7.6 pad_maximum_fusion
  773.6 9.9 shard_map.656
  783.9 21.4 %shard_map.657 = f32[512,256]{1,0:T(8,128)S(1)} custom-call(bf16[4,512,256]{2,1,0:T(8,128)(2,1)S(1)} %pad_maximum_fusion.5.x_ref), custom_call_target="tpu_custom_call" | custom-call | bytes 60000000 | tf_op jit(solution)/shard_map/pallas_call | solution.py:562
  810.3 53.4 %shard_map.658 = bf16[4,1536,256]{2,1,0:T(8,128)(2,1)S(1)} custom-call(bf16[1536,256]{1,0:T(8,128)(2,1)S(1)} %pad_maximum_fusion.6.x_ref), custom_call_target="tpu_custom_call" | custom-call | bytes 165000000 | tf_op jit(solution)/shard_map/pallas_call | solution.py:415
  877.4 9.7 all-to-all-done.4
  898.5 5.2 all-to-all-start.6
  944.0 5.8 copy.434
  949.9 20.9 %all-to-all-done.9 = bf16[4,1,256,4,128]{4,2,0,1,3:T(8,128)(2,1)} async-done(((bf16[4,1,256,4,128]{4,2,0,1,3:T(8,128)(2,1)}), bf16[4,1,256,4,128]{4,2,0,1,3:T(8,128)(2,1)}, u32[]{:S(2)}, u32[]{:S(2)}) %all-to-all-start.9) | async-done | bytes 1048608 | tf_op jit(solution)/shard_map/all_to_all | solution.py:794
  970.8 5.1 all-to-all-start.8
  977.8 43.1 %shard_map.660 = f32[4,128]{1,0:T(4,128)S(1)} custom-call(f32[4,128]{1,0:T(4,128)S(1)} %bitcast.396), custom_call_target="tpu_custom_call" | custom-call | bytes 12000000 | tf_op jit(solution)/shard_map/pallas_call | solution.py:670
  1021.2 14.3 %shard_map.662 = f32[128,128]{1,0:T(8,128)S(1)} custom-call(f32[128,128]{1,0:T(8,128)S(1)} %pad_maximum_fusion.11.x_ref), custom_call_target="tpu_custom_call" | custom-call | bytes 36000000 | tf_op jit(solution)/shard_map/pallas_call | solution.py:670
  1048.0 17.6 %reduce-scatter.26.cloned.1.call-done = bf16[1,320,128]{2,1,0:T(8,128)(2,1)} async-done(((bf16[4,320,128]{2,1,0:T(8,128)(2,1)}), bf16[1,320,128]{2,1,0:T(8,128)(2,1)}) %reduce-scatter.26.cloned.1.call-update) | async-done | bytes 81936
  1070.1 4.9 fusion
  1078.9 10.5 shard_map.661
  1111.6 5.9 mul.1721
  1121.8 9.6 multiply_subtract_fusion
  (538 shorter events, 266.9 us)
Async XLA Ops:
  7.2 154.5 %copy-start = (s32[4,2]{0,1:T(2,128)S(1)}, s32[4,2]{0,1:T(2,128)}, u32[]{:S(2)}) copy-start(s32[4,2]{0,1:T(2,128)} %param.44) | copy-start | bytes 100
  7.2 50.2 %copy-start.28 = (f32[4096,128]{1,0:T(8,128)S(1)}, f32[4096,128]{1,0:T(8,128)}, u32[]{:S(2)}) copy-start(f32[4096,128]{1,0:T(8,128)} %param.57) | copy-start | bytes 6291460
  7.2 50.1 %all-gather.20.cloned.1.call-start = ((), (), s32[]{:S(2)}) async-start(), calls=%async_computation.23 | async-start | bytes 1638400 | tf_op jit(solution)/shard_map/all_gather | solution.py:873
  22.6 191.8 %all-gather.18.cloned.1.call-start = ((), (), s32[]{:S(2)}) async-start(), calls=%async_computation.22 | async-start | bytes 1310720 | tf_op jit(solution)/shard_map/all_gather | solution.py:861
  37.4 178.6 %all-gather.12.cloned.1.call-start = ((), (), s32[]{:S(2)}) async-start(), calls=%async_computation.16 | async-start | bytes 2621440 | tf_op jit(solution)/shard_map/all_gather | solution.py:850
  39.6 319.1 %all-gather.22.cloned.1.call-start = ((), (), s32[]{:S(2)}) async-start(), calls=%async_computation.24 | async-start | bytes 3932160 | tf_op jit(solution)/shard_map/all_gather | solution.py:873
  57.4 385.7 %all-gather.16.cloned.1.call-start = ((), (), s32[]{:S(2)}) async-start(), calls=%async_computation.18 | async-start | bytes 5242880 | tf_op jit(solution)/shard_map/all_gather | solution.py:868
  87.0 17.6 %all-to-all-start = ((bf16[4,128,512]{2,1,0:T(8,128)(2,1)}), bf16[4,128,512]{2,1,0:T(8,128)(2,1)S(1)}, u32[]{:S(2)}, u32[]{:S(2)}) async-start(bf16[4,128,512]{2,1,0:T(8,128)(2,1)} %bitcast), calls=%async_computation | async-start | bytes 1048576 | tf_op jit(solution)/shard_map/all_to_all | solution.py:794
  90.5 71.4 %copy-start.117 = (s32[4]{0:T(128)S(1)}, s32[4]{0:T(128)}, u32[]{:S(2)}) copy-start(s32[4]{0:T(128)} %param.43) | copy-start | bytes 52
  104.6 64.7 %copy-start.47 = (bf16[4,128,512]{2,1,0:T(8,128)(2,1)}, bf16[4,128,512]{2,1,0:T(8,128)(2,1)S(1)}, u32[]{:S(2)}) copy-start(bf16[4,128,512]{2,1,0:T(8,128)(2,1)S(1)} %all-to-all-done) | copy-start | bytes 1572868
  104.6 68.5 %all-to-all-start.2 = ((bf16[2,512,1024]{1,0,2:T(2,128)(2,1)}), bf16[2,512,1024]{1,0,2:T(2,128)(2,1)S(1)}, u32[]{:S(2)}, u32[]{:S(2)}) async-start(bf16[2,512,1024]{1,0,2:T(2,128)(2,1)} %copy.421), calls=%async_computation.2 | async-start | bytes 4194304 | tf_op jit(solution)/shard_map/all_to_all | solution.py:794
  108.3 64.8 %copy-start.80 = (f32[1,512]{1,0:T(1,128)}, f32[1,512]{1,0:T(1,128)S(1)}, u32[]{:S(2)}) copy-start(f32[1,512]{1,0:T(1,128)S(1)} %dynamic_slice.36) | copy-start | bytes 6148
  161.7 348.3 %copy-start.60 = (f32[1,2048]{1,0:T(1,128)}, f32[1,2048]{1,0:T(1,128)S(1)}, u32[]{:S(2)}) copy-start(f32[1,2048]{1,0:T(1,128)S(1)} %get-tuple-element.426) | copy-start | bytes 24580
  169.3 36.1 %copy-start.82 = (f32[512]{0:T(512)}, f32[512]{0:T(512)S(1)}, u32[]{:S(2)}) copy-start(f32[512]{0:T(512)S(1)} %rsqrt_bitcast_fusion) | copy-start | bytes 6148
  173.0 50.9 %copy-start.2 = (bf16[2,512,512]{2,1,0:T(8,128)(2,1)}, bf16[2,512,512]{2,1,0:T(8,128)(2,1)S(1)}, u32[]{:S(2)}) copy-start(bf16[2,512,512]{2,1,0:T(8,128)(2,1)S(1)} %shard_map.646) | copy-start | bytes 3145732
  173.1 111.3 %copy-start.108 = (f32[128]{0:T(128)}, f32[128]{0:T(128)S(1)}, u32[]{:S(2)}) copy-start(f32[128]{0:T(128)S(1)} %negate_power_fusion) | copy-start | bytes 1540
  173.1 111.3 %copy-start.74 = (f32[1024]{0:T(1024)}, f32[1024]{0:T(1024)S(1)}, u32[]{:S(2)}) copy-start(f32[1024]{0:T(1024)S(1)} %iota_convert_fusion) | copy-start | bytes 12292
  173.1 38.3 %all-to-all-start.5 = ((bf16[4,128,512]{2,1,0:T(8,128)(2,1)}), bf16[4,128,512]{2,1,0:T(8,128)(2,1)}, u32[]{:S(2)}, u32[]{:S(2)}) async-start(bf16[4,128,512]{2,1,0:T(8,128)(2,1)} %bitcast.445), calls=%async_computation.5 | async-start | bytes 1048576 | tf_op jit(solution)/shard_map/all_to_all | solution.py:794
  177.3 272.0 %all-gather.14.cloned.1.call-start = ((), (), s32[]{:S(2)}) async-start(), calls=%async_computation.17 | async-start | bytes 10485760 | tf_op jit(solution)/shard_map/all_gather | solution.py:864
  205.3 669.7 %all-reduce.6.cloned.1.call-start = ((), (), s32[]{:S(2)}) async-start(), calls=%async_computation.25 | async-start | bytes 2097152
  209.1 74.9 %copy-start.98 = (f32[1,256]{1,0:T(1,128)}, f32[1,256]{1,0:T(1,128)S(1)}, u32[]{:S(2)}) copy-start(f32[1,256]{1,0:T(1,128)S(1)} %get-tuple-element.431) | copy-start | bytes 3076
  209.1 75.1 %copy-start.85 = (f32[1,256]{1,0:T(1,128)}, f32[1,256]{1,0:T(1,128)S(1)}, u32[]{:S(2)}) copy-start(f32[1,256]{1,0:T(1,128)S(1)} %get-tuple-element.432) | copy-start | bytes 3076
  216.0 100.5 %copy-start.32 = (bf16[1,256,4,4,128]{1,4,3,2,0:T(8,128)(2,1)}, bf16[1,256,4,4,128]{1,4,3,2,0:T(8,128)(2,1)S(1)}, u32[]{:S(2)}) copy-start(bf16[1,256,4,4,128]{1,4,3,2,0:T(8,128)(2,1)S(1)} %copy.416) | copy-start | bytes 3145732
  387.2 45.3 %copy-start.104 = (f32[128]{0:T(128)}, f32[128]{0:T(128)S(1)}, u32[]{:S(2)}) copy-start(f32[128]{0:T(128)S(1)} %get-tuple-element.446) | copy-start | bytes 1540
  390.3 47.1 %copy-start.110 = (f32[128]{0:T(128)}, f32[128]{0:T(128)S(1)}, u32[]{:S(2)}) copy-start(f32[128]{0:T(128)S(1)} %get-tuple-element.383) | copy-start | bytes 1540
  468.5 41.7 %copy-start.27 = (bf16[32,8,4,512]{3,1,2,0:T(8,128)(2,1)S(1)}, bf16[32,8,4,512]{3,1,2,0:T(8,128)(2,1)}, u32[]{:S(2)}) copy-start(bf16[32,8,4,512]{3,1,2,0:T(8,128)(2,1)} %copy.472) | copy-start | bytes 3145732
  591.1 40.7 %copy-start.111 = (f32[128]{0:T(128)S(1)}, f32[128]{0:T(128)}, u32[]{:S(2)}) copy-start(f32[128]{0:T(128)} %copy-done.110) | copy-start | bytes 1540
  591.1 41.7 %copy-start.114 = (f32[128]{0:T(128)S(1)}, f32[128]{0:T(128)}, u32[]{:S(2)}) copy-start(f32[128]{0:T(128)} %get-tuple-element.382) | copy-start | bytes 1540
  685.5 240.6 %reduce-scatter.24.cloned.1.call-start = ((), (), s32[]{:S(2)}) async-start(), calls=%async_computation.27 | async-start | bytes 5242880
  708.0 230.7 %reduce-scatter.18.cloned.1.call-start = ((), (), s32[]{:S(2)}) async-start(), calls=%async_computation.20 | async-start | bytes 3932160 | tf_op jit(solution)/shard_map/reduce_scatter | solution.py:1076
  744.6 199.5 %reduce-scatter.16.cloned.1.call-start = ((), (), s32[]{:S(2)}) async-start(), calls=%async_computation.19 | async-start | bytes 10485760 | tf_op jit(solution)/shard_map/reduce_scatter | solution.py:1050
  768.9 269.3 %reduce-scatter.22.cloned.1.call-start = ((), (), s32[]{:S(2)}) async-start(), calls=%async_computation.26 | async-start | bytes 2621440
  809.7 54.0 %copy-start.3 = (bf16[2,512,512]{2,1,0:T(8,128)(2,1)S(1)}, bf16[2,512,512]{2,1,0:T(8,128)(2,1)}, u32[]{:S(2)}) copy-start(bf16[2,512,512]{2,1,0:T(8,128)(2,1)} %copy-done.2) | copy-start | bytes 3145732
  870.3 16.8 %all-to-all-start.4 = ((bf16[128,4,512]{2,0,1:T(8,128)(2,1)}), bf16[128,4,512]{2,0,1:T(8,128)(2,1)}, u32[]{:S(2)}, u32[]{:S(2)}) async-start(bf16[128,4,512]{2,0,1:T(8,128)(2,1)} %bitcast.425), calls=%async_computation.4 | async-start | bytes 1048576 | tf_op jit(solution)/shard_map/all_to_all | solution.py:794
  887.1 11.4 all-to-all-start.7
  898.5 27.7 %all-to-all-start.6 = ((bf16[2,128,2048]{1,0,2:T(2,128)(2,1)}), bf16[2,128,2048]{1,0,2:T(2,128)(2,1)}, u32[]{:S(2)}, u32[]{:S(2)}) async-start(bf16[2,128,2048]{1,0,2:T(2,128)(2,1)} %copy.430), calls=%async_computation.6 | async-start | bytes 2097152 | tf_op jit(solution)/shard_map/all_to_all | solution.py:794
  926.2 44.6 %all-to-all-start.9 = ((bf16[4,1,256,4,128]{4,2,0,1,3:T(8,128)(2,1)}), bf16[4,1,256,4,128]{4,2,0,1,3:T(8,128)(2,1)}, u32[]{:S(2)}, u32[]{:S(2)}) async-start(bf16[4,1,256,4,128]{4,2,0,1,3:T(8,128)(2,1)} %bitcast.439), calls=%async_computation.10 | async-start | bytes 2097152 | tf_op jit(solution)/shard_map/all_to_all | solution.py:794
  930.8 110.5 %reduce-scatter.20.cloned.1.call-start = ((), (), s32[]{:S(2)}) async-start(), calls=%async_computation.21 | async-start | bytes 1638400 | tf_op jit(solution)/shard_map/reduce_scatter | solution.py:1077
  944.0 32.1 %copy-start.83 = (f32[512]{0:T(512)S(1)}, f32[512]{0:T(512)}, u32[]{:S(2)}) copy-start(f32[512]{0:T(512)} %copy-done.82) | copy-start | bytes 6148
  949.8 71.1 %copy-start.76 = (f32[2048]{0:T(1024)S(1)}, f32[2048]{0:T(1024)}, u32[]{:S(2)}) copy-start(f32[2048]{0:T(1024)} %get-tuple-element.320) | copy-start | bytes 24580
  949.8 71.1 %copy-start.77 = (f32[2048]{0:T(1024)S(1)}, f32[2048]{0:T(1024)}, u32[]{:S(2)}) copy-start(f32[2048]{0:T(1024)} %get-tuple-element.322) | copy-start | bytes 24580
  949.8 71.1 %copy-start.78 = (f32[2048]{0:T(1024)S(1)}, f32[2048]{0:T(1024)}, u32[]{:S(2)}) copy-start(f32[2048]{0:T(1024)} %get-tuple-element.324) | copy-start | bytes 24580
  949.8 71.1 %copy-start.79 = (f32[2048]{0:T(1024)S(1)}, f32[2048]{0:T(1024)}, u32[]{:S(2)}) copy-start(f32[2048]{0:T(1024)} %get-tuple-element.338) | copy-start | bytes 24580
  970.8 99.3 %all-to-all-start.8 = ((bf16[2,2048,256]{2,0,1:T(2,128)(2,1)}), bf16[2,2048,256]{2,0,1:T(2,128)(2,1)S(1)}, u32[]{:S(2)}, u32[]{:S(2)}) async-start(bf16[2,2048,256]{2,0,1:T(2,128)(2,1)} %copy.434), calls=%async_computation.9 | async-start | bytes 4194304 | tf_op jit(solution)/shard_map/all_to_all | solution.py:794
  975.9 89.6 %reduce-scatter.26.cloned.1.call-start = ((), (), s32[]{:S(2)}) async-start(), calls=%async_computation.28 | async-start | bytes 409600
  1036.6 33.5 %copy-start.115 = (f32[1,8]{1,0:T(1,128)}, f32[1,8]{1,0:T(1,128)S(1)}, u32[]{:S(2)}) copy-start(f32[1,8]{1,0:T(1,128)S(1)} %get-tuple-element.376) | copy-start | bytes 100
  1041.2 2.6 collective-permute-start
  1043.9 48.2 %copy-start.44 = (f32[512,256]{0,1:T(8,128)S(1)}, f32[512,256]{0,1:T(8,128)}, u32[]{:S(2)}) copy-start(f32[512,256]{0,1:T(8,128)} %copy.451) | copy-start | bytes 1572868
  (98 other events, 899.7 us)
Sparse Core Ops, SparseCore 0:
  22.7 34.5 all-gather.19
  59.2 24.5 all-gather.17
  86.2 35.2 all-gather.11
  122.9 11.3 all-gather.21
  136.0 53.8 all-gather.15
  205.5 87.3 all-gather.13
  685.7 50.2 all-reduce.5
  738.9 52.6 reduce-scatter.23
  794.0 10.1 reduce-scatter.17
  807.1 87.5 reduce-scatter.15
  898.5 35.1 reduce-scatter.21
  938.9 45.4 reduce-scatter.19
  1041.4 24.1 reduce-scatter.25

commit v2 on v1

--- a/solution.py
+++ b/solution.py
@@ -435,6 +435,8 @@
     count = lax.axis_size("row")
     high, wide = parts.shape[-2:]
     chunk = min(high, max(16, 65536 // wide))
+    while high % chunk:
+        chunk //= 2
 
     def kernel(x_ref, o_ref, c_buf, l_buf, r_buf, s_buf, send_l, send_r, send_c, recv_l, recv_r, recv_c):
         me = lax.axis_index("row")
@@ -576,58 +578,341 @@
     )(parts)
 
 
-def core_gather(block, ident):
-    def kernel(x_ref, o_ref, send, recv, local):
-        column = lax.axis_index("col")
+class Line:
+    def __init__(self, source, shape, place, core=False):
+        self.source, self.shape, self.place, self.core = source, shape, place, core
+
+    def semaphores(self, count, data):
+        dma = pltpu.SemaphoreType.DMA
+        return [dma((count,)), dma((count,)), dma((2 * count,))] * 2 + [dma]
+
+    def bind(self, x_ref, o_ref, sems, spots, sizes):
+        self.x_ref, self.o_ref, self.sems = x_ref, o_ref, sems
+        self.me, self.column, self.at = spots
+        self.count = sizes[0]
+
+    def slot(self, source):
+        return self.place(self.o_ref, self.column, source)
+
+    def other(self, source):
+        return self.place(self.o_ref, 1 - self.column, source)
+
+    def to_left(self, source, k):
+        origin = self.x_ref if k == 0 else self.slot(source)
+        return push(origin, self.slot(source), self.sems[0].at[k], self.sems[4].at[k], {"row": self.me - 1})
+
+    def to_right(self, source, k):
+        origin = self.x_ref if k == 0 else self.slot(source)
+        return push(origin, self.slot(source), self.sems[1].at[k], self.sems[3].at[k], {"row": self.me + 1})
+
+    def to_core(self, source, k):
+        origin = self.x_ref if k == 0 else self.slot(source)
+        return push(origin, self.slot(source), self.sems[2].at[k], self.sems[5].at[k], {"col": 1 - self.column})
+
+    def from_core(self, source, k):
+        there = self.other(source)
+        return push(there, there, self.sems[2].at[k], self.sems[5].at[k], {"col": 1 - self.column})
+
+    def from_left(self, source, k):
+        there = self.slot(source)
+        return push(there, there, self.sems[1].at[k], self.sems[3].at[k - 1], {"row": self.me - 1})
+
+    def from_right(self, source, k):
+        there = self.slot(source)
+        return push(there, there, self.sems[0].at[k], self.sems[4].at[k - 1], {"row": self.me + 1})
+
+    def own(self):
+        return pltpu.make_async_copy(self.x_ref, self.slot(self.me), self.sems[6])
+
+    def start(self):
+        me, count = self.me, self.count
+
+        @pl.when(me > 0)
+        def _():
+            self.to_left(me, 0).start()
+
+        @pl.when(me < count - 1)
+        def _():
+            self.to_right(me, 0).start()
+
+        if self.core:
+            self.to_core(me, 0).start()
+        self.own().start()
+
+    def step(self, k):
+        me, count = self.me, self.count
+
+        @pl.when(me - k >= 0)
+        def _():
+            self.from_left(me - k, k).wait_recv()
+
+            @pl.when(me < count - 1)
+            def _():
+                self.to_right(me - k, k).start()
+
+            if self.core:
+                self.to_core(me - k, k).start()
+
+        @pl.when(me + k < count)
+        def _():
+            self.from_right(me + k, k).wait_recv()
+
+            @pl.when(me > 0)
+            def _():
+                self.to_left(me + k, k).start()
+
+            if self.core:
+                self.to_core(me + k, count - 1 + k).start()
+
+    def finish(self):
+        me, count = self.me, self.count
+        self.own().wait()
+
+        @pl.when(me > 0)
+        def _():
+            self.to_left(me, 0).wait_send()
+
+        @pl.when(me < count - 1)
+        def _():
+            self.to_right(me, 0).wait_send()
+
+        if self.core:
+            self.to_core(me, 0).wait_send()
+            self.from_core(me, 0).wait_recv()
+        for k in range(1, count):
+
+            @pl.when(me - k >= 0)
+            def _():
+                @pl.when(me < count - 1)
+                def _():
+                    self.to_right(me - k, k).wait_send()
+
+                if self.core:
+                    self.to_core(me - k, k).wait_send()
+                    self.from_core(me - k, k).wait_recv()
+
+            @pl.when(me + k < count)
+            def _():
+                @pl.when(me > 0)
+                def _():
+                    self.to_left(me + k, k).wait_send()
+
+                if self.core:
+                    self.to_core(me + k, count - 1 + k).wait_send()
+                    self.from_core(me + k, count - 1 + k).wait_recv()
+
+
+class Swap:
+    def __init__(self, source, shape, take, place, axis="row"):
+        self.source, self.shape, self.take, self.place = source, shape, take, place
+        self.axis = axis
+
+    def semaphores(self, count, data):
+        size = count if self.axis == "row" else data
+        return [pltpu.SemaphoreType.DMA((size,)), pltpu.SemaphoreType.DMA((size,))]
+
+    def bind(self, x_ref, o_ref, sems, spots, sizes):
+        self.x_ref, self.o_ref, self.sems = x_ref, o_ref, sems
+        self.me = spots[0] if self.axis == "row" else spots[2]
+        self.count = sizes[0] if self.axis == "row" else sizes[1]
+
+    def copy(self, k):
+        target = lax.rem(self.me + k, self.count)
+        return push(
+            self.take(self.x_ref, target),
+            self.place(self.o_ref, self.me),
+            self.sems[0].at[k],
+            self.sems[1].at[k],
+            {self.axis: target},
+        )
+
+    def own(self):
+        return pltpu.make_async_copy(
+            self.take(self.x_ref, self.me), self.place(self.o_ref, self.me), self.sems[0].at[0]
+        )
+
+    def start(self):
+        for k in range(1, self.count):
+            self.copy(k).start()
+        self.own().start()
+
+    def step(self, k):
+        pass
+
+    def finish(self):
+        self.own().wait()
+        for k in range(1, self.count):
+            self.copy(k).wait_send()
+            origin = lax.rem(self.me + self.count - k, self.count)
+            there = self.place(self.o_ref, origin)
+            push(there, there, self.sems[0].at[k], self.sems[1].at[k], {self.axis: origin}).wait_recv()
+
+
+class Pair:
+    core = True
+
+    def __init__(self, source):
+        self.source, self.shape = source, source.shape
+
+    def semaphores(self, count, data):
+        dma = pltpu.SemaphoreType.DMA
+        return [dma, dma, dma]
+
+    def bind(self, x_ref, o_ref, sems, spots, sizes):
+        self.x_ref, self.o_ref, self.sems = x_ref, o_ref, sems
+        self.column = spots[1]
+
+    def copy(self):
+        other = 1 - self.column
+        return push(self.x_ref.at[other], self.o_ref.at[1], self.sems[0], self.sems[1], {"col": other})
+
+    def own(self):
+        return pltpu.make_async_copy(self.x_ref.at[self.column], self.o_ref.at[0], self.sems[2])
+
+    def start(self):
+        self.copy().start()
+        self.own().start()
+
+    def step(self, k):
+        pass
+
+    def finish(self):
+        self.own().wait()
+        self.copy().wait()
+
+
+def transfers(items, ident, micros):
+    count, data = lax.axis_size("row"), lax.axis_size("dp")
+    kinds = [item.semaphores(count, data) for item in items]
+    number = len(items)
+    across = any(getattr(item, "axis", None) == "dp" for item in items)
+    cores = any(getattr(item, "core", False) for item in items)
+
+    def kernel(*refs):
+        x_refs, o_refs, sems = refs[:number], refs[number : 2 * number], refs[2 * number :]
+        me, column, at = lax.axis_index("row"), lax.axis_index("col"), lax.axis_index("dp")
+        for item, x_ref, o_ref, kind in zip(items, x_refs, o_refs, kinds):
+            item.bind(x_ref, o_ref, sems[: len(kind)], (me, column, at), (count, data))
+            sems = sems[len(kind) :]
         barrier = pltpu.get_barrier_semaphore()
-        pl.semaphore_signal(barrier, inc=1, device_id={"col": 1 - column}, device_id_type=MESH)
-        pl.semaphore_wait(barrier, 1)
-        copy = push(x_ref, o_ref.at[column], send, recv, {"col": 1 - column})
-        copy.start()
-        own = pltpu.make_async_copy(x_ref, o_ref.at[column], local)
-        own.start()
-        own.wait()
-        copy.wait_send()
-        push(x_ref, o_ref.at[1 - column], send, recv, {"col": 1 - column}).wait_recv()
-
-    dma = pltpu.SemaphoreType.DMA
+        for k in range(1, count):
+            pl.semaphore_signal(
+                barrier, inc=1, device_id={"row": lax.rem(me + k, count)}, device_id_type=MESH
+            )
+        if across:
+            for k in range(1, data):
+                pl.semaphore_signal(
+                    barrier, inc=1, device_id={"dp": lax.rem(at + k, data)}, device_id_type=MESH
+                )
+        if cores:
+            pl.semaphore_signal(barrier, inc=1, device_id={"col": 1 - column}, device_id_type=MESH)
+        pl.semaphore_wait(barrier, count - 1 + (data - 1) * int(across) + int(cores))
+        for item in items:
+            item.start()
+        for k in range(1, count):
+            for item in items:
+                item.step(k)
+        for item in items:
+            item.finish()
+
+    anywhere = pl.BlockSpec(memory_space=pl.ANY)
     return pl.pallas_call(
         kernel,
-        out_shape=jax.ShapeDtypeStruct((2,) + block.shape, block.dtype),
-        in_specs=[pl.BlockSpec(memory_space=pl.ANY)],
-        out_specs=pl.BlockSpec(memory_space=pl.ANY),
-        scratch_shapes=[dma, dma, dma],
-        compiler_params=params(ident),
-        cost_estimate=cost(6),
-    )(block)
-
-
-def core_reduce(parts, ident):
-    def kernel(x_ref, o_ref, buf, send, recv):
-        column = lax.axis_index("col")
+        out_shape=[jax.ShapeDtypeStruct(item.shape, item.source.dtype) for item in items],
+        in_specs=[anywhere] * number,
+        out_specs=[anywhere] * number,
+        scratch_shapes=sum(kinds, []),
+        compiler_params=params(ident, 16),
+        cost_estimate=cost(micros),
+    )(*[item.source for item in items])
+
+
+def shard_total(query_parts, kv_parts, flat_parts, ident):
+    data = lax.axis_size("dp")
+    half = data // 2
+
+    def kernel(q_ref, kv_ref, f_ref, oq_ref, okv_ref, of_ref, q_buf, kv_buf, f_buf, *sems):
+        column, at = lax.axis_index("col"), lax.axis_index("dp")
         barrier = pltpu.get_barrier_semaphore()
+        for k in range(1, data):
+            pl.semaphore_signal(barrier, inc=1, device_id={"dp": lax.rem(at + k, data)}, device_id_type=MESH)
         pl.semaphore_signal(barrier, inc=1, device_id={"col": 1 - column}, device_id_type=MESH)
-        pl.semaphore_wait(barrier, 1)
-        copy = push(x_ref.at[1 - column], buf, send, recv, {"col": 1 - column})
-        copy.start()
-        copy.wait()
-
-        @pl.loop(0, o_ref.shape[0] // 64)
-        def _(at):
-            rows = pl.ds(pl.multiple_of(at * 64, 64), 64)
-            o_ref[rows] = x_ref[column, rows].astype(FULL) + buf[rows].astype(FULL)
-
+        pl.semaphore_wait(barrier, data)
+        mine = lax.rem(at, 2) == column
+
+        def copies(k):
+            target = lax.rem(at + k, data)
+            device = {"dp": target}
+            return (
+                push(q_ref.at[target], q_buf.at[k], sems[0].at[k], sems[1].at[k], device),
+                push(kv_ref.at[target // 2], kv_buf.at[k], sems[2].at[k], sems[3].at[k], device),
+                push(f_ref.at[target], f_buf.at[k], sems[4].at[k], sems[5].at[k], device),
+                lax.rem(target, 2) == column,
+            )
+
+        for k in range(1, data):
+            query_copy, kv_copy, flat_copy, there = copies(k)
+            query_copy.start()
+            flat_copy.start()
+
+            @pl.when(there)
+            def _():
+                kv_copy.start()
+
+        for k in range(1, data):
+            query_copy, kv_copy, flat_copy, there = copies(k)
+            query_copy.wait()
+            flat_copy.wait()
+
+            @pl.when(there)
+            def _():
+                kv_copy.wait_send()
+
+            @pl.when(mine)
+            def _():
+                kv_copy.wait_recv()
+
+        def added(target, own, buf, chunk):
+            @pl.loop(0, target.shape[0] // chunk)
+            def _(step):
+                rows = pl.ds(pl.multiple_of(step * chunk, chunk), chunk)
+                total = own[rows].astype(FULL)
+                for k in range(1, data):
+                    total = total + buf[k, rows].astype(FULL)
+                target[rows] = total
+
+        share = push(okv_ref, okv_ref, sems[6], sems[7], {"col": 1 - column})
+
+        @pl.when(mine)
+        def _():
+            added(okv_ref, kv_ref.at[at // 2], kv_buf, 128)
+            share.start()
+
+        added(oq_ref, q_ref.at[at], q_buf, 128)
+        added(of_ref, f_ref.at[at], f_buf, 64)
+
+        @pl.when(mine)
+        def _():
+            share.wait_send()
+
+        @pl.when(jnp.logical_not(mine))
+        def _():
+            share.wait_recv()
+
+    vmem = pl.BlockSpec(memory_space=pltpu.VMEM)
     dma = pltpu.SemaphoreType.DMA
-    vmem = pl.BlockSpec(memory_space=pltpu.VMEM)
+    shapes = [query_parts.shape[1:], kv_parts.shape[1:], flat_parts.shape[1:]]
     return pl.pallas_call(
         kernel,
-        out_shape=jax.ShapeDtypeStruct(parts.shape[1:], FULL),
-        in_specs=[vmem],
-        out_specs=vmem,
-        scratch_shapes=[pltpu.VMEM(parts.shape[1:], parts.dtype), dma, dma],
+        out_shape=[jax.ShapeDtypeStruct(shape, FULL) for shape in shapes],
+        in_specs=[vmem] * 3,
+        out_specs=[vmem] * 3,
+        scratch_shapes=[pltpu.VMEM((data,) + shape, LOW) for shape in shapes]
+        + [dma((data,))] * 6
+        + [dma, dma],
         compiler_params=params(ident),
-        cost_estimate=cost(6),
-    )(parts)
+        cost_estimate=cost(20),
+    )(query_parts, kv_parts, flat_parts)
 
 
 def small_total(values_in, axes, max_rows, ident):
@@ -846,31 +1131,111 @@
     quarter = tokens // rows_n
     width = width_a * rows_n
 
+    ff_part = w_gateup.shape[2] // rows_n
+    out_cols = w_down.shape[1]
     heads_here = data_n
-    qkv = lax.all_gather(
-        jnp.concatenate([w_query, key_value_weight], axis=1).astype(LOW), "dp", axis=0
-    )
-    query_w = qkv[:, :, : w_query.shape[1]]
-    kv_w = qkv[:, :, w_query.shape[1] :]
+    smalls = (w_left, w_right, w_pergate, w_perproj)
+    flat = jnp.concatenate([w.astype(LOW).reshape(-1) for w in smalls]).reshape(-1, 128)
+    flat_rows = flat.shape[0]
+
+    def columns_of(at, size):
+        return pl.ds(pl.multiple_of(at * size, size), size)
+
+    gateup_own, down_own, attend_own, upstream, qkv_w, flat = transfers(
+        [
+            Swap(
+                w_gateup.astype(LOW),
+                (2, width, ff_part),
+                lambda ref, q: ref.at[:, :, columns_of(q, ff_part)],
+                lambda ref, at: ref.at[:, columns_of(at, width_a), :],
+            ),
+            Swap(
+                w_down.astype(LOW).reshape(data_n, rows_n, ff_part, out_cols),
+                (data_n, ff_part, rows_n * out_cols),
+                lambda ref, q: ref.at[:, q],
+                lambda ref, at: ref.at[:, :, columns_of(at, out_cols)],
+            ),
+            Swap(
+                w_attend.astype(LOW).reshape(rows_n, HEAD_WIDTH, out_cols),
+                (HEAD_WIDTH, rows_n * out_cols),
+                lambda ref, q: ref.at[q],
+                lambda ref, at: ref.at[:, columns_of(at, out_cols)],
+            ),
+            Swap(
+                cotangent,
+                (share, width),
+                lambda ref, q: ref.at[columns_of(q, share)],
+                lambda ref, at: ref.at[:, columns_of(at, width_a)],
+            ),
+            Swap(
+                jnp.concatenate([w_query, key_value_weight], axis=1).astype(LOW),
+                (data_n, width_a, 2 * HEAD_WIDTH),
+                lambda ref, q: ref,
+                lambda ref, at: ref.at[at],
+                "dp",
+            ),
+            Swap(
+                flat,
+                (data_n * flat_rows, 128),
+                lambda ref, q: ref,
+                lambda ref, at: ref.at[columns_of(at, flat_rows)],
+                "dp",
+            ),
+        ],
+        1,
+        90,
+    )
+    gateup_all = lax.all_gather(gateup_own, "dp")
+    down_all = lax.all_gather(down_own, "dp")
+    query_w = qkv_w[:, :, :HEAD_WIDTH]
+    kv_w = qkv_w[:, :, HEAD_WIDTH:]
     key_w = lax.dynamic_index_in_dim(kv_w, column, 0, False)
     value_w = lax.dynamic_index_in_dim(kv_w, KEY_VALUE_HEADS + column, 0, False)
-    attend_cols = w_attend.shape[1]
-    attend_w = swap_row(
-        w_attend.astype(LOW).reshape(rows_n, -1, attend_cols), 0, 1, False
-    )
-    attend_w = lax.all_gather(attend_w, "dp", axis=2).reshape(-1, width)
-    gateup_w = swap_row(w_gateup.astype(LOW), 2, 1)
-    ff_part = gateup_w.shape[2]
-    gateup_w = lax.all_gather(gateup_w, "dp", axis=2, tiled=True)
-    down_w = swap_row(
-        w_down.astype(LOW).reshape(data_n, rows_n, ff_part, w_down.shape[1]), 1, 2, False
-    )
-    down_w = lax.all_gather(
-        down_w.reshape(data_n * ff_part, rows_n, w_down.shape[1]), "dp", axis=2
-    ).reshape(data_n * ff_part, width)
-    smalls = (w_left, w_right, w_pergate, w_perproj)
-    flat = jnp.concatenate([w.astype(LOW).reshape(-1) for w in smalls]).reshape(-1, 128)
-    flat = lax.all_gather(lax.all_gather(lax.all_gather(flat, "dp"), "row"), "col")
+    whole_acts, whole_kv, head_w, flat, gains, extras, attend_all = transfers(
+        [
+            Line(
+                activations,
+                (tokens, width),
+                lambda ref, c, r: ref.at[columns_of(c, half_tok), columns_of(r, width_a)],
+                True,
+            ),
+            Line(
+                jnp.stack([key_w, value_w]),
+                (2, width, HEAD_WIDTH),
+                lambda ref, c, r: ref.at[:, columns_of(r, width_a)],
+            ),
+            Swap(
+                query_w,
+                (width, HEAD_WIDTH),
+                lambda ref, q: ref.at[q],
+                lambda ref, at: ref.at[columns_of(at, width_a)],
+            ),
+            Line(
+                flat, (cols_n, rows_n) + flat.shape, lambda ref, c, r: ref.at[c, r], True
+            ),
+            Line(w_gains, (6, width), lambda ref, c, r: ref.at[:, columns_of(r, width_a)]),
+            Line(
+                per_layer,
+                (tokens, PLD),
+                lambda ref, c, r: ref.at[columns_of(r, quarter), columns_of(c, PLD // cols_n)],
+                True,
+            ),
+            Swap(
+                attend_own,
+                (data_n, HEAD_WIDTH, rows_n * out_cols),
+                lambda ref, q: ref,
+                lambda ref, at: ref.at[at],
+                "dp",
+            ),
+        ],
+        2,
+        115,
+    )
+    attend_w = (
+        attend_all.reshape(data_n, HEAD_WIDTH, rows_n, out_cols)
+        .transpose(1, 2, 0, 3)
+        .reshape(HEAD_WIDTH, width)
+    )
     flat = flat.reshape(cols_n, rows_n, data_n, -1)
     cuts = []
     start = 0
@@ -881,48 +1246,39 @@
     right_w = cuts[1].transpose(0, 3, 1, 2, 4).reshape(-1, width)
     pergate_w = cuts[2].transpose(1, 3, 0, 2, 4).reshape(width, -1)
     perproj_w = cuts[3].transpose(0, 3, 1, 2, 4).reshape(-1, width)
-
-    inputs = swap_row(activations, 0, 1).astype(FULL)
-    upstream = swap_row(cotangent, 0, 1).astype(FULL)
-    extras = lax.all_gather(lax.all_gather(per_layer, "row"), "col", axis=2)
-    extras = extras.reshape(tokens, -1)
+    upstream = upstream.astype(FULL)
     token_at = column * half_tok + me * share
     extras = lax.dynamic_slice_in_dim(extras, token_at, share, 0).astype(FULL)
     length = lax.dynamic_index_in_dim(lengths, data_at, 0, keepdims=True)
     piece_starts = lax.dynamic_index_in_dim(starts, data_at, 0, keepdims=False)
     spans = jnp.concatenate([length, piece_starts])
-    gains_here = lax.dynamic_slice_in_dim(w_gains, 0, 1, 0)[0]
-    gains = lax.all_gather(w_gains, "row", axis=1, tiled=True)
-
-    acts = activations.astype(FULL)
-    sums = jnp.sum(acts * acts, axis=1)
-    sums = small_total(sums.reshape(-1, 128), ("row",), 0, 1).reshape(-1, 1)
-    scale_here = lax.rsqrt(sums / MODEL_WIDTH + EPS)
-    hidden_here = (acts * scale_here * gains_here).astype(LOW)
-    spread_h = core_gather(hidden_here, 2).reshape(tokens, width_a)
-
-    raw_q = [flat_dot(spread_h, query_w[k]).astype(LOW) for k in range(heads_here)]
-    raw_k = flat_dot(spread_h, key_w).astype(LOW).reshape(rows_n, quarter, HEAD_WIDTH)
-    raw_v = flat_dot(spread_h, value_w).astype(LOW).reshape(rows_n, quarter, HEAD_WIDTH)
-    qkv_parts = jnp.concatenate([jnp.stack(raw_q), raw_k, raw_v], axis=1)
-    qkv_raw = line_reduce(qkv_parts, 3, False, 55)
-    query_raw = qkv_raw[:tokens]
-    key_raw = qkv_raw[tokens : tokens + quarter]
-    value_raw = qkv_raw[tokens + quarter :]
+
+    whole_hidden, whole_scale = whole_norm(whole_acts.astype(FULL), gains[0])
+    whole_hidden = whole_hidden.astype(LOW)
+    inputs = lax.dynamic_slice_in_dim(whole_acts, token_at, share, 0).astype(FULL)
+    query_raw = flat_dot(whole_hidden, head_w)
+    all_key_raw = flat_dot(whole_hidden, whole_kv[0])
+    all_value_raw = flat_dot(whole_hidden, whole_kv[1])
     query_gain = lax.dynamic_index_in_dim(w_heads, column * rows_n + me, 0, True)
-    key_gain = w_heads[QUERY_HEADS :]
+    key_gain = w_heads[QUERY_HEADS:]
     all_cos, all_sin = rope_tables(jnp.arange(tokens, dtype=jnp.int32), HEAD_WIDTH)
     own_cos = lax.dynamic_slice_in_dim(all_cos, me * quarter, quarter, 0)
     own_sin = lax.dynamic_slice_in_dim(all_sin, me * quarter, quarter, 0)
     query_n, query_scale = whole_norm(query_raw, query_gain)
     queries = turn(query_n, all_cos, all_sin).astype(LOW)
-    key_n, key_scale = whole_norm(key_raw, key_gain)
-    value_n, value_scale = whole_norm(value_raw, 1.0)
-    kv_here = jnp.concatenate([turn(key_n, own_cos, own_sin), value_n], axis=0).astype(LOW)
-    kv_all = line_gather(kv_here, 4, False, 20)
-    keys = kv_all[:, :quarter].reshape(tokens, HEAD_WIDTH)
-    values = kv_all[:, quarter:].reshape(tokens, HEAD_WIDTH)
+    keys = turn(whole_norm(all_key_raw, key_gain)[0], all_cos, all_sin).astype(LOW)
+    values = whole_norm(all_value_raw, 1.0)[0].astype(LOW)
     attended, top = head_forward(queries, keys, values, spans)
+    key_raw = lax.dynamic_slice_in_dim(all_key_raw, me * quarter, quarter, 0)
+    value_raw = lax.dynamic_slice_in_dim(all_value_raw, me * quarter, quarter, 0)
+    _, key_scale = whole_norm(key_raw, key_gain)
+    _, value_scale = whole_norm(value_raw, 1.0)
+    gateup_w = gateup_all.transpose(1, 2, 0, 3).reshape(2, width, -1)
+    down_w = (
+        down_all.reshape(data_n, data_n, ff_part, rows_n, out_cols)
+        .transpose(1, 2, 3, 0, 4)
+        .reshape(-1, width)
+    )
 
     def shares(parts):
         return parts.astype(LOW).reshape(cols_n, rows_n, share, width)
@@ -948,7 +1304,7 @@
     pact = (jax.nn.gelu(pgate, approximate=True) * extras).astype(LOW)
     perproj = flat_dot(pact, perproj_w)
     perproj_n, scale_pp = whole_norm(perproj, gains[5])
-    result = swap_row((block_out + perproj_n).astype(LOW), 1, 0)
+    result = (block_out + perproj_n).astype(LOW)
 
     gain_grads = [None] * 6
     d_perproj, gain_grads[5] = whole_norm_backward(perproj, scale_pp, gains[5], upstream)
@@ -961,7 +1317,25 @@
     dw_pergate = inner_rows(out_low, d_pgate)
     d_out = upstream + against(d_pgate, pergate_w)
     d_down, gain_grads[4] = whole_norm_backward(down_raw, scale_d, gains[4], d_out)
-    spread_d = line_gather(d_down.astype(LOW), 8, True, 40).reshape(tokens, width)
+    spread_d, result = transfers(
+        [
+            Line(
+                d_down.astype(LOW),
+                (cols_n, rows_n, share, width),
+                lambda ref, c, r: ref.at[c, r],
+                True,
+            ),
+            Swap(
+                result,
+                (half_tok, width_a),
+                lambda ref, q: ref.at[:, columns_of(q, width_a)],
+                lambda ref, at: ref.at[columns_of(at, share)],
+            ),
+        ],
+        8,
+        50,
+    )
+    spread_d = spread_d.reshape(tokens, width)
     d_act = against(spread_d, down_w)
     _, pullback = jax.vjp(
         lambda a, b: jax.nn.gelu(a, approximate=True) * b, gate_raw, up_raw
@@ -969,11 +1343,21 @@
     d_gate, d_up = pullback(d_act)
     d_gate, d_up = d_gate.astype(LOW), d_up.astype(LOW)
     d_ffn = against(d_gate, gateup_w[0]) + against(d_up, gateup_w[1])
-    d_ffn = line_reduce(shares(d_ffn), 9, True, 45)
     dw_down = inner_rows(act, spread_d).astype(LOW)
+    dw_down = dw_down.reshape(data_n, ff_part, rows_n, data_n, out_cols).transpose(3, 0, 1, 2, 4)
     dw_gateup = jnp.stack(
-        [inner_rows(spread_f, d_gate).astype(LOW), inner_rows(spread_f, d_up).astype(LOW)]
-    )
+        [
+            inner_rows(spread_f, grad[:, k * ff_part : (k + 1) * ff_part]).astype(LOW)
+            for k in range(data_n)
+            for grad in (d_gate, d_up)
+        ]
+    ).reshape(data_n, 2, width, ff_part)
+    d_ffn, dw_down, dw_gateup = lax.optimization_barrier((shares(d_ffn), dw_down, dw_gateup))
+    g_gateup = lax.psum_scatter(dw_gateup, "dp", scatter_dimension=0)
+    g_down = lax.psum_scatter(
+        dw_down.reshape(data_n, data_n, ff_part, -1), "dp", scatter_dimension=0
+    )
+    d_ffn = line_reduce(d_ffn, 9, True, 45)
     d_mix, gain_grads[3] = whole_norm_backward(mixture, scale_f, gains[3], d_ffn)
     d_half = (d_out + d_mix) * HALF_ROOT
     d_proj, gain_grads[2] = whole_norm_backward(projected, scale_p, gains[2], d_half)
@@ -984,8 +1368,8 @@
     d_middle = against(d_right, right_w).astype(LOW)
     dw_left = inner_rows(hidden_low, d_middle)
     d_hidden_share = d_half + against(d_middle, left_w)
-    both = jnp.stack([d_half, d_hidden_share]).astype(LOW)
-    both = swap_row(both, 2, 1)
+    inner_share = jnp.sum(d_hidden_share * gains[0] * inputs, axis=1)
+    half_low, share_low = d_half.astype(LOW), d_hidden_share.astype(LOW)
     d_attended = against(spread_p, attend_w).astype(LOW)
     dw_attend = inner_rows(attended, spread_p).astype(LOW)
     d_queries, d_keys, d_values = head_backward(queries, keys, values, d_attended, spans)
@@ -1012,56 +1396,31 @@
     d_hidden = against(d_k_all, key_w) + against(d_v_all, value_w)
     for k in range(heads_here):
         d_hidden = d_hidden + against(d_q_all[k], query_w[k])
-    d_hidden = core_reduce(d_hidden.astype(LOW).reshape(cols_n, half_tok, width_a), 13)
-    d_hidden = d_hidden + both[1].astype(FULL)
-    weighted = d_hidden * gains_here
-    inner = jnp.sum(weighted * acts, axis=1)
-    inner = small_total(inner.reshape(-1, 128), ("row",), 0, 14).reshape(-1, 1) / MODEL_WIDTH
-    grad_input = (
-        both[0].astype(FULL)
-        + scale_here * weighted
-        - acts * (scale_here * scale_here * scale_here) * inner
-    ).astype(LOW)
-    gain_zero = jnp.sum(d_hidden * acts * scale_here, axis=0)
-
-    dw_query = jnp.stack([inner_rows(spread_h, d_q_all[k]) for k in range(heads_here)])
-    dw_key = inner_rows(spread_h, d_k_all)
-    dw_value = inner_rows(spread_h, d_v_all)
-    zero = jnp.zeros_like(dw_key)
-    first = column == 0
+    acts = activations.astype(FULL)
+    gains_here = lax.dynamic_slice_in_dim(w_gains, 0, 1, 0)[0]
+    scale_here = lax.dynamic_slice_in_dim(whole_scale, column * half_tok, half_tok, 0)
+    own_acts = lax.dynamic_slice_in_dim(whole_acts, me * width_a, width_a, 1).astype(FULL)
+    inner = jnp.sum(d_hidden * gains_here * own_acts, axis=1)
+    inner = lax.dynamic_update_slice_in_dim(
+        inner, lax.dynamic_slice_in_dim(inner, token_at, share, 0) + inner_share, token_at, 0
+    ).reshape(-1, 128)
+
+    spread_h = lax.dynamic_slice_in_dim(whole_hidden, me * width_a, width_a, 1)
+    dw_query = jnp.stack([inner_rows(spread_h, d_q_all[k]).astype(LOW) for k in range(heads_here)])
     dw_kv = jnp.stack(
-        [
-            jnp.where(first, dw_key, zero),
-            jnp.where(first, zero, dw_key),
-            jnp.where(first, dw_value, zero),
-            jnp.where(first, zero, dw_value),
-        ]
-    )
-    g_qkv = lax.psum_scatter(
-        jnp.concatenate([dw_query, dw_kv], axis=2).astype(LOW), "dp", scatter_dimension=0
-    ).astype(FULL)
-    g_query = g_qkv[:, : w_query.shape[1]]
-    g_keyval = g_qkv[:, w_query.shape[1] :]
-    g_keyval = g_keyval + lax.ppermute(g_keyval, "col", [(0, 1), (1, 0)])
+        [inner_rows(spread_h, d_k_all).astype(LOW), inner_rows(spread_h, d_v_all).astype(LOW)]
+    )
     g_attend = lax.psum_scatter(
-        dw_attend.reshape(HEAD_WIDTH, rows_n, data_n, attend_cols), "dp", scatter_dimension=2
-    )
-    g_attend = swap_row(g_attend, 1, 0, False).reshape(w_attend.shape).astype(FULL)
-    g_gateup = lax.psum_scatter(dw_gateup, "dp", scatter_dimension=2, tiled=True)
-    g_gateup = swap_row(g_gateup, 1, 2).astype(FULL)
-    g_down = lax.psum_scatter(
-        dw_down.reshape(data_n * ff_part, rows_n, data_n, w_down.shape[1]),
+        dw_attend.reshape(HEAD_WIDTH, rows_n, data_n, out_cols).transpose(2, 0, 1, 3).reshape(data_n, HEAD_WIDTH, -1),
         "dp",
-        scatter_dimension=2,
-    )
-    g_down = swap_row(g_down.reshape(data_n, ff_part, rows_n, w_down.shape[1]), 2, 1, False)
-    g_down = g_down.reshape(w_down.shape).astype(FULL)
+        scatter_dimension=0,
+    )
 
     def to_shards(grad, rows_first):
         if rows_first:
             cut = grad.reshape(rows_n, width_a, cols_n, data_n, -1).transpose(2, 0, 3, 1, 4)
         else:
-            cut = grad.reshape(cols_n, -1, rows_n, data_n, width_a // data_n).transpose(0, 2, 3, 1, 4)
+            cut = grad.reshape(cols_n, -1, rows_n, data_n, out_cols).transpose(0, 2, 3, 1, 4)
         return cut.astype(LOW).reshape(cols_n, rows_n, data_n, -1)
 
     flat_grads = jnp.concatenate(
@@ -1072,16 +1431,71 @@
             to_shards(dw_perproj, False),
         ],
         axis=3,
-    ).reshape(cols_n, rows_n, data_n, -1, 128)
-    flat_grads = lax.psum_scatter(flat_grads, "col", scatter_dimension=0)
-    flat_grads = lax.psum_scatter(flat_grads, "row", scatter_dimension=0)
-    flat_grads = lax.psum_scatter(flat_grads, "dp", scatter_dimension=0).astype(FULL).reshape(-1)
+    ).reshape(cols_n, rows_n, data_n * flat_rows, 128)
+    flat_grads = line_reduce(flat_grads, 17, True, 28).astype(LOW).reshape(data_n, flat_rows, 128)
+    g_query, g_keyval, flat_grads = shard_total(dw_query, dw_kv, flat_grads, 13)
+    squares = jnp.where(column == 0, jnp.sum(g_keyval * g_keyval), 0.0)
+    for gradient in (g_query, g_attend, g_gateup, g_down, flat_grads):
+        gradient = gradient.astype(FULL)
+        squares = squares + jnp.sum(gradient * gradient)
+    g_gateup, g_down, g_attend, half_here, share_here, d_hidden, inner = transfers(
+        [
+            Swap(
+                g_gateup,
+                w_gateup.shape,
+                lambda ref, q: ref.at[:, columns_of(q, width_a), :],
+                lambda ref, at: ref.at[:, :, columns_of(at, ff_part)],
+            ),
+            Swap(
+                g_down,
+                (data_n, rows_n, ff_part, out_cols),
+                lambda ref, q: ref.at[:, :, columns_of(q, out_cols)],
+                lambda ref, at: ref.at[:, at],
+            ),
+            Swap(
+                g_attend,
+                (rows_n, HEAD_WIDTH, out_cols),
+                lambda ref, q: ref.at[:, columns_of(q, out_cols)],
+                lambda ref, at: ref.at[at],
+            ),
+            Swap(
+                half_low,
+                (half_tok, width_a),
+                lambda ref, q: ref.at[:, columns_of(q, width_a)],
+                lambda ref, at: ref.at[columns_of(at, share)],
+            ),
+            Swap(
+                share_low,
+                (half_tok, width_a),
+                lambda ref, q: ref.at[:, columns_of(q, width_a)],
+                lambda ref, at: ref.at[columns_of(at, share)],
+            ),
+            Pair(d_hidden.astype(LOW).reshape(cols_n, half_tok, width_a)),
+            Line(inner, (cols_n, rows_n) + inner.shape, lambda ref, c, r: ref.at[c, r], True),
+        ],
+        14,
+        100,
+    )
+    g_gateup = g_gateup.astype(FULL)
+    g_down = g_down.reshape(w_down.shape).astype(FULL)
+    g_attend = g_attend.reshape(w_attend.shape).astype(FULL)
+    flat_grads = flat_grads.reshape(-1)
     small_grads = []
     start = 0
     for w in smalls:
         small_grads.append(flat_grads[start : start + w.size].reshape(w.shape))
         start += w.size
     g_left, g_right, g_pergate, g_perproj = small_grads
+
+    inner = jnp.sum(inner, axis=(0, 1)).reshape(cols_n, half_tok) / MODEL_WIDTH
+    inner = lax.dynamic_index_in_dim(inner, column, 0, False)[:, None]
+    d_hidden = d_hidden[0].astype(FULL) + d_hidden[1].astype(FULL) + share_here.astype(FULL)
+    grad_input = (
+        half_here.astype(FULL)
+        + scale_here * d_hidden * gains_here
+        - acts * (scale_here * scale_here * scale_here) * inner
+    ).astype(LOW)
+    gain_zero = jnp.sum(d_hidden * acts * scale_here, axis=0)
 
     gain_full = jnp.stack(
         [
@@ -1105,7 +1519,7 @@
         [
             gain_full.reshape(-1, 128),
             head_full.reshape(-1, 128),
-            jnp.zeros((pad_rows, 128), FULL),
+            jnp.broadcast_to(squares, (pad_rows, 128)),
             jnp.broadcast_to(logit_row[None], (8, 128)),
         ]
     )
@@ -1114,10 +1528,7 @@
     head_sum = small[gain_rows : gain_rows + head_rows].reshape(QUERY_HEADS + 1, HEAD_WIDTH)
     logit_top = small[-1, :QUERY_HEADS]
     g_gains = lax.dynamic_slice_in_dim(gain_sum, me * width_a, width_a, 1)
-    squares = jnp.where(first, jnp.sum(g_keyval * g_keyval), 0.0)
-    for gradient in (g_query, g_attend, g_gateup, g_down, g_left, g_right, g_pergate, g_perproj):
-        squares = squares + jnp.sum(gradient * gradient)
-    squares = small_total(jnp.broadcast_to(squares, (8, 128)), ("col", "row", "dp"), 0, 16)[0, 0]
+    squares = small[gain_rows + head_rows, 0]
     squares = squares + jnp.sum(gain_sum * gain_sum) + jnp.sum(head_sum * head_sum)
     grad_norm = jnp.sqrt(squares)
     clip_scale = CLIP / jnp.maximum(grad_norm, CLIP)

time: 1160 us -> 1190 us (1.026)
  Pallas kernels: 500 us -> 733 us
  blocking collectives: 132 us -> 0 us
  waiting for transfers between devices: 73.8 us -> 0.78 us
  local copies, waits for them, and re-layouts: 175 us -> 215 us
  starting transfers between devices: 35.4 us -> 0.2 us
    pallas_call x2 -> x5, Pallas kernels: 4.07 us -> 390 us  [the longest x4 366 us: transfers(): pl.pallas_call(kernel, out_shape=[jax.ShapeDtypeStruct(item.shape, item.s...]
    all_gather x4 -> x0, blocking collectives: 89.2 us -> none  [the longest x1 53.3 us: line_device(): gains = lax.all_gather(w_gains, 'row', axis=1, tiled=True)]
    pallas_call x5 -> x3, Pallas kernels: 203 us -> 136 us  [line_gather(): pl.pallas_call(kernel, out_shape=jax.ShapeDtypeStruct(shape, block.dtype)...]
    pallas_call x4 -> x1, Pallas kernels: 73.4 us -> 14.6 us  [small_total(): pl.pallas_call(kernel, out_shape=jax.ShapeDtypeStruct(values_in.shape, FU...]
    all_to_all x2 -> x0, blocking collectives: 43 us -> none  [swap_row(): return lax.all_to_all(values_in, 'row', split, concat, tiled=tiled)]
    all_to_all x8 -> x0, waiting for transfers between devices: 38.2 us -> none  [swap_row(): return lax.all_to_all(values_in, 'row', split, concat, tiled=tiled)]
    all_to_all x8 -> x0, starting transfers between devices: 34.4 us -> none  [swap_row(): return lax.all_to_all(values_in, 'row', split, concat, tiled=tiled)]
    reshape x4 -> x9, local copies, waits for them, and re-layouts: 15 us -> 47.1 us  [the longest x2 16.6 us: line_device(): down_all.reshape(data_n, data_n, ff_part, rows_n, out_cols)]
  transfers between devices with their start and end apart: 22 -> 5, of which waited for: 6 -> 0; matrix products, arithmetic and copies ran while one was open for 22% -> 18% of each run, Pallas kernels for 28% -> 29%
where the time goes in v2:
time: 1190 us; the launch traced here: 1180 us
  Pallas kernels  733 us (62%)
  local copies, waits for them, and re-layouts  215 us (18%)
  matrix products  116 us (10%)
  other arithmetic  89.3 us (8%)
  between operations  23.3 us (2%)
    pallas_call x4, Pallas kernels, transfers(): pl.pallas_call(kernel, out_shape=[jax.ShapeDtypeStruct(item.shape, item.s...  366 us
    pallas_call x5, Pallas kernels, line_reduce(): pl.pallas_call(kernel, out_shape=jax.ShapeDtypeStruct((high, wide), FULL)...  173 us
    pallas_call x3, Pallas kernels, line_gather(): pl.pallas_call(kernel, out_shape=jax.ShapeDtypeStruct(shape, block.dtype)...  136 us
    unnamed x322, local copies, waits for them, and re-layouts  54.6 us
    dot_general x14, matrix products, against(): lax.dot_general(grad_mat, weight_mat, (((1,), (1,)), ((), ())), preferred...  47.4 us
    dot_general x11, matrix products, flat_dot(): return jnp.dot(left_mat, right_mat, preferred_element_type=jnp.float32)  36 us
    dot_general x20, matrix products, inner_rows(): lax.dot_general(left_mat, right_mat, (((0,), (0,)), ((), ())), preferred_...  32.3 us
    pallas_call x1, Pallas kernels, shard_total(): pl.pallas_call(kernel, out_shape=[jax.ShapeDtypeStruct(shape, FULL) for s...  24.5 us
  transfers between devices with their start and end apart: 5, of which 0 were waited for; matrix products, arithmetic and copies ran while one was open for 18% of the time, Pallas kernels for 29%

profile of v2, /device:TPU:0, one launch (start us, length us, event | category | flops | bytes accessed | tf_op | source)
XLA Modules:
  0.0 1177.2 jit_solution(7256751692488871849)
XLA Ops:
  20.0 90.0 %shard_map.645 = (bf16[2,2048,256]{2,1,0:T(8,128)(2,1)S(1)}, bf16[4,256,512]{2,1,0:T(8,128)(2,1)S(1)}, bf16[256,512]{1,0:T(8,128)(2,1)S(1)}, bf16[128,2048]{1,0:...) custom-call(bf16[2,512,1024]{2,1,0:T(8,128)(2,1)S(1)} %convert_element_type.311.refs_0_, ...), custom_call_target="tpu_custom_call" | custom-call | bytes 270000000 | tf_op jit(solution)/shard_map/pallas_call | solution.py:819
  125.3 117.5 %shard_map.646 = (bf16[1024,2048]{1,0:T(8,128)(2,1)S(1)}, bf16[2,2048,256]{2,1,0:T(8,128)(2,1)S(1)}, bf16[2048,256]{1,0:T(8,128)(2,1)S(1)}, bf16[2,4,1280,128]{3...) custom-call(bf16[512,512]{1,0:T(8,128)(2,1)S(1)} %copy-done.27, ...), custom_call_target="tpu_custom_call" | custom-call | bytes 345000000 | tf_op jit(solution)/shard_map/pallas_call | solution.py:819
  253.2 5.8 reshape.568
  259.0 3.6 copy.319
  264.5 3.6 fusion
  274.6 3.8 multiply_reduce_fusion.20
  278.7 5.2 multiply_reduce_fusion.18
  296.5 9.0 shard_map.647
  306.8 39.7 %shard_map.648 = f32[128,2048]{1,0:T(8,128)S(1)} custom-call(bf16[2,4,128,2048]{3,2,1,0:T(8,128)(2,1)S(1)} %bitcast.280), custom_call_target="tpu_custom_call" | custom-call | bytes 135000000 | tf_op jit(solution)/shard_map/pallas_call | solution.py:564
  352.2 44.8 %shard_map.649 = bf16[2,4,128,2048]{3,2,1,0:T(8,128)(2,1)S(1)} custom-call(bf16[128,2048]{1,0:T(8,128)(2,1)S(1)} %multiply_convert_fusion.2.x_ref), custom_call_target="tpu_custom_call" | custom-call | bytes 120000000 | tf_op jit(solution)/shard_map/pallas_call | solution.py:415
  401.3 5.2 reshape.576
  406.5 4.7 copy.324
  422.2 6.9 reshape.573
  429.2 9.6 copy.351
  438.8 7.8 reshape.574
  446.5 5.9 fusion.172
  452.4 6.3 copy.321
  458.7 6.3 copy.322
  465.0 8.1 fusion.179
  473.2 6.9 multiply_convert_fusion.1
  481.4 4.8 convolution_convert_fusion.2
  486.1 40.3 %shard_map.650 = f32[128,2048]{1,0:T(8,128)S(1)} custom-call(bf16[2,4,128,2048]{3,2,1,0:T(8,128)(2,1)S(1)} %bitcast.284), custom_call_target="tpu_custom_call" | custom-call | bytes 135000000 | tf_op jit(solution)/shard_map/pallas_call | solution.py:564
  532.8 51.1 %shard_map.651 = (bf16[2,4,128,2048]{3,2,1,0:T(8,128)(2,1)S(1)}, bf16[512,512]{1,0:T(8,128)(2,1)S(1)}) custom-call(bf16[128,2048]{1,0:T(8,128)(2,1)S(1)} %subtract_convert_fusion.3.refs_0_, bf16[128,2048]{1,0:T(8,128)(2,1)S(1)} %get-tuple-element.377.refs_1_), custom_call_target="tpu_custom_call" | custom-call | bytes 150000000 | tf_op jit(solution)/shard_map/pallas_call | solution.py:819
  583.9 6.3 convolution_convert_fusion.1
  590.2 10.2 multiply_convert_fusion
  600.4 6.9 fusion.180
  609.6 8.1 reshape.582
  617.8 12.0 %add_convert_fusion = bf16[1024,2048]{1,0:T(8,128)(2,1)} fusion(f32[1024,2048]{1,0:T(8,128)} %fusion.180, bf16[1024,1024]{1,0:T(8,128)(2,1)} %get-tuple-element.359, bf16[2048,1024]{0,1:T(8,128)(2,1)} %bitcast.318), kind=kOutput, calls=%fused_computation.5 | convolution fusion | flops 4299161600 | bytes 18874368 | tf_op jit(solution)/shard_map/dot_general | solution.py:79
  639.8 3.3 copy-done.73
  645.4 43.5 %shard_map.652 = f32[128,2048]{1,0:T(8,128)S(1)} custom-call(bf16[2,4,128,2048]{3,2,1,0:T(8,128)(2,1)S(1)} %bitcast.283), custom_call_target="tpu_custom_call" | custom-call | bytes 135000000 | tf_op jit(solution)/shard_map/pallas_call | solution.py:564
  693.1 39.0 %shard_map.653 = bf16[2,4,128,2048]{3,2,1,0:T(8,128)(2,1)S(1)} custom-call(bf16[128,2048]{1,0:T(8,128)(2,1)S(1)} %get-tuple-element.387.x_ref), custom_call_target="tpu_custom_call" | custom-call | bytes 120000000 | tf_op jit(solution)/shard_map/pallas_call | solution.py:415
  741.8 6.2 copy.326
  748.1 7.2 reshape.584
  759.5 3.7 convolution_convert_fusion.16.g_ref
  763.2 9.9 shard_map.654
  773.3 22.5 %shard_map.655 = f32[512,256]{1,0:T(8,128)S(1)} custom-call(bf16[4,512,256]{2,1,0:T(8,128)(2,1)S(1)} %pad_maximum_fusion.2.x_ref), custom_call_target="tpu_custom_call" | custom-call | bytes 60000000 | tf_op jit(solution)/shard_map/pallas_call | solution.py:564
  809.5 52.1 %shard_map.656 = bf16[4,1536,256]{2,1,0:T(8,128)(2,1)S(1)} custom-call(bf16[1536,256]{1,0:T(8,128)(2,1)S(1)} %pad_maximum_fusion.4.x_ref), custom_call_target="tpu_custom_call" | custom-call | bytes 165000000 | tf_op jit(solution)/shard_map/pallas_call | solution.py:415
  874.7 4.6 copy.336
  879.3 6.5 reshape.599
  895.4 6.2 reshape.597
  907.6 5.4 reshape.601.x_ref
  914.7 27.0 %shard_map.658 = f32[1280,128]{1,0:T(8,128)S(1)} custom-call(bf16[2,4,1280,128]{3,2,1,0:T(8,128)(2,1)S(1)} %copy-done.4), custom_call_target="tpu_custom_call" | custom-call | bytes 84000000 | tf_op jit(solution)/shard_map/pallas_call | solution.py:564
  945.1 24.5 %shard_map.659 = (f32[512,256]{1,0:T(8,128)S(1)}, f32[512,256]{1,0:T(8,128)S(1)}, f32[320,128]{1,0:T(8,128)S(1)}) custom-call(bf16[4,512,256]{2,1,0:T(8,128)(2,1)S(1)} %pad_maximum_fusion.3.q_ref, bf16[2,512,256]{2,1,0:T(8,128)(2,1)S(1)} %pad_maximum_fusion.9.kv_ref, bf16[4,320,128]{2,1,0:T(8,128)(2,1)S(1)} %bitcast.299), custom_call_target="tpu_custom_call" | custom-call | bytes 60000000 | tf_op jit(solution)/shard_map/pallas_call | solution.py:905
  983.7 3.3 multiply_reduce_fusion.2
  999.2 107.1 %shard_map.657 = (bf16[2,512,1024]{2,1,0:T(8,128)(2,1)S(1)}, bf16[4,4,256,128]{3,2,1,0:T(8,128)(2,1)S(1)}, bf16[4,256,128]{2,1,0:T(8,128)(2,1)S(1)}, bf16[512,51...) custom-call(bf16[2,2048,256]{2,1,0:T(8,128)(2,1)S(1)} %bitcast.281, ...), custom_call_target="tpu_custom_call" | custom-call | bytes 300000000 | tf_op jit(solution)/shard_map/pallas_call | solution.py:819
  1118.0 14.6 %shard_map.660 = f32[128,128]{1,0:T(8,128)S(1)} custom-call(f32[128,128]{1,0:T(8,128)S(1)} %pad_maximum_fusion.11.x_ref), custom_call_target="tpu_custom_call" | custom-call | bytes 36000000 | tf_op jit(solution)/shard_map/pallas_call | solution.py:955
  1153.9 8.0 multiply_subtract_fusion
  1162.1 3.9 multiply_subtract_fusion.1
  (538 shorter events, 225.4 us)
Async XLA Ops:
  7.2 256.4 %copy-start = (s32[4,2]{0,1:T(2,128)S(1)}, s32[4,2]{0,1:T(2,128)}, u32[]{:S(2)}) copy-start(s32[4,2]{0,1:T(2,128)} %param.44) | copy-start | bytes 100
  7.2 415.0 %all-gather.7.cloned.1.call-start = ((), (), s32[]{:S(2)}) async-start(), calls=%async_computation.4 | async-start | bytes 5242880 | tf_op jit(solution)/shard_map/all_gather | solution.py:1189
  115.0 331.5 %all-gather.5.cloned.1.call-start = ((), (), s32[]{:S(2)}) async-start(), calls=%async_computation.3 | async-start | bytes 10485760 | tf_op jit(solution)/shard_map/all_gather | solution.py:1188
  115.8 871.6 %reduce-scatter.14.cloned.1.call-start = ((), (), s32[]{:S(2)}) async-start(), calls=%async_computation.7 | async-start | bytes 1310720
  263.6 85.8 %copy-start.85 = (bf16[64,2048]{1,0:T(8,128)(2,1)}, bf16[64,2048]{1,0:T(8,128)(2,1)S(1)}, u32[]{:S(2)}) copy-start(bf16[64,2048]{1,0:T(8,128)(2,1)S(1)} %reshape.571) | copy-start | bytes 786436
  268.1 81.8 %copy-start.111 = (f32[1,2048]{1,0:T(1,128)}, f32[1,2048]{1,0:T(1,128)S(1)}, u32[]{:S(2)}) copy-start(f32[1,2048]{1,0:T(1,128)S(1)} %get-tuple-element.399) | copy-start | bytes 24580
  278.7 14.7 %copy-start.59 = (f32[1024,256]{1,0:T(8,128)}, f32[1024,256]{1,0:T(8,128)S(1)}, u32[]{:S(2)}) copy-start(f32[1024,256]{1,0:T(8,128)S(1)} %copy.315) | copy-start | bytes 3145732
  293.6 11.9 %copy-start.76 = (bf16[4,256,4,128]{1,3,0,2:T(8,128)(2,1)S(1)}, bf16[4,256,4,128]{1,3,0,2:T(8,128)(2,1)}, u32[]{:S(2)}) copy-start(bf16[4,256,4,128]{1,3,0,2:T(8,128)(2,1)} %copy.318) | copy-start | bytes 3145732
  347.9 49.1 %copy-start.146 = (f32[128]{0:T(128)}, f32[128]{0:T(128)S(1)}, u32[]{:S(2)}) copy-start(f32[128]{0:T(128)S(1)} %add_rsqrt_fusion.10) | copy-start | bytes 1540
  349.4 47.6 %copy-start.113 = (bf16[128,64]{0,1:T(8,128)(2,1)}, bf16[128,64]{0,1:T(8,128)(2,1)S(1)}, u32[]{:S(2)}) copy-start(bf16[128,64]{0,1:T(8,128)(2,1)S(1)} %convolution_convert_fusion.24) | copy-start | bytes 49156
  349.9 47.2 %copy-start.61 = (f32[128,2048]{1,0:T(8,128)}, f32[128,2048]{1,0:T(8,128)S(1)}, u32[]{:S(2)}) copy-start(f32[128,2048]{1,0:T(8,128)S(1)} %get-tuple-element.421) | copy-start | bytes 3145732
  349.9 49.1 %copy-start.65 = (bf16[2,4,4,40960]{3,2,1,0:T(4,128)(2,1)S(1)}, bf16[2,4,4,40960]{3,2,1,0:T(4,128)(2,1)}, u32[]{:S(2)}) copy-start(bf16[2,4,4,40960]{3,2,1,0:T(4,128)(2,1)} %reshape.567) | copy-start | bytes 7864324
  352.0 49.3 %copy-start.55 = (f32[128,2048]{1,0:T(8,128)}, f32[128,2048]{1,0:T(8,128)S(1)}, u32[]{:S(2)}) copy-start(f32[128,2048]{1,0:T(8,128)S(1)} %get-tuple-element.358) | copy-start | bytes 3145732
  486.1 40.5 %copy-start.56 = (f32[128,2048]{1,0:T(8,128)S(1)}, f32[128,2048]{1,0:T(8,128)}, u32[]{:S(2)}) copy-start(f32[128,2048]{1,0:T(8,128)} %copy-done.55) | copy-start | bytes 3145732
  486.1 40.7 %copy-start.66 = (bf16[32,8,4,512]{3,1,2,0:T(8,128)(2,1)S(1)}, bf16[32,8,4,512]{3,1,2,0:T(8,128)(2,1)}, u32[]{:S(2)}) copy-start(bf16[32,8,4,512]{3,1,2,0:T(8,128)(2,1)} %copy.346) | copy-start | bytes 3145732
  531.2 59.0 %copy-start.105 = (bf16[128,256]{1,0:T(8,128)(2,1)}, bf16[128,256]{1,0:T(8,128)(2,1)S(1)}, u32[]{:S(2)}) copy-start(bf16[128,256]{1,0:T(8,128)(2,1)S(1)} %fusion.139) | copy-start | bytes 196612
  531.2 52.7 %copy-start.156 = (bf16[1024,1024]{1,0:T(8,128)(2,1)S(1)}, bf16[1024,1024]{1,0:T(8,128)(2,1)}, u32[]{:S(2)}) copy-start(bf16[1024,1024]{1,0:T(8,128)(2,1)} %copy-done.155) | copy-start | bytes 6291460
  617.7 12.0 %copy-start.13 = (bf16[2,4,128,2048]{3,2,1,0:T(8,128)(2,1)S(1)}, bf16[2,4,128,2048]{3,2,1,0:T(8,128)(2,1)}, u32[]{:S(2)}) copy-start(bf16[2,4,128,2048]{3,2,1,0:T(8,128)(2,1)} %copy-done.11) | copy-start | bytes 12582916
  617.8 12.0 %copy-start.72 = (bf16[8,2048,256]{2,1,0:T(8,128)(2,1)S(1)}, bf16[8,2048,256]{2,1,0:T(8,128)(2,1)}, u32[]{:S(2)}) copy-start(bf16[8,2048,256]{2,1,0:T(8,128)(2,1)} %fusion.12) | copy-start | bytes 25165828
  617.8 12.0 %copy-start.152 = (bf16[1024,1024]{1,0:T(8,128)(2,1)S(1)}, bf16[1024,1024]{1,0:T(8,128)(2,1)}, u32[]{:S(2)}) copy-start(bf16[1024,1024]{1,0:T(8,128)(2,1)} %get-tuple-element.359) | copy-start | bytes 6291460
  645.4 43.5 %copy-start.57 = (f32[128,2048]{1,0:T(8,128)S(1)}, f32[128,2048]{1,0:T(8,128)}, u32[]{:S(2)}) copy-start(f32[128,2048]{1,0:T(8,128)} %copy-done.55) | copy-start | bytes 3145732
  645.4 43.9 %copy-start.68 = (f32[128,2048]{1,0:T(8,128)S(1)}, f32[128,2048]{1,0:T(8,128)}, u32[]{:S(2)}) copy-start(f32[128,2048]{1,0:T(8,128)} %copy-done.67) | copy-start | bytes 3145732
  691.8 42.3 %copy-start.31 = (bf16[1024,256]{1,0:T(8,128)(2,1)S(1)}, bf16[1024,256]{1,0:T(8,128)(2,1)}, u32[]{:S(2)}) copy-start(bf16[1024,256]{1,0:T(8,128)(2,1)} %copy-done.30) | copy-start | bytes 1572868
  741.8 247.9 %reduce-scatter.12.cloned.1.call-start = ((), (), s32[]{:S(2)}) async-start(), calls=%async_computation.6 | async-start | bytes 5242880
  755.3 236.8 %reduce-scatter.10.cloned.1.call-start = ((), (), s32[]{:S(2)}) async-start(), calls=%async_computation.5 | async-start | bytes 10485760
  758.9 41.2 %copy-start.139 = (f32[256]{0:T(256)}, f32[256]{0:T(256)S(1)}, u32[]{:S(2)}) copy-start(f32[256]{0:T(256)S(1)} %get-tuple-element.409) | copy-start | bytes 3076
  773.1 23.9 %copy-start.145 = (f32[128]{0:T(128)S(1)}, f32[128]{0:T(128)}, u32[]{:S(2)}) copy-start(f32[128]{0:T(128)} %copy-done.144) | copy-start | bytes 1540
  773.2 26.8 %copy-start.129 = (f32[1,256]{1,0:T(1,128)S(1)}, f32[1,256]{1,0:T(1,128)}, u32[]{:S(2)}) copy-start(f32[1,256]{1,0:T(1,128)} %copy-done.128) | copy-start | bytes 3076
  807.8 53.8 %copy-start.141 = (f32[256]{0:T(256)S(1)}, f32[256]{0:T(256)}, u32[]{:S(2)}) copy-start(f32[256]{0:T(256)} %get-tuple-element.308) | copy-start | bytes 3076
  807.8 53.9 %copy-start.142 = (f32[256]{0:T(256)S(1)}, f32[256]{0:T(256)}, u32[]{:S(2)}) copy-start(f32[256]{0:T(256)} %get-tuple-element.312) | copy-start | bytes 3076
  809.5 57.5 %copy-start.106 = (bf16[128,256]{1,0:T(8,128)(2,1)S(1)}, bf16[128,256]{1,0:T(8,128)(2,1)}, u32[]{:S(2)}) copy-start(bf16[128,256]{1,0:T(8,128)(2,1)} %copy-done.105) | copy-start | bytes 196612
  879.3 11.7 copy-start.112
  879.3 11.7 copy-start.147
  914.7 27.2 %copy-start.79 = (bf16[1024,2048]{1,0:T(8,128)(2,1)S(1)}, bf16[1024,2048]{1,0:T(8,128)(2,1)}, u32[]{:S(2)}) copy-start(bf16[1024,2048]{1,0:T(8,128)(2,1)} %copy-done.78) | copy-start | bytes 12582916
  987.0 124.1 %copy-start.28 = (bf16[512,512]{1,0:T(8,128)(2,1)S(1)}, bf16[512,512]{1,0:T(8,128)(2,1)}, u32[]{:S(2)}) copy-start(bf16[512,512]{1,0:T(8,128)(2,1)} %refs_0_.1) | copy-start | bytes 1572868
  987.0 124.1 %copy-start.140 = (f32[512,1]{0,1:T(1,128)S(1)}, f32[512,1]{0,1:T(1,128)}, u32[]{:S(2)}) copy-start(f32[512,1]{0,1:T(1,128)} %multiply_multiply_fusion.19) | copy-start | bytes 6148
  999.2 114.8 %copy-start.122 = (f32[2048]{0:T(1024)S(1)}, f32[2048]{0:T(1024)}, u32[]{:S(2)}) copy-start(f32[2048]{0:T(1024)} %get-tuple-element.315) | copy-start | bytes 24580
  999.2 114.9 %copy-start.6 = (bf16[1,2,2048,256]{3,2,1,0:T(8,128)(2,1)S(1)}, bf16[1,2,2048,256]{3,2,1,0:T(8,128)(2,1)}, u32[]{:S(2)}) copy-start(bf16[1,2,2048,256]{3,2,1,0:T(8,128)(2,1)} %reduce-scatter.10.cloned.1.call-done) | copy-start | bytes 6291460
  999.2 118.7 %copy-start.149 = (f32[128]{0:T(128)S(1)}, f32[128]{0:T(128)}, u32[]{:S(2)}) copy-start(f32[128]{0:T(128)} %copy-done.148) | copy-start | bytes 1540
  1111.1 27.3 %copy-start.143 = (s32[256]{0:T(256)S(1)}, s32[256]{0:T(256)}, u32[]{:S(2)}) copy-start(s32[256]{0:T(256)} %get-tuple-element.437) | copy-start | bytes 3076
  1111.1 31.2 %copy-start.118 = (f32[32,128]{1,0:T(8,128)S(1)}, f32[32,128]{1,0:T(8,128)}, u32[]{:S(2)}) copy-start(f32[32,128]{1,0:T(8,128)} %param.63) | copy-start | bytes 49156
  1111.1 31.2 %copy-start.131 = (f32[32,128]{1,0:T(8,128)S(1)}, f32[32,128]{1,0:T(8,128)}, u32[]{:S(2)}) copy-start(f32[32,128]{1,0:T(8,128)} %param.65) | copy-start | bytes 49156
  1111.2 31.2 %copy-start.132 = (f32[32,128]{1,0:T(8,128)S(1)}, f32[32,128]{1,0:T(8,128)}, u32[]{:S(2)}) copy-start(f32[32,128]{1,0:T(8,128)} %param.64) | copy-start | bytes 49156
  1113.9 29.9 %copy-start.110 = (f32[128,128]{1,0:T(8,128)S(1)}, f32[128,128]{1,0:T(8,128)}, u32[]{:S(2)}) copy-start(f32[128,128]{1,0:T(8,128)} %param.69) | copy-start | bytes 196612
  1113.9 29.9 %copy-start.120 = (f32[128,128]{1,0:T(8,128)S(1)}, f32[128,128]{1,0:T(8,128)}, u32[]{:S(2)}) copy-start(f32[128,128]{1,0:T(8,128)} %param.71) | copy-start | bytes 196612
  1113.9 29.9 %copy-start.121 = (f32[128,128]{1,0:T(8,128)S(1)}, f32[128,128]{1,0:T(8,128)}, u32[]{:S(2)}) copy-start(f32[128,128]{1,0:T(8,128)} %param.70) | copy-start | bytes 196612
  1114.1 31.5 %copy-start.25 = (f32[512,256]{1,0:T(8,128)S(1)}, f32[512,256]{1,0:T(8,128)}, u32[]{:S(2)}) copy-start(f32[512,256]{1,0:T(8,128)} %copy-done.24) | copy-start | bytes 1572868
  1115.8 29.8 %copy-start.97 = (f32[512,256]{1,0:T(8,128)S(1)}, f32[512,256]{1,0:T(8,128)}, u32[]{:S(2)}) copy-start(f32[512,256]{1,0:T(8,128)} %param.45) | copy-start | bytes 1572868
  (116 other events, 430.9 us)
Sparse Core Ops, SparseCore 0:
  115.2 64.7 all-gather.6
  182.3 87.5 all-gather.4
  741.9 25.9 reduce-scatter.13
  771.0 52.6 reduce-scatter.11
  826.7 86.3 reduce-scatter.9

commit v3 on v2

--- a/solution.py
+++ b/solution.py
@@ -913,6 +913,518 @@
         compiler_params=params(ident),
         cost_estimate=cost(20),
     )(query_parts, kv_parts, flat_parts)
+
+
+class Flow:
+    def __init__(self, x_ref, blocks, own, core_out, core_in, left_in, right_in, sems):
+        self.x_ref, self.blocks, self.own = x_ref, blocks, own
+        self.core_out, self.core_in = core_out, core_in
+        self.left_in, self.right_in = left_in, right_in
+        self.sems = sems
+        self.me, self.column = lax.axis_index("row"), lax.axis_index("col")
+        self.count = blocks.shape[0]
+
+    @staticmethod
+    def scratch(count, share, width):
+        dma = pltpu.SemaphoreType.DMA
+        slots = (count, share, width)
+        return [
+            pltpu.VMEM((count, 2, share, width), LOW),
+            pltpu.VMEM(slots, FULL),
+            pltpu.VMEM(slots, LOW),
+            pltpu.VMEM(slots, LOW),
+            pltpu.VMEM(slots, LOW),
+            pltpu.VMEM(slots, LOW),
+        ], [dma((count,))] * 12 + [dma]
+
+    def left(self):
+        return {"row": self.me - 1}
+
+    def right(self):
+        return {"row": self.me + 1}
+
+    def beside(self):
+        return {"col": 1 - self.column}
+
+    def to_left(self, source, k, origin):
+        return push(origin, self.blocks.at[source, 0], self.sems[0].at[k], self.sems[4].at[k], self.left())
+
+    def to_right(self, source, k, origin):
+        return push(origin, self.blocks.at[source, 0], self.sems[1].at[k], self.sems[3].at[k], self.right())
+
+    def to_core(self, source, origin):
+        return push(origin, self.blocks.at[source, 1], self.sems[2].at[source], self.sems[5].at[source], self.beside())
+
+    def back_core(self, q):
+        return push(self.core_out.at[q], self.core_in.at[q], self.sems[6].at[q], self.sems[9].at[q], self.beside())
+
+    def back_left(self, q):
+        return push(self.core_out.at[q], self.left_in.at[q], self.sems[7].at[q], self.sems[10].at[q], self.left())
+
+    def back_right(self, q):
+        return push(self.core_out.at[q], self.right_in.at[q], self.sems[8].at[q], self.sems[11].at[q], self.right())
+
+    def mine(self):
+        return pltpu.make_async_copy(self.x_ref, self.blocks.at[self.me, 0], self.sems[12])
+
+    def start(self):
+        me, count = self.me, self.count
+        greet_line(me, count, self.column, True)
+
+        @pl.when(me > 0)
+        def _():
+            self.to_left(me, 0, self.x_ref).start()
+
+        @pl.when(me < count - 1)
+        def _():
+            self.to_right(me, 0, self.x_ref).start()
+
+        self.to_core(me, self.x_ref).start()
+        self.mine().start()
+
+    def arrive(self, k):
+        me, count = self.me, self.count
+
+        @pl.when(k == 0)
+        def _():
+            self.mine().wait()
+            self.to_core(me, self.x_ref).wait()
+
+        @pl.when((k > 0) & (me - k >= 0))
+        def _():
+            source = me - k
+            block = self.blocks.at[source, 0]
+            push(block, block, self.sems[1].at[k], self.sems[3].at[k - 1], self.left()).wait_recv()
+
+            @pl.when(me < count - 1)
+            def _():
+                self.to_right(source, k, block).start()
+
+            self.to_core(source, block).start()
+
+        @pl.when((k > 0) & (me + k < count))
+        def _():
+            source = me + k
+            block = self.blocks.at[source, 0]
+            push(block, block, self.sems[0].at[k], self.sems[4].at[k - 1], self.right()).wait_recv()
+
+            @pl.when(me > 0)
+            def _():
+                self.to_left(source, k, block).start()
+
+            self.to_core(source, block).start()
+
+        @pl.when((k > 0) & (me - k >= 0))
+        def _():
+            self.to_core(me - k, self.x_ref).wait()
+
+        @pl.when((k > 0) & (me + k < count))
+        def _():
+            self.to_core(me + k, self.x_ref).wait()
+
+    def visit(self, body):
+        me, count = self.me, self.count
+
+        @pl.loop(0, count)
+        def _(k):
+            self.arrive(k)
+
+            @pl.loop(0, 2)
+            def _(side):
+                source = jnp.where(side == 0, me - k, me + k)
+
+                @pl.when((source >= 0) & (source < count) & ((side == 0) | (k > 0)))
+                def _():
+                    body(source)
+                    self.back_core(source).start()
+
+    def added(self, target, terms):
+        high, wide = target.shape
+        step = min(high, max(16, 65536 // wide))
+
+        @pl.loop(0, high // step)
+        def _(at):
+            rows = pl.ds(pl.multiple_of(at * step, step), step)
+            total = terms[0][rows]
+            for term in terms[1:]:
+                total = total + term[rows].astype(FULL)
+            target[rows] = total.astype(target.dtype)
+
+    def give_back(self, t):
+        me, count = self.me, self.count
+        q_left = t - (count - 1 - me)
+        q_right = count - 1 - (t - me)
+
+        def leftward():
+            q = q_left
+            self.back_core(q).wait()
+
+            @pl.when(me < count - 1)
+            def _():
+                push(self.left_in.at[q], self.left_in.at[q], self.sems[7].at[q], self.sems[10].at[q], self.right()).wait_recv()
+                self.added(self.core_out.at[q], [self.own.at[q], self.core_in.at[q], self.left_in.at[q]])
+
+            @pl.when(me == count - 1)
+            def _():
+                self.added(self.core_out.at[q], [self.own.at[q], self.core_in.at[q]])
+
+            self.back_left(q).start()
+
+        def rightward():
+            q = q_right
+            self.back_core(q).wait()
+
+            @pl.when(me > 0)
+            def _():
+                push(self.right_in.at[q], self.right_in.at[q], self.sems[8].at[q], self.sems[11].at[q], self.left()).wait_recv()
+                self.added(self.core_out.at[q], [self.own.at[q], self.core_in.at[q], self.right_in.at[q]])
+
+            @pl.when(me == 0)
+            def _():
+                self.added(self.core_out.at[q], [self.own.at[q], self.core_in.at[q]])
+
+            self.back_right(q).start()
+
+        pl.when((q_left >= 0) & (q_left < me))(leftward)
+        pl.when((t >= me) & (q_right > me))(rightward)
+
+    def finish(self, o_ref):
+        me, count = self.me, self.count
+        self.back_core(me).wait()
+
+        @pl.when(me < count - 1)
+        def _():
+            push(self.left_in.at[me], self.left_in.at[me], self.sems[7].at[me], self.sems[10].at[me], self.right()).wait_recv()
+
+        @pl.when(me > 0)
+        def _():
+            push(self.right_in.at[me], self.right_in.at[me], self.sems[8].at[me], self.sems[11].at[me], self.left()).wait_recv()
+
+        base = [self.own.at[me], self.core_in.at[me]]
+
+        @pl.when(me == 0)
+        def _():
+            self.added(o_ref, base + [self.left_in.at[me]])
+
+        @pl.when(me == count - 1)
+        def _():
+            self.added(o_ref, base + [self.right_in.at[me]])
+
+        @pl.when((me > 0) & (me < count - 1))
+        def _():
+            self.added(o_ref, base + [self.left_in.at[me], self.right_in.at[me]])
+
+        @pl.when(me > 0)
+        def _():
+            self.to_left(me, 0, self.x_ref).wait_send()
+
+        @pl.when(me < count - 1)
+        def _():
+            self.to_right(me, 0, self.x_ref).wait_send()
+
+        @pl.loop(1, count)
+        def _(k):
+            @pl.when((me - k >= 0) & (me < count - 1))
+            def _():
+                self.to_right(me - k, k, self.x_ref).wait_send()
+
+            @pl.when((me + k < count) & (me > 0))
+            def _():
+                self.to_left(me + k, k, self.x_ref).wait_send()
+
+        @pl.loop(0, count)
+        def _(q):
+            @pl.when(q < me)
+            def _():
+                self.back_left(q).wait_send()
+
+            @pl.when(q > me)
+            def _():
+                self.back_right(q).wait_send()
+
+
+GELU_ONE = 0.7978845608028654
+GELU_TWO = 0.044715
+
+
+def gelu_of(values_in):
+    inner = GELU_ONE * (values_in + GELU_TWO * values_in * values_in * values_in)
+    bend = jnp.tanh(inner)
+    half = 0.5 * (1.0 + bend)
+    slope = half + 0.5 * values_in * (1.0 - bend * bend) * GELU_ONE * (
+        1.0 + 3.0 * GELU_TWO * values_in * values_in
+    )
+    return values_in * half, slope
+
+
+def ffn_forward(block, gateup, down, ident):
+    count = lax.axis_size("row")
+    share, width = block.shape
+    groups, _, _, part = gateup.shape
+    hidden = groups * part
+    out_cols = down.shape[2] // count
+    rows = 2 * share
+
+    def kernel(x_ref, gw_hbm, dw_hbm, o_ref, xt_hbm, at_hbm, g_hbm, u_hbm, *scratch):
+        flow = Flow(x_ref, *scratch[:6], scratch[6:19])
+        gw, dw, xt, at, act, gate, up = scratch[19:26]
+        gw_sem, dw_sem, xt_sem, at_sem, g_sem, u_sem = scratch[26:]
+        gw_load = pltpu.make_async_copy(gw_hbm, gw, gw_sem)
+        dw_load = pltpu.make_async_copy(dw_hbm, dw, dw_sem)
+        gw_load.start()
+        dw_load.start()
+        flow.start()
+        gw_load.wait()
+        dw_load.wait()
+
+        def stores(source):
+            return (
+                pltpu.make_async_copy(gate.at[source], g_hbm.at[source], g_sem.at[source]),
+                pltpu.make_async_copy(up.at[source], u_hbm.at[source], u_sem.at[source]),
+            )
+
+        def body(source):
+            here = pl.ds(pl.multiple_of(source * rows, rows), rows)
+            x = flow.blocks[source].reshape(rows, width)
+            xt[:, here] = x.T
+
+            @pl.loop(0, groups)
+            def _(d):
+                columns = pl.ds(pl.multiple_of(d * part, part), part)
+                g = flat_dot(x, gw[d, 0])
+                u = flat_dot(x, gw[d, 1])
+                gate[source, :, columns] = g
+                up[source, :, columns] = u
+                act[:, columns] = (gelu_of(g)[0] * u).astype(LOW)
+
+            for copy in stores(source):
+                copy.start()
+            at[:, here] = act[...].T
+            for d in range(groups):
+                out = flat_dot(act[...], dw[d])
+                for s in range(count):
+                    columns = slice((s * groups + d) * out_cols, (s * groups + d + 1) * out_cols)
+                    piece = out[:, s * out_cols : (s + 1) * out_cols]
+                    flow.own[source, :, columns] = piece[:share]
+                    flow.core_out[source, :, columns] = piece[share:].astype(LOW)
+
+        flow.visit(body)
+        xt_store = pltpu.make_async_copy(xt, xt_hbm, xt_sem)
+        at_store = pltpu.make_async_copy(at, at_hbm, at_sem)
+        xt_store.start()
+        at_store.start()
+
+        @pl.loop(0, count - 1)
+        def _(t):
+            flow.give_back(t)
+
+        flow.finish(o_ref)
+        xt_store.wait()
+        at_store.wait()
+
+        @pl.loop(0, count)
+        def _(source):
+            for copy in stores(source):
+                copy.wait()
+
+    dma = pltpu.SemaphoreType.DMA
+    buffers, sems = Flow.scratch(count, share, width)
+    vmem, anywhere = pl.BlockSpec(memory_space=pltpu.VMEM), pl.BlockSpec(memory_space=pl.ANY)
+    tokens = count * rows
+    return pl.pallas_call(
+        kernel,
+        out_shape=[
+            jax.ShapeDtypeStruct((share, width), FULL),
+            jax.ShapeDtypeStruct((width, tokens), LOW),
+            jax.ShapeDtypeStruct((hidden, tokens), LOW),
+            jax.ShapeDtypeStruct((count, rows, hidden), FULL),
+            jax.ShapeDtypeStruct((count, rows, hidden), FULL),
+        ],
+        in_specs=[vmem, anywhere, anywhere],
+        out_specs=[vmem] + [anywhere] * 4,
+        scratch_shapes=buffers
+        + sems
+        + [
+            pltpu.VMEM(gateup.shape, LOW),
+            pltpu.VMEM(down.shape, LOW),
+            pltpu.VMEM((width, tokens), LOW),
+            pltpu.VMEM((hidden, tokens), LOW),
+            pltpu.VMEM((rows, hidden), LOW),
+            pltpu.VMEM((count, rows, hidden), FULL),
+            pltpu.VMEM((count, rows, hidden), FULL),
+        ]
+        + [dma, dma, dma, dma, dma((count,)), dma((count,))],
+        compiler_params=params(ident, 60),
+        cost_estimate=cost(80),
+    )(block, gateup, down)
+
+
+def ffn_backward(block, gateup, down, xt, at, gate, up, ident):
+    count = lax.axis_size("row")
+    share, width = block.shape
+    groups, _, _, part = gateup.shape
+    hidden = groups * part
+    out_cols = down.shape[2] // count
+    rows = 2 * share
+    tokens = count * rows
+    pieces = 3 * groups
+
+    def kernel(x_ref, gw_hbm, dw_hbm, xt_hbm, at_hbm, g_hbm, u_hbm, o_ref, dgu_hbm, ddn_hbm, *scratch):
+        flow = Flow(x_ref, *scratch[:6], scratch[6:19])
+        gw, dw, xt_own, at_own, gate_own, up_own, d_gate, d_up, total, stage, stage_down = scratch[19:30]
+        load_sems, g_sem, u_sem, out_sem, down_sem = scratch[30:]
+        loads = [
+            pltpu.make_async_copy(source, target, load_sems.at[k])
+            for k, (source, target) in enumerate(
+                [(dw_hbm, dw), (gw_hbm, gw), (xt_hbm, xt_own), (at_hbm, at_own)]
+            )
+        ]
+
+        def fetches(source):
+            return (
+                pltpu.make_async_copy(g_hbm.at[source], gate_own.at[source], g_sem.at[source]),
+                pltpu.make_async_copy(u_hbm.at[source], up_own.at[source], u_sem.at[source]),
+            )
+
+        for load in loads[:2]:
+            load.start()
+
+        @pl.loop(0, count)
+        def _(source):
+            for copy in fetches(source):
+                copy.start()
+
+        for load in loads[2:]:
+            load.start()
+        flow.start()
+        loads[0].wait()
+        loads[1].wait()
+
+        def columns_of(s, d):
+            return pl.ds(pl.multiple_of((s * groups + d) * out_cols, out_cols), out_cols)
+
+        def body(source):
+            for copy in fetches(source):
+                copy.wait()
+            grad = flow.blocks[source].reshape(rows, width)
+            d_act = None
+            for d in range(groups):
+                cut = jnp.concatenate(
+                    [
+                        grad[:, (s * groups + d) * out_cols : (s * groups + d + 1) * out_cols]
+                        for s in range(count)
+                    ],
+                    axis=1,
+                )
+                term = against(cut, dw[d])
+                d_act = term if d_act is None else d_act + term
+            total[:, :hidden] = d_act
+
+            @pl.loop(0, groups)
+            def _(d):
+                columns = pl.ds(pl.multiple_of(d * part, part), part)
+                grad_act = total[:, columns]
+                curve, slope = gelu_of(gate_own[source, :, columns])
+                d_gate[source, :, columns] = (grad_act * up_own[source, :, columns] * slope).astype(LOW)
+                d_up[source, :, columns] = (grad_act * curve).astype(LOW)
+
+            total[...] = jnp.zeros(total.shape, FULL)
+
+            @pl.loop(0, groups)
+            def _(d):
+                columns = pl.ds(pl.multiple_of(d * part, part), part)
+                total[...] += against(d_gate[source, :, columns], gw[d, 0]) + against(
+                    d_up[source, :, columns], gw[d, 1]
+                )
+
+            flow.own[source] = total[:share]
+            flow.core_out[source] = total[share:].astype(LOW)
+
+        flow.visit(body)
+        loads[2].wait()
+        loads[3].wait()
+
+        def gateup_store(d, which):
+            return pltpu.make_async_copy(stage.at[which], dgu_hbm.at[d, which], out_sem.at[which])
+
+        def down_store(d):
+            return pltpu.make_async_copy(stage_down, ddn_hbm.at[d], down_sem)
+
+        def weights(d):
+            columns = pl.ds(pl.multiple_of(d * part, part), part)
+            for which, grads in ((0, d_gate), (1, d_up)):
+
+                @pl.when(d > 0)
+                def _():
+                    gateup_store(d - 1, which).wait()
+
+                right = grads[:, :, columns].reshape(tokens, part)
+
+                @pl.loop(0, width // 512)
+                def _(k):
+                    high = pl.ds(pl.multiple_of(k * 512, 512), 512)
+                    stage[which, high] = flat_dot(xt_own[high], right).astype(LOW)
+
+                gateup_store(d, which).start()
+
+            @pl.when(d > 0)
+            def _():
+                down_store(d - 1).wait()
+
+            right = jnp.concatenate(
+                [flow.blocks[:, :, :, columns_of(s, d)].reshape(tokens, out_cols) for s in range(count)],
+                axis=1,
+            )
+
+            @pl.loop(0, hidden // 256)
+            def _(k):
+                high = pl.ds(pl.multiple_of(k * 256, 256), 256)
+                stage_down[high] = flat_dot(at_own[high], right).astype(LOW)
+
+            down_store(d).start()
+
+        @pl.loop(0, count - 1)
+        def _(t):
+            flow.give_back(t)
+            weights(t)
+
+        weights(groups - 1)
+        for which in range(2):
+            gateup_store(groups - 1, which).wait()
+        down_store(groups - 1).wait()
+        flow.finish(o_ref)
+
+    dma = pltpu.SemaphoreType.DMA
+    buffers, sems = Flow.scratch(count, share, width)
+    vmem, anywhere = pl.BlockSpec(memory_space=pltpu.VMEM), pl.BlockSpec(memory_space=pl.ANY)
+    return pl.pallas_call(
+        kernel,
+        out_shape=[
+            jax.ShapeDtypeStruct((share, width), FULL),
+            jax.ShapeDtypeStruct(gateup.shape, LOW),
+            jax.ShapeDtypeStruct(down.shape, LOW),
+        ],
+        in_specs=[vmem] + [anywhere] * 6,
+        out_specs=[vmem, anywhere, anywhere],
+        scratch_shapes=buffers
+        + sems
+        + [
+            pltpu.VMEM(gateup.shape, LOW),
+            pltpu.VMEM(down.shape, LOW),
+            pltpu.VMEM((width, tokens), LOW),
+            pltpu.VMEM((hidden, tokens), LOW),
+            pltpu.VMEM((count, rows, hidden), FULL),
+            pltpu.VMEM((count, rows, hidden), FULL),
+            pltpu.VMEM((count, rows, hidden), LOW),
+            pltpu.VMEM((count, rows, hidden), LOW),
+            pltpu.VMEM((rows, width), FULL),
+            pltpu.VMEM((2, width, part), LOW),
+            pltpu.VMEM((hidden, count * out_cols), LOW),
+        ]
+        + [dma((4,)), dma((count,)), dma((count,)), dma((2,)), dma],
+        compiler_params=params(ident, 62),
+        cost_estimate=cost(90),
+    )(block, gateup, down, xt, at, gate, up)
 
 
 def small_total(values_in, axes, max_rows, ident):
@@ -1273,12 +1785,7 @@
     value_raw = lax.dynamic_slice_in_dim(all_value_raw, me * quarter, quarter, 0)
     _, key_scale = whole_norm(key_raw, key_gain)
     _, value_scale = whole_norm(value_raw, 1.0)
-    gateup_w = gateup_all.transpose(1, 2, 0, 3).reshape(2, width, -1)
-    down_w = (
-        down_all.reshape(data_n, data_n, ff_part, rows_n, out_cols)
-        .transpose(1, 2, 3, 0, 4)
-        .reshape(-1, width)
-    )
+    down_all = down_all.reshape(data_n, data_n * ff_part, -1)
 
     def shares(parts):
         return parts.astype(LOW).reshape(cols_n, rows_n, share, width)
@@ -1292,11 +1799,9 @@
     proj_n, scale_p = whole_norm(projected, gains[2])
     mixture = ((inputs + proj_n) + (hidden + right_n)) * HALF_ROOT
     ffn_n, scale_f = whole_norm(mixture, gains[3])
-    spread_f = line_gather(ffn_n.astype(LOW), 6, True, 40).reshape(tokens, width)
-    gate_raw = flat_dot(spread_f, gateup_w[0])
-    up_raw = flat_dot(spread_f, gateup_w[1])
-    act = (jax.nn.gelu(gate_raw, approximate=True) * up_raw).astype(LOW)
-    down_raw = line_reduce(shares(flat_dot(act, down_w)), 7, True, 45)
+    down_raw, spread_ft, act_t, gate_raw, up_raw = ffn_forward(
+        ffn_n.astype(LOW), gateup_all, down_all, 6
+    )
     down_n, scale_d = whole_norm(down_raw, gains[4])
     block_out = mixture + down_n
     out_low = block_out.astype(LOW)
@@ -1317,10 +1822,20 @@
     dw_pergate = inner_rows(out_low, d_pgate)
     d_out = upstream + against(d_pgate, pergate_w)
     d_down, gain_grads[4] = whole_norm_backward(down_raw, scale_d, gains[4], d_out)
-    spread_d, result = transfers(
+    d_ffn, dw_gateup, dw_down = ffn_backward(
+        d_down.astype(LOW), gateup_all, down_all, spread_ft, act_t, gate_raw, up_raw, 8
+    )
+    g_gateup = lax.psum_scatter(dw_gateup, "dp", scatter_dimension=0)
+    g_down = lax.psum_scatter(
+        dw_down.reshape(data_n, data_n, ff_part, -1), "dp", scatter_dimension=0
+    )
+    d_mix, gain_grads[3] = whole_norm_backward(mixture, scale_f, gains[3], d_ffn)
+    d_half = (d_out + d_mix) * HALF_ROOT
+    d_proj, gain_grads[2] = whole_norm_backward(projected, scale_p, gains[2], d_half)
+    spread_p, result = transfers(
         [
             Line(
-                d_down.astype(LOW),
+                d_proj.astype(LOW),
                 (cols_n, rows_n, share, width),
                 lambda ref, c, r: ref.at[c, r],
                 True,
@@ -1332,36 +1847,10 @@
                 lambda ref, at: ref.at[columns_of(at, share)],
             ),
         ],
-        8,
+        10,
         50,
     )
-    spread_d = spread_d.reshape(tokens, width)
-    d_act = against(spread_d, down_w)
-    _, pullback = jax.vjp(
-        lambda a, b: jax.nn.gelu(a, approximate=True) * b, gate_raw, up_raw
-    )
-    d_gate, d_up = pullback(d_act)
-    d_gate, d_up = d_gate.astype(LOW), d_up.astype(LOW)
-    d_ffn = against(d_gate, gateup_w[0]) + against(d_up, gateup_w[1])
-    dw_down = inner_rows(act, spread_d).astype(LOW)
-    dw_down = dw_down.reshape(data_n, ff_part, rows_n, data_n, out_cols).transpose(3, 0, 1, 2, 4)
-    dw_gateup = jnp.stack(
-        [
-            inner_rows(spread_f, grad[:, k * ff_part : (k + 1) * ff_part]).astype(LOW)
-            for k in range(data_n)
-            for grad in (d_gate, d_up)
-        ]
-    ).reshape(data_n, 2, width, ff_part)
-    d_ffn, dw_down, dw_gateup = lax.optimization_barrier((shares(d_ffn), dw_down, dw_gateup))
-    g_gateup = lax.psum_scatter(dw_gateup, "dp", scatter_dimension=0)
-    g_down = lax.psum_scatter(
-        dw_down.reshape(data_n, data_n, ff_part, -1), "dp", scatter_dimension=0
-    )
-    d_ffn = line_reduce(d_ffn, 9, True, 45)
-    d_mix, gain_grads[3] = whole_norm_backward(mixture, scale_f, gains[3], d_ffn)
-    d_half = (d_out + d_mix) * HALF_ROOT
-    d_proj, gain_grads[2] = whole_norm_backward(projected, scale_p, gains[2], d_half)
-    spread_p = line_gather(d_proj.astype(LOW), 10, True, 40).reshape(tokens, width)
+    spread_p = spread_p.reshape(tokens, width)
     d_right, gain_grads[1] = whole_norm_backward(right_raw, scale_r, gains[1], d_half)
     d_right = d_right.astype(LOW)
     dw_right = inner_rows(middle, d_right)

time: 1190 us -> 1050 us (0.88)
  local copies, waits for them, and re-layouts: 215 us -> 133 us
  matrix products: 116 us -> 40.1 us
  Pallas kernels: 733 us -> 747 us
    pallas_call x0 -> x2, Pallas kernels: none -> 182 us  [the longest x1 92.2 us: ffn_forward(): pl.pallas_call(kernel, out_shape=[jax.ShapeDtypeStruct((share, width), FU...]
    pallas_call x5 -> x3, Pallas kernels: 173 us -> 88 us  [line_reduce(): pl.pallas_call(kernel, out_shape=jax.ShapeDtypeStruct((high, wide), FULL)...]
    pallas_call x3 -> x1, Pallas kernels: 136 us -> 53.4 us  [line_gather(): pl.pallas_call(kernel, out_shape=jax.ShapeDtypeStruct(shape, block.dtype)...]
    reshape x5 -> x0, local copies, waits for them, and re-layouts: 39.6 us -> none  [the longest x2 16.6 us: line_device(): down_all.reshape(data_n, data_n, ff_part, rows_n, out_cols)]
    dot_general x14 -> x11, matrix products: 47.4 us -> 15.2 us  [against(): lax.dot_general(grad_mat, weight_mat, (((1,), (1,)), ((), ())), preferred...]
    dot_general x20 -> x11, matrix products: 32.3 us -> 9.77 us  [inner_rows(): lax.dot_general(left_mat, right_mat, (((0,), (0,)), ((), ())), preferred_...]
    dot_general x11 -> x8, matrix products: 36 us -> 15.2 us  [flat_dot(): return jnp.dot(left_mat, right_mat, preferred_element_type=jnp.float32)]
    slice x3 -> x0, local copies, waits for them, and re-layouts: 18.5 us -> none  [the longest x2 12.2 us: line_device(): gate_raw = flat_dot(spread_f, gateup_w[0])]
  transfers between devices with their start and end apart: 5 -> 5, of which waited for: 0 -> 0; matrix products, arithmetic and copies ran while one was open for 18% -> 15% of each run, Pallas kernels for 29% -> 29%
where the time goes in v3:
time: 1050 us; the launch traced here: 1040 us
  Pallas kernels  747 us (71%)
  local copies, waits for them, and re-layouts  133 us (13%)
  other arithmetic  94.6 us (9%)
  matrix products  40.1 us (4%)
  between operations  22.9 us (2%)
    pallas_call x4, Pallas kernels, transfers(): pl.pallas_call(kernel, out_shape=[jax.ShapeDtypeStruct(item.shape, item.s...  366 us
    pallas_call x1, Pallas kernels, ffn_forward(): pl.pallas_call(kernel, out_shape=[jax.ShapeDtypeStruct((share, width), FU...  92.2 us
    pallas_call x1, Pallas kernels, ffn_backward(): pl.pallas_call(kernel, out_shape=[jax.ShapeDtypeStruct((share, width), FU...  89.4 us
    pallas_call x3, Pallas kernels, line_reduce(): pl.pallas_call(kernel, out_shape=jax.ShapeDtypeStruct((high, wide), FULL)...  88 us
    pallas_call x1, Pallas kernels, line_gather(): pl.pallas_call(kernel, out_shape=jax.ShapeDtypeStruct(shape, block.dtype)...  53.4 us
    unnamed x260, local copies, waits for them, and re-layouts  45.8 us
    pallas_call x1, Pallas kernels, shard_total(): pl.pallas_call(kernel, out_shape=[jax.ShapeDtypeStruct(shape, FULL) for s...  24.8 us
  transfers between devices with their start and end apart: 5, of which 0 were waited for; matrix products, arithmetic and copies ran while one was open for 15% of the time, Pallas kernels for 29%

profile of v3, /device:TPU:0, one launch (start us, length us, event | category | flops | bytes accessed | tf_op | source)
XLA Modules:
  0.0 1039.4 jit_solution(2998453855559324764)
XLA Ops:
  15.9 90.0 %shard_map.645 = (bf16[2,2048,256]{2,1,0:T(8,128)(2,1)S(1)}, bf16[4,256,512]{2,1,0:T(8,128)(2,1)}, bf16[256,512]{1,0:T(8,128)(2,1)S(1)}, bf16[128,2048]{1,0:T(8,...) custom-call(bf16[2,512,1024]{2,1,0:T(8,128)(2,1)S(1)} %convert_element_type.269.refs_0_, ...), custom_call_target="tpu_custom_call" | custom-call | bytes 270000000 | tf_op jit(solution)/shard_map/pallas_call | solution.py:819
  115.5 117.6 %shard_map.646 = (bf16[1024,2048]{1,0:T(8,128)(2,1)S(1)}, bf16[2,2048,256]{2,1,0:T(8,128)(2,1)S(1)}, bf16[2048,256]{1,0:T(8,128)(2,1)S(1)}, bf16[2,4,1280,128]{3...) custom-call(bf16[512,512]{1,0:T(8,128)(2,1)S(1)} %copy-done.28, ...), custom_call_target="tpu_custom_call" | custom-call | bytes 345000000 | tf_op jit(solution)/shard_map/pallas_call | solution.py:819
  241.2 2.5 reshape.538
  243.7 2.4 copy.260
  246.1 2.4 reshape.541
  248.5 3.3 fusion.142
  257.6 3.2 fusion
  262.2 2.3 multiply_reduce_fusion.20
  264.5 2.6 copy.257
  267.1 3.5 multiply_reduce_fusion.19
  271.9 4.5 multiply_reduce_fusion.18
  281.9 2.5 fusion.55
  284.8 8.8 shard_map.647
  294.9 39.7 %shard_map.648 = f32[128,2048]{1,0:T(8,128)S(1)} custom-call(bf16[2,4,128,2048]{3,2,1,0:T(8,128)(2,1)S(1)} %bitcast.215), custom_call_target="tpu_custom_call" | custom-call | bytes 135000000 | tf_op jit(solution)/shard_map/pallas_call | solution.py:564
  334.7 5.8 reshape.542
  340.5 4.5 copy.261
  346.0 3.7 reshape.547
  349.7 3.7 copy.263
  362.6 92.2 %shard_map.649 = (f32[128,2048]{1,0:T(8,128)}, bf16[2048,1024]{1,0:T(8,128)(2,1)}, bf16[1024,1024]{1,0:T(8,128)(2,1)}, f32[4,256,1024]{2,1,0:T(8,128)}, f32[4,256,1024]{2,1,0:T(8,128)}) custom-call(bf16[128,2048]{1,0:T(8,128)(2,1)} %multiply_convert_fusion.x_ref, bf16[4,2,2048,256]{3,2,1,0:T(8,128)(2,1)} %bitcast.226, bf16[4,1024,512]{2,1,0:T(8,128)(2,1)} %bitcast.229), custom_call_target="tpu_custom_call" | custom-call | bytes 240000000 | tf_op jit(solution)/shard_map/pallas_call | solution.py:1234
  465.4 89.4 %shard_map.650 = (f32[128,2048]{1,0:T(8,128)}, bf16[4,2,2048,256]{3,2,1,0:T(8,128)(2,1)}, bf16[4,1024,512]{2,1,0:T(8,128)(2,1)}) custom-call(bf16[128,2048]{1,0:T(8,128)(2,1)} %subtract_convert_fusion.3.x_ref, bf16[4,2,2048,256]{3,2,1,0:T(8,128)(2,1)} %bitcast.227, bf16[4,1024,512]{2,1,0:T(8,128)(2,1)} %bitcast.230, ...), custom_call_target="tpu_custom_call" | custom-call | bytes 270000000 | tf_op jit(solution)/shard_map/pallas_call | solution.py:1400
  556.8 3.0 multiply_convert_fusion.2
  561.2 51.6 %shard_map.651 = (bf16[2,4,128,2048]{3,2,1,0:T(8,128)(2,1)S(1)}, bf16[512,512]{1,0:T(8,128)(2,1)S(1)}) custom-call(bf16[128,2048]{1,0:T(8,128)(2,1)S(1)} %get-tuple-element.356.refs_0_, bf16[128,2048]{1,0:T(8,128)(2,1)S(1)} %copy-done.27), custom_call_target="tpu_custom_call" | custom-call | bytes 150000000 | tf_op jit(solution)/shard_map/pallas_call | solution.py:819
  613.6 2.0 copy-done.50
  615.6 2.2 convolution_convert_fusion.3
  621.0 2.2 reshape.554
  631.7 2.3 copy.273
  640.0 3.2 copy.274
  643.3 6.6 reshape.566
  649.8 3.5 convolution_convert_fusion.6.g_ref
  653.4 9.9 shard_map.652
  663.5 21.4 %shard_map.653 = f32[512,256]{1,0:T(8,128)S(1)} custom-call(bf16[4,512,256]{2,1,0:T(8,128)(2,1)S(1)} %pad_maximum_fusion.2.x_ref), custom_call_target="tpu_custom_call" | custom-call | bytes 60000000 | tf_op jit(solution)/shard_map/pallas_call | solution.py:564
  684.8 3.2 fusion.48
  698.0 53.4 %shard_map.654 = bf16[4,1536,256]{2,1,0:T(8,128)(2,1)S(1)} custom-call(bf16[1536,256]{1,0:T(8,128)(2,1)S(1)} %pad_maximum_fusion.4.x_ref), custom_call_target="tpu_custom_call" | custom-call | bytes 165000000 | tf_op jit(solution)/shard_map/pallas_call | solution.py:415
  753.1 3.0 copy.271
  756.1 6.1 reshape.564
  765.0 5.2 pad_maximum_fusion
  770.1 5.3 reshape.568.x_ref
  777.2 26.9 %shard_map.656 = f32[1280,128]{1,0:T(8,128)S(1)} custom-call(bf16[2,4,1280,128]{3,2,1,0:T(8,128)(2,1)S(1)} %copy-done.4), custom_call_target="tpu_custom_call" | custom-call | bytes 84000000 | tf_op jit(solution)/shard_map/pallas_call | solution.py:564
  807.5 24.8 %shard_map.657 = (f32[512,256]{1,0:T(8,128)S(1)}, f32[512,256]{1,0:T(8,128)S(1)}, f32[320,128]{1,0:T(8,128)S(1)}) custom-call(bf16[4,512,256]{2,1,0:T(8,128)(2,1)S(1)} %pad_maximum_fusion.3.q_ref, bf16[2,512,256]{2,1,0:T(8,128)(2,1)S(1)} %pad_maximum_fusion.9.kv_ref, bf16[4,320,128]{2,1,0:T(8,128)(2,1)S(1)} %bitcast.220), custom_call_target="tpu_custom_call" | custom-call | bytes 60000000 | tf_op jit(solution)/shard_map/pallas_call | solution.py:905
  838.4 2.7 fusion.28
  844.7 3.2 multiply_reduce_fusion.2
  850.5 2.4 multiply_reduce_fusion.1
  860.0 107.1 %shard_map.655 = (bf16[2,512,1024]{2,1,0:T(8,128)(2,1)S(1)}, bf16[4,4,256,128]{3,2,1,0:T(8,128)(2,1)S(1)}, bf16[4,256,128]{2,1,0:T(8,128)(2,1)S(1)}, bf16[512,51...) custom-call(bf16[2,2048,256]{2,1,0:T(8,128)(2,1)S(1)} %bitcast.216, ...), custom_call_target="tpu_custom_call" | custom-call | bytes 300000000 | tf_op jit(solution)/shard_map/pallas_call | solution.py:819
  972.0 2.8 fusion.20
  979.3 14.2 %shard_map.658 = f32[128,128]{1,0:T(8,128)S(1)} custom-call(f32[128,128]{1,0:T(8,128)S(1)} %pad_maximum_fusion.11.x_ref), custom_call_target="tpu_custom_call" | custom-call | bytes 36000000 | tf_op jit(solution)/shard_map/pallas_call | solution.py:1467
  1010.4 2.8 subtract_multiply_fusion
  1017.2 3.9 multiply_subtract_fusion.1
  1024.6 6.2 multiply_subtract_fusion
  (450 shorter events, 150.9 us)
Async XLA Ops:
  7.2 105.2 %copy-start = (s32[4,2]{0,1:T(2,128)S(1)}, s32[4,2]{0,1:T(2,128)}, u32[]{:S(2)}) copy-start(s32[4,2]{0,1:T(2,128)} %param.44) | copy-start | bytes 100
  7.2 7.5 copy-start.67
  7.2 355.4 %all-gather.7.cloned.1.call-start = ((), (), s32[]{:S(2)}) async-start(), calls=%async_computation.4 | async-start | bytes 5242880 | tf_op jit(solution)/shard_map/all_gather | solution.py:1701
  108.7 253.9 %all-gather.5.cloned.1.call-start = ((), (), s32[]{:S(2)}) async-start(), calls=%async_computation.3 | async-start | bytes 10485760 | tf_op jit(solution)/shard_map/all_gather | solution.py:1700
  109.5 738.6 %reduce-scatter.14.cloned.1.call-start = ((), (), s32[]{:S(2)}) async-start(), calls=%async_computation.7 | async-start | bytes 1310720
  278.1 6.5 copy-start.71
  278.1 6.3 copy-start.119
  284.4 9.2 copy-start.75
  284.5 9.1 copy-start.7
  284.5 9.1 copy-start.9
  294.9 39.7 %copy-start.98 = (bf16[2,4,4,4096]{3,2,1,0:T(4,128)(2,1)S(1)}, bf16[2,4,4,4096]{3,2,1,0:T(4,128)(2,1)}, u32[]{:S(2)}) copy-start(bf16[2,4,4,4096]{3,2,1,0:T(4,128)(2,1)} %get-tuple-element.337) | copy-start | bytes 786436
  346.0 10.6 %copy-start.97 = (bf16[8,8,4,512]{3,1,2,0:T(8,128)(2,1)}, bf16[8,8,4,512]{3,1,2,0:T(8,128)(2,1)S(1)}, u32[]{:S(2)}) copy-start(bf16[8,8,4,512]{3,1,2,0:T(8,128)(2,1)S(1)} %copy.283) | copy-start | bytes 786436
  361.1 95.3 %copy-start.55 = (f32[128,2048]{1,0:T(8,128)}, f32[128,2048]{1,0:T(8,128)S(1)}, u32[]{:S(2)}) copy-start(f32[128,2048]{1,0:T(8,128)S(1)} %get-tuple-element.331) | copy-start | bytes 3145732
  465.4 91.4 %copy-start.125 = (f32[128]{0:T(128)S(1)}, f32[128]{0:T(128)}, u32[]{:S(2)}) copy-start(f32[128]{0:T(128)} %get-tuple-element.328) | copy-start | bytes 1540
  560.6 55.0 %copy-start.32 = (bf16[1024,256]{1,0:T(8,128)(2,1)S(1)}, bf16[1024,256]{1,0:T(8,128)(2,1)}, u32[]{:S(2)}) copy-start(bf16[1024,256]{1,0:T(8,128)(2,1)} %copy-done.31) | copy-start | bytes 1572868
  561.2 74.6 %copy-start.72 = (bf16[128,2048]{1,0:T(8,128)(2,1)}, bf16[128,2048]{1,0:T(8,128)(2,1)S(1)}, u32[]{:S(2)}) copy-start(bf16[128,2048]{1,0:T(8,128)(2,1)S(1)} %get-tuple-element.355) | copy-start | bytes 1572868
  623.3 7.0 copy-start.57
  623.3 7.0 copy-start.104
  623.3 227.2 %reduce-scatter.12.cloned.1.call-start = ((), (), s32[]{:S(2)}) async-start(), calls=%async_computation.6 | async-start | bytes 5242880
  623.9 229.0 %reduce-scatter.10.cloned.1.call-start = ((), (), s32[]{:S(2)}) async-start(), calls=%async_computation.5 | async-start | bytes 10485760
  624.6 11.2 %copy-start.107 = (f32[512]{0:T(512)}, f32[512]{0:T(512)S(1)}, u32[]{:S(2)}) copy-start(f32[512]{0:T(512)S(1)} %dynamic-slice.11) | copy-start | bytes 6148
  643.2 6.6 copy-start.76
  663.3 21.6 %copy-start.120 = (f32[128]{0:T(128)S(1)}, f32[128]{0:T(128)}, u32[]{:S(2)}) copy-start(f32[128]{0:T(128)} %copy-done.119) | copy-start | bytes 1540
  688.0 6.0 copy-start.116
  688.0 8.3 copy-start.114
  697.9 53.5 %copy-start.73 = (bf16[128,2048]{1,0:T(8,128)(2,1)S(1)}, bf16[128,2048]{1,0:T(8,128)(2,1)}, u32[]{:S(2)}) copy-start(bf16[128,2048]{1,0:T(8,128)(2,1)} %copy-done.72) | copy-start | bytes 1572868
  697.9 53.8 %copy-start.122 = (f32[128]{0:T(128)S(1)}, f32[128]{0:T(128)}, u32[]{:S(2)}) copy-start(f32[128]{0:T(128)} %copy-done.121) | copy-start | bytes 1540
  777.2 27.1 %copy-start.79 = (bf16[1024,2048]{1,0:T(8,128)(2,1)S(1)}, bf16[1024,2048]{1,0:T(8,128)(2,1)}, u32[]{:S(2)}) copy-start(bf16[1024,2048]{1,0:T(8,128)(2,1)} %copy-done.78) | copy-start | bytes 12582916
  850.4 121.5 %copy-start.29 = (bf16[512,512]{1,0:T(8,128)(2,1)S(1)}, bf16[512,512]{1,0:T(8,128)(2,1)}, u32[]{:S(2)}) copy-start(bf16[512,512]{1,0:T(8,128)(2,1)} %refs_0_.1) | copy-start | bytes 1572868
  850.4 121.5 %copy-start.108 = (f32[512]{0:T(512)S(1)}, f32[512]{0:T(512)}, u32[]{:S(2)}) copy-start(f32[512]{0:T(512)} %copy-done.107) | copy-start | bytes 6148
  850.4 121.5 %copy-start.115 = (f32[512,1]{0,1:T(1,128)S(1)}, f32[512,1]{0,1:T(1,128)}, u32[]{:S(2)}) copy-start(f32[512,1]{0,1:T(1,128)} %multiply_multiply_fusion.16) | copy-start | bytes 6148
  860.0 114.9 %copy-start.6 = (bf16[1,2,2048,256]{3,2,1,0:T(8,128)(2,1)S(1)}, bf16[1,2,2048,256]{3,2,1,0:T(8,128)(2,1)}, u32[]{:S(2)}) copy-start(bf16[1,2,2048,256]{3,2,1,0:T(8,128)(2,1)} %reduce-scatter.10.cloned.1.call-done) | copy-start | bytes 6291460
  971.9 24.8 %copy-start.118 = (s32[256]{0:T(256)S(1)}, s32[256]{0:T(256)}, u32[]{:S(2)}) copy-start(s32[256]{0:T(256)} %get-tuple-element.404) | copy-start | bytes 3076
  971.9 27.6 %copy-start.105 = (f32[128,128]{1,0:T(8,128)S(1)}, f32[128,128]{1,0:T(8,128)}, u32[]{:S(2)}) copy-start(f32[128,128]{1,0:T(8,128)} %param.69) | copy-start | bytes 196612
  974.7 29.3 %copy-start.35 = (bf16[4,4,256,128]{3,2,1,0:T(8,128)(2,1)S(1)}, bf16[4,4,256,128]{3,2,1,0:T(8,128)(2,1)}, u32[]{:S(2)}) copy-start(bf16[4,4,256,128]{3,2,1,0:T(8,128)(2,1)} %copy-done.34) | copy-start | bytes 3145732
  979.3 25.0 %copy-start.117 = (s32[256]{0:T(256)S(1)}, s32[256]{0:T(256)}, u32[]{:S(2)}) copy-start(s32[256]{0:T(256)} %get-tuple-element.405) | copy-start | bytes 3076
  996.4 10.9 %copy-start.126 = (f32[1,8]{1,0:T(1,128)}, f32[1,8]{1,0:T(1,128)S(1)}, u32[]{:S(2)}) copy-start(f32[1,8]{1,0:T(1,128)S(1)} %get-tuple-element.322) | copy-start | bytes 100
  999.5 9.5 copy-start.106
  1001.1 9.3 copy-start.26
  1001.1 9.3 copy-start.90
  1004.0 9.1 copy-start.24
  1004.0 9.1 copy-start.91
  1004.1 9.1 copy-start.101
  1004.1 9.1 copy-start.102
  1017.2 6.2 copy-start.81
  1017.2 7.4 copy-start.82
  1024.6 6.2 copy-start.40
  1024.6 7.0 copy-start.1
  (85 other events, 205.2 us)
Sparse Core Ops, SparseCore 0:
  108.8 62.6 all-gather.6
  174.0 87.5 all-gather.4
  623.4 25.1 reduce-scatter.13
  651.7 52.6 reduce-scatter.11
  707.4 86.4 reduce-scatter.9

commit v4 on v3

--- a/solution.py
+++ b/solution.py
@@ -309,128 +309,6 @@
         pl.semaphore_wait(barrier, 2 + int(core))
 
 
-def line_gather(block, ident, core, micros):
-    count = lax.axis_size("row")
-
-    def kernel(x_ref, o_ref, send_l, send_r, send_c, recv_l, recv_r, recv_c, local):
-        me = lax.axis_index("row")
-        column = lax.axis_index("col")
-
-        def slot(source):
-            return o_ref.at[column, source] if core else o_ref.at[source]
-
-        def other(source):
-            return o_ref.at[1 - column, source]
-
-        def to_left(source, k):
-            origin = x_ref if k == 0 else slot(source)
-            return push(origin, slot(source), send_l.at[k], recv_r.at[k], {"row": me - 1})
-
-        def to_right(source, k):
-            origin = x_ref if k == 0 else slot(source)
-            return push(origin, slot(source), send_r.at[k], recv_l.at[k], {"row": me + 1})
-
-        def to_core(source, k):
-            origin = x_ref if k == 0 else slot(source)
-            return push(origin, slot(source), send_c.at[k], recv_c.at[k], {"col": 1 - column})
-
-        def from_core(source, k):
-            return push(other(source), other(source), send_c.at[k], recv_c.at[k], {"col": 1 - column})
-
-        greet_line(me, count, column, core)
-
-        @pl.when(me > 0)
-        def _():
-            to_left(me, 0).start()
-
-        @pl.when(me < count - 1)
-        def _():
-            to_right(me, 0).start()
-
-        if core:
-            to_core(me, 0).start()
-        own = pltpu.make_async_copy(x_ref, slot(me), local)
-        own.start()
-        for k in range(1, count):
-
-            @pl.when(me - k >= 0)
-            def _():
-                push(slot(me - k), slot(me - k), send_r.at[k], recv_l.at[k - 1], {"row": me - 1}).wait_recv()
-
-                @pl.when(me < count - 1)
-                def _():
-                    to_right(me - k, k).start()
-
-                if core:
-                    to_core(me - k, k).start()
-
-            @pl.when(me + k < count)
-            def _():
-                push(slot(me + k), slot(me + k), send_l.at[k], recv_r.at[k - 1], {"row": me + 1}).wait_recv()
-
-                @pl.when(me > 0)
-                def _():
-                    to_left(me + k, k).start()
-
-                if core:
-                    to_core(me + k, count - 1 + k).start()
-
-        own.wait()
-
-        @pl.when(me > 0)
-        def _():
-            to_left(me, 0).wait_send()
-
-        @pl.when(me < count - 1)
-        def _():
-            to_right(me, 0).wait_send()
-
-        if core:
-            to_core(me, 0).wait_send()
-            from_core(me, 0).wait_recv()
-        for k in range(1, count):
-
-            @pl.when(me - k >= 0)
-            def _():
-                @pl.when(me < count - 1)
-                def _():
-                    to_right(me - k, k).wait_send()
-
-                if core:
-                    to_core(me - k, k).wait_send()
-                    from_core(me - k, k).wait_recv()
-
-            @pl.when(me + k < count)
-            def _():
-                @pl.when(me > 0)
-                def _():
-                    to_left(me + k, k).wait_send()
-
-                if core:
-                    to_core(me + k, count - 1 + k).wait_send()
-                    from_core(me + k, count - 1 + k).wait_recv()
-
-    shape = ((2, count) if core else (count,)) + block.shape
-    dma = pltpu.SemaphoreType.DMA
-    return pl.pallas_call(
-        kernel,
-        out_shape=jax.ShapeDtypeStruct(shape, block.dtype),
-        in_specs=[pl.BlockSpec(memory_space=pl.ANY)],
-        out_specs=pl.BlockSpec(memory_space=pl.ANY),
-        scratch_shapes=[
-            dma((count,)),
-            dma((count,)),
-            dma((2 * count,)),
-            dma((count,)),
-            dma((count,)),
-            dma((2 * count,)),
-            dma,
-        ],
-        compiler_params=params(ident),
-        cost_estimate=cost(micros),
-    )(block)
-
-
 def line_reduce(parts, ident, core, micros):
     count = lax.axis_size("row")
     high, wide = parts.shape[-2:]
@@ -597,16 +475,13 @@
     def other(self, source):
         return self.place(self.o_ref, 1 - self.column, source)
 
-    def to_left(self, source, k):
-        origin = self.x_ref if k == 0 else self.slot(source)
+    def to_left(self, source, k, origin):
         return push(origin, self.slot(source), self.sems[0].at[k], self.sems[4].at[k], {"row": self.me - 1})
 
-    def to_right(self, source, k):
-        origin = self.x_ref if k == 0 else self.slot(source)
+    def to_right(self, source, k, origin):
         return push(origin, self.slot(source), self.sems[1].at[k], self.sems[3].at[k], {"row": self.me + 1})
 
-    def to_core(self, source, k):
-        origin = self.x_ref if k == 0 else self.slot(source)
+    def to_core(self, source, k, origin):
         return push(origin, self.slot(source), self.sems[2].at[k], self.sems[5].at[k], {"col": 1 - self.column})
 
     def from_core(self, source, k):
@@ -629,14 +504,14 @@
 
         @pl.when(me > 0)
         def _():
-            self.to_left(me, 0).start()
+            self.to_left(me, 0, self.x_ref).start()
 
         @pl.when(me < count - 1)
         def _():
-            self.to_right(me, 0).start()
+            self.to_right(me, 0, self.x_ref).start()
 
         if self.core:
-            self.to_core(me, 0).start()
+            self.to_core(me, 0, self.x_ref).start()
         self.own().start()
 
     def step(self, k):
@@ -645,24 +520,26 @@
         @pl.when(me - k >= 0)
         def _():
             self.from_left(me - k, k).wait_recv()
+            block = self.slot(me - k)
 
             @pl.when(me < count - 1)
             def _():
-                self.to_right(me - k, k).start()
+                self.to_right(me - k, k, block).start()
 
             if self.core:
-                self.to_core(me - k, k).start()
+                self.to_core(me - k, k, block).start()
 
         @pl.when(me + k < count)
         def _():
             self.from_right(me + k, k).wait_recv()
+            block = self.slot(me + k)
 
             @pl.when(me > 0)
             def _():
-                self.to_left(me + k, k).start()
+                self.to_left(me + k, k, block).start()
 
             if self.core:
-                self.to_core(me + k, count - 1 + k).start()
+                self.to_core(me + k, count - 1 + k, block).start()
 
     def finish(self):
         me, count = self.me, self.count
@@ -670,35 +547,36 @@
 
         @pl.when(me > 0)
         def _():
-            self.to_left(me, 0).wait_send()
+            self.to_left(me, 0, self.x_ref).wait_send()
 
         @pl.when(me < count - 1)
         def _():
-            self.to_right(me, 0).wait_send()
+            self.to_right(me, 0, self.x_ref).wait_send()
 
         if self.core:
-            self.to_core(me, 0).wait_send()
+            self.to_core(me, 0, self.x_ref).wait_send()
             self.from_core(me, 0).wait_recv()
-        for k in range(1, count):
-
+
+        @pl.loop(1, count)
+        def _(k):
             @pl.when(me - k >= 0)
             def _():
                 @pl.when(me < count - 1)
                 def _():
-                    self.to_right(me - k, k).wait_send()
+                    self.to_right(me - k, k, self.x_ref).wait_send()
 
                 if self.core:
-                    self.to_core(me - k, k).wait_send()
+                    self.to_core(me - k, k, self.x_ref).wait_send()
                     self.from_core(me - k, k).wait_recv()
 
             @pl.when(me + k < count)
             def _():
                 @pl.when(me > 0)
                 def _():
-                    self.to_left(me + k, k).wait_send()
+                    self.to_left(me + k, k, self.x_ref).wait_send()
 
                 if self.core:
-                    self.to_core(me + k, count - 1 + k).wait_send()
+                    self.to_core(me + k, count - 1 + k, self.x_ref).wait_send()
                     self.from_core(me + k, count - 1 + k).wait_recv()
 
 
@@ -781,19 +659,29 @@
         self.copy().wait()
 
 
-def transfers(items, ident, micros):
-    count, data = lax.axis_size("row"), lax.axis_size("dp")
-    kinds = [item.semaphores(count, data) for item in items]
-    number = len(items)
-    across = any(getattr(item, "axis", None) == "dp" for item in items)
-    cores = any(getattr(item, "core", False) for item in items)
-
-    def kernel(*refs):
-        x_refs, o_refs, sems = refs[:number], refs[number : 2 * number], refs[2 * number :]
-        me, column, at = lax.axis_index("row"), lax.axis_index("col"), lax.axis_index("dp")
-        for item, x_ref, o_ref, kind in zip(items, x_refs, o_refs, kinds):
-            item.bind(x_ref, o_ref, sems[: len(kind)], (me, column, at), (count, data))
+class Bundle:
+    def __init__(self, items):
+        self.items = items
+        self.number = len(items)
+        self.sizes = lax.axis_size("row"), lax.axis_size("dp")
+        self.kinds = [item.semaphores(*self.sizes) for item in items]
+        self.across = any(getattr(item, "axis", None) == "dp" for item in items)
+        self.cores = any(getattr(item, "core", False) for item in items)
+        self.sources = [item.source for item in items]
+        self.shapes = [jax.ShapeDtypeStruct(item.shape, item.source.dtype) for item in items]
+        self.specs = [pl.BlockSpec(memory_space=pl.ANY)] * self.number
+        self.scratch = sum(self.kinds, [])
+
+    def bind(self, x_refs, o_refs, sems):
+        self.spots = lax.axis_index("row"), lax.axis_index("col"), lax.axis_index("dp")
+        for item, x_ref, o_ref, kind in zip(self.items, x_refs, o_refs, self.kinds):
+            item.bind(x_ref, o_ref, sems[: len(kind)], self.spots, self.sizes)
             sems = sems[len(kind) :]
+
+    def greet(self, across=False, cores=False):
+        me, column, at = self.spots
+        count, data = self.sizes
+        across, cores = across or self.across, cores or self.cores
         barrier = pltpu.get_barrier_semaphore()
         for k in range(1, count):
             pl.semaphore_signal(
@@ -807,37 +695,58 @@
         if cores:
             pl.semaphore_signal(barrier, inc=1, device_id={"col": 1 - column}, device_id_type=MESH)
         pl.semaphore_wait(barrier, count - 1 + (data - 1) * int(across) + int(cores))
-        for item in items:
+
+    def start(self):
+        for item in self.items:
             item.start()
-        for k in range(1, count):
-            for item in items:
-                item.step(k)
-        for item in items:
+
+    def step(self, k):
+        for item in self.items:
+            item.step(k)
+
+    def finish(self):
+        for item in self.items:
             item.finish()
 
-    anywhere = pl.BlockSpec(memory_space=pl.ANY)
+
+def transfers(items, ident, micros):
+    bundle = Bundle(items)
+    number = bundle.number
+
+    def kernel(*refs):
+        bundle.bind(refs[:number], refs[number : 2 * number], refs[2 * number :])
+        bundle.greet()
+        bundle.start()
+        for k in range(1, bundle.sizes[0]):
+            bundle.step(k)
+        bundle.finish()
+
     return pl.pallas_call(
         kernel,
-        out_shape=[jax.ShapeDtypeStruct(item.shape, item.source.dtype) for item in items],
-        in_specs=[anywhere] * number,
-        out_specs=[anywhere] * number,
-        scratch_shapes=sum(kinds, []),
+        out_shape=bundle.shapes,
+        in_specs=bundle.specs,
+        out_specs=bundle.specs,
+        scratch_shapes=bundle.scratch,
         compiler_params=params(ident, 16),
         cost_estimate=cost(micros),
-    )(*[item.source for item in items])
-
-
-def shard_total(query_parts, kv_parts, flat_parts, ident):
+    )(*bundle.sources)
+
+
+def shard_total(query_parts, kv_parts, flat_parts, items, ident):
     data = lax.axis_size("dp")
-    half = data // 2
-
-    def kernel(q_ref, kv_ref, f_ref, oq_ref, okv_ref, of_ref, q_buf, kv_buf, f_buf, *sems):
+    bundle = Bundle(items)
+    number = bundle.number
+
+    def kernel(q_ref, kv_ref, f_ref, *refs):
+        x_refs, refs = refs[:number], refs[number:]
+        oq_ref, okv_ref, of_ref = refs[:3]
+        o_refs, refs = refs[3 : 3 + number], refs[3 + number :]
+        q_buf, kv_buf, f_buf = refs[:3]
+        sems = refs[3:11]
+        bundle.bind(x_refs, o_refs, refs[11:])
         column, at = lax.axis_index("col"), lax.axis_index("dp")
-        barrier = pltpu.get_barrier_semaphore()
-        for k in range(1, data):
-            pl.semaphore_signal(barrier, inc=1, device_id={"dp": lax.rem(at + k, data)}, device_id_type=MESH)
-        pl.semaphore_signal(barrier, inc=1, device_id={"col": 1 - column}, device_id_type=MESH)
-        pl.semaphore_wait(barrier, data)
+        bundle.greet(True, True)
+        bundle.start()
         mine = lax.rem(at, 2) == column
 
         def copies(k):
@@ -899,20 +808,25 @@
         def _():
             share.wait_recv()
 
+        for k in range(1, bundle.sizes[0]):
+            bundle.step(k)
+        bundle.finish()
+
     vmem = pl.BlockSpec(memory_space=pltpu.VMEM)
     dma = pltpu.SemaphoreType.DMA
     shapes = [query_parts.shape[1:], kv_parts.shape[1:], flat_parts.shape[1:]]
     return pl.pallas_call(
         kernel,
-        out_shape=[jax.ShapeDtypeStruct(shape, FULL) for shape in shapes],
-        in_specs=[vmem] * 3,
-        out_specs=[vmem] * 3,
+        out_shape=[jax.ShapeDtypeStruct(shape, FULL) for shape in shapes] + bundle.shapes,
+        in_specs=[vmem] * 3 + bundle.specs,
+        out_specs=[vmem] * 3 + bundle.specs,
         scratch_shapes=[pltpu.VMEM((data,) + shape, LOW) for shape in shapes]
         + [dma((data,))] * 6
-        + [dma, dma],
+        + [dma, dma]
+        + bundle.scratch,
         compiler_params=params(ident),
-        cost_estimate=cost(20),
-    )(query_parts, kv_parts, flat_parts)
+        cost_estimate=cost(40),
+    )(query_parts, kv_parts, flat_parts, *bundle.sources)
 
 
 class Flow:
@@ -969,7 +883,6 @@
 
     def start(self):
         me, count = self.me, self.count
-        greet_line(me, count, self.column, True)
 
         @pl.when(me > 0)
         def _():
@@ -1022,12 +935,16 @@
         def _():
             self.to_core(me + k, self.x_ref).wait()
 
-    def visit(self, body):
+    def visit(self, body, bundle):
         me, count = self.me, self.count
 
         @pl.loop(0, count)
         def _(k):
             self.arrive(k)
+
+            @pl.when(k > 0)
+            def _():
+                bundle.step(k)
 
             @pl.loop(0, 2)
             def _(side):
@@ -1157,23 +1074,31 @@
     return values_in * half, slope
 
 
-def ffn_forward(block, gateup, down, ident):
+def ffn_forward(block, gateup, down, items, ident):
     count = lax.axis_size("row")
     share, width = block.shape
     groups, _, _, part = gateup.shape
     hidden = groups * part
     out_cols = down.shape[2] // count
     rows = 2 * share
-
-    def kernel(x_ref, gw_hbm, dw_hbm, o_ref, xt_hbm, at_hbm, g_hbm, u_hbm, *scratch):
+    bundle = Bundle(items)
+    number = bundle.number
+
+    def kernel(x_ref, gw_hbm, dw_hbm, *refs):
+        x_refs, refs = refs[:number], refs[number:]
+        o_ref, xt_hbm, at_hbm, g_hbm, u_hbm = refs[:5]
+        o_refs, scratch = refs[5 : 5 + number], refs[5 + number :]
         flow = Flow(x_ref, *scratch[:6], scratch[6:19])
         gw, dw, xt, at, act, gate, up = scratch[19:26]
-        gw_sem, dw_sem, xt_sem, at_sem, g_sem, u_sem = scratch[26:]
+        gw_sem, dw_sem, xt_sem, at_sem, g_sem, u_sem = scratch[26:32]
+        bundle.bind(x_refs, o_refs, scratch[32:])
         gw_load = pltpu.make_async_copy(gw_hbm, gw, gw_sem)
         dw_load = pltpu.make_async_copy(dw_hbm, dw, dw_sem)
         gw_load.start()
         dw_load.start()
+        bundle.greet(False, True)
         flow.start()
+        bundle.start()
         gw_load.wait()
         dw_load.wait()
 
@@ -1208,7 +1133,7 @@
                     flow.own[source, :, columns] = piece[:share]
                     flow.core_out[source, :, columns] = piece[share:].astype(LOW)
 
-        flow.visit(body)
+        flow.visit(body, bundle)
         xt_store = pltpu.make_async_copy(xt, xt_hbm, xt_sem)
         at_store = pltpu.make_async_copy(at, at_hbm, at_sem)
         xt_store.start()
@@ -1219,6 +1144,7 @@
             flow.give_back(t)
 
         flow.finish(o_ref)
+        bundle.finish()
         xt_store.wait()
         at_store.wait()
 
@@ -1239,9 +1165,10 @@
             jax.ShapeDtypeStruct((hidden, tokens), LOW),
             jax.ShapeDtypeStruct((count, rows, hidden), FULL),
             jax.ShapeDtypeStruct((count, rows, hidden), FULL),
-        ],
-        in_specs=[vmem, anywhere, anywhere],
-        out_specs=[vmem] + [anywhere] * 4,
+        ]
+        + bundle.shapes,
+        in_specs=[vmem, anywhere, anywhere] + bundle.specs,
+        out_specs=[vmem] + [anywhere] * 4 + bundle.specs,
         scratch_shapes=buffers
         + sems
         + [
@@ -1253,13 +1180,14 @@
             pltpu.VMEM((count, rows, hidden), FULL),
             pltpu.VMEM((count, rows, hidden), FULL),
         ]
-        + [dma, dma, dma, dma, dma((count,)), dma((count,))],
+        + [dma, dma, dma, dma, dma((count,)), dma((count,))]
+        + bundle.scratch,
         compiler_params=params(ident, 60),
         cost_estimate=cost(80),
-    )(block, gateup, down)
-
-
-def ffn_backward(block, gateup, down, xt, at, gate, up, ident):
+    )(block, gateup, down, *bundle.sources)
+
+
+def ffn_backward(block, gateup, down, xt, at, gate, up, items, ident):
     count = lax.axis_size("row")
     share, width = block.shape
     groups, _, _, part = gateup.shape
@@ -1267,12 +1195,17 @@
     out_cols = down.shape[2] // count
     rows = 2 * share
     tokens = count * rows
-    pieces = 3 * groups
-
-    def kernel(x_ref, gw_hbm, dw_hbm, xt_hbm, at_hbm, g_hbm, u_hbm, o_ref, dgu_hbm, ddn_hbm, *scratch):
+    bundle = Bundle(items)
+    number = bundle.number
+
+    def kernel(x_ref, gw_hbm, dw_hbm, xt_hbm, at_hbm, g_hbm, u_hbm, *refs):
+        x_refs, refs = refs[:number], refs[number:]
+        o_ref, dgu_hbm, ddn_hbm = refs[:3]
+        o_refs, scratch = refs[3 : 3 + number], refs[3 + number :]
         flow = Flow(x_ref, *scratch[:6], scratch[6:19])
         gw, dw, xt_own, at_own, gate_own, up_own, d_gate, d_up, total, stage, stage_down = scratch[19:30]
-        load_sems, g_sem, u_sem, out_sem, down_sem = scratch[30:]
+        load_sems, g_sem, u_sem, out_sem, down_sem = scratch[30:35]
+        bundle.bind(x_refs, o_refs, scratch[35:])
         loads = [
             pltpu.make_async_copy(source, target, load_sems.at[k])
             for k, (source, target) in enumerate(
@@ -1296,7 +1229,9 @@
 
         for load in loads[2:]:
             load.start()
+        bundle.greet(False, True)
         flow.start()
+        bundle.start()
         loads[0].wait()
         loads[1].wait()
 
@@ -1340,7 +1275,7 @@
             flow.own[source] = total[:share]
             flow.core_out[source] = total[share:].astype(LOW)
 
-        flow.visit(body)
+        flow.visit(body, bundle)
         loads[2].wait()
         loads[3].wait()
 
@@ -1393,6 +1328,7 @@
             gateup_store(groups - 1, which).wait()
         down_store(groups - 1).wait()
         flow.finish(o_ref)
+        bundle.finish()
 
     dma = pltpu.SemaphoreType.DMA
     buffers, sems = Flow.scratch(count, share, width)
@@ -1403,9 +1339,10 @@
             jax.ShapeDtypeStruct((share, width), FULL),
             jax.ShapeDtypeStruct(gateup.shape, LOW),
             jax.ShapeDtypeStruct(down.shape, LOW),
-        ],
-        in_specs=[vmem] + [anywhere] * 6,
-        out_specs=[vmem, anywhere, anywhere],
+        ]
+        + bundle.shapes,
+        in_specs=[vmem] + [anywhere] * 6 + bundle.specs,
+        out_specs=[vmem, anywhere, anywhere] + bundle.specs,
         scratch_shapes=buffers
         + sems
         + [
@@ -1421,25 +1358,42 @@
             pltpu.VMEM((2, width, part), LOW),
             pltpu.VMEM((hidden, count * out_cols), LOW),
         ]
-        + [dma((4,)), dma((count,)), dma((count,)), dma((2,)), dma],
+        + [dma((4,)), dma((count,)), dma((count,)), dma((2,)), dma]
+        + bundle.scratch,
         compiler_params=params(ident, 62),
         cost_estimate=cost(90),
-    )(block, gateup, down, xt, at, gate, up)
-
-
-def small_total(values_in, axes, max_rows, ident):
+    )(block, gateup, down, xt, at, gate, up, *bundle.sources)
+
+
+def finish_step(small, sum_rows, groups, ident):
+    axes = ("col", "row", "dp")
     sizes = [lax.axis_size(axis) for axis in axes]
-    high = values_in.shape[0]
-
-    def kernel(x_ref, o_ref, *scratch):
-        slots, sends, recvs = (scratch[k :: 3] for k in range(3))
+    high = small.shape[0]
+    number = len(groups)
+    arrays = [array for group in groups for array in group[:4]]
+
+    def kernel(x_ref, *refs):
+        sources, refs = refs[: 4 * number], refs[4 * number :]
+        o_ref, outs, refs = refs[0], refs[1 : 1 + 3 * number], refs[1 + 3 * number :]
+        held, refs = refs[: 4 * number], refs[4 * number :]
+        load_sem, store_sem, refs = refs[0], refs[1], refs[2:]
+        slots, sends, recvs = (refs[k::3] for k in range(3))
+
+        def load(k):
+            return pltpu.make_async_copy(sources[k], held[k], load_sem.at[k])
+
+        def store(group, k):
+            return pltpu.make_async_copy(held[4 * group + (1, 2, 0)[k]], outs[3 * group + k], store_sem.at[3 * group + k])
+
+        spots = [lax.axis_index(axis) for axis in axes]
         barrier = pltpu.get_barrier_semaphore()
-        spots = [lax.axis_index(axis) for axis in axes]
         for axis, size, me in zip(axes, sizes, spots):
             for k in range(1, size):
                 pl.semaphore_signal(
                     barrier, inc=1, device_id={axis: lax.rem(me + k, size)}, device_id_type=MESH
                 )
+        for k in range(4 * number):
+            load(k).start()
         pl.semaphore_wait(barrier, sum(sizes) - len(sizes))
         for at, (axis, size, me) in enumerate(zip(axes, sizes, spots)):
             buf, send, recv = slots[at], sends[at], recvs[at]
@@ -1450,29 +1404,70 @@
                 origin = lax.rem(me + size - k, size)
                 push(buf.at[origin], buf.at[origin], send.at[k], recv.at[k], {axis: origin}).wait()
             total = buf[0]
+            top = buf[0, high - 8 :]
             for k in range(1, size):
                 total = total + buf[k]
+                top = jnp.maximum(top, buf[k, high - 8 :])
             o_ref[...] = total
-            if max_rows:
-                top = buf[0, high - max_rows :]
-                for k in range(1, size):
-                    top = jnp.maximum(top, buf[k, high - max_rows :])
-                o_ref[high - max_rows :] = top
+            o_ref[high - 8 :] = top
+        sums = o_ref[:sum_rows]
+        squares = jnp.sum(jnp.sum(sums * sums, axis=1, keepdims=True), axis=0, keepdims=True)
+        squares = squares + o_ref[sum_rows : sum_rows + 1, :1]
+        clip = CLIP / jnp.maximum(jnp.sqrt(squares), CLIP)
+        tops = o_ref[high - 1 :]
+        lanes = lax.broadcasted_iota(jnp.int32, (1, 128), 1)
+        group_size = QUERY_HEADS // KEY_VALUE_HEADS
+
+        def factor(first, count):
+            chosen = (lanes >= first) & (lanes < first + count)
+            top = jnp.max(jnp.where(chosen, tops, NEGATIVE), axis=1, keepdims=True)
+            return jnp.sqrt(LOGIT_CAP / jnp.maximum(top, LOGIT_CAP))
+
+        factors = {
+            "query": factor(spots[0] * sizes[2] + spots[2], 1),
+            "keyval": jnp.where(
+                spots[2] < KEY_VALUE_HEADS, factor(spots[2] * group_size, group_size), 1.0
+            ),
+        }
+        for group in range(number):
+            rate, kind = groups[group][4:]
+            for k in range(4):
+                load(4 * group + k).wait()
+            w_ref, m_ref, v_ref, g_ref = held[4 * group : 4 * group + 4]
+            rows, cols = w_ref.shape
+            step = min(rows, max(16, 32768 // max(cols, 128)))
+
+            @pl.loop(0, rows // step)
+            def _(at):
+                here = pl.ds(pl.multiple_of(at * step, step), step)
+                new = adamw_step(
+                    w_ref[here], m_ref[here], v_ref[here], g_ref[here].astype(FULL) * clip, rate, DECAY
+                )
+                m_ref[here], v_ref[here] = new[0], new[1]
+                w_ref[here] = new[2] * factors[kind] if kind else new[2]
+
+            for k in range(3):
+                store(group, k).start()
+        for group in range(number):
+            for k in range(3):
+                store(group, k).wait()
 
     dma = pltpu.SemaphoreType.DMA
-    vmem = pl.BlockSpec(memory_space=pltpu.VMEM)
-    scratch = []
+    vmem, anywhere = pl.BlockSpec(memory_space=pltpu.VMEM), pl.BlockSpec(memory_space=pl.ANY)
+    scratch = [pltpu.VMEM(array.shape, array.dtype) for array in arrays]
+    scratch += [dma((4 * number,)), dma((3 * number,))]
     for size in sizes:
-        scratch += [pltpu.VMEM((size,) + values_in.shape, FULL), dma((size,)), dma((size,))]
+        scratch += [pltpu.VMEM((size,) + small.shape, FULL), dma((size,)), dma((size,))]
+    outs = [jax.ShapeDtypeStruct(group[0].shape, FULL) for group in groups for _ in range(3)]
     return pl.pallas_call(
         kernel,
-        out_shape=jax.ShapeDtypeStruct(values_in.shape, FULL),
-        in_specs=[vmem],
-        out_specs=vmem,
+        out_shape=[jax.ShapeDtypeStruct(small.shape, FULL)] + outs,
+        in_specs=[vmem] + [anywhere] * (4 * number),
+        out_specs=[vmem] + [anywhere] * (3 * number),
         scratch_shapes=scratch,
-        compiler_params=params(ident, 16),
-        cost_estimate=cost(4 * len(sizes)),
-    )(values_in)
+        compiler_params=params(ident, 56),
+        cost_estimate=cost(25),
+    )(small, *arrays)
 
 
 def allowed_block(at, high, width, spans):
@@ -1499,40 +1494,92 @@
     return raw_weights / jnp.sum(raw_weights, axis=-1, keepdims=True), peak_row
 
 
-def head_forward(queries, keys, values, spans):
-    rows = queries.shape[0]
-    step = min(256, rows)
-
-    def kernel(spans_ref, q_ref, k_ref, v_ref, o_ref, top_ref):
-        top_ref[...] = jnp.full(top_ref.shape, NEGATIVE, FULL)
-
-        @pl.loop(0, rows // step)
-        def _(at):
+def attention_forward_head(acts, gain, head_w, kv_w, query_gain, key_gain, cos_tab, sin_tab, spans, items, ident):
+    tokens, width = acts.shape
+    step = 256
+    bundle = Bundle(items)
+    number = bundle.number
+
+    def kernel(spans_ref, x_ref, gain_ref, qw_ref, kvw_ref, qg_ref, kg_ref, cos_ref, sin_ref, *refs):
+        x_refs, refs = refs[:number], refs[number:]
+        h_ref, scale_ref, qr_ref, kr_ref, vr_ref, q_ref, k_ref, v_ref, o_ref, top_ref = refs[:10]
+        o_refs, sems = refs[10 : 10 + number], refs[10 + number :]
+        bundle.bind(x_refs, o_refs, sems)
+        bundle.greet()
+        bundle.start()
+
+        def project(at):
             here = pl.ds(pl.multiple_of(at * step, step), step)
-            allowed = allowed_block(at, step, keys.shape[0], spans_ref)
+            rows = x_ref[here].astype(FULL)
+            scale = lax.rsqrt(jnp.mean(rows * rows, axis=-1, keepdims=True) + EPS)
+            scale_ref[here] = jnp.broadcast_to(scale, (step, 128))
+            h_ref[here] = (rows * scale * gain_ref[...]).astype(LOW)
+            hidden = h_ref[here]
+            cos_rows, sin_rows = cos_ref[here], sin_ref[here]
+            query = flat_dot(hidden, qw_ref[...])
+            qr_ref[here] = query
+            q_ref[here] = turn(whole_norm(query, qg_ref[...])[0], cos_rows, sin_rows).astype(LOW)
+            key = flat_dot(hidden, kvw_ref[0])
+            kr_ref[here] = key
+            k_ref[here] = turn(whole_norm(key, kg_ref[...])[0], cos_rows, sin_rows).astype(LOW)
+            value = flat_dot(hidden, kvw_ref[1])
+            vr_ref[here] = value
+            v_ref[here] = whole_norm(value, 1.0)[0].astype(LOW)
+
+        def attend(at):
+            here = pl.ds(pl.multiple_of(at * step, step), step)
+            allowed = allowed_block(at, step, tokens, spans_ref)
             probs, peak_row = softmax_block(q_ref[here], k_ref[...], allowed)
             o_ref[here] = flat_dot(probs.astype(LOW), v_ref[...]).astype(LOW)
             top_ref[...] = jnp.maximum(top_ref[...], jnp.max(peak_row))
 
+        top_ref[...] = jnp.full(top_ref.shape, NEGATIVE, FULL)
+        pl.loop(0, tokens // step)(project)
+        bundle.step(1)
+        pl.loop(0, tokens // step)(attend)
+        for k in range(2, bundle.sizes[0]):
+            bundle.step(k)
+        bundle.finish()
+
     vmem = pl.BlockSpec(memory_space=pltpu.VMEM)
+    low = jax.ShapeDtypeStruct((tokens, HEAD_WIDTH), LOW)
+    full = jax.ShapeDtypeStruct((tokens, HEAD_WIDTH), FULL)
     return pl.pallas_call(
         kernel,
-        out_shape=(
-            jax.ShapeDtypeStruct(queries.shape, LOW),
+        out_shape=[
+            jax.ShapeDtypeStruct((tokens, width), LOW),
+            jax.ShapeDtypeStruct((tokens, 128), FULL),
+            full,
+            full,
+            full,
+            low,
+            low,
+            low,
+            low,
             jax.ShapeDtypeStruct((8, 128), FULL),
-        ),
-        in_specs=[pl.BlockSpec(memory_space=pltpu.SMEM), vmem, vmem, vmem],
-        out_specs=(vmem, vmem),
-        compiler_params=pltpu.CompilerParams(vmem_limit_bytes=48 * 2**20),
-        cost_estimate=cost(10),
-    )(spans, queries, keys, values)
-
-
-def head_backward(queries, keys, values, grads, spans):
+        ]
+        + bundle.shapes,
+        in_specs=[pl.BlockSpec(memory_space=pltpu.SMEM)] + [vmem] * 8 + bundle.specs,
+        out_specs=[vmem] * 10 + bundle.specs,
+        scratch_shapes=bundle.scratch,
+        compiler_params=params(ident),
+        cost_estimate=cost(40),
+    )(spans, acts, gain, head_w, kv_w, query_gain, key_gain, cos_tab, sin_tab, *bundle.sources)
+
+
+def head_backward(queries, keys, values, grads, spans, items, ident):
     rows = queries.shape[0]
     step = min(256, rows)
 
-    def kernel(spans_ref, q_ref, k_ref, v_ref, g_ref, dq_ref, dk_ref, dv_ref):
+    bundle = Bundle(items)
+    number = bundle.number
+
+    def kernel(spans_ref, q_ref, k_ref, v_ref, g_ref, *refs):
+        x_refs, refs = refs[:number], refs[number:]
+        dq_ref, dk_ref, dv_ref = refs[:3]
+        bundle.bind(x_refs, refs[3 : 3 + number], refs[3 + number :])
+        bundle.greet()
+        bundle.start()
         dk_ref[...] = jnp.zeros(dk_ref.shape, FULL)
         dv_ref[...] = jnp.zeros(dv_ref.shape, FULL)
 
@@ -1549,16 +1596,22 @@
             dk_ref[...] += inner_rows(grad_scores, block_rows)
             dv_ref[...] += inner_rows(probs.astype(LOW), grad_rows)
 
+        for k in range(1, bundle.sizes[0]):
+            bundle.step(k)
+        bundle.finish()
+
     vmem = pl.BlockSpec(memory_space=pltpu.VMEM)
     return pl.pallas_call(
         kernel,
-        out_shape=(jax.ShapeDtypeStruct(queries.shape, FULL),)
-        + (jax.ShapeDtypeStruct(keys.shape, FULL),) * 2,
-        in_specs=[pl.BlockSpec(memory_space=pltpu.SMEM)] + [vmem] * 4,
-        out_specs=(vmem, vmem, vmem),
-        compiler_params=pltpu.CompilerParams(vmem_limit_bytes=48 * 2**20),
-        cost_estimate=cost(20),
-    )(spans, queries, keys, values, grads)
+        out_shape=[jax.ShapeDtypeStruct(queries.shape, FULL)]
+        + [jax.ShapeDtypeStruct(keys.shape, FULL)] * 2
+        + bundle.shapes,
+        in_specs=[pl.BlockSpec(memory_space=pltpu.SMEM)] + [vmem] * 4 + bundle.specs,
+        out_specs=[vmem] * 3 + bundle.specs,
+        scratch_shapes=bundle.scratch,
+        compiler_params=params(ident),
+        cost_estimate=cost(25),
+    )(spans, queries, keys, values, grads, *bundle.sources)
 
 
 def whole_norm(values_in, gain_vec):
@@ -1585,10 +1638,6 @@
 
 def turn_back(values_in, cos_tab, sin_tab):
     return turn(values_in, cos_tab, -sin_tab)
-
-
-def swap_row(values_in, split, concat, tiled=True):
-    return lax.all_to_all(values_in, "row", split, concat, tiled=tiled)
 
 
 def line_device(
@@ -1646,26 +1695,47 @@
     ff_part = w_gateup.shape[2] // rows_n
     out_cols = w_down.shape[1]
     heads_here = data_n
-    smalls = (w_left, w_right, w_pergate, w_perproj)
-    flat = jnp.concatenate([w.astype(LOW).reshape(-1) for w in smalls]).reshape(-1, 128)
-    flat_rows = flat.shape[0]
+    left_cols, right_rows = w_left.shape[1], w_right.shape[0]
+    gate_cols, proj_rows = w_pergate.shape[1], w_perproj.shape[0]
 
     def columns_of(at, size):
         return pl.ds(pl.multiple_of(at * size, size), size)
 
-    gateup_own, down_own, attend_own, upstream, qkv_w, flat = transfers(
+    def across(source, by_rows):
+        high, wide = source.shape
+        if by_rows:
+            return Swap(
+                source,
+                (data_n * high, wide),
+                lambda ref, q: ref,
+                lambda ref, at: ref.at[columns_of(at, high)],
+                "dp",
+            )
+        return Swap(
+            source,
+            (high, data_n * wide),
+            lambda ref, q: ref,
+            lambda ref, at: ref.at[:, columns_of(at, wide)],
+            "dp",
+        )
+
+    def along(source):
+        high, wide = source.shape
+        return Line(
+            source,
+            (cols_n * high, rows_n * wide),
+            lambda ref, c, r: ref.at[columns_of(c, high), columns_of(r, wide)],
+            True,
+        )
+
+    whole_acts, gateup_own, attend_own, qkv_w, left_t, right_w, pergate_t, perproj_w = transfers(
         [
+            along(activations),
             Swap(
                 w_gateup.astype(LOW),
                 (2, width, ff_part),
                 lambda ref, q: ref.at[:, :, columns_of(q, ff_part)],
                 lambda ref, at: ref.at[:, columns_of(at, width_a), :],
-            ),
-            Swap(
-                w_down.astype(LOW).reshape(data_n, rows_n, ff_part, out_cols),
-                (data_n, ff_part, rows_n * out_cols),
-                lambda ref, q: ref.at[:, q],
-                lambda ref, at: ref.at[:, :, columns_of(at, out_cols)],
             ),
             Swap(
                 w_attend.astype(LOW).reshape(rows_n, HEAD_WIDTH, out_cols),
@@ -1674,43 +1744,27 @@
                 lambda ref, at: ref.at[:, columns_of(at, out_cols)],
             ),
             Swap(
-                cotangent,
-                (share, width),
-                lambda ref, q: ref.at[columns_of(q, share)],
-                lambda ref, at: ref.at[:, columns_of(at, width_a)],
-            ),
-            Swap(
                 jnp.concatenate([w_query, key_value_weight], axis=1).astype(LOW),
                 (data_n, width_a, 2 * HEAD_WIDTH),
                 lambda ref, q: ref,
                 lambda ref, at: ref.at[at],
                 "dp",
             ),
-            Swap(
-                flat,
-                (data_n * flat_rows, 128),
-                lambda ref, q: ref,
-                lambda ref, at: ref.at[columns_of(at, flat_rows)],
-                "dp",
-            ),
+            across(w_left.T, True),
+            across(w_right.astype(LOW), False),
+            across(w_pergate.T.astype(LOW), True),
+            across(w_perproj.astype(LOW), False),
         ],
         1,
         90,
     )
     gateup_all = lax.all_gather(gateup_own, "dp")
-    down_all = lax.all_gather(down_own, "dp")
     query_w = qkv_w[:, :, :HEAD_WIDTH]
     kv_w = qkv_w[:, :, HEAD_WIDTH:]
     key_w = lax.dynamic_index_in_dim(kv_w, column, 0, False)
     value_w = lax.dynamic_index_in_dim(kv_w, KEY_VALUE_HEADS + column, 0, False)
-    whole_acts, whole_kv, head_w, flat, gains, extras, attend_all = transfers(
+    whole_kv, head_w, gains, extras, attend_all = transfers(
         [
-            Line(
-                activations,
-                (tokens, width),
-                lambda ref, c, r: ref.at[columns_of(c, half_tok), columns_of(r, width_a)],
-                True,
-            ),
             Line(
                 jnp.stack([key_w, value_w]),
                 (2, width, HEAD_WIDTH),
@@ -1721,9 +1775,6 @@
                 (width, HEAD_WIDTH),
                 lambda ref, q: ref.at[q],
                 lambda ref, at: ref.at[columns_of(at, width_a)],
-            ),
-            Line(
-                flat, (cols_n, rows_n) + flat.shape, lambda ref, c, r: ref.at[c, r], True
             ),
             Line(w_gains, (6, width), lambda ref, c, r: ref.at[:, columns_of(r, width_a)]),
             Line(
@@ -1741,71 +1792,102 @@
             ),
         ],
         2,
-        115,
+        60,
     )
     attend_w = (
         attend_all.reshape(data_n, HEAD_WIDTH, rows_n, out_cols)
         .transpose(1, 2, 0, 3)
         .reshape(HEAD_WIDTH, width)
     )
-    flat = flat.reshape(cols_n, rows_n, data_n, -1)
-    cuts = []
-    start = 0
-    for w in smalls:
-        cuts.append(flat[..., start : start + w.size].reshape((cols_n, rows_n, data_n) + w.shape))
-        start += w.size
-    left_w = cuts[0].transpose(1, 3, 0, 2, 4).reshape(width, -1)
-    right_w = cuts[1].transpose(0, 3, 1, 2, 4).reshape(-1, width)
-    pergate_w = cuts[2].transpose(1, 3, 0, 2, 4).reshape(width, -1)
-    perproj_w = cuts[3].transpose(0, 3, 1, 2, 4).reshape(-1, width)
-    upstream = upstream.astype(FULL)
     token_at = column * half_tok + me * share
     extras = lax.dynamic_slice_in_dim(extras, token_at, share, 0).astype(FULL)
     length = lax.dynamic_index_in_dim(lengths, data_at, 0, keepdims=True)
     piece_starts = lax.dynamic_index_in_dim(starts, data_at, 0, keepdims=False)
     spans = jnp.concatenate([length, piece_starts])
 
-    whole_hidden, whole_scale = whole_norm(whole_acts.astype(FULL), gains[0])
-    whole_hidden = whole_hidden.astype(LOW)
-    inputs = lax.dynamic_slice_in_dim(whole_acts, token_at, share, 0).astype(FULL)
-    query_raw = flat_dot(whole_hidden, head_w)
-    all_key_raw = flat_dot(whole_hidden, whole_kv[0])
-    all_value_raw = flat_dot(whole_hidden, whole_kv[1])
     query_gain = lax.dynamic_index_in_dim(w_heads, column * rows_n + me, 0, True)
     key_gain = w_heads[QUERY_HEADS:]
     all_cos, all_sin = rope_tables(jnp.arange(tokens, dtype=jnp.int32), HEAD_WIDTH)
     own_cos = lax.dynamic_slice_in_dim(all_cos, me * quarter, quarter, 0)
     own_sin = lax.dynamic_slice_in_dim(all_sin, me * quarter, quarter, 0)
-    query_n, query_scale = whole_norm(query_raw, query_gain)
-    queries = turn(query_n, all_cos, all_sin).astype(LOW)
-    keys = turn(whole_norm(all_key_raw, key_gain)[0], all_cos, all_sin).astype(LOW)
-    values = whole_norm(all_value_raw, 1.0)[0].astype(LOW)
-    attended, top = head_forward(queries, keys, values, spans)
+    (
+        whole_hidden,
+        whole_scale,
+        query_raw,
+        all_key_raw,
+        all_value_raw,
+        queries,
+        keys,
+        values,
+        attended,
+        top,
+        down_own,
+        left_t,
+        right_w,
+    ) = attention_forward_head(
+        whole_acts,
+        gains[:1],
+        head_w,
+        whole_kv,
+        query_gain,
+        key_gain,
+        all_cos,
+        all_sin,
+        spans,
+        [
+            Swap(
+                w_down.astype(LOW).reshape(data_n, rows_n, ff_part, out_cols),
+                (data_n, ff_part, rows_n * out_cols),
+                lambda ref, q: ref.at[:, q],
+                lambda ref, at: ref.at[:, :, columns_of(at, out_cols)],
+            ),
+            along(left_t.astype(LOW)),
+            along(right_w),
+        ],
+        3,
+    )
+    down_own, gateup_all = lax.optimization_barrier((down_own, gateup_all))
+    down_all = lax.all_gather(down_own, "dp").reshape(data_n, data_n * ff_part, -1)
+    inputs = lax.dynamic_slice_in_dim(whole_acts, token_at, share, 0).astype(FULL)
     key_raw = lax.dynamic_slice_in_dim(all_key_raw, me * quarter, quarter, 0)
     value_raw = lax.dynamic_slice_in_dim(all_value_raw, me * quarter, quarter, 0)
+    _, query_scale = whole_norm(query_raw, query_gain)
     _, key_scale = whole_norm(key_raw, key_gain)
     _, value_scale = whole_norm(value_raw, 1.0)
-    down_all = down_all.reshape(data_n, data_n * ff_part, -1)
 
     def shares(parts):
         return parts.astype(LOW).reshape(cols_n, rows_n, share, width)
 
     hidden, _ = whole_norm(inputs, gains[0])
     hidden_low = hidden.astype(LOW)
-    middle = flat_dot(hidden_low, left_w).astype(LOW)
+    middle = against(hidden_low, left_t).astype(LOW)
     right_raw = flat_dot(middle, right_w)
     right_n, scale_r = whole_norm(right_raw, gains[1])
     projected = line_reduce(shares(flat_dot(attended, attend_w)), 5, True, 45)
     proj_n, scale_p = whole_norm(projected, gains[2])
     mixture = ((inputs + proj_n) + (hidden + right_n)) * HALF_ROOT
     ffn_n, scale_f = whole_norm(mixture, gains[3])
-    down_raw, spread_ft, act_t, gate_raw, up_raw = ffn_forward(
-        ffn_n.astype(LOW), gateup_all, down_all, 6
-    )
+    down_raw, spread_ft, act_t, gate_raw, up_raw, upstream, pergate_t, perproj_w = ffn_forward(
+        ffn_n.astype(LOW),
+        gateup_all,
+        down_all,
+        [
+            Swap(
+                cotangent,
+                (share, width),
+                lambda ref, q: ref.at[columns_of(q, share)],
+                lambda ref, at: ref.at[:, columns_of(at, width_a)],
+            ),
+            along(pergate_t),
+            along(perproj_w),
+        ],
+        6,
+    )
+    upstream = upstream.astype(FULL)
     down_n, scale_d = whole_norm(down_raw, gains[4])
     block_out = mixture + down_n
     out_low = block_out.astype(LOW)
-    pgate = flat_dot(out_low, pergate_w)
+    pgate = against(out_low, pergate_t)
     pact = (jax.nn.gelu(pgate, approximate=True) * extras).astype(LOW)
     perproj = flat_dot(pact, perproj_w)
     perproj_n, scale_pp = whole_norm(perproj, gains[5])
@@ -1819,49 +1901,94 @@
     _, pullback = jax.vjp(lambda v: jax.nn.gelu(v, approximate=True), pgate)
     (d_pgate,) = pullback(d_pact * extras)
     d_pgate = d_pgate.astype(LOW)
-    dw_pergate = inner_rows(out_low, d_pgate)
-    d_out = upstream + against(d_pgate, pergate_w)
+    dw_pergate = inner_rows(d_pgate, out_low)
+    d_out = upstream + flat_dot(d_pgate, pergate_t)
     d_down, gain_grads[4] = whole_norm_backward(down_raw, scale_d, gains[4], d_out)
-    d_ffn, dw_gateup, dw_down = ffn_backward(
-        d_down.astype(LOW), gateup_all, down_all, spread_ft, act_t, gate_raw, up_raw, 8
+    d_ffn, dw_gateup, dw_down, result = ffn_backward(
+        d_down.astype(LOW),
+        gateup_all,
+        down_all,
+        spread_ft,
+        act_t,
+        gate_raw,
+        up_raw,
+        [
+            Swap(
+                result,
+                (half_tok, width_a),
+                lambda ref, q: ref.at[:, columns_of(q, width_a)],
+                lambda ref, at: ref.at[columns_of(at, share)],
+            )
+        ],
+        8,
     )
     g_gateup = lax.psum_scatter(dw_gateup, "dp", scatter_dimension=0)
-    g_down = lax.psum_scatter(
-        dw_down.reshape(data_n, data_n, ff_part, -1), "dp", scatter_dimension=0
-    )
     d_mix, gain_grads[3] = whole_norm_backward(mixture, scale_f, gains[3], d_ffn)
     d_half = (d_out + d_mix) * HALF_ROOT
     d_proj, gain_grads[2] = whole_norm_backward(projected, scale_p, gains[2], d_half)
-    spread_p, result = transfers(
+    (spread_p,) = transfers(
         [
             Line(
                 d_proj.astype(LOW),
                 (cols_n, rows_n, share, width),
                 lambda ref, c, r: ref.at[c, r],
                 True,
-            ),
-            Swap(
-                result,
-                (half_tok, width_a),
-                lambda ref, q: ref.at[:, columns_of(q, width_a)],
-                lambda ref, at: ref.at[columns_of(at, share)],
-            ),
+            )
         ],
         10,
-        50,
+        40,
     )
     spread_p = spread_p.reshape(tokens, width)
     d_right, gain_grads[1] = whole_norm_backward(right_raw, scale_r, gains[1], d_half)
     d_right = d_right.astype(LOW)
     dw_right = inner_rows(middle, d_right)
     d_middle = against(d_right, right_w).astype(LOW)
-    dw_left = inner_rows(hidden_low, d_middle)
-    d_hidden_share = d_half + against(d_middle, left_w)
+    dw_left = inner_rows(d_middle, hidden_low)
+    d_hidden_share = d_half + flat_dot(d_middle, left_t)
     inner_share = jnp.sum(d_hidden_share * gains[0] * inputs, axis=1)
-    half_low, share_low = d_half.astype(LOW), d_hidden_share.astype(LOW)
     d_attended = against(spread_p, attend_w).astype(LOW)
     dw_attend = inner_rows(attended, spread_p).astype(LOW)
-    d_queries, d_keys, d_values = head_backward(queries, keys, values, d_attended, spans)
+    d_queries, d_keys, d_values, half_here, middle_here = head_backward(
+        queries,
+        keys,
+        values,
+        d_attended,
+        spans,
+        [
+            Swap(
+                d_half.astype(LOW),
+                (half_tok, width_a),
+                lambda ref, q: ref.at[:, columns_of(q, width_a)],
+                lambda ref, at: ref.at[columns_of(at, share)],
+            ),
+            Line(
+                d_middle, (half_tok, d_middle.shape[1]), lambda ref, c, r: ref.at[columns_of(r, share)]
+            ),
+        ],
+        4,
+    )
+
+    d_queries, dw_down, dw_attend, g_gateup = lax.optimization_barrier(
+        (d_queries, dw_down, dw_attend, g_gateup)
+    )
+    g_down = lax.psum_scatter(
+        dw_down.reshape(data_n, data_n, ff_part, -1), "dp", scatter_dimension=0
+    )
+    g_attend = lax.psum_scatter(
+        dw_attend.reshape(HEAD_WIDTH, rows_n, data_n, out_cols)
+        .transpose(2, 0, 1, 3)
+        .reshape(data_n, HEAD_WIDTH, -1),
+        "dp",
+        scatter_dimension=0,
+    )
+
+    def to_shards(grad):
+        return grad.astype(LOW).reshape(cols_n, -1, rows_n, width_a).transpose(0, 2, 1, 3)
+
+    small_parts = jnp.concatenate(
+        [to_shards(grad) for grad in (dw_left, dw_right, dw_pergate, dw_perproj)], axis=2
+    )
+    small_parts = line_reduce(small_parts, 17, True, 28).astype(LOW)
     kv_parts = jnp.concatenate(
         [
             d_keys.astype(LOW).reshape(rows_n, quarter, HEAD_WIDTH),
@@ -1878,7 +2005,20 @@
     )
     d_v_raw, _ = whole_norm_backward(value_raw, value_scale, 1.0, d_kv[quarter:])
     d_raw = jnp.concatenate([d_q_raw, d_k_raw, d_v_raw], axis=0).astype(LOW)
-    spread_q = line_gather(d_raw, 12, False, 55)
+    gateup_squares = jnp.sum(jnp.square(g_gateup.astype(FULL)))
+    spread_q, g_gateup = transfers(
+        [
+            Line(d_raw, (rows_n,) + d_raw.shape, lambda ref, c, r: ref.at[r]),
+            Swap(
+                g_gateup,
+                w_gateup.shape,
+                lambda ref, q: ref.at[:, columns_of(q, width_a), :],
+                lambda ref, at: ref.at[:, :, columns_of(at, ff_part)],
+            ),
+        ],
+        12,
+        100,
+    )
     d_q_all = spread_q[:, :tokens]
     d_k_all = spread_q[:, tokens : tokens + quarter].reshape(tokens, HEAD_WIDTH)
     d_v_all = spread_q[:, tokens + quarter :].reshape(tokens, HEAD_WIDTH)
@@ -1887,7 +2027,7 @@
         d_hidden = d_hidden + against(d_q_all[k], query_w[k])
     acts = activations.astype(FULL)
     gains_here = lax.dynamic_slice_in_dim(w_gains, 0, 1, 0)[0]
-    scale_here = lax.dynamic_slice_in_dim(whole_scale, column * half_tok, half_tok, 0)
+    scale_here = lax.dynamic_slice_in_dim(whole_scale[:, :1], column * half_tok, half_tok, 0)
     own_acts = lax.dynamic_slice_in_dim(whole_acts, me * width_a, width_a, 1).astype(FULL)
     inner = jnp.sum(d_hidden * gains_here * own_acts, axis=1)
     inner = lax.dynamic_update_slice_in_dim(
@@ -1899,42 +2039,30 @@
     dw_kv = jnp.stack(
         [inner_rows(spread_h, d_k_all).astype(LOW), inner_rows(spread_h, d_v_all).astype(LOW)]
     )
-    g_attend = lax.psum_scatter(
-        dw_attend.reshape(HEAD_WIDTH, rows_n, data_n, out_cols).transpose(2, 0, 1, 3).reshape(data_n, HEAD_WIDTH, -1),
-        "dp",
-        scatter_dimension=0,
-    )
-
-    def to_shards(grad, rows_first):
-        if rows_first:
-            cut = grad.reshape(rows_n, width_a, cols_n, data_n, -1).transpose(2, 0, 3, 1, 4)
+    cuts = []
+    start = 0
+    for rows, by_rows in (
+        (data_n * left_cols, True),
+        (right_rows, False),
+        (data_n * gate_cols, True),
+        (proj_rows, False),
+    ):
+        cut = small_parts[start : start + rows]
+        start += rows
+        if by_rows:
+            cut = cut.reshape(data_n, -1, width_a)
+            cut = [cut[:, :, k * out_cols : (k + 1) * out_cols] for k in range(data_n)]
+            cuts.append(jnp.concatenate(cut, axis=1))
         else:
-            cut = grad.reshape(cols_n, -1, rows_n, data_n, out_cols).transpose(0, 2, 3, 1, 4)
-        return cut.astype(LOW).reshape(cols_n, rows_n, data_n, -1)
-
-    flat_grads = jnp.concatenate(
+            cuts.append(jnp.stack([cut[:, k * out_cols : (k + 1) * out_cols] for k in range(data_n)]))
+    squares = gateup_squares
+    for gradient in (g_attend, g_down):
+        squares = squares + jnp.sum(jnp.square(gradient.astype(FULL)))
+    g_query, g_keyval, flat_grads, g_down, g_attend, d_hidden, inner = shard_total(
+        dw_query,
+        dw_kv,
+        jnp.concatenate(cuts, axis=1),
         [
-            to_shards(dw_left, True),
-            to_shards(dw_right, False),
-            to_shards(dw_pergate, True),
-            to_shards(dw_perproj, False),
-        ],
-        axis=3,
-    ).reshape(cols_n, rows_n, data_n * flat_rows, 128)
-    flat_grads = line_reduce(flat_grads, 17, True, 28).astype(LOW).reshape(data_n, flat_rows, 128)
-    g_query, g_keyval, flat_grads = shard_total(dw_query, dw_kv, flat_grads, 13)
-    squares = jnp.where(column == 0, jnp.sum(g_keyval * g_keyval), 0.0)
-    for gradient in (g_query, g_attend, g_gateup, g_down, flat_grads):
-        gradient = gradient.astype(FULL)
-        squares = squares + jnp.sum(gradient * gradient)
-    g_gateup, g_down, g_attend, half_here, share_here, d_hidden, inner = transfers(
-        [
-            Swap(
-                g_gateup,
-                w_gateup.shape,
-                lambda ref, q: ref.at[:, columns_of(q, width_a), :],
-                lambda ref, at: ref.at[:, :, columns_of(at, ff_part)],
-            ),
             Swap(
                 g_down,
                 (data_n, rows_n, ff_part, out_cols),
@@ -1947,40 +2075,36 @@
                 lambda ref, q: ref.at[:, columns_of(q, out_cols)],
                 lambda ref, at: ref.at[at],
             ),
-            Swap(
-                half_low,
-                (half_tok, width_a),
-                lambda ref, q: ref.at[:, columns_of(q, width_a)],
-                lambda ref, at: ref.at[columns_of(at, share)],
-            ),
-            Swap(
-                share_low,
-                (half_tok, width_a),
-                lambda ref, q: ref.at[:, columns_of(q, width_a)],
-                lambda ref, at: ref.at[columns_of(at, share)],
-            ),
             Pair(d_hidden.astype(LOW).reshape(cols_n, half_tok, width_a)),
             Line(inner, (cols_n, rows_n) + inner.shape, lambda ref, c, r: ref.at[c, r], True),
         ],
-        14,
-        100,
-    )
-    g_gateup = g_gateup.astype(FULL)
-    g_down = g_down.reshape(w_down.shape).astype(FULL)
-    g_attend = g_attend.reshape(w_attend.shape).astype(FULL)
-    flat_grads = flat_grads.reshape(-1)
+        13,
+    )
+    squares = squares + jnp.where(column == 0, jnp.sum(g_keyval * g_keyval), 0.0)
+    squares = squares + jnp.sum(g_query * g_query) + jnp.sum(flat_grads * flat_grads)
+    g_down = g_down.reshape(w_down.shape)
+    g_attend = g_attend.reshape(w_attend.shape)
     small_grads = []
     start = 0
-    for w in smalls:
-        small_grads.append(flat_grads[start : start + w.size].reshape(w.shape))
-        start += w.size
+    for w, by_rows in ((w_left, True), (w_right, False), (w_pergate, True), (w_perproj, False)):
+        rows = w.size // out_cols
+        cut = flat_grads[start : start + rows]
+        start += rows
+        if by_rows:
+            high = rows // data_n
+            cut = [cut[k * high : (k + 1) * high] for k in range(data_n)]
+            cut = jnp.concatenate(cut, axis=1).T
+        small_grads.append(cut)
     g_left, g_right, g_pergate, g_perproj = small_grads
 
     inner = jnp.sum(inner, axis=(0, 1)).reshape(cols_n, half_tok) / MODEL_WIDTH
     inner = lax.dynamic_index_in_dim(inner, column, 0, False)[:, None]
-    d_hidden = d_hidden[0].astype(FULL) + d_hidden[1].astype(FULL) + share_here.astype(FULL)
+    half_here = half_here.astype(FULL)
+    own_left = lax.dynamic_slice_in_dim(left_t, me * width_a, width_a, 1)
+    d_hidden = d_hidden[0].astype(FULL) + d_hidden[1].astype(FULL) + half_here
+    d_hidden = d_hidden + flat_dot(middle_here, own_left)
     grad_input = (
-        half_here.astype(FULL)
+        half_here
         + scale_here * d_hidden * gains_here
         - acts * (scale_here * scale_here * scale_here) * inner
     ).astype(LOW)
@@ -2012,16 +2136,6 @@
             jnp.broadcast_to(logit_row[None], (8, 128)),
         ]
     )
-    small = small_total(small, ("col", "row", "dp"), 8, 15)
-    gain_sum = small[:gain_rows].reshape(6, width)
-    head_sum = small[gain_rows : gain_rows + head_rows].reshape(QUERY_HEADS + 1, HEAD_WIDTH)
-    logit_top = small[-1, :QUERY_HEADS]
-    g_gains = lax.dynamic_slice_in_dim(gain_sum, me * width_a, width_a, 1)
-    squares = small[gain_rows + head_rows, 0]
-    squares = squares + jnp.sum(gain_sum * gain_sum) + jnp.sum(head_sum * head_sum)
-    grad_norm = jnp.sqrt(squares)
-    clip_scale = CLIP / jnp.maximum(grad_norm, CLIP)
-    scale_factors = LOGIT_CAP / jnp.maximum(logit_top, LOGIT_CAP)
     weights = (
         w_query,
         key_value_weight,
@@ -2032,8 +2146,6 @@
         w_right,
         w_pergate,
         w_perproj,
-        w_gains,
-        w_heads,
     )
     moments = (
         m_query,
@@ -2045,8 +2157,6 @@
         m_right,
         m_pergate,
         m_perproj,
-        m_gains,
-        m_heads,
     )
     seconds = (
         v_query,
@@ -2058,8 +2168,6 @@
         v_right,
         v_pergate,
         v_perproj,
-        v_gains,
-        v_heads,
     )
     gradients = (
         g_query,
@@ -2071,61 +2179,48 @@
         g_right,
         g_pergate,
         g_perproj,
-        g_gains,
-        head_sum,
-    )
-    step_rates = (
-        MODEL_WIDTH ** (-0.5),
-        MODEL_WIDTH ** (-0.5),
-        (QUERY_HEADS * HEAD_WIDTH) ** (-0.5),
-        MODEL_WIDTH ** (-0.5),
-        FF ** (-0.5),
-        MODEL_WIDTH ** (-0.5),
-        RANK ** (-0.5),
-        MODEL_WIDTH ** (-0.5),
-        PLD ** (-0.5),
-        GAIN_RATE,
-        HEAD_RATE,
-    )
-    decays = (DECAY, DECAY, DECAY, DECAY, DECAY, DECAY, DECAY, DECAY, DECAY, 0.0, 0.0)
-    updated = [
-        adamw_step(
-            weights[k], moments[k], seconds[k], gradients[k] * clip_scale, step_rates[k], decays[k]
+    )
+    fan_ins = (
+        MODEL_WIDTH,
+        MODEL_WIDTH,
+        QUERY_HEADS * HEAD_WIDTH,
+        MODEL_WIDTH,
+        FF,
+        MODEL_WIDTH,
+        RANK,
+        MODEL_WIDTH,
+        PLD,
+    )
+    kinds = ("query", "keyval") + (None,) * 7
+    order = (3, 4, 0, 1, 2, 5, 6, 7, 8)
+    groups = [
+        tuple(
+            array.reshape(-1, array.shape[-1])
+            for array in (weights[k], moments[k], seconds[k], gradients[k])
         )
-        for k in range(11)
+        + (fan_ins[k] ** (-0.5), kinds[k])
+        for k in order
     ]
-    head_scale = jnp.sqrt(scale_factors)
-    q_width = w_query.shape[1]
-    q_head = (
-        (column * data_n + data_at) * q_width + jnp.arange(q_width, dtype=jnp.int32)
-    ) // HEAD_WIDTH
-    q_factor = jnp.sum(
-        jnp.where(
-            q_head[:, None] == jnp.arange(QUERY_HEADS, dtype=jnp.int32)[None, :],
-            head_scale[None, :],
-            0.0,
-        ),
-        axis=1,
-    )
-    new_query = updated[0][2] * q_factor[None, :]
-    kv_width = key_value_weight.shape[1]
-    key_value_index = data_at * kv_width + jnp.arange(kv_width, dtype=jnp.int32)
-    key_value_scale = jnp.sqrt(
-        jnp.min(scale_factors.reshape(KEY_VALUE_HEADS, QUERY_HEADS // KEY_VALUE_HEADS), axis=1)
-    )
-    key_value_choice = jnp.sum(
-        jnp.where(
-            (key_value_index // HEAD_WIDTH)[:, None]
-            == jnp.arange(KEY_VALUE_HEADS, dtype=jnp.int32)[None, :],
-            key_value_scale[None, :],
-            0.0,
-        ),
-        axis=1,
-    )
-    key_value_factor = jnp.where(
-        key_value_index < KEY_VALUE_HEADS * HEAD_WIDTH, key_value_choice, 1.0
-    )
-    new_keyval = updated[1][2] * key_value_factor[None, :]
+    small, *stepped = finish_step(small, gain_rows + head_rows, groups, 15)
+    updated = [None] * 9
+    for at, k in enumerate(order):
+        updated[k] = [array.reshape(weights[k].shape) for array in stepped[3 * at : 3 * at + 3]]
+    gain_sum = small[:gain_rows].reshape(6, width)
+    head_sum = small[gain_rows : gain_rows + head_rows].reshape(QUERY_HEADS + 1, HEAD_WIDTH)
+    logit_top = small[-1, :QUERY_HEADS]
+    g_gains = lax.dynamic_slice_in_dim(gain_sum, me * width_a, width_a, 1)
+    squares = small[gain_rows + head_rows, 0]
+    squares = squares + jnp.sum(gain_sum * gain_sum) + jnp.sum(head_sum * head_sum)
+    grad_norm = jnp.sqrt(squares)
+    clip_scale = CLIP / jnp.maximum(grad_norm, CLIP)
+    scale_factors = LOGIT_CAP / jnp.maximum(logit_top, LOGIT_CAP)
+    updated.append(
+        adamw_step(w_gains, m_gains, v_gains, g_gains * clip_scale, GAIN_RATE, 0.0)
+    )
+    updated.append(
+        adamw_step(w_heads, m_heads, v_heads, head_sum * clip_scale, HEAD_RATE, 0.0)
+    )
+    new_query, new_keyval = updated[0][2], updated[1][2]
     return (
         result,
         grad_input,

time: 1050 us -> 955 us (0.910)
  other arithmetic: 94.6 us -> 55.4 us
  local copies, waits for them, and re-layouts: 133 us -> 94.3 us
    pallas_call x8 -> x7, Pallas kernels: 452 us -> 404 us  [the longest x4 304 us: transfers(): pl.pallas_call(kernel, out_shape=bundle.shapes, in_specs=bundle.specs, ou...]
    reshape x14 -> x6, local copies, waits for them, and re-layouts: 35.9 us -> 8.64 us  [the longest x4 6.39 us: to_shards(): grad.astype(LOW).reshape(cols_n, -1, rows_n, width_a).transpose(0, 2, 1, 3)]
    unnamed x260 -> x300, local copies, waits for them, and re-layouts: 45.8 us -> 65.4 us
    pallas_call x1, Pallas kernels: 92.2 us -> 112 us  [ffn_forward(): pl.pallas_call(kernel, out_shape=[jax.ShapeDtypeStruct((share, width), FU...]
    sub x9 -> x2, other arithmetic: 20.5 us -> 1.27 us  [adamw_step(): weight - rate * (mean_step / (jnp.sqrt(spread) + ADAM_EPS) + decay * weight)]
    convert_element_type x8 -> x0, local copies, waits for them, and re-layouts: 13.1 us -> none  [the longest x6 12.8 us: to_shards(): return cut.astype(LOW).reshape(cols_n, rows_n, data_n, -1)]
    pallas_call x1, Pallas kernels: 24.8 us -> 37.3 us  [shard_total(): pl.pallas_call(kernel, out_shape=[jax.ShapeDtypeStruct(shape, FULL) for s...]
  transfers between devices with their start and end apart: 5 -> 5, of which waited for: 0 -> 0; matrix products, arithmetic and copies ran while one was open for 15% -> 9% of each run, Pallas kernels for 29% -> 39%
where the time goes in v4:
time: 955 us; the launch traced here: 945 us
  Pallas kernels  740 us (77%)
  local copies, waits for them, and re-layouts  94.3 us (10%)
  other arithmetic  55.4 us (6%)
  matrix products  31.8 us (3%)
  between operations  22.8 us (2%)
    pallas_call x4, Pallas kernels, transfers(): pl.pallas_call(kernel, out_shape=bundle.shapes, in_specs=bundle.specs, ou...  304 us
    pallas_call x1, Pallas kernels, ffn_forward(): pl.pallas_call(kernel, out_shape=[jax.ShapeDtypeStruct((share, width), FU...  112 us
    pallas_call x1, Pallas kernels, ffn_backward(): pl.pallas_call(kernel, out_shape=[jax.ShapeDtypeStruct((share, width), FU...  96.5 us
    pallas_call x3, Pallas kernels, line_reduce(): pl.pallas_call(kernel, out_shape=jax.ShapeDtypeStruct((high, wide), FULL)...  90.9 us
    unnamed x300, local copies, waits for them, and re-layouts  65.4 us
    pallas_call x1, Pallas kernels, attention_forward_head(): pl.pallas_call(kernel, out_shape=[jax.ShapeDtypeStruct((tokens, width), L...  46.4 us
    pallas_call x1, Pallas kernels, shard_total(): pl.pallas_call(kernel, out_shape=[jax.ShapeDtypeStruct(shape, FULL) for s...  37.3 us
    pallas_call x1, Pallas kernels, finish_step(): pl.pallas_call(kernel, out_shape=[jax.ShapeDtypeStruct(small.shape, FULL)...  30.9 us
  transfers between devices with their start and end apart: 5, of which 0 were waited for; matrix products, arithmetic and copies ran while one was open for 9% of the time, Pallas kernels for 39%

profile of v4, /device:TPU:0, one launch (start us, length us, event | category | flops | bytes accessed | tf_op | source)
XLA Modules:
  0.0 945.0 jit_solution(13732306567234995363)
XLA Ops:
  7.4 2.6 convert_element_type.195.refs_1_
  11.0 94.0 %shard_map.645 = (bf16[1024,2048]{1,0:T(8,128)(2,1)S(1)}, bf16[2,2048,256]{2,1,0:T(8,128)(2,1)S(1)}, bf16[256,512]{1,0:T(8,128)(2,1)S(1)}, bf16[4,512,512]{2,1,0...) custom-call(bf16[512,512]{1,0:T(8,128)(2,1)S(1)} %copy-done.24, ...), custom_call_target="tpu_custom_call" | custom-call | bytes 270000000 | tf_op jit(solution)/shard_map/pallas_call | solution.py:724
  105.0 2.0 copy-done.2
  110.7 2.7 convert_element_type.204
  114.4 66.7 %shard_map.646 = (bf16[2,2048,256]{2,1,0:T(8,128)(2,1)S(1)}, bf16[2048,256]{1,0:T(8,128)(2,1)S(1)}, f32[6,2048]{1,0:T(8,128)S(1)}, bf16[1024,256]{1,0:T(8,128)(2,1)S(1)}, bf16[4,256,512]{2,1,0:T(8,128)(2,1)S(1)}) custom-call(bf16[2,512,256]{2,1,0:T(8,128)(2,1)S(1)} %pad_maximum_fusion.6.refs_0_, bf16[4,512,256]{2,1,0:T(8,128)(2,1)S(1)} %get-tuple-element.368.refs_1_, ...), custom_call_target="tpu_custom_call" | custom-call | bytes 180000000 | tf_op jit(solution)/shard_map/pallas_call | solution.py:724
  184.7 1.9 multiply_sine_fusion
  186.6 46.4 %shard_map.647 = (bf16[1024,2048]{1,0:T(8,128)(2,1)}, f32[1024,128]{1,0:T(8,128)S(1)}, f32[1024,256]{1,0:T(8,128)S(1)}, f32[1024,256]{1,0:T(8,128)}, f32[1024,25...) custom-call(s32[3]{0:T(128)S(1)} %pad_add_fusion.spans_ref, ...), custom_call_target="tpu_custom_call" | custom-call | bytes 120000000 | tf_op jit(solution)/shard_map/pallas_call | solution.py:1547
  241.5 41.4 %shard_map.648 = f32[128,2048]{1,0:T(8,128)S(1)} custom-call(bf16[2,4,128,2048]{3,2,1,0:T(8,128)(2,1)S(1)} %bitcast.175), custom_call_target="tpu_custom_call" | custom-call | bytes 135000000 | tf_op jit(solution)/shard_map/pallas_call | solution.py:442
  287.2 1.7 multiply_reduce_fusion.16
  290.0 111.6 %shard_map.649 = (f32[128,2048]{1,0:T(8,128)}, bf16[2048,1024]{1,0:T(8,128)(2,1)}, bf16[1024,1024]{1,0:T(8,128)(2,1)}, f32[4,256,1024]{2,1,0:T(8,128)}, f32[4,25...) custom-call(bf16[128,2048]{1,0:T(8,128)(2,1)} %multiply_convert_fusion.x_ref, ...), custom_call_target="tpu_custom_call" | custom-call | bytes 240000000 | tf_op jit(solution)/shard_map/pallas_call | solution.py:1160
  412.2 96.5 %shard_map.650 = (f32[128,2048]{1,0:T(8,128)}, bf16[4,2,2048,256]{3,2,1,0:T(8,128)(2,1)}, bf16[4,1024,512]{2,1,0:T(8,128)(2,1)}, bf16[512,512]{1,0:T(8,128)(2,1)}) custom-call(bf16[128,2048]{1,0:T(8,128)(2,1)} %subtract_convert_fusion.3.x_ref, bf16[4,2,2048,256]{3,2,1,0:T(8,128)(2,1)} %bitcast.197, bf16[4,1024,512]{2,1,0:T(8,128)(2,1)} %bitcast.199, ...), custom_call_target="tpu_custom_call" | custom-call | bytes 270000000 | tf_op jit(solution)/shard_map/pallas_call | solution.py:1336
  517.5 1.8 dynamic-slice_reduce_fusion
  520.1 2.5 multiply_reduce_fusion.5
  525.0 41.2 %shard_map.651 = bf16[2,4,128,2048]{3,2,1,0:T(8,128)(2,1)S(1)} custom-call(bf16[128,2048]{1,0:T(8,128)(2,1)S(1)} %get-tuple-element.378.refs_0_), custom_call_target="tpu_custom_call" | custom-call | bytes 120000000 | tf_op jit(solution)/shard_map/pallas_call | solution.py:724
  569.0 23.0 %shard_map.652 = (f32[1024,256]{1,0:T(8,128)S(1)}, f32[1024,256]{1,0:T(8,128)S(1)}, f32[1024,256]{1,0:T(8,128)}, bf16[512,512]{1,0:T(8,128)(2,1)S(1)}, bf16[512,64]{1,0:T(8,128)(2,1)S(1)}) custom-call(s32[3]{0:T(128)S(1)} %pad_add_fusion.spans_ref, bf16[1024,256]{1,0:T(8,128)(2,1)S(1)} %copy-done.27, bf16[1024,256]{1,0:T(8,128)(2,1)S(1)} %copy-done.29, ...), custom_call_target="tpu_custom_call" | custom-call | bytes 75000000 | tf_op jit(solution)/shard_map/pallas_call | solution.py:1604
  592.2 1.8 convert_element_type.226
  594.1 17.9 %shard_map.653 = f32[512,256]{1,0:T(8,128)S(1)} custom-call(bf16[4,512,256]{2,1,0:T(8,128)(2,1)S(1)} %pad_maximum_fusion.2.x_ref), custom_call_target="tpu_custom_call" | custom-call | bytes 60000000 | tf_op jit(solution)/shard_map/pallas_call | solution.py:442
  614.8 2.7 convolution_convert_fusion.2
  617.5 2.6 reshape.401
  620.1 2.5 convolution_convert_fusion.1
  622.6 2.7 reshape.402
  625.3 3.5 copy_bitcast_fusion
  628.7 2.3 convolution_convert_fusion.3
  631.0 2.6 reshape.406
  633.6 2.6 copy.130
  636.2 2.2 reshape.407
  638.6 1.7 pad_maximum_fusion.x_ref
  640.3 31.6 %shard_map.655 = f32[320,512]{1,0:T(8,128)S(1)} custom-call(bf16[2,4,320,512]{3,2,1,0:T(8,128)(2,1)S(1)} %pad_maximum_fusion.x_ref), custom_call_target="tpu_custom_call" | custom-call | bytes 84000000 | tf_op jit(solution)/shard_map/pallas_call | solution.py:442
  673.5 2.3 fusion.4
  676.8 1.9 multiply_reduce_fusion.22
  679.6 2.3 multiply_subtract_fusion
  683.4 1.7 subtract_convert_fusion
  686.3 101.9 %shard_map.654 = (bf16[4,1536,256]{2,1,0:T(8,128)(2,1)S(1)}, bf16[2,512,1024]{2,1,0:T(8,128)(2,1)S(1)}) custom-call(bf16[1536,256]{1,0:T(8,128)(2,1)S(1)} %pad_maximum_fusion.4.refs_0_, bf16[2,2048,256]{2,1,0:T(8,128)(2,1)S(1)} %bitcast.176), custom_call_target="tpu_custom_call" | custom-call | bytes 300000000 | tf_op jit(solution)/shard_map/pallas_call | solution.py:724
  795.6 3.2 multiply_reduce_fusion.2
  798.9 1.7 multiply_reduce_fusion
  800.6 1.7 multiply_reduce_fusion.21
  805.6 37.3 %shard_map.656 = (f32[512,256]{1,0:T(8,128)S(1)}, f32[512,256]{1,0:T(8,128)S(1)}, f32[320,128]{1,0:T(8,128)S(1)}, bf16[4,4,256,128]{3,2,1,0:T(8,128)(2,1)S(1)}, ...) custom-call(bf16[4,512,256]{2,1,0:T(8,128)(2,1)S(1)} %pad_maximum_fusion.3.q_ref, ...), custom_call_target="tpu_custom_call" | custom-call | bytes 120000000 | tf_op jit(solution)/shard_map/pallas_call | solution.py:818
  850.8 2.9 fusion.18
  858.5 30.9 %shard_map.657 = (f32[128,128]{1,0:T(8,128)}, f32[1024,1024]{1,0:T(8,128)}, f32[1024,1024]{1,0:T(8,128)}, f32[1024,1024]{1,0:T(8,128)}, f32[4096,128]{1,0:T(8,12...) custom-call(f32[128,128]{1,0:T(8,128)} %pad_maximum_fusion.9.x_ref, ...), custom_call_target="tpu_custom_call" | custom-call | bytes 75000000 | tf_op jit(solution)/shard_map/pallas_call | solution.py:1462
  897.4 1.7 copy.142
  899.2 1.7 copy.143
  900.8 1.7 copy.144
  902.5 1.7 copy.139
  904.2 1.7 copy.140
  905.9 1.7 copy.141
  916.8 2.1 copy.196
  920.5 2.1 copy.197
  924.2 2.1 copy.198
  (442 shorter events, 105.4 us)
Async XLA Ops:
  7.2 103.3 %copy-start = (s32[4,2]{0,1:T(2,128)S(1)}, s32[4,2]{0,1:T(2,128)}, u32[]{:S(2)}) copy-start(s32[4,2]{0,1:T(2,128)} %param.44) | copy-start | bytes 100
  7.3 229.9 %all-gather.5.cloned.1.call-start = ((), (), s32[]{:S(2)}) async-start(), calls=%async_computation.3 | async-start | bytes 10485760 | tf_op jit(solution)/shard_map/all_gather | solution.py:1761
  10.2 99.5 %copy-start.128 = (s32[4]{0:T(128)S(1)}, s32[4]{0:T(128)}, u32[]{:S(2)}) copy-start(s32[4]{0:T(128)} %param.43) | copy-start | bytes 52
  109.7 180.3 %all-gather.7.cloned.1.call-start = ((), (), s32[]{:S(2)}) async-start(), calls=%async_computation.4 | async-start | bytes 5242880 | tf_op jit(solution)/shard_map/all_gather | solution.py:1850
  237.2 47.2 %copy-start.33 = (bf16[64,2048]{1,0:T(8,128)(2,1)}, bf16[64,2048]{1,0:T(8,128)(2,1)S(1)}, u32[]{:S(2)}) copy-start(bf16[64,2048]{1,0:T(8,128)(2,1)S(1)} %get-tuple-element.145) | copy-start | bytes 786436
  237.2 393.8 %reduce-scatter.10.cloned.1.call-start = ((), (), s32[]{:S(2)}) async-start(), calls=%async_computation.5 | async-start | bytes 10485760
  288.9 114.3 %copy-start.46 = (f32[128,2048]{1,0:T(8,128)}, f32[128,2048]{1,0:T(8,128)S(1)}, u32[]{:S(2)}) copy-start(f32[128,2048]{1,0:T(8,128)S(1)} %get-tuple-element.363) | copy-start | bytes 3145732
  508.7 5.4 copy-start.100
  508.7 10.5 %copy-start.4 = (f32[1024,256]{1,0:T(8,128)S(1)}, f32[1024,256]{1,0:T(8,128)}, u32[]{:S(2)}) copy-start(f32[1024,256]{1,0:T(8,128)} %copy-done.3) | copy-start | bytes 3145732
  508.8 291.8 %reduce-scatter.14.cloned.1.call-start = ((), (), s32[]{:S(2)}) async-start(), calls=%async_computation.7 | async-start | bytes 1310720
  514.9 7.7 copy-start.47
  514.9 7.7 copy-start.54
  514.9 7.7 copy-start.67
  524.9 42.9 %copy-start.57 = (bf16[128,2048]{1,0:T(8,128)(2,1)}, bf16[128,2048]{1,0:T(8,128)(2,1)S(1)}, u32[]{:S(2)}) copy-start(bf16[128,2048]{1,0:T(8,128)(2,1)S(1)} %get-tuple-element.377) | copy-start | bytes 1572868
  525.0 41.6 %copy-start.62 = (bf16[4,256,4,128]{1,3,0,2:T(8,128)(2,1)S(1)}, bf16[4,256,4,128]{1,3,0,2:T(8,128)(2,1)}, u32[]{:S(2)}) copy-start(bf16[4,256,4,128]{1,3,0,2:T(8,128)(2,1)} %copy-done.61) | copy-start | bytes 3145732
  592.1 20.0 %copy-start.44 = (bf16[512,64]{1,0:T(8,128)(2,1)}, bf16[512,64]{1,0:T(8,128)(2,1)S(1)}, u32[]{:S(2)}) copy-start(bf16[512,64]{1,0:T(8,128)(2,1)S(1)} %get-tuple-element.184) | copy-start | bytes 196612
  592.1 21.5 %copy-start.58 = (bf16[128,2048]{1,0:T(8,128)(2,1)S(1)}, bf16[128,2048]{1,0:T(8,128)(2,1)}, u32[]{:S(2)}) copy-start(bf16[128,2048]{1,0:T(8,128)(2,1)} %copy-done.57) | copy-start | bytes 1572868
  613.4 6.7 copy-start.82
  622.6 6.2 copy-start.18
  638.5 165.1 %reduce-scatter.12.cloned.1.call-start = ((), (), s32[]{:S(2)}) async-start(), calls=%async_computation.6 | async-start | bytes 5242880
  672.1 7.4 copy-start.21
  672.1 7.4 copy-start.123
  676.8 6.6 copy-start.109
  685.1 103.2 %copy-start.127 = (bf16[1024,2048]{1,0:T(8,128)(2,1)S(1)}, bf16[1024,2048]{1,0:T(8,128)(2,1)}, u32[]{:S(2)}) copy-start(bf16[1024,2048]{1,0:T(8,128)(2,1)} %get-tuple-element.169) | copy-start | bytes 12582916
  805.6 45.2 %copy-start.25 = (bf16[512,512]{1,0:T(8,128)(2,1)S(1)}, bf16[512,512]{1,0:T(8,128)(2,1)}, u32[]{:S(2)}) copy-start(bf16[512,512]{1,0:T(8,128)(2,1)} %refs_0_.2) | copy-start | bytes 1572868
  805.6 45.2 %copy-start.45 = (bf16[512,64]{1,0:T(8,128)(2,1)S(1)}, bf16[512,64]{1,0:T(8,128)(2,1)}, u32[]{:S(2)}) copy-start(bf16[512,64]{1,0:T(8,128)(2,1)} %copy-done.44) | copy-start | bytes 196612
  805.6 45.2 %copy-start.120 = (f32[512]{0:T(512)S(1)}, f32[512]{0:T(512)}, u32[]{:S(2)}) copy-start(f32[512]{0:T(512)} %get-tuple-element.350) | copy-start | bytes 6148
  805.6 45.2 %copy-start.121 = (f32[512]{0:T(512)S(1)}, f32[512]{0:T(512)}, u32[]{:S(2)}) copy-start(f32[512]{0:T(512)} %get-tuple-element.351) | copy-start | bytes 6148
  845.6 8.1 copy-start.15
  845.6 8.1 copy-start.16
  847.6 6.2 copy-start.104
  847.6 6.2 copy-start.105
  847.6 6.2 copy-start.106
  847.6 6.2 copy-start.107
  848.4 5.5 copy-start.60
  850.0 7.7 copy-start.126
  858.4 49.1 %copy-start.108 = (f32[9,256]{1,0:T(8,128)S(1)}, f32[9,256]{1,0:T(8,128)}, u32[]{:S(2)}) copy-start(f32[9,256]{1,0:T(8,128)} %param.75) | copy-start | bytes 27652
  858.4 49.1 %copy-start.112 = (f32[9,256]{1,0:T(8,128)S(1)}, f32[9,256]{1,0:T(8,128)}, u32[]{:S(2)}) copy-start(f32[9,256]{1,0:T(8,128)} %param.77) | copy-start | bytes 27652
  858.4 49.1 %copy-start.113 = (f32[9,256]{1,0:T(8,128)S(1)}, f32[9,256]{1,0:T(8,128)}, u32[]{:S(2)}) copy-start(f32[9,256]{1,0:T(8,128)} %param.76) | copy-start | bytes 27652
  858.5 49.8 %copy-start.114 = (f32[6,512]{1,0:T(8,128)S(1)}, f32[6,512]{1,0:T(8,128)}, u32[]{:S(2)}) copy-start(f32[6,512]{1,0:T(8,128)} %param.74) | copy-start | bytes 36868
  858.5 49.8 %copy-start.115 = (f32[6,512]{1,0:T(8,128)S(1)}, f32[6,512]{1,0:T(8,128)}, u32[]{:S(2)}) copy-start(f32[6,512]{1,0:T(8,128)} %param.73) | copy-start | bytes 36868
  858.5 50.4 %copy-start.84 = (bf16[512,512]{1,0:T(8,128)(2,1)S(1)}, bf16[512,512]{1,0:T(8,128)(2,1)}, u32[]{:S(2)}) copy-start(bf16[512,512]{1,0:T(8,128)(2,1)} %get-tuple-element.474) | copy-start | bytes 1572868
  889.4 20.3 %copy-start.93 = (f32[512,256]{1,0:T(8,128)S(1)}, f32[512,256]{1,0:T(8,128)}, u32[]{:S(2)}) copy-start(f32[512,256]{1,0:T(8,128)} %get-tuple-element.478) | copy-start | bytes 1572868
  889.4 21.1 %copy-start.92 = (f32[512,256]{1,0:T(8,128)S(1)}, f32[512,256]{1,0:T(8,128)}, u32[]{:S(2)}) copy-start(f32[512,256]{1,0:T(8,128)} %get-tuple-element.479) | copy-start | bytes 1572868
  889.4 21.8 %copy-start.91 = (f32[512,256]{1,0:T(8,128)S(1)}, f32[512,256]{1,0:T(8,128)}, u32[]{:S(2)}) copy-start(f32[512,256]{1,0:T(8,128)} %get-tuple-element.480) | copy-start | bytes 1572868
  897.4 14.6 %copy-start.90 = (f32[512,256]{1,0:T(8,128)S(1)}, f32[512,256]{1,0:T(8,128)}, u32[]{:S(2)}) copy-start(f32[512,256]{1,0:T(8,128)} %get-tuple-element.481) | copy-start | bytes 1572868
  902.5 10.3 %copy-start.89 = (f32[512,256]{1,0:T(8,128)S(1)}, f32[512,256]{1,0:T(8,128)}, u32[]{:S(2)}) copy-start(f32[512,256]{1,0:T(8,128)} %get-tuple-element.482) | copy-start | bytes 1572868
  929.7 7.4 copy-start.1
  (86 other events, 200.8 us)
Sparse Core Ops, SparseCore 0:
  109.8 93.4 all-gather.4
  237.4 51.9 all-gather.6
  508.9 86.5 reduce-scatter.9
  638.6 31.6 reduce-scatter.13
  673.1 52.9 reduce-scatter.11

commit v5 on v4

--- a/solution.py
+++ b/solution.py
@@ -457,17 +457,19 @@
 
 
 class Line:
-    def __init__(self, source, shape, place, core=False):
+    def __init__(self, source, shape, place, core=False, view=None):
         self.source, self.shape, self.place, self.core = source, shape, place, core
+        self.view = view
 
     def semaphores(self, count, data):
         dma = pltpu.SemaphoreType.DMA
         return [dma((count,)), dma((count,)), dma((2 * count,))] * 2 + [dma]
 
     def bind(self, x_ref, o_ref, sems, spots, sizes):
-        self.x_ref, self.o_ref, self.sems = x_ref, o_ref, sems
+        self.o_ref, self.sems = o_ref, sems
         self.me, self.column, self.at = spots
         self.count = sizes[0]
+        self.x_ref = self.view(x_ref, self.column) if self.view else x_ref
 
     def slot(self, source):
         return self.place(self.o_ref, self.column, source)
@@ -659,6 +661,206 @@
         self.copy().wait()
 
 
+class Reduce:
+    core = True
+
+    def __init__(self, source):
+        self.source = source
+        self.high, self.wide = source.shape[1], source.shape[2] // lax.axis_size("row")
+        self.shape, self.dtype = (self.high, self.wide), FULL
+
+    def semaphores(self, count, data):
+        dma = pltpu.SemaphoreType.DMA
+        slots = pltpu.VMEM((count, self.high, self.wide), self.source.dtype)
+        whole = pltpu.VMEM(self.source.shape[1:], self.source.dtype)
+        stage = pltpu.VMEM(self.shape, FULL)
+        return [whole, stage, slots, slots, slots, slots] + [dma((count,))] * 6 + [dma, dma]
+
+    def bind(self, x_ref, o_ref, sems, spots, sizes):
+        self.x_ref, self.o_ref = x_ref, o_ref
+        self.mine, self.stage, self.core_in, self.left_in, self.right_in, self.out = sems[:6]
+        self.sems = sems[6:]
+        self.me, self.column = spots[0], spots[1]
+        self.count = sizes[0]
+
+    def cut(self, ref, q):
+        return ref.at[:, pl.ds(pl.multiple_of(q * self.wide, self.wide), self.wide)]
+
+    def beside(self, q):
+        return push(
+            self.cut(self.x_ref.at[1 - self.column], q),
+            self.core_in.at[q],
+            self.sems[0].at[q],
+            self.sems[3].at[q],
+            {"col": 1 - self.column},
+        )
+
+    def to_left(self, q):
+        return push(self.out.at[q], self.left_in.at[q], self.sems[1].at[q], self.sems[4].at[q], {"row": self.me - 1})
+
+    def to_right(self, q):
+        return push(self.out.at[q], self.right_in.at[q], self.sems[2].at[q], self.sems[5].at[q], {"row": self.me + 1})
+
+    def from_right(self, q):
+        return push(self.left_in.at[q], self.left_in.at[q], self.sems[1].at[q], self.sems[4].at[q], {"row": self.me + 1})
+
+    def from_left(self, q):
+        return push(self.right_in.at[q], self.right_in.at[q], self.sems[2].at[q], self.sems[5].at[q], {"row": self.me - 1})
+
+    def own(self):
+        return pltpu.make_async_copy(self.x_ref.at[self.column], self.mine, self.sems[6])
+
+    def start(self):
+        self.own().start()
+        for q in range(self.count):
+            self.beside(q).start()
+
+    def added(self, target, q, others):
+        step = 64
+        cut = self.cut(self.mine, q)
+
+        @pl.loop(0, self.high // step)
+        def _(at):
+            rows = pl.ds(pl.multiple_of(at * step, step), step)
+            total = cut[rows].astype(FULL) + self.core_in[q, rows].astype(FULL)
+            for other in others:
+                total = total + other[q, rows].astype(FULL)
+            target[rows] = total.astype(target.dtype)
+
+    def step(self, k):
+        me, count = self.me, self.count
+        t = k - 1
+        q_left = t - (count - 1 - me)
+        q_right = count - 1 - (t - me)
+
+        @pl.when(t == 0)
+        def _():
+            self.own().wait()
+
+        @pl.when((q_left >= 0) & (q_left < me))
+        def _():
+            self.beside(q_left).wait()
+
+            @pl.when(me < count - 1)
+            def _():
+                self.from_right(q_left).wait_recv()
+                self.added(self.out.at[q_left], q_left, [self.left_in])
+
+            @pl.when(me == count - 1)
+            def _():
+                self.added(self.out.at[q_left], q_left, [])
+
+            self.to_left(q_left).start()
+
+        @pl.when((t >= me) & (q_right > me))
+        def _():
+            self.beside(q_right).wait()
+
+            @pl.when(me > 0)
+            def _():
+                self.from_left(q_right).wait_recv()
+                self.added(self.out.at[q_right], q_right, [self.right_in])
+
+            @pl.when(me == 0)
+            def _():
+                self.added(self.out.at[q_right], q_right, [])
+
+            self.to_right(q_right).start()
+
+    def finish(self):
+        me, count = self.me, self.count
+        self.beside(me).wait()
+
+        @pl.when(me < count - 1)
+        def _():
+            self.from_right(me).wait_recv()
+
+        @pl.when(me > 0)
+        def _():
+            self.from_left(me).wait_recv()
+
+        @pl.when(me == 0)
+        def _():
+            self.added(self.stage, me, [self.left_in])
+
+        @pl.when(me == count - 1)
+        def _():
+            self.added(self.stage, me, [self.right_in])
+
+        @pl.when((me > 0) & (me < count - 1))
+        def _():
+            self.added(self.stage, me, [self.left_in, self.right_in])
+
+        out = pltpu.make_async_copy(self.stage, self.o_ref, self.sems[7])
+        out.start()
+
+        @pl.loop(0, count)
+        def _(q):
+            @pl.when(q < me)
+            def _():
+                self.to_left(q).wait_send()
+
+            @pl.when(q > me)
+            def _():
+                self.to_right(q).wait_send()
+
+        out.wait()
+
+
+class ShardSum:
+    axis = "dp"
+
+    def __init__(self, source, out_cols):
+        self.source, self.out_cols = source, out_cols
+        self.parts = source.shape[1] // out_cols // lax.axis_size("dp")
+        self.shape = (source.shape[0], self.parts * out_cols)
+
+    def semaphores(self, count, data):
+        dma = pltpu.SemaphoreType.DMA
+        buf = pltpu.VMEM((data,) + self.shape, self.source.dtype)
+        stage = pltpu.VMEM(self.shape, self.source.dtype)
+        return [buf, stage, dma((data, self.parts)), dma((data, self.parts)), dma]
+
+    def bind(self, x_ref, o_ref, sems, spots, sizes):
+        self.x_ref, self.o_ref = x_ref, o_ref
+        self.buf, self.stage, self.send, self.recv, self.local = sems
+        self.at, self.data = spots[2], sizes[1]
+
+    def copy(self, k, s):
+        target = lax.rem(self.at + k, self.data)
+        wide = self.out_cols
+        source = self.x_ref.at[:, pl.ds(pl.multiple_of((s * self.data + target) * wide, wide), wide)]
+        slot = self.buf.at[k, :, pl.ds(s * wide, wide)]
+        if k == 0:
+            return pltpu.make_async_copy(source, slot, self.send.at[k, s])
+        return push(source, slot, self.send.at[k, s], self.recv.at[k, s], {"dp": target})
+
+    def start(self):
+        for k in range(self.data):
+            for s in range(self.parts):
+                self.copy(k, s).start()
+
+    def step(self, k):
+        pass
+
+    def finish(self):
+        for k in range(self.data):
+            for s in range(self.parts):
+                self.copy(k, s).wait()
+
+        @pl.loop(0, self.shape[0] // 64)
+        def _(at):
+            rows = pl.ds(pl.multiple_of(at * 64, 64), 64)
+            total = self.buf[0, rows].astype(FULL)
+            for k in range(1, self.data):
+                total = total + self.buf[k, rows].astype(FULL)
+            self.stage[rows] = total.astype(self.stage.dtype)
+
+        out = pltpu.make_async_copy(self.stage, self.o_ref, self.local)
+        out.start()
+        out.wait()
+
+
 class Bundle:
     def __init__(self, items):
         self.items = items
@@ -668,7 +870,9 @@
         self.across = any(getattr(item, "axis", None) == "dp" for item in items)
         self.cores = any(getattr(item, "core", False) for item in items)
         self.sources = [item.source for item in items]
-        self.shapes = [jax.ShapeDtypeStruct(item.shape, item.source.dtype) for item in items]
+        self.shapes = [
+            jax.ShapeDtypeStruct(item.shape, getattr(item, "dtype", item.source.dtype)) for item in items
+        ]
         self.specs = [pl.BlockSpec(memory_space=pl.ANY)] * self.number
         self.scratch = sum(self.kinds, [])
 
@@ -1365,26 +1569,13 @@
     )(block, gateup, down, xt, at, gate, up, *bundle.sources)
 
 
-def finish_step(small, sum_rows, groups, ident):
+def last_sums(small, ident):
     axes = ("col", "row", "dp")
     sizes = [lax.axis_size(axis) for axis in axes]
     high = small.shape[0]
-    number = len(groups)
-    arrays = [array for group in groups for array in group[:4]]
-
-    def kernel(x_ref, *refs):
-        sources, refs = refs[: 4 * number], refs[4 * number :]
-        o_ref, outs, refs = refs[0], refs[1 : 1 + 3 * number], refs[1 + 3 * number :]
-        held, refs = refs[: 4 * number], refs[4 * number :]
-        load_sem, store_sem, refs = refs[0], refs[1], refs[2:]
+
+    def kernel(x_ref, o_ref, *refs):
         slots, sends, recvs = (refs[k::3] for k in range(3))
-
-        def load(k):
-            return pltpu.make_async_copy(sources[k], held[k], load_sem.at[k])
-
-        def store(group, k):
-            return pltpu.make_async_copy(held[4 * group + (1, 2, 0)[k]], outs[3 * group + k], store_sem.at[3 * group + k])
-
         spots = [lax.axis_index(axis) for axis in axes]
         barrier = pltpu.get_barrier_semaphore()
         for axis, size, me in zip(axes, sizes, spots):
@@ -1392,8 +1583,6 @@
                 pl.semaphore_signal(
                     barrier, inc=1, device_id={axis: lax.rem(me + k, size)}, device_id_type=MESH
                 )
-        for k in range(4 * number):
-            load(k).start()
         pl.semaphore_wait(barrier, sum(sizes) - len(sizes))
         for at, (axis, size, me) in enumerate(zip(axes, sizes, spots)):
             buf, send, recv = slots[at], sends[at], recvs[at]
@@ -1410,13 +1599,68 @@
                 top = jnp.maximum(top, buf[k, high - 8 :])
             o_ref[...] = total
             o_ref[high - 8 :] = top
-        sums = o_ref[:sum_rows]
+
+    dma = pltpu.SemaphoreType.DMA
+    vmem = pl.BlockSpec(memory_space=pltpu.VMEM)
+    scratch = []
+    for size in sizes:
+        scratch += [pltpu.VMEM((size,) + small.shape, FULL), dma((size,)), dma((size,))]
+    return pl.pallas_call(
+        kernel,
+        out_shape=jax.ShapeDtypeStruct(small.shape, FULL),
+        in_specs=[vmem],
+        out_specs=vmem,
+        scratch_shapes=scratch,
+        compiler_params=params(ident, 16),
+        cost_estimate=cost(14),
+    )(small)
+
+
+def adam_all(small, sum_rows, groups):
+    high = small.shape[0]
+    number = len(groups)
+    arrays = [array for group in groups for array in group[:4]]
+    cuts = []
+    for group in range(number):
+        rows, cols = arrays[4 * group].shape
+        pieces = max(1, rows * cols // 262144)
+        cuts += [(group, piece, rows // pieces) for piece in range(pieces)]
+
+    def kernel(x_ref, *refs):
+        sources, refs = refs[: 4 * number], refs[4 * number :]
+        info_ref, outs, refs = refs[0], refs[1 : 1 + 3 * number], refs[1 + 3 * number :]
+        held, load_sem, store_sem = refs[: 4 * number], refs[4 * number], refs[4 * number + 1]
+
+        def rows_of(at):
+            group, piece, rows = cuts[at]
+            return pl.ds(piece * rows, rows) if rows < arrays[4 * group].shape[0] else slice(None)
+
+        def load(at, k):
+            here, array = rows_of(at), 4 * cuts[at][0] + k
+            return pltpu.make_async_copy(
+                sources[array].at[here], held[array].at[here], load_sem.at[at, k]
+            )
+
+        def store(at, k):
+            here, group = rows_of(at), cuts[at][0]
+            return pltpu.make_async_copy(
+                held[4 * group + (1, 2, 0)[k]].at[here], outs[3 * group + k].at[here], store_sem.at[at, k]
+            )
+
+        for at in range(len(cuts)):
+            for k in range(4):
+                load(at, k).start()
+        column, data_at = lax.axis_index("col"), lax.axis_index("dp")
+        sums = x_ref[:sum_rows]
         squares = jnp.sum(jnp.sum(sums * sums, axis=1, keepdims=True), axis=0, keepdims=True)
-        squares = squares + o_ref[sum_rows : sum_rows + 1, :1]
-        clip = CLIP / jnp.maximum(jnp.sqrt(squares), CLIP)
-        tops = o_ref[high - 1 :]
+        squares = squares + x_ref[sum_rows : sum_rows + 1, :1]
+        norm = jnp.sqrt(squares)
+        clip = CLIP / jnp.maximum(norm, CLIP)
+        tops = x_ref[high - 1 :]
         lanes = lax.broadcasted_iota(jnp.int32, (1, 128), 1)
         group_size = QUERY_HEADS // KEY_VALUE_HEADS
+        info_ref[0:1] = jnp.broadcast_to(norm, (1, 128))
+        info_ref[1:2] = LOGIT_CAP / jnp.maximum(tops, LOGIT_CAP)
 
         def factor(first, count):
             chosen = (lanes >= first) & (lanes < first + count)
@@ -1424,48 +1668,51 @@
             return jnp.sqrt(LOGIT_CAP / jnp.maximum(top, LOGIT_CAP))
 
         factors = {
-            "query": factor(spots[0] * sizes[2] + spots[2], 1),
+            "query": factor(column * lax.axis_size("dp") + data_at, 1),
             "keyval": jnp.where(
-                spots[2] < KEY_VALUE_HEADS, factor(spots[2] * group_size, group_size), 1.0
+                data_at < KEY_VALUE_HEADS, factor(data_at * group_size, group_size), 1.0
             ),
         }
-        for group in range(number):
-            rate, kind = groups[group][4:]
+        for at, (group, piece, rows) in enumerate(cuts):
+            rate, decay, kind = groups[group][4:]
             for k in range(4):
-                load(4 * group + k).wait()
+                load(at, k).wait()
             w_ref, m_ref, v_ref, g_ref = held[4 * group : 4 * group + 4]
-            rows, cols = w_ref.shape
-            step = min(rows, max(16, 32768 // max(cols, 128)))
-
-            @pl.loop(0, rows // step)
-            def _(at):
-                here = pl.ds(pl.multiple_of(at * step, step), step)
+            cols = w_ref.shape[1]
+            step = rows if rows % 8 else min(rows, max(16, 32768 // max(cols, 128)))
+
+            def stepped(here):
                 new = adamw_step(
-                    w_ref[here], m_ref[here], v_ref[here], g_ref[here].astype(FULL) * clip, rate, DECAY
+                    w_ref[here], m_ref[here], v_ref[here], g_ref[here].astype(FULL) * clip, rate, decay
                 )
                 m_ref[here], v_ref[here] = new[0], new[1]
                 w_ref[here] = new[2] * factors[kind] if kind else new[2]
 
+            if step == rows:
+                stepped(rows_of(at))
+            else:
+
+                @pl.loop(0, rows // step)
+                def _(k):
+                    stepped(pl.ds(pl.multiple_of(piece * rows + k * step, step), step))
+
             for k in range(3):
-                store(group, k).start()
-        for group in range(number):
+                store(at, k).start()
+        for at in range(len(cuts)):
             for k in range(3):
-                store(group, k).wait()
+                store(at, k).wait()
 
     dma = pltpu.SemaphoreType.DMA
     vmem, anywhere = pl.BlockSpec(memory_space=pltpu.VMEM), pl.BlockSpec(memory_space=pl.ANY)
-    scratch = [pltpu.VMEM(array.shape, array.dtype) for array in arrays]
-    scratch += [dma((4 * number,)), dma((3 * number,))]
-    for size in sizes:
-        scratch += [pltpu.VMEM((size,) + small.shape, FULL), dma((size,)), dma((size,))]
     outs = [jax.ShapeDtypeStruct(group[0].shape, FULL) for group in groups for _ in range(3)]
     return pl.pallas_call(
         kernel,
-        out_shape=[jax.ShapeDtypeStruct(small.shape, FULL)] + outs,
+        out_shape=[jax.ShapeDtypeStruct((8, 128), FULL)] + outs,
         in_specs=[vmem] + [anywhere] * (4 * number),
         out_specs=[vmem] + [anywhere] * (3 * number),
-        scratch_shapes=scratch,
-        compiler_params=params(ident, 56),
+        scratch_shapes=[pltpu.VMEM(array.shape, array.dtype) for array in arrays]
+        + [dma((len(cuts), 4)), dma((len(cuts), 3))],
+        compiler_params=pltpu.CompilerParams(vmem_limit_bytes=56 * 2**20),
         cost_estimate=cost(25),
     )(small, *arrays)
 
@@ -1494,13 +1741,13 @@
     return raw_weights / jnp.sum(raw_weights, axis=-1, keepdims=True), peak_row
 
 
-def attention_forward_head(acts, gain, head_w, kv_w, query_gain, key_gain, cos_tab, sin_tab, spans, items, ident):
+def attention_forward_head(acts, gain, head_w, key_w, value_w, query_gain, key_gain, cos_tab, sin_tab, spans, items, ident):
     tokens, width = acts.shape
     step = 256
     bundle = Bundle(items)
     number = bundle.number
 
-    def kernel(spans_ref, x_ref, gain_ref, qw_ref, kvw_ref, qg_ref, kg_ref, cos_ref, sin_ref, *refs):
+    def kernel(spans_ref, x_ref, gain_ref, qw_ref, kw_ref, vw_ref, qg_ref, kg_ref, cos_ref, sin_ref, *refs):
         x_refs, refs = refs[:number], refs[number:]
         h_ref, scale_ref, qr_ref, kr_ref, vr_ref, q_ref, k_ref, v_ref, o_ref, top_ref = refs[:10]
         o_refs, sems = refs[10 : 10 + number], refs[10 + number :]
@@ -1519,10 +1766,10 @@
             query = flat_dot(hidden, qw_ref[...])
             qr_ref[here] = query
             q_ref[here] = turn(whole_norm(query, qg_ref[...])[0], cos_rows, sin_rows).astype(LOW)
-            key = flat_dot(hidden, kvw_ref[0])
+            key = flat_dot(hidden, kw_ref[...])
             kr_ref[here] = key
             k_ref[here] = turn(whole_norm(key, kg_ref[...])[0], cos_rows, sin_rows).astype(LOW)
-            value = flat_dot(hidden, kvw_ref[1])
+            value = flat_dot(hidden, vw_ref[...])
             vr_ref[here] = value
             v_ref[here] = whole_norm(value, 1.0)[0].astype(LOW)
 
@@ -1559,12 +1806,12 @@
             jax.ShapeDtypeStruct((8, 128), FULL),
         ]
         + bundle.shapes,
-        in_specs=[pl.BlockSpec(memory_space=pltpu.SMEM)] + [vmem] * 8 + bundle.specs,
+        in_specs=[pl.BlockSpec(memory_space=pltpu.SMEM)] + [vmem] * 9 + bundle.specs,
         out_specs=[vmem] * 10 + bundle.specs,
         scratch_shapes=bundle.scratch,
         compiler_params=params(ident),
         cost_estimate=cost(40),
-    )(spans, acts, gain, head_w, kv_w, query_gain, key_gain, cos_tab, sin_tab, *bundle.sources)
+    )(spans, acts, gain, head_w, key_w, value_w, query_gain, key_gain, cos_tab, sin_tab, *bundle.sources)
 
 
 def head_backward(queries, keys, values, grads, spans, items, ident):
@@ -1583,8 +1830,15 @@
         dk_ref[...] = jnp.zeros(dk_ref.shape, FULL)
         dv_ref[...] = jnp.zeros(dv_ref.shape, FULL)
 
-        @pl.loop(0, rows // step)
+        blocks = rows // step
+        ahead = min(blocks, bundle.sizes[0])
+
+        @pl.loop(0, blocks)
         def _(at):
+            @pl.when((at > 0) & (at < ahead))
+            def _():
+                bundle.step(at)
+
             here = pl.ds(pl.multiple_of(at * step, step), step)
             allowed = allowed_block(at, step, keys.shape[0], spans_ref)
             block_rows, grad_rows = q_ref[here], g_ref[here]
@@ -1596,7 +1850,7 @@
             dk_ref[...] += inner_rows(grad_scores, block_rows)
             dv_ref[...] += inner_rows(probs.astype(LOW), grad_rows)
 
-        for k in range(1, bundle.sizes[0]):
+        for k in range(ahead, bundle.sizes[0]):
             bundle.step(k)
         bundle.finish()
 
@@ -1728,9 +1982,8 @@
             True,
         )
 
-    whole_acts, gateup_own, attend_own, qkv_w, left_t, right_w, pergate_t, perproj_w = transfers(
+    gateup_own, attend_own, qkv_w, left_t, right_w, pergate_t, perproj_w = transfers(
         [
-            along(activations),
             Swap(
                 w_gateup.astype(LOW),
                 (2, width, ff_part),
@@ -1756,24 +2009,35 @@
             across(w_perproj.astype(LOW), False),
         ],
         1,
-        90,
+        60,
     )
     gateup_all = lax.all_gather(gateup_own, "dp")
     query_w = qkv_w[:, :, :HEAD_WIDTH]
     kv_w = qkv_w[:, :, HEAD_WIDTH:]
     key_w = lax.dynamic_index_in_dim(kv_w, column, 0, False)
     value_w = lax.dynamic_index_in_dim(kv_w, KEY_VALUE_HEADS + column, 0, False)
-    whole_kv, head_w, gains, extras, attend_all = transfers(
+    last = pl.ds(HEAD_WIDTH, HEAD_WIDTH)
+    whole_acts, whole_key, whole_value, head_w, gains, extras, attend_all = transfers(
         [
+            along(activations),
             Line(
-                jnp.stack([key_w, value_w]),
-                (2, width, HEAD_WIDTH),
-                lambda ref, c, r: ref.at[:, columns_of(r, width_a)],
+                qkv_w,
+                (width, HEAD_WIDTH),
+                lambda ref, c, r: ref.at[columns_of(r, width_a)],
+                False,
+                lambda ref, c: ref.at[c, :, last],
+            ),
+            Line(
+                qkv_w,
+                (width, HEAD_WIDTH),
+                lambda ref, c, r: ref.at[columns_of(r, width_a)],
+                False,
+                lambda ref, c: ref.at[KEY_VALUE_HEADS + c, :, last],
             ),
             Swap(
-                query_w,
+                qkv_w,
                 (width, HEAD_WIDTH),
-                lambda ref, q: ref.at[q],
+                lambda ref, q: ref.at[q, :, pl.ds(0, HEAD_WIDTH)],
                 lambda ref, at: ref.at[columns_of(at, width_a)],
             ),
             Line(w_gains, (6, width), lambda ref, c, r: ref.at[:, columns_of(r, width_a)]),
@@ -1792,7 +2056,7 @@
             ),
         ],
         2,
-        60,
+        95,
     )
     attend_w = (
         attend_all.reshape(data_n, HEAD_WIDTH, rows_n, out_cols)
@@ -1828,7 +2092,8 @@
         whole_acts,
         gains[:1],
         head_w,
-        whole_kv,
+        whole_key,
+        whole_value,
         query_gain,
         key_gain,
         all_cos,
@@ -1948,13 +2213,21 @@
     inner_share = jnp.sum(d_hidden_share * gains[0] * inputs, axis=1)
     d_attended = against(spread_p, attend_w).astype(LOW)
     dw_attend = inner_rows(attended, spread_p).astype(LOW)
-    d_queries, d_keys, d_values, half_here, middle_here = head_backward(
+    small_parts = jnp.concatenate(
+        [
+            grad.astype(LOW).reshape(cols_n, -1, width)
+            for grad in (dw_left, dw_right, dw_pergate, dw_perproj)
+        ],
+        axis=1,
+    )
+    d_queries, d_keys, d_values, small_parts, half_here, middle_here = head_backward(
         queries,
         keys,
         values,
         d_attended,
         spans,
         [
+            Reduce(small_parts),
             Swap(
                 d_half.astype(LOW),
                 (half_tok, width_a),
@@ -1968,27 +2241,11 @@
         4,
     )
 
-    d_queries, dw_down, dw_attend, g_gateup = lax.optimization_barrier(
-        (d_queries, dw_down, dw_attend, g_gateup)
-    )
+    small_parts = small_parts.astype(LOW)
+    d_queries, dw_down, g_gateup = lax.optimization_barrier((d_queries, dw_down, g_gateup))
     g_down = lax.psum_scatter(
         dw_down.reshape(data_n, data_n, ff_part, -1), "dp", scatter_dimension=0
     )
-    g_attend = lax.psum_scatter(
-        dw_attend.reshape(HEAD_WIDTH, rows_n, data_n, out_cols)
-        .transpose(2, 0, 1, 3)
-        .reshape(data_n, HEAD_WIDTH, -1),
-        "dp",
-        scatter_dimension=0,
-    )
-
-    def to_shards(grad):
-        return grad.astype(LOW).reshape(cols_n, -1, rows_n, width_a).transpose(0, 2, 1, 3)
-
-    small_parts = jnp.concatenate(
-        [to_shards(grad) for grad in (dw_left, dw_right, dw_pergate, dw_perproj)], axis=2
-    )
-    small_parts = line_reduce(small_parts, 17, True, 28).astype(LOW)
     kv_parts = jnp.concatenate(
         [
             d_keys.astype(LOW).reshape(rows_n, quarter, HEAD_WIDTH),
@@ -2006,7 +2263,7 @@
     d_v_raw, _ = whole_norm_backward(value_raw, value_scale, 1.0, d_kv[quarter:])
     d_raw = jnp.concatenate([d_q_raw, d_k_raw, d_v_raw], axis=0).astype(LOW)
     gateup_squares = jnp.sum(jnp.square(g_gateup.astype(FULL)))
-    spread_q, g_gateup = transfers(
+    spread_q, g_gateup, g_attend = transfers(
         [
             Line(d_raw, (rows_n,) + d_raw.shape, lambda ref, c, r: ref.at[r]),
             Swap(
@@ -2015,6 +2272,7 @@
                 lambda ref, q: ref.at[:, columns_of(q, width_a), :],
                 lambda ref, at: ref.at[:, :, columns_of(at, ff_part)],
             ),
+            ShardSum(dw_attend, out_cols),
         ],
         12,
         100,
@@ -2136,129 +2394,70 @@
             jnp.broadcast_to(logit_row[None], (8, 128)),
         ]
     )
-    weights = (
-        w_query,
-        key_value_weight,
-        w_attend,
-        w_gateup,
-        w_down,
-        w_left,
-        w_right,
-        w_pergate,
-        w_perproj,
-    )
-    moments = (
-        m_query,
-        key_value_first_moment,
-        m_attend,
-        m_gateup,
-        m_down,
-        m_left,
-        m_right,
-        m_pergate,
-        m_perproj,
-    )
-    seconds = (
-        v_query,
-        key_value_second_moment,
-        v_attend,
-        v_gateup,
-        v_down,
-        v_left,
-        v_right,
-        v_pergate,
-        v_perproj,
-    )
-    gradients = (
-        g_query,
-        g_keyval,
-        g_attend,
-        g_gateup,
-        g_down,
-        g_left,
-        g_right,
-        g_pergate,
-        g_perproj,
-    )
-    fan_ins = (
-        MODEL_WIDTH,
-        MODEL_WIDTH,
-        QUERY_HEADS * HEAD_WIDTH,
-        MODEL_WIDTH,
-        FF,
-        MODEL_WIDTH,
-        RANK,
-        MODEL_WIDTH,
-        PLD,
-    )
-    kinds = ("query", "keyval") + (None,) * 7
-    order = (3, 4, 0, 1, 2, 5, 6, 7, 8)
-    groups = [
-        tuple(
-            array.reshape(-1, array.shape[-1])
-            for array in (weights[k], moments[k], seconds[k], gradients[k])
-        )
-        + (fan_ins[k] ** (-0.5), kinds[k])
-        for k in order
-    ]
-    small, *stepped = finish_step(small, gain_rows + head_rows, groups, 15)
-    updated = [None] * 9
-    for at, k in enumerate(order):
-        updated[k] = [array.reshape(weights[k].shape) for array in stepped[3 * at : 3 * at + 3]]
+    small = last_sums(small, 15)
     gain_sum = small[:gain_rows].reshape(6, width)
     head_sum = small[gain_rows : gain_rows + head_rows].reshape(QUERY_HEADS + 1, HEAD_WIDTH)
-    logit_top = small[-1, :QUERY_HEADS]
     g_gains = lax.dynamic_slice_in_dim(gain_sum, me * width_a, width_a, 1)
-    squares = small[gain_rows + head_rows, 0]
-    squares = squares + jnp.sum(gain_sum * gain_sum) + jnp.sum(head_sum * head_sum)
-    grad_norm = jnp.sqrt(squares)
-    clip_scale = CLIP / jnp.maximum(grad_norm, CLIP)
-    scale_factors = LOGIT_CAP / jnp.maximum(logit_top, LOGIT_CAP)
-    updated.append(
-        adamw_step(w_gains, m_gains, v_gains, g_gains * clip_scale, GAIN_RATE, 0.0)
-    )
-    updated.append(
-        adamw_step(w_heads, m_heads, v_heads, head_sum * clip_scale, HEAD_RATE, 0.0)
-    )
-    new_query, new_keyval = updated[0][2], updated[1][2]
+    matrix_rate = MODEL_WIDTH ** (-0.5)
+
+    def flat_rows_of(array):
+        return array.reshape(-1, array.shape[-1])
+
+    def kept(array):
+        return array
+
+    def turned(array):
+        return array.T
+
+    groups = [
+        tuple(change(array) for array in arrays) + rest
+        for arrays, change, rest in (
+            ((w_gateup, m_gateup, v_gateup, g_gateup), flat_rows_of, (matrix_rate, DECAY, None)),
+            ((w_down, m_down, v_down, g_down), kept, (FF ** (-0.5), DECAY, None)),
+            ((w_query, m_query, v_query, g_query), kept, (matrix_rate, DECAY, "query")),
+            (
+                (key_value_weight, key_value_first_moment, key_value_second_moment, g_keyval),
+                kept,
+                (matrix_rate, DECAY, "keyval"),
+            ),
+            (
+                (w_attend, m_attend, v_attend, g_attend),
+                kept,
+                ((QUERY_HEADS * HEAD_WIDTH) ** (-0.5), DECAY, None),
+            ),
+            ((w_left, m_left, v_left, g_left), turned, (matrix_rate, DECAY, None)),
+            ((w_right, m_right, v_right, g_right), kept, (RANK ** (-0.5), DECAY, None)),
+            ((w_pergate, m_pergate, v_pergate, g_pergate), turned, (matrix_rate, DECAY, None)),
+            ((w_perproj, m_perproj, v_perproj, g_perproj), kept, (PLD ** (-0.5), DECAY, None)),
+            ((w_gains, m_gains, v_gains, g_gains), kept, (GAIN_RATE, 0.0, None)),
+            ((w_heads, m_heads, v_heads, head_sum), kept, (HEAD_RATE, 0.0, None)),
+        )
+    ]
+    info, *stepped = adam_all(small, gain_rows + head_rows, groups)
+    grad_norm = info[0, 0]
+    scale_factors = info[1, :QUERY_HEADS]
+    gateup, down, query, keyval, attend, left, right, pergate, perproj, gain, head = (
+        stepped[3 * k : 3 * k + 3] for k in range(11)
+    )
+    gateup = [array.reshape(w_gateup.shape) for array in gateup]
+    left = [array.T for array in left]
+    pergate = [array.T for array in pergate]
     return (
         result,
         grad_input,
         grad_norm,
         scale_factors,
-        updated[0][0],
-        updated[0][1],
-        new_query,
-        updated[1][0],
-        updated[1][1],
-        new_keyval,
-        updated[2][0],
-        updated[2][1],
-        updated[2][2],
-        updated[3][0],
-        updated[3][1],
-        updated[3][2],
-        updated[4][0],
-        updated[4][1],
-        updated[4][2],
-        updated[5][0],
-        updated[5][1],
-        updated[5][2],
-        updated[6][0],
-        updated[6][1],
-        updated[6][2],
-        updated[7][0],
-        updated[7][1],
-        updated[7][2],
-        updated[8][0],
-        updated[8][1],
-        updated[8][2],
-        updated[9][0],
-        updated[9][1],
-        updated[9][2],
-        updated[10][0],
-        updated[10][1],
-        updated[10][2],
+        *query,
+        *keyval,
+        *attend,
+        *gateup,
+        *down,
+        *left,
+        *right,
+        *pergate,
+        *perproj,
+        *gain,
+        *head,
     )
 
 

time: 955 us -> 866 us (0.907)
  local copies, waits for them, and re-layouts: 94.3 us -> 43.9 us
  Pallas kernels: 740 us -> 712 us
    unnamed x300 -> x247, local copies, waits for them, and re-layouts: 65.4 us -> 30.5 us
    pallas_call x3 -> x2, Pallas kernels: 90.9 us -> 64.1 us  [line_reduce(): pl.pallas_call(kernel, out_shape=jax.ShapeDtypeStruct((high, wide), FULL)...]
    pallas_call x4, Pallas kernels: 304 us -> 284 us  [transfers(): pl.pallas_call(kernel, out_shape=bundle.shapes, in_specs=bundle.specs, ou...]
    pallas_call x1, Pallas kernels: 23 us -> 38.9 us  [head_backward(): pl.pallas_call(kernel, out_shape=[jax.ShapeDtypeStruct(queries.shape, FUL...]
    reshape x6 -> x1, local copies, waits for them, and re-layouts: 11.2 us -> 0.6 us  [line_device(): small[gain_rows:gain_rows + head_rows].reshape(QUERY_HEADS + 1, HEAD_WIDTH)]
    pallas_call x1 -> x2, Pallas kernels: 30.9 us -> 34.9 us  [the longest x1 20.4 us: adam_all(): pl.pallas_call(kernel, out_shape=[jax.ShapeDtypeStruct((8, 128), FULL)] +...]
  transfers between devices with their start and end apart: 5 -> 4, of which waited for: 0 -> 0; matrix products, arithmetic and copies ran while one was open for 9% -> 8% of each run, Pallas kernels for 39% -> 44%
where the time goes in v5:
time: 866 us; the launch traced here: 857 us
  Pallas kernels  712 us (82%)
  other arithmetic  50.4 us (6%)
  local copies, waits for them, and re-layouts  43.9 us (5%)
  matrix products  30.4 us (4%)
  between operations  19.9 us (2%)
    pallas_call x4, Pallas kernels, transfers(): pl.pallas_call(kernel, out_shape=bundle.shapes, in_specs=bundle.specs, ou...  284 us
    pallas_call x1, Pallas kernels, ffn_forward(): pl.pallas_call(kernel, out_shape=[jax.ShapeDtypeStruct((share, width), FU...  112 us
    pallas_call x1, Pallas kernels, ffn_backward(): pl.pallas_call(kernel, out_shape=[jax.ShapeDtypeStruct((share, width), FU...  96.3 us
    pallas_call x2, Pallas kernels, line_reduce(): pl.pallas_call(kernel, out_shape=jax.ShapeDtypeStruct((high, wide), FULL)...  64.1 us
    pallas_call x1, Pallas kernels, attention_forward_head(): pl.pallas_call(kernel, out_shape=[jax.ShapeDtypeStruct((tokens, width), L...  46.3 us
    pallas_call x1, Pallas kernels, head_backward(): pl.pallas_call(kernel, out_shape=[jax.ShapeDtypeStruct(queries.shape, FUL...  38.9 us
    pallas_call x1, Pallas kernels, shard_total(): pl.pallas_call(kernel, out_shape=[jax.ShapeDtypeStruct(shape, FULL) for s...  36.1 us
    unnamed x247, local copies, waits for them, and re-layouts  30.5 us
  transfers between devices with their start and end apart: 4, of which 0 were waited for; matrix products, arithmetic and copies ran while one was open for 8% of the time, Pallas kernels for 44%

profile of v5, /device:TPU:0, one launch (start us, length us, event | category | flops | bytes accessed | tf_op | source)
XLA Modules:
  0.0 857.0 jit_solution(1884563349362343646)
XLA Ops:
  7.4 2.6 convert_element_type.193.refs_0_
  10.7 57.4 %shard_map.645 = (bf16[2,2048,256]{2,1,0:T(8,128)(2,1)}, bf16[256,512]{1,0:T(8,128)(2,1)S(1)}, bf16[4,512,512]{2,1,0:T(8,128)(2,1)S(1)}, f32[32,512]{1,0:T(8,128...) custom-call(bf16[2,512,1024]{2,1,0:T(8,128)(2,1)S(1)} %convert_element_type.193.refs_, ...), custom_call_target="tpu_custom_call" | custom-call | bytes 180000000 | tf_op jit(solution)/shard_map/pallas_call | solution.py:928
  68.1 1.3 copy-done.2
  72.3 2.8 convert_element_type.201
  76.1 95.5 %shard_map.646 = (bf16[1024,2048]{1,0:T(8,128)(2,1)S(1)}, bf16[2048,256]{1,0:T(8,128)(2,1)S(1)}, bf16[2048,256]{1,0:T(8,128)(2,1)S(1)}, bf16[2048,256]{1,0:T(8,1...) custom-call(bf16[512,512]{1,0:T(8,128)(2,1)S(1)} %copy-done.29, ...), custom_call_target="tpu_custom_call" | custom-call | bytes 285000000 | tf_op jit(solution)/shard_map/pallas_call | solution.py:928
  171.6 2.0 copy-done.5
  177.8 1.9 multiply_sine_fusion
  180.4 46.3 %shard_map.647 = (bf16[1024,2048]{1,0:T(8,128)(2,1)}, f32[1024,128]{1,0:T(8,128)S(1)}, f32[1024,256]{1,0:T(8,128)S(1)}, f32[1024,256]{1,0:T(8,128)}, f32[1024,25...) custom-call(s32[3]{0:T(128)S(1)} %pad_add_fusion.spans_ref, ...), custom_call_target="tpu_custom_call" | custom-call | bytes 120000000 | tf_op jit(solution)/shard_map/pallas_call | solution.py:1794
  234.2 1.3 convolution_convert_fusion
  235.6 41.7 %shard_map.648 = f32[128,2048]{1,0:T(8,128)S(1)} custom-call(bf16[2,4,128,2048]{3,2,1,0:T(8,128)(2,1)S(1)} %bitcast.176), custom_call_target="tpu_custom_call" | custom-call | bytes 135000000 | tf_op jit(solution)/shard_map/pallas_call | solution.py:442
  277.3 1.2 fusion.22
  278.7 1.4 convolution_convert_fusion.14
  281.6 1.7 multiply_reduce_fusion.16
  284.9 111.6 %shard_map.649 = (f32[128,2048]{1,0:T(8,128)}, bf16[2048,1024]{1,0:T(8,128)(2,1)}, bf16[1024,1024]{1,0:T(8,128)(2,1)}, f32[4,256,1024]{2,1,0:T(8,128)}, f32[4,25...) custom-call(bf16[128,2048]{1,0:T(8,128)(2,1)} %multiply_convert_fusion.x_ref, ...), custom_call_target="tpu_custom_call" | custom-call | bytes 240000000 | tf_op jit(solution)/shard_map/pallas_call | solution.py:1364
  396.5 1.5 multiply_reduce_fusion.15
  398.1 1.5 multiply_add_fusion
  399.6 1.5 fusion.69
  401.5 2.0 fusion.20
  403.9 1.4 fusion.76
  407.6 96.3 %shard_map.650 = (f32[128,2048]{1,0:T(8,128)}, bf16[4,2,2048,256]{3,2,1,0:T(8,128)(2,1)}, bf16[4,1024,512]{2,1,0:T(8,128)(2,1)}, bf16[512,512]{1,0:T(8,128)(2,1)}) custom-call(bf16[128,2048]{1,0:T(8,128)(2,1)} %subtract_convert_fusion.3.x_ref, bf16[4,2,2048,256]{3,2,1,0:T(8,128)(2,1)} %bitcast.198, bf16[4,1024,512]{2,1,0:T(8,128)(2,1)} %bitcast.201, ...), custom_call_target="tpu_custom_call" | custom-call | bytes 270000000 | tf_op jit(solution)/shard_map/pallas_call | solution.py:1540
  504.0 1.5 copy-done.4
  510.3 1.8 dynamic-slice_reduce_fusion
  512.0 1.4 multiply_reduce_fusion.9
  513.5 2.5 multiply_reduce_fusion.5
  517.3 1.4 multiply_reduce_fusion.6
  519.2 41.3 %shard_map.651 = bf16[2,4,128,2048]{3,2,1,0:T(8,128)(2,1)S(1)} custom-call(bf16[128,2048]{1,0:T(8,128)(2,1)S(1)} %get-tuple-element.275.refs_0_), custom_call_target="tpu_custom_call" | custom-call | bytes 120000000 | tf_op jit(solution)/shard_map/pallas_call | solution.py:928
  560.8 2.6 convolution_convert_fusion.5
  564.6 1.7 pad_maximum_fusion.refs_0_
  566.3 1.2 convolution_convert_fusion.6.g_ref
  567.6 38.9 %shard_map.652 = (f32[1024,256]{1,0:T(8,128)S(1)}, f32[1024,256]{1,0:T(8,128)S(1)}, f32[1024,256]{1,0:T(8,128)}, f32[320,512]{1,0:T(8,128)S(1)}, bf16[512,512]{1...) custom-call(s32[3]{0:T(128)S(1)} %pad_add_fusion.spans_ref, bf16[1024,256]{1,0:T(8,128)(2,1)S(1)} %copy-done.31, ...), custom_call_target="tpu_custom_call" | custom-call | bytes 75000000 | tf_op jit(solution)/shard_map/pallas_call | solution.py:1858
  607.6 2.3 convert_element_type.226
  610.7 1.3 pad_maximum_fusion.2.x_ref
  612.0 22.4 %shard_map.653 = f32[512,256]{1,0:T(8,128)S(1)} custom-call(bf16[4,512,256]{2,1,0:T(8,128)(2,1)S(1)} %pad_maximum_fusion.2.x_ref), custom_call_target="tpu_custom_call" | custom-call | bytes 60000000 | tf_op jit(solution)/shard_map/pallas_call | solution.py:442
  635.6 2.4 fusion.4
  639.7 2.2 convolution_convert_fusion.3.refs_2_
  641.9 2.3 multiply_subtract_fusion
  646.2 2.1 subtract_convert_fusion
  648.7 89.7 %shard_map.654 = (bf16[4,1536,256]{2,1,0:T(8,128)(2,1)S(1)}, bf16[2,512,1024]{2,1,0:T(8,128)(2,1)S(1)}, bf16[256,512]{1,0:T(8,128)(2,1)S(1)}) custom-call(bf16[1536,256]{1,0:T(8,128)(2,1)S(1)} %pad_maximum_fusion.4.refs_0_, bf16[2,2048,256]{2,1,0:T(8,128)(2,1)S(1)} %bitcast.177, bf16[256,2048]{1,0:T(8,128)(2,1)S(1)} %copy-done.27), custom_call_target="tpu_custom_call" | custom-call | bytes 300000000 | tf_op jit(solution)/shard_map/pallas_call | solution.py:928
  738.5 1.7 copy-done.11
  740.1 1.3 copy-done.17
  742.2 1.7 multiply_reduce_fusion
  745.2 1.4 fusion.94
  746.6 1.9 fusion.9
  754.5 3.2 multiply_reduce_fusion.2
  760.1 36.1 %shard_map.655 = (f32[512,256]{1,0:T(8,128)S(1)}, f32[512,256]{1,0:T(8,128)S(1)}, f32[320,128]{1,0:T(8,128)S(1)}, bf16[4,4,256,128]{3,2,1,0:T(8,128)(2,1)S(1)}, ...) custom-call(bf16[4,512,256]{2,1,0:T(8,128)(2,1)S(1)} %pad_maximum_fusion.3.q_ref, ...), custom_call_target="tpu_custom_call" | custom-call | bytes 120000000 | tf_op jit(solution)/shard_map/pallas_call | solution.py:1022
  801.7 3.1 fusion.18
  808.9 14.5 %shard_map.656.x_ref = f32[128,128]{1,0:T(8,128)S(1)} custom-call(f32[128,128]{1,0:T(8,128)S(1)} %pad_maximum_fusion.8.x_ref), custom_call_target="tpu_custom_call" | custom-call | bytes 42000000 | tf_op jit(solution)/shard_map/pallas_call | solution.py:1608
  826.5 20.4 %shard_map.657 = (f32[8,128]{1,0:T(8,128)}, f32[1024,1024]{1,0:T(8,128)}, f32[1024,1024]{1,0:T(8,128)}, f32[1024,1024]{1,0:T(8,128)}, f32[4096,128]{1,0:T(8,128)...) custom-call(f32[128,128]{1,0:T(8,128)} %copy-done.28, ...), custom_call_target="tpu_custom_call" | custom-call | bytes 75000000 | tf_op jit(solution)/shard_map/pallas_call | solution.py:1708
  (371 shorter events, 60.0 us)
Async XLA Ops:
  7.2 64.8 %copy-start = (s32[4,2]{0,1:T(2,128)S(1)}, s32[4,2]{0,1:T(2,128)}, u32[]{:S(2)}) copy-start(s32[4,2]{0,1:T(2,128)} %param.44) | copy-start | bytes 100
  7.3 225.9 %all-gather.5.cloned.1.call-start = ((), (), s32[]{:S(2)}) async-start(), calls=%async_computation.2 | async-start | bytes 10485760 | tf_op jit(solution)/shard_map/all_gather | solution.py:2014
  10.2 61.3 %copy-start.118 = (s32[4]{0:T(128)S(1)}, s32[4]{0:T(128)}, u32[]{:S(2)}) copy-start(s32[4]{0:T(128)} %param.43) | copy-start | bytes 52
  71.4 213.5 %all-gather.7.cloned.1.call-start = ((), (), s32[]{:S(2)}) async-start(), calls=%async_computation.3 | async-start | bytes 5242880 | tf_op jit(solution)/shard_map/all_gather | solution.py:2115
  76.1 104.3 %copy-start.49 = (bf16[32,512]{1,0:T(8,128)(2,1)S(1)}, bf16[32,512]{1,0:T(8,128)(2,1)}, u32[]{:S(2)}) copy-start(bf16[32,512]{1,0:T(8,128)(2,1)} %copy-done.48) | copy-start | bytes 98308
  176.3 4.0 copy-start.22
  176.3 4.0 copy-start.107
  180.4 101.3 %copy-start.92 = (f32[1,2048]{1,0:T(1,128)}, f32[1,2048]{1,0:T(1,128)S(1)}, u32[]{:S(2)}) copy-start(f32[1,2048]{1,0:T(1,128)S(1)} %get-tuple-element.297) | copy-start | bytes 24580
  180.4 101.3 %copy-start.94 = (f32[1,2048]{1,0:T(1,128)}, f32[1,2048]{1,0:T(1,128)S(1)}, u32[]{:S(2)}) copy-start(f32[1,2048]{1,0:T(1,128)S(1)} %get-tuple-element.296) | copy-start | bytes 24580
  180.4 217.7 %copy-start.89 = (f32[1,2048]{1,0:T(1,128)}, f32[1,2048]{1,0:T(1,128)S(1)}, u32[]{:S(2)}) copy-start(f32[1,2048]{1,0:T(1,128)S(1)} %get-tuple-element.294) | copy-start | bytes 24580
  233.2 377.4 %reduce-scatter.7.cloned.1.call-start = ((), (), s32[]{:S(2)}) async-start(), calls=%async_computation.4 | async-start | bytes 10485760
  235.6 43.1 %copy-start.40 = (bf16[64,2048]{1,0:T(8,128)(2,1)S(1)}, bf16[64,2048]{1,0:T(8,128)(2,1)}, u32[]{:S(2)}) copy-start(bf16[64,2048]{1,0:T(8,128)(2,1)} %copy-done.39) | copy-start | bytes 786436
  278.7 4.6 copy-start.111
  280.1 4.7 copy-start.97
  280.5 116.0 %copy-start.59 = (f32[128,2048]{1,0:T(8,128)}, f32[128,2048]{1,0:T(8,128)S(1)}, u32[]{:S(2)}) copy-start(f32[128,2048]{1,0:T(8,128)S(1)} %get-tuple-element.318) | copy-start | bytes 3145732
  283.3 114.8 %copy-start.55 = (f32[128,2048]{1,0:T(8,128)}, f32[128,2048]{1,0:T(8,128)S(1)}, u32[]{:S(2)}) copy-start(f32[128,2048]{1,0:T(8,128)S(1)} %get-tuple-element.262) | copy-start | bytes 3145732
  283.9 112.6 %copy-start.110 = (f32[128]{0:T(128)}, f32[128]{0:T(128)S(1)}, u32[]{:S(2)}) copy-start(f32[128]{0:T(128)S(1)} %get-tuple-element.260) | copy-start | bytes 1540
  396.5 4.6 copy-start.80
  503.9 9.6 %copy-start.95 = (f32[1,2048]{1,0:T(1,128)S(1)}, f32[1,2048]{1,0:T(1,128)}, u32[]{:S(2)}) copy-start(f32[1,2048]{1,0:T(1,128)} %copy-done.94) | copy-start | bytes 24580
  503.9 9.6 %copy-start.93 = (f32[1,2048]{1,0:T(1,128)S(1)}, f32[1,2048]{1,0:T(1,128)}, u32[]{:S(2)}) copy-start(f32[1,2048]{1,0:T(1,128)} %copy-done.92) | copy-start | bytes 24580
  503.9 254.2 %reduce-scatter.9.cloned.1.call-start = ((), (), s32[]{:S(2)}) async-start(), calls=%async_computation.5 | async-start | bytes 5242880
  507.6 8.5 copy-start.56
  507.6 8.5 copy-start.65
  507.6 8.5 copy-start.73
  519.2 41.6 %copy-start.112 = (f32[128]{0:T(128)S(1)}, f32[128]{0:T(128)}, u32[]{:S(2)}) copy-start(f32[128]{0:T(128)} %copy-done.111) | copy-start | bytes 1540
  519.2 44.2 %copy-start.98 = (bf16[128,64]{0,1:T(8,128)(2,1)S(1)}, bf16[128,64]{0,1:T(8,128)(2,1)}, u32[]{:S(2)}) copy-start(bf16[128,64]{0,1:T(8,128)(2,1)} %copy-done.97) | copy-start | bytes 49156
  519.2 44.5 %copy-start.79 = (bf16[128,2048]{1,0:T(8,128)(2,1)S(1)}, bf16[128,2048]{1,0:T(8,128)(2,1)}, u32[]{:S(2)}) copy-start(bf16[128,2048]{1,0:T(8,128)(2,1)} %copy-done.78) | copy-start | bytes 1572868
  560.5 5.8 copy-start.9
  610.7 24.8 %copy-start.88 = (f32[1024,256]{1,0:T(8,128)S(1)}, f32[1024,256]{1,0:T(8,128)}, u32[]{:S(2)}) copy-start(f32[1024,256]{1,0:T(8,128)} %get-tuple-element.187) | copy-start | bytes 3145732
  610.7 24.9 %copy-start.41 = (bf16[64,2048]{1,0:T(8,128)(2,1)S(1)}, bf16[64,2048]{1,0:T(8,128)(2,1)}, u32[]{:S(2)}) copy-start(bf16[64,2048]{1,0:T(8,128)(2,1)} %copy-done.39) | copy-start | bytes 786436
  610.7 24.9 %copy-start.63 = (f32[128,2048]{1,0:T(8,128)S(1)}, f32[128,2048]{1,0:T(8,128)}, u32[]{:S(2)}) copy-start(f32[128,2048]{1,0:T(8,128)} %copy-done.62) | copy-start | bytes 3145732
  612.0 27.1 %copy-start.81 = (f32[1024,256]{1,0:T(8,128)S(1)}, f32[1024,256]{1,0:T(8,128)}, u32[]{:S(2)}) copy-start(f32[1024,256]{1,0:T(8,128)} %get-tuple-element.184) | copy-start | bytes 3145732
  634.4 5.2 copy-start.10
  634.4 5.2 copy-start.20
  635.4 4.0 copy-start.36
  639.7 5.4 copy-start.7
  754.5 47.2 %copy-start.54 = (bf16[512,64]{1,0:T(8,128)(2,1)S(1)}, bf16[512,64]{1,0:T(8,128)(2,1)}, u32[]{:S(2)}) copy-start(bf16[512,64]{1,0:T(8,128)(2,1)} %copy-done.53) | copy-start | bytes 196612
  798.9 7.2 copy-start.15
  798.9 7.2 copy-start.16
  798.9 5.9 copy-start.102
  798.9 5.9 copy-start.103
  798.9 5.9 copy-start.104
  798.9 5.9 copy-start.105
  798.9 6.0 copy-start.71
  800.9 7.9 copy-start.116
  800.9 7.9 copy-start.99
  826.5 22.7 %copy-start.83 = (bf16[512,512]{1,0:T(8,128)(2,1)S(1)}, bf16[512,512]{1,0:T(8,128)(2,1)}, u32[]{:S(2)}) copy-start(bf16[512,512]{1,0:T(8,128)(2,1)} %get-tuple-element.363) | copy-start | bytes 1572868
  826.5 23.5 %copy-start.1 = (s32[4,2]{0,1:T(2,128)S(1)}, s32[4,2]{0,1:T(2,128)}, u32[]{:S(2)}) copy-start(s32[4,2]{0,1:T(2,128)} %param.44) | copy-start | bytes 100
  (75 other events, 145.7 us)
Sparse Core Ops, SparseCore 0:
  71.5 93.2 all-gather.4
  233.3 51.0 all-gather.6
  504.0 85.7 reduce-scatter.6
  610.8 60.1 reduce-scatter.8

commit v6 on v5

--- a/solution.py
+++ b/solution.py
@@ -284,178 +284,6 @@
     )
 
 
-def greet_line(me, count, column, core):
-    barrier = pltpu.get_barrier_semaphore()
-
-    @pl.when(me > 0)
-    def _():
-        pl.semaphore_signal(barrier, inc=1, device_id={"row": me - 1}, device_id_type=MESH)
-
-    @pl.when(me < count - 1)
-    def _():
-        pl.semaphore_signal(barrier, inc=1, device_id={"row": me + 1}, device_id_type=MESH)
-
-    if core:
-        pl.semaphore_signal(barrier, inc=1, device_id={"col": 1 - column}, device_id_type=MESH)
-
-    ends = (me == 0) | (me == count - 1)
-
-    @pl.when(ends)
-    def _():
-        pl.semaphore_wait(barrier, 1 + int(core))
-
-    @pl.when(jnp.logical_not(ends))
-    def _():
-        pl.semaphore_wait(barrier, 2 + int(core))
-
-
-def line_reduce(parts, ident, core, micros):
-    count = lax.axis_size("row")
-    high, wide = parts.shape[-2:]
-    chunk = min(high, max(16, 65536 // wide))
-    while high % chunk:
-        chunk //= 2
-
-    def kernel(x_ref, o_ref, c_buf, l_buf, r_buf, s_buf, send_l, send_r, send_c, recv_l, recv_r, recv_c):
-        me = lax.axis_index("row")
-        column = lax.axis_index("col")
-
-        def mine(q):
-            return x_ref.at[column, q] if core else x_ref.at[q]
-
-        def core_copy(q):
-            return push(x_ref.at[1 - column, q], c_buf.at[q], send_c.at[q], recv_c.at[q], {"col": 1 - column})
-
-        def left_copy(q):
-            return push(s_buf.at[q], l_buf.at[q], send_l.at[q], recv_l.at[q], {"row": me - 1})
-
-        def right_copy(q):
-            return push(s_buf.at[q], r_buf.at[q], send_r.at[q], recv_r.at[q], {"row": me + 1})
-
-        def left_arrival(q):
-            return push(s_buf.at[q], l_buf.at[q], send_l.at[q], recv_l.at[q], {"row": me + 1})
-
-        def right_arrival(q):
-            return push(s_buf.at[q], r_buf.at[q], send_r.at[q], recv_r.at[q], {"row": me - 1})
-
-        def added(target, terms):
-            @pl.loop(0, high // chunk)
-            def _(at):
-                rows = pl.ds(pl.multiple_of(at * chunk, chunk), chunk)
-                total = terms[0][rows].astype(FULL)
-                for term in terms[1:]:
-                    total = total + term[rows].astype(FULL)
-                target[rows] = total.astype(target.dtype)
-
-        def base(q):
-            return [mine(q)] + ([c_buf.at[q]] if core else [])
-
-        greet_line(me, count, column, core)
-        if core:
-            for q in range(count):
-                core_copy(q).start()
-
-        def leftward(q):
-            @pl.when(me > q)
-            def _():
-                if core:
-                    core_copy(q).wait_recv()
-
-                @pl.when(me < count - 1)
-                def _():
-                    left_arrival(q).wait_recv()
-                    added(s_buf.at[q], base(q) + [l_buf.at[q]])
-
-                @pl.when(me == count - 1)
-                def _():
-                    added(s_buf.at[q], base(q))
-
-                left_copy(q).start()
-
-        def rightward(q):
-            @pl.when(me < q)
-            def _():
-                if core:
-                    core_copy(q).wait_recv()
-
-                @pl.when(me > 0)
-                def _():
-                    right_arrival(q).wait_recv()
-                    added(s_buf.at[q], base(q) + [r_buf.at[q]])
-
-                @pl.when(me == 0)
-                def _():
-                    added(s_buf.at[q], base(q))
-
-                right_copy(q).start()
-
-        for j in range(count - 1):
-
-            @pl.when(me < count // 2)
-            def _():
-                rightward(count - 1 - j)
-
-            leftward(j)
-
-            @pl.when(me >= count // 2)
-            def _():
-                rightward(count - 1 - j)
-
-        if core:
-            core_copy(me).wait_recv()
-
-        @pl.when(me < count - 1)
-        def _():
-            left_arrival(me).wait_recv()
-
-        @pl.when(me > 0)
-        def _():
-            right_arrival(me).wait_recv()
-
-        @pl.when(me == 0)
-        def _():
-            added(o_ref, base(me) + [l_buf.at[me]])
-
-        @pl.when(me == count - 1)
-        def _():
-            added(o_ref, base(me) + [r_buf.at[me]])
-
-        @pl.when((me > 0) & (me < count - 1))
-        def _():
-            added(o_ref, base(me) + [l_buf.at[me], r_buf.at[me]])
-
-        for q in range(count):
-            if core:
-                core_copy(q).wait_send()
-
-            @pl.when(me > q)
-            def _():
-                left_copy(q).wait_send()
-
-            @pl.when(me < q)
-            def _():
-                right_copy(q).wait_send()
-
-    dma = pltpu.SemaphoreType.DMA
-    slots = (count, high, wide)
-    vmem = pl.BlockSpec(memory_space=pltpu.VMEM)
-    return pl.pallas_call(
-        kernel,
-        out_shape=jax.ShapeDtypeStruct((high, wide), FULL),
-        in_specs=[vmem],
-        out_specs=vmem,
-        scratch_shapes=[
-            pltpu.VMEM(slots if core else (1, 16, 128), parts.dtype),
-            pltpu.VMEM(slots, parts.dtype),
-            pltpu.VMEM(slots, parts.dtype),
-            pltpu.VMEM(slots, parts.dtype),
-        ]
-        + [dma((count,))] * 6,
-        compiler_params=params(ident),
-        cost_estimate=cost(micros),
-    )(parts)
-
-
 class Line:
     def __init__(self, source, shape, place, core=False, view=None):
         self.source, self.shape, self.place, self.core = source, shape, place, core
@@ -662,29 +490,25 @@
 
 
 class Reduce:
-    core = True
-
-    def __init__(self, source):
-        self.source = source
-        self.high, self.wide = source.shape[1], source.shape[2] // lax.axis_size("row")
-        self.shape, self.dtype = (self.high, self.wide), FULL
+    def __init__(self, source, shape, cut, core=True):
+        self.source, self.shape, self.cut, self.core = source, shape, cut, core
+        self.high, self.wide = shape
+        self.dtype = FULL
 
     def semaphores(self, count, data):
         dma = pltpu.SemaphoreType.DMA
-        slots = pltpu.VMEM((count, self.high, self.wide), self.source.dtype)
-        whole = pltpu.VMEM(self.source.shape[1:], self.source.dtype)
+        slots = pltpu.VMEM((count,) + self.shape, self.source.dtype)
+        whole = pltpu.VMEM(self.source.shape[1:] if self.core else self.source.shape, self.source.dtype)
         stage = pltpu.VMEM(self.shape, FULL)
-        return [whole, stage, slots, slots, slots, slots] + [dma((count,))] * 6 + [dma, dma]
+        fourth = slots if self.core else pltpu.VMEM((1, 16, 128), self.source.dtype)
+        return [whole, stage, slots, slots, slots, fourth] + [dma((count,))] * 6 + [dma, dma]
 
     def bind(self, x_ref, o_ref, sems, spots, sizes):
         self.x_ref, self.o_ref = x_ref, o_ref
-        self.mine, self.stage, self.core_in, self.left_in, self.right_in, self.out = sems[:6]
+        self.mine, self.stage, self.out, self.left_in, self.right_in, self.core_in = sems[:6]
         self.sems = sems[6:]
         self.me, self.column = spots[0], spots[1]
         self.count = sizes[0]
-
-    def cut(self, ref, q):
-        return ref.at[:, pl.ds(pl.multiple_of(q * self.wide, self.wide), self.wide)]
 
     def beside(self, q):
         return push(
@@ -708,21 +532,27 @@
         return push(self.right_in.at[q], self.right_in.at[q], self.sems[2].at[q], self.sems[5].at[q], {"row": self.me - 1})
 
     def own(self):
-        return pltpu.make_async_copy(self.x_ref.at[self.column], self.mine, self.sems[6])
+        return pltpu.make_async_copy(
+            self.x_ref.at[self.column] if self.core else self.x_ref, self.mine, self.sems[6]
+        )
 
     def start(self):
         self.own().start()
-        for q in range(self.count):
-            self.beside(q).start()
+        if self.core:
+            for q in range(self.count):
+                self.beside(q).start()
 
     def added(self, target, q, others):
-        step = 64
+        step = min(self.high, max(16, 65536 // self.wide))
+        while self.high % step:
+            step //= 2
         cut = self.cut(self.mine, q)
+        others = ([self.core_in] if self.core else []) + others
 
         @pl.loop(0, self.high // step)
         def _(at):
             rows = pl.ds(pl.multiple_of(at * step, step), step)
-            total = cut[rows].astype(FULL) + self.core_in[q, rows].astype(FULL)
+            total = cut[rows].astype(FULL)
             for other in others:
                 total = total + other[q, rows].astype(FULL)
             target[rows] = total.astype(target.dtype)
@@ -739,7 +569,8 @@
 
         @pl.when((q_left >= 0) & (q_left < me))
         def _():
-            self.beside(q_left).wait()
+            if self.core:
+                self.beside(q_left).wait()
 
             @pl.when(me < count - 1)
             def _():
@@ -754,7 +585,8 @@
 
         @pl.when((t >= me) & (q_right > me))
         def _():
-            self.beside(q_right).wait()
+            if self.core:
+                self.beside(q_right).wait()
 
             @pl.when(me > 0)
             def _():
@@ -769,7 +601,8 @@
 
     def finish(self):
         me, count = self.me, self.count
-        self.beside(me).wait()
+        if self.core:
+            self.beside(me).wait()
 
         @pl.when(me < count - 1)
         def _():
@@ -913,7 +746,7 @@
             item.finish()
 
 
-def transfers(items, ident, micros):
+def transfers(items, ident, micros, mebibytes=16):
     bundle = Bundle(items)
     number = bundle.number
 
@@ -931,7 +764,7 @@
         in_specs=bundle.specs,
         out_specs=bundle.specs,
         scratch_shapes=bundle.scratch,
-        compiler_params=params(ident, 16),
+        compiler_params=params(ident, mebibytes),
         cost_estimate=cost(micros),
     )(*bundle.sources)
 
@@ -1033,6 +866,9 @@
     )(query_parts, kv_parts, flat_parts, *bundle.sources)
 
 
+CHUNKS = 4
+
+
 class Flow:
     def __init__(self, x_ref, blocks, own, core_out, core_in, left_in, right_in, sems):
         self.x_ref, self.blocks, self.own = x_ref, blocks, own
@@ -1053,7 +889,9 @@
             pltpu.VMEM(slots, LOW),
             pltpu.VMEM(slots, LOW),
             pltpu.VMEM(slots, LOW),
-        ], [dma((count,))] * 12 + [dma]
+        ], [dma((count,))] * 7 + [dma((count * CHUNKS,))] * 2 + [dma((count,))] + [
+            dma((count * CHUNKS,))
+        ] * 2 + [dma]
 
     def left(self):
         return {"row": self.me - 1}
@@ -1076,11 +914,37 @@
     def back_core(self, q):
         return push(self.core_out.at[q], self.core_in.at[q], self.sems[6].at[q], self.sems[9].at[q], self.beside())
 
-    def back_left(self, q):
-        return push(self.core_out.at[q], self.left_in.at[q], self.sems[7].at[q], self.sems[10].at[q], self.left())
-
-    def back_right(self, q):
-        return push(self.core_out.at[q], self.right_in.at[q], self.sems[8].at[q], self.sems[11].at[q], self.right())
+    def part(self, ref, q, j):
+        size = ref.shape[1] // CHUNKS
+        return ref.at[q, pl.ds(pl.multiple_of(j * size, size), size)]
+
+    def back_left(self, q, j):
+        at = q * CHUNKS + j
+        return push(
+            self.part(self.core_out, q, j),
+            self.part(self.left_in, q, j),
+            self.sems[7].at[at],
+            self.sems[10].at[at],
+            self.left(),
+        )
+
+    def back_right(self, q, j):
+        at = q * CHUNKS + j
+        return push(
+            self.part(self.core_out, q, j),
+            self.part(self.right_in, q, j),
+            self.sems[8].at[at],
+            self.sems[11].at[at],
+            self.right(),
+        )
+
+    def from_right(self, q, j):
+        at, there = q * CHUNKS + j, self.part(self.left_in, q, j)
+        return push(there, there, self.sems[7].at[at], self.sems[10].at[at], self.right())
+
+    def from_left(self, q, j):
+        at, there = q * CHUNKS + j, self.part(self.right_in, q, j)
+        return push(there, there, self.sems[8].at[at], self.sems[11].at[at], self.left())
 
     def mine(self):
         return pltpu.make_async_copy(self.x_ref, self.blocks.at[self.me, 0], self.sems[12])
@@ -1146,9 +1010,13 @@
         def _(k):
             self.arrive(k)
 
-            @pl.when(k > 0)
+            @pl.when(k == count - 2)
             def _():
-                bundle.step(k)
+                bundle.start()
+
+            @pl.when(k == count - 1)
+            def _():
+                bundle.step(1)
 
             @pl.loop(0, 2)
             def _(side):
@@ -1159,81 +1027,93 @@
                     body(source)
                     self.back_core(source).start()
 
+            self.give_back(k)
+
     def added(self, target, terms):
-        high, wide = target.shape
-        step = min(high, max(16, 65536 // wide))
-
-        @pl.loop(0, high // step)
-        def _(at):
-            rows = pl.ds(pl.multiple_of(at * step, step), step)
-            total = terms[0][rows]
-            for term in terms[1:]:
-                total = total + term[rows].astype(FULL)
-            target[rows] = total.astype(target.dtype)
+        total = terms[0][...]
+        for term in terms[1:]:
+            total = total + term[...].astype(FULL)
+        target[...] = total.astype(target.dtype)
 
     def give_back(self, t):
         me, count = self.me, self.count
-        q_left = t - (count - 1 - me)
-        q_right = count - 1 - (t - me)
+        q_left = 2 * (count - 1) - me - t
+        q_right = t - me
 
         def leftward():
             q = q_left
             self.back_core(q).wait()
 
-            @pl.when(me < count - 1)
-            def _():
-                push(self.left_in.at[q], self.left_in.at[q], self.sems[7].at[q], self.sems[10].at[q], self.right()).wait_recv()
-                self.added(self.core_out.at[q], [self.own.at[q], self.core_in.at[q], self.left_in.at[q]])
-
-            @pl.when(me == count - 1)
-            def _():
-                self.added(self.core_out.at[q], [self.own.at[q], self.core_in.at[q]])
-
-            self.back_left(q).start()
+            @pl.loop(0, CHUNKS)
+            def _(j):
+                base = [self.part(self.own, q, j), self.part(self.core_in, q, j)]
+                target = self.part(self.core_out, q, j)
+
+                @pl.when(me < count - 1)
+                def _():
+                    self.from_right(q, j).wait_recv()
+                    self.added(target, base + [self.part(self.left_in, q, j)])
+
+                @pl.when(me == count - 1)
+                def _():
+                    self.added(target, base)
+
+                self.back_left(q, j).start()
 
         def rightward():
             q = q_right
             self.back_core(q).wait()
 
-            @pl.when(me > 0)
-            def _():
-                push(self.right_in.at[q], self.right_in.at[q], self.sems[8].at[q], self.sems[11].at[q], self.left()).wait_recv()
-                self.added(self.core_out.at[q], [self.own.at[q], self.core_in.at[q], self.right_in.at[q]])
-
-            @pl.when(me == 0)
-            def _():
-                self.added(self.core_out.at[q], [self.own.at[q], self.core_in.at[q]])
-
-            self.back_right(q).start()
+            @pl.loop(0, CHUNKS)
+            def _(j):
+                base = [self.part(self.own, q, j), self.part(self.core_in, q, j)]
+                target = self.part(self.core_out, q, j)
+
+                @pl.when(me > 0)
+                def _():
+                    self.from_left(q, j).wait_recv()
+                    self.added(target, base + [self.part(self.right_in, q, j)])
+
+                @pl.when(me == 0)
+                def _():
+                    self.added(target, base)
+
+                self.back_right(q, j).start()
 
         pl.when((q_left >= 0) & (q_left < me))(leftward)
-        pl.when((t >= me) & (q_right > me))(rightward)
+        pl.when((q_right > me) & (q_right < count))(rightward)
 
     def finish(self, o_ref):
         me, count = self.me, self.count
         self.back_core(me).wait()
 
-        @pl.when(me < count - 1)
-        def _():
-            push(self.left_in.at[me], self.left_in.at[me], self.sems[7].at[me], self.sems[10].at[me], self.right()).wait_recv()
-
-        @pl.when(me > 0)
-        def _():
-            push(self.right_in.at[me], self.right_in.at[me], self.sems[8].at[me], self.sems[11].at[me], self.left()).wait_recv()
-
-        base = [self.own.at[me], self.core_in.at[me]]
-
-        @pl.when(me == 0)
-        def _():
-            self.added(o_ref, base + [self.left_in.at[me]])
-
-        @pl.when(me == count - 1)
-        def _():
-            self.added(o_ref, base + [self.right_in.at[me]])
-
-        @pl.when((me > 0) & (me < count - 1))
-        def _():
-            self.added(o_ref, base + [self.left_in.at[me], self.right_in.at[me]])
+        @pl.loop(0, CHUNKS)
+        def _(j):
+            size = o_ref.shape[0] // CHUNKS
+            target = o_ref.at[pl.ds(pl.multiple_of(j * size, size), size)]
+            base = [self.part(self.own, me, j), self.part(self.core_in, me, j)]
+
+            @pl.when(me < count - 1)
+            def _():
+                self.from_right(me, j).wait_recv()
+
+            @pl.when(me > 0)
+            def _():
+                self.from_left(me, j).wait_recv()
+
+            @pl.when(me == 0)
+            def _():
+                self.added(target, base + [self.part(self.left_in, me, j)])
+
+            @pl.when(me == count - 1)
+            def _():
+                self.added(target, base + [self.part(self.right_in, me, j)])
+
+            @pl.when((me > 0) & (me < count - 1))
+            def _():
+                self.added(
+                    target, base + [self.part(self.left_in, me, j), self.part(self.right_in, me, j)]
+                )
 
         @pl.when(me > 0)
         def _():
@@ -1253,15 +1133,17 @@
             def _():
                 self.to_left(me + k, k, self.x_ref).wait_send()
 
-        @pl.loop(0, count)
-        def _(q):
+        @pl.loop(0, count * CHUNKS)
+        def _(at):
+            q, j = at // CHUNKS, lax.rem(at, CHUNKS)
+
             @pl.when(q < me)
             def _():
-                self.back_left(q).wait_send()
+                self.back_left(q, j).wait_send()
 
             @pl.when(q > me)
             def _():
-                self.back_right(q).wait_send()
+                self.back_right(q, j).wait_send()
 
 
 GELU_ONE = 0.7978845608028654
@@ -1302,7 +1184,6 @@
         dw_load.start()
         bundle.greet(False, True)
         flow.start()
-        bundle.start()
         gw_load.wait()
         dw_load.wait()
 
@@ -1313,9 +1194,7 @@
             )
 
         def body(source):
-            here = pl.ds(pl.multiple_of(source * rows, rows), rows)
             x = flow.blocks[source].reshape(rows, width)
-            xt[:, here] = x.T
 
             @pl.loop(0, groups)
             def _(d):
@@ -1324,13 +1203,12 @@
                 u = flat_dot(x, gw[d, 1])
                 gate[source, :, columns] = g
                 up[source, :, columns] = u
-                act[:, columns] = (gelu_of(g)[0] * u).astype(LOW)
+                act[source, :, columns] = (gelu_of(g)[0] * u).astype(LOW)
 
             for copy in stores(source):
                 copy.start()
-            at[:, here] = act[...].T
             for d in range(groups):
-                out = flat_dot(act[...], dw[d])
+                out = flat_dot(act[source], dw[d])
                 for s in range(count):
                     columns = slice((s * groups + d) * out_cols, (s * groups + d + 1) * out_cols)
                     piece = out[:, s * out_cols : (s + 1) * out_cols]
@@ -1338,15 +1216,24 @@
                     flow.core_out[source, :, columns] = piece[share:].astype(LOW)
 
         flow.visit(body, bundle)
+
+        @pl.loop(0, count)
+        def _(source):
+            here = pl.ds(pl.multiple_of(source * rows, rows), rows)
+            xt[:, here] = flow.blocks[source].reshape(rows, width).T
+            at[:, here] = act[source].T
+
         xt_store = pltpu.make_async_copy(xt, xt_hbm, xt_sem)
         at_store = pltpu.make_async_copy(at, at_hbm, at_sem)
         xt_store.start()
         at_store.start()
 
-        @pl.loop(0, count - 1)
+        @pl.loop(count, 2 * count - 2)
         def _(t):
             flow.give_back(t)
 
+        for k in range(2, count):
+            bundle.step(k)
         flow.finish(o_ref)
         bundle.finish()
         xt_store.wait()
@@ -1380,7 +1267,7 @@
             pltpu.VMEM(down.shape, LOW),
             pltpu.VMEM((width, tokens), LOW),
             pltpu.VMEM((hidden, tokens), LOW),
-            pltpu.VMEM((rows, hidden), LOW),
+            pltpu.VMEM((count, rows, hidden), LOW),
             pltpu.VMEM((count, rows, hidden), FULL),
             pltpu.VMEM((count, rows, hidden), FULL),
         ]
@@ -1435,7 +1322,6 @@
             load.start()
         bundle.greet(False, True)
         flow.start()
-        bundle.start()
         loads[0].wait()
         loads[1].wait()
 
@@ -1522,12 +1408,18 @@
 
             down_store(d).start()
 
-        @pl.loop(0, count - 1)
+        @pl.loop(0, count - 2)
         def _(t):
-            flow.give_back(t)
             weights(t)
-
-        weights(groups - 1)
+            flow.give_back(count + t)
+
+        for k in range(2, count):
+            bundle.step(k)
+
+        @pl.loop(count - 2, groups)
+        def _(d):
+            weights(d)
+
         for which in range(2):
             gateup_store(groups - 1, which).wait()
         down_store(groups - 1).wait()
@@ -2128,11 +2020,22 @@
     middle = against(hidden_low, left_t).astype(LOW)
     right_raw = flat_dot(middle, right_w)
     right_n, scale_r = whole_norm(right_raw, gains[1])
-    projected = line_reduce(shares(flat_dot(attended, attend_w)), 5, True, 45)
+    projected, pergate_t, perproj_w = transfers(
+        [
+            Reduce(
+                shares(flat_dot(attended, attend_w)), (share, width), lambda ref, q: ref.at[q]
+            ),
+            along(pergate_t),
+            along(perproj_w),
+        ],
+        5,
+        45,
+        30,
+    )
     proj_n, scale_p = whole_norm(projected, gains[2])
     mixture = ((inputs + proj_n) + (hidden + right_n)) * HALF_ROOT
     ffn_n, scale_f = whole_norm(mixture, gains[3])
-    down_raw, spread_ft, act_t, gate_raw, up_raw, upstream, pergate_t, perproj_w = ffn_forward(
+    down_raw, spread_ft, act_t, gate_raw, up_raw, upstream = ffn_forward(
         ffn_n.astype(LOW),
         gateup_all,
         down_all,
@@ -2143,8 +2046,6 @@
                 lambda ref, q: ref.at[columns_of(q, share)],
                 lambda ref, at: ref.at[:, columns_of(at, width_a)],
             ),
-            along(pergate_t),
-            along(perproj_w),
         ],
         6,
     )
@@ -2191,19 +2092,6 @@
     d_mix, gain_grads[3] = whole_norm_backward(mixture, scale_f, gains[3], d_ffn)
     d_half = (d_out + d_mix) * HALF_ROOT
     d_proj, gain_grads[2] = whole_norm_backward(projected, scale_p, gains[2], d_half)
-    (spread_p,) = transfers(
-        [
-            Line(
-                d_proj.astype(LOW),
-                (cols_n, rows_n, share, width),
-                lambda ref, c, r: ref.at[c, r],
-                True,
-            )
-        ],
-        10,
-        40,
-    )
-    spread_p = spread_p.reshape(tokens, width)
     d_right, gain_grads[1] = whole_norm_backward(right_raw, scale_r, gains[1], d_half)
     d_right = d_right.astype(LOW)
     dw_right = inner_rows(middle, d_right)
@@ -2211,8 +2099,6 @@
     dw_left = inner_rows(d_middle, hidden_low)
     d_hidden_share = d_half + flat_dot(d_middle, left_t)
     inner_share = jnp.sum(d_hidden_share * gains[0] * inputs, axis=1)
-    d_attended = against(spread_p, attend_w).astype(LOW)
-    dw_attend = inner_rows(attended, spread_p).astype(LOW)
     small_parts = jnp.concatenate(
         [
             grad.astype(LOW).reshape(cols_n, -1, width)
@@ -2220,14 +2106,34 @@
         ],
         axis=1,
     )
-    d_queries, d_keys, d_values, small_parts, half_here, middle_here = head_backward(
+    spread_p, small_parts = transfers(
+        [
+            Line(
+                d_proj.astype(LOW),
+                (cols_n, rows_n, share, width),
+                lambda ref, c, r: ref.at[c, r],
+                True,
+            ),
+            Reduce(
+                small_parts,
+                (small_parts.shape[1], width_a),
+                lambda ref, q: ref.at[:, columns_of(q, width_a)],
+            ),
+        ],
+        10,
+        50,
+        30,
+    )
+    spread_p = spread_p.reshape(tokens, width)
+    d_attended = against(spread_p, attend_w).astype(LOW)
+    dw_attend = inner_rows(attended, spread_p).astype(LOW)
+    d_queries, d_keys, d_values, half_here, middle_here = head_backward(
         queries,
         keys,
         values,
         d_attended,
         spans,
         [
-            Reduce(small_parts),
             Swap(
                 d_half.astype(LOW),
                 (half_tok, width_a),
@@ -2253,19 +2159,33 @@
         ],
         axis=1,
     )
-    d_kv = line_reduce(kv_parts, 11, False, 20)
     d_q_raw, dg_query = whole_norm_backward(
         query_raw, query_scale, query_gain, turn_back(d_queries, all_cos, all_sin)
     )
+    d_q_all, d_kv = transfers(
+        [
+            Line(
+                d_q_raw.astype(LOW), (rows_n,) + d_q_raw.shape, lambda ref, c, r: ref.at[r]
+            ),
+            Reduce(kv_parts, kv_parts.shape[1:], lambda ref, q: ref.at[q], False),
+        ],
+        11,
+        45,
+        30,
+    )
     d_k_raw, dg_key = whole_norm_backward(
         key_raw, key_scale, key_gain, turn_back(d_kv[:quarter], own_cos, own_sin)
     )
     d_v_raw, _ = whole_norm_backward(value_raw, value_scale, 1.0, d_kv[quarter:])
-    d_raw = jnp.concatenate([d_q_raw, d_k_raw, d_v_raw], axis=0).astype(LOW)
+    d_raw = jnp.stack([d_k_raw, d_v_raw]).astype(LOW)
     gateup_squares = jnp.sum(jnp.square(g_gateup.astype(FULL)))
-    spread_q, g_gateup, g_attend = transfers(
+    d_kv_all, g_gateup, g_attend = transfers(
         [
-            Line(d_raw, (rows_n,) + d_raw.shape, lambda ref, c, r: ref.at[r]),
+            Line(
+                d_raw,
+                (2, tokens, HEAD_WIDTH),
+                lambda ref, c, r: ref.at[:, columns_of(r, quarter)],
+            ),
             Swap(
                 g_gateup,
                 w_gateup.shape,
@@ -2277,9 +2197,7 @@
         12,
         100,
     )
-    d_q_all = spread_q[:, :tokens]
-    d_k_all = spread_q[:, tokens : tokens + quarter].reshape(tokens, HEAD_WIDTH)
-    d_v_all = spread_q[:, tokens + quarter :].reshape(tokens, HEAD_WIDTH)
+    d_k_all, d_v_all = d_kv_all[0], d_kv_all[1]
     d_hidden = against(d_k_all, key_w) + against(d_v_all, value_w)
     for k in range(heads_here):
         d_hidden = d_hidden + against(d_q_all[k], query_w[k])

time: 866 us -> 815 us (0.941)
  Pallas kernels: 712 us -> 659 us
    pallas_call x2 -> x0, Pallas kernels: 64.1 us -> none  [line_reduce(): pl.pallas_call(kernel, out_shape=jax.ShapeDtypeStruct((high, wide), FULL)...]
    pallas_call x4 -> x6, Pallas kernels: 284 us -> 347 us  [transfers(): pl.pallas_call(kernel, out_shape=bundle.shapes, in_specs=bundle.specs, ou...]
    pallas_call x1, Pallas kernels: 112 us -> 81.7 us  [ffn_forward(): pl.pallas_call(kernel, out_shape=[jax.ShapeDtypeStruct((share, width), FU...]
    pallas_call x1, Pallas kernels: 38.9 us -> 22.9 us  [head_backward(): pl.pallas_call(kernel, out_shape=[jax.ShapeDtypeStruct(queries.shape, FUL...]
    unnamed x247 -> x249, local copies, waits for them, and re-layouts: 30.5 us -> 33.4 us
where the time goes in v6:
time: 815 us; the launch traced here: 806 us
  Pallas kernels  659 us (81%)
  other arithmetic  47.8 us (6%)
  local copies, waits for them, and re-layouts  45.9 us (6%)
  matrix products  33 us (4%)
  between operations  19.9 us (2%)
    pallas_call x6, Pallas kernels, transfers(): pl.pallas_call(kernel, out_shape=bundle.shapes, in_specs=bundle.specs, ou...  347 us
    pallas_call x1, Pallas kernels, ffn_backward(): pl.pallas_call(kernel, out_shape=[jax.ShapeDtypeStruct((share, width), FU...  90.9 us
    pallas_call x1, Pallas kernels, ffn_forward(): pl.pallas_call(kernel, out_shape=[jax.ShapeDtypeStruct((share, width), FU...  81.7 us
    pallas_call x1, Pallas kernels, attention_forward_head(): pl.pallas_call(kernel, out_shape=[jax.ShapeDtypeStruct((tokens, width), L...  46.3 us
    pallas_call x1, Pallas kernels, shard_total(): pl.pallas_call(kernel, out_shape=[jax.ShapeDtypeStruct(shape, FULL) for s...  35.8 us
    unnamed x249, local copies, waits for them, and re-layouts  33.4 us
    pallas_call x1, Pallas kernels, head_backward(): pl.pallas_call(kernel, out_shape=[jax.ShapeDtypeStruct(queries.shape, FUL...  22.9 us
    pallas_call x1, Pallas kernels, adam_all(): pl.pallas_call(kernel, out_shape=[jax.ShapeDtypeStruct((8, 128), FULL)] +...  20.4 us
  transfers between devices with their start and end apart: 4, of which 0 were waited for; matrix products, arithmetic and copies ran while one was open for 8% of the time, Pallas kernels for 44%

profile of v6, /device:TPU:0, one launch (start us, length us, event | category | flops | bytes accessed | tf_op | source)
XLA Modules:
  0.0 806.0 jit_solution(16430555428703893427)
XLA Ops:
  7.3 2.6 convert_element_type.196.refs_0_
  10.9 57.5 %shard_map.645 = (bf16[2,2048,256]{2,1,0:T(8,128)(2,1)}, bf16[256,512]{1,0:T(8,128)(2,1)S(1)}, bf16[4,512,512]{2,1,0:T(8,128)(2,1)S(1)}, f32[32,512]{1,0:T(8,128...) custom-call(bf16[2,512,1024]{2,1,0:T(8,128)(2,1)S(1)} %convert_element_type.196.refs_, ...), custom_call_target="tpu_custom_call" | custom-call | bytes 180000000 | tf_op jit(solution)/shard_map/pallas_call | solution.py:761
  68.4 1.3 copy-done.2
  71.9 2.7 convert_element_type.204
  74.6 1.6 copy-done.3
  76.2 95.5 %shard_map.646 = (bf16[1024,2048]{1,0:T(8,128)(2,1)S(1)}, bf16[2048,256]{1,0:T(8,128)(2,1)S(1)}, bf16[2048,256]{1,0:T(8,128)(2,1)S(1)}, bf16[2048,256]{1,0:T(8,1...) custom-call(bf16[512,512]{1,0:T(8,128)(2,1)S(1)} %copy-done.30, ...), custom_call_target="tpu_custom_call" | custom-call | bytes 285000000 | tf_op jit(solution)/shard_map/pallas_call | solution.py:761
  171.7 2.0 copy-done.5
  177.2 1.9 multiply_sine_fusion
  179.1 46.3 %shard_map.647 = (bf16[1024,2048]{1,0:T(8,128)(2,1)}, f32[1024,128]{1,0:T(8,128)S(1)}, f32[1024,256]{1,0:T(8,128)S(1)}, f32[1024,256]{1,0:T(8,128)}, f32[1024,25...) custom-call(s32[3]{0:T(128)S(1)} %pad_add_fusion.spans_ref, ...), custom_call_target="tpu_custom_call" | custom-call | bytes 120000000 | tf_op jit(solution)/shard_map/pallas_call | solution.py:1686
  234.3 47.2 %shard_map.648 = (f32[128,2048]{1,0:T(8,128)S(1)}, bf16[256,2048]{1,0:T(8,128)(2,1)S(1)}, bf16[256,2048]{1,0:T(8,128)(2,1)S(1)}) custom-call(bf16[2,4,128,2048]{3,2,1,0:T(8,128)(2,1)S(1)} %bitcast.184, bf16[128,512]{1,0:T(8,128)(2,1)S(1)} %copy-done.44, bf16[128,512]{1,0:T(8,128)(2,1)S(1)} %copy-done.46), custom_call_target="tpu_custom_call" | custom-call | bytes 135000000 | tf_op jit(solution)/shard_map/pallas_call | solution.py:761
  282.9 1.4 convolution_convert_fusion.14
  285.9 1.7 multiply_reduce_fusion.16
  289.5 81.7 %shard_map.649 = (f32[128,2048]{1,0:T(8,128)}, bf16[2048,1024]{1,0:T(8,128)(2,1)}, bf16[1024,1024]{1,0:T(8,128)(2,1)}, f32[4,256,1024]{2,1,0:T(8,128)}, f32[4,25...) custom-call(bf16[128,2048]{1,0:T(8,128)(2,1)} %multiply_convert_fusion.x_ref, bf16[4,2,2048,256]{3,2,1,0:T(8,128)(2,1)} %bitcast.205, ...), custom_call_target="tpu_custom_call" | custom-call | bytes 240000000 | tf_op jit(solution)/shard_map/pallas_call | solution.py:1251
  371.2 1.4 multiply_reduce_fusion.15
  372.6 1.8 multiply_add_fusion
  374.4 1.5 fusion.77
  376.3 1.9 fusion.20
  378.6 1.4 fusion.84
  382.3 90.9 %shard_map.650 = (f32[128,2048]{1,0:T(8,128)}, bf16[4,2,2048,256]{3,2,1,0:T(8,128)(2,1)}, bf16[4,1024,512]{2,1,0:T(8,128)(2,1)}, bf16[512,512]{1,0:T(8,128)(2,1)}) custom-call(bf16[128,2048]{1,0:T(8,128)(2,1)} %subtract_convert_fusion.3.x_ref, bf16[4,2,2048,256]{3,2,1,0:T(8,128)(2,1)} %bitcast.206, bf16[4,1024,512]{2,1,0:T(8,128)(2,1)} %bitcast.209, ...), custom_call_target="tpu_custom_call" | custom-call | bytes 270000000 | tf_op jit(solution)/shard_map/pallas_call | solution.py:1432
  473.3 1.5 copy-done.4
  478.3 1.3 multiply_reduce_fusion.26
  479.6 1.8 dynamic-slice_reduce_fusion
  481.4 1.4 multiply_reduce_fusion.9
  484.0 1.7 multiply_reduce_fusion.5
  487.0 1.4 multiply_reduce_fusion.6
  489.2 1.7 convolution_convert_fusion.5
  492.5 44.9 %shard_map.651 = (bf16[2,4,128,2048]{3,2,1,0:T(8,128)(2,1)S(1)}, f32[320,512]{1,0:T(8,128)S(1)}) custom-call(bf16[128,2048]{1,0:T(8,128)(2,1)S(1)} %get-tuple-element.281.refs_0_, bf16[2,320,2048]{2,1,0:T(8,128)(2,1)S(1)} %pad_maximum_fusion.refs_1_), custom_call_target="tpu_custom_call" | custom-call | bytes 150000000 | tf_op jit(solution)/shard_map/pallas_call | solution.py:761
  540.2 22.9 %shard_map.652 = (f32[1024,256]{1,0:T(8,128)S(1)}, f32[1024,256]{1,0:T(8,128)S(1)}, f32[1024,256]{1,0:T(8,128)}, bf16[512,512]{1,0:T(8,128)(2,1)S(1)}, bf16[512,64]{1,0:T(8,128)(2,1)S(1)}) custom-call(s32[3]{0:T(128)S(1)} %pad_add_fusion.spans_ref, bf16[1024,256]{1,0:T(8,128)(2,1)S(1)} %copy-done.32, bf16[1024,256]{1,0:T(8,128)(2,1)S(1)} %copy-done.34, ...), custom_call_target="tpu_custom_call" | custom-call | bytes 75000000 | tf_op jit(solution)/shard_map/pallas_call | solution.py:1750
  569.2 2.1 fusion.4
  571.4 2.2 convolution_convert_fusion.3.refs_2_
  573.6 2.3 multiply_subtract_fusion
  576.9 40.3 %shard_map.653 = (bf16[4,1024,256]{2,1,0:T(8,128)(2,1)S(1)}, f32[512,256]{1,0:T(8,128)S(1)}) custom-call(bf16[1024,256]{1,0:T(8,128)(2,1)S(1)} %subtract_convert_fusion.refs_0_, bf16[4,512,256]{2,1,0:T(8,128)(2,1)S(1)} %pad_maximum_fusion.2.refs_1_), custom_call_target="tpu_custom_call" | custom-call | bytes 135000000 | tf_op jit(solution)/shard_map/pallas_call | solution.py:761
  617.2 1.3 copy-done.16
  619.5 1.3 multiply_reduce_fusion.22
  623.4 1.6 copy-done.8
  625.0 61.4 %shard_map.654 = (bf16[2,1024,256]{2,1,0:T(8,128)(2,1)S(1)}, bf16[2,512,1024]{2,1,0:T(8,128)(2,1)S(1)}, bf16[256,512]{1,0:T(8,128)(2,1)S(1)}) custom-call(bf16[2,256,256]{2,1,0:T(8,128)(2,1)S(1)} %pad_maximum_fusion.7.refs_0_, bf16[2,2048,256]{2,1,0:T(8,128)(2,1)S(1)} %bitcast.185, bf16[256,2048]{1,0:T(8,128)(2,1)S(1)} %copy-done.25), custom_call_target="tpu_custom_call" | custom-call | bytes 300000000 | tf_op jit(solution)/shard_map/pallas_call | solution.py:761
  686.3 1.3 copy-done.14
  688.5 1.7 multiply_reduce_fusion
  691.5 1.7 fusion.9
  693.3 1.9 fusion.10
  696.0 1.9 fusion.5
  697.8 1.7 fusion.6
  704.2 3.2 multiply_reduce_fusion.2
  709.5 35.8 %shard_map.655 = (f32[512,256]{1,0:T(8,128)S(1)}, f32[512,256]{1,0:T(8,128)S(1)}, f32[320,128]{1,0:T(8,128)S(1)}, bf16[4,4,256,128]{3,2,1,0:T(8,128)(2,1)S(1)}, ...) custom-call(bf16[4,512,256]{2,1,0:T(8,128)(2,1)S(1)} %pad_maximum_fusion.3.q_ref, ...), custom_call_target="tpu_custom_call" | custom-call | bytes 120000000 | tf_op jit(solution)/shard_map/pallas_call | solution.py:855
  749.9 3.2 fusion.18
  757.2 14.3 %shard_map.656.x_ref = f32[128,128]{1,0:T(8,128)S(1)} custom-call(f32[128,128]{1,0:T(8,128)S(1)} %pad_maximum_fusion.8.x_ref), custom_call_target="tpu_custom_call" | custom-call | bytes 42000000 | tf_op jit(solution)/shard_map/pallas_call | solution.py:1500
  771.6 1.5 slice.288.refs_35_
  775.5 20.4 %shard_map.657 = (f32[8,128]{1,0:T(8,128)}, f32[1024,1024]{1,0:T(8,128)}, f32[1024,1024]{1,0:T(8,128)}, f32[1024,1024]{1,0:T(8,128)}, f32[4096,128]{1,0:T(8,128)...) custom-call(f32[128,128]{1,0:T(8,128)} %copy-done.29, ...), custom_call_target="tpu_custom_call" | custom-call | bytes 75000000 | tf_op jit(solution)/shard_map/pallas_call | solution.py:1600
  (372 shorter events, 64.3 us)
Async XLA Ops:
  7.2 64.5 %copy-start = (s32[4,2]{0,1:T(2,128)S(1)}, s32[4,2]{0,1:T(2,128)}, u32[]{:S(2)}) copy-start(s32[4,2]{0,1:T(2,128)} %param.44) | copy-start | bytes 100
  7.3 224.6 %all-gather.5.cloned.1.call-start = ((), (), s32[]{:S(2)}) async-start(), calls=%async_computation.2 | async-start | bytes 10485760 | tf_op jit(solution)/shard_map/all_gather | solution.py:1906
  10.9 60.2 %copy-start.119 = (s32[4]{0:T(128)S(1)}, s32[4]{0:T(128)}, u32[]{:S(2)}) copy-start(s32[4]{0:T(128)} %param.43) | copy-start | bytes 52
  71.1 3.6 copy-start.30
  71.1 3.6 copy-start.48
  71.1 3.5 copy-start.50
  71.1 218.4 %all-gather.7.cloned.1.call-start = ((), (), s32[]{:S(2)}) async-start(), calls=%async_computation.3 | async-start | bytes 5242880 | tf_op jit(solution)/shard_map/all_gather | solution.py:2007
  175.6 3.5 copy-start.21
  175.6 49.8 %copy-start.51 = (bf16[1024,256]{1,0:T(8,128)(2,1)}, bf16[1024,256]{1,0:T(8,128)(2,1)S(1)}, u32[]{:S(2)}) copy-start(bf16[1024,256]{1,0:T(8,128)(2,1)S(1)} %get-tuple-element.170) | copy-start | bytes 1572868
  175.7 3.5 copy-start.107
  179.1 106.8 %copy-start.90 = (f32[1,2048]{1,0:T(1,128)}, f32[1,2048]{1,0:T(1,128)S(1)}, u32[]{:S(2)}) copy-start(f32[1,2048]{1,0:T(1,128)S(1)} %get-tuple-element.302) | copy-start | bytes 24580
  231.9 333.8 %reduce-scatter.7.cloned.1.call-start = ((), (), s32[]{:S(2)}) async-start(), calls=%async_computation.4 | async-start | bytes 10485760
  234.3 48.6 %copy-start.41 = (bf16[64,2048]{1,0:T(8,128)(2,1)S(1)}, bf16[64,2048]{1,0:T(8,128)(2,1)}, u32[]{:S(2)}) copy-start(bf16[64,2048]{1,0:T(8,128)(2,1)} %copy-done.40) | copy-start | bytes 786436
  282.9 4.6 copy-start.111
  284.4 3.2 copy-start.93
  285.9 3.6 copy-start.102
  288.2 83.0 %copy-start.109 = (f32[128]{0:T(128)}, f32[128]{0:T(128)S(1)}, u32[]{:S(2)}) copy-start(f32[128]{0:T(128)S(1)} %get-tuple-element.268) | copy-start | bytes 1540
  473.2 10.8 %copy-start.91 = (f32[1,2048]{1,0:T(1,128)S(1)}, f32[1,2048]{1,0:T(1,128)}, u32[]{:S(2)}) copy-start(f32[1,2048]{1,0:T(1,128)} %copy-done.90) | copy-start | bytes 24580
  473.2 10.8 %copy-start.110 = (f32[128]{0:T(128)S(1)}, f32[128]{0:T(128)}, u32[]{:S(2)}) copy-start(f32[128]{0:T(128)} %copy-done.109) | copy-start | bytes 1540
  473.2 234.2 %reduce-scatter.9.cloned.1.call-start = ((), (), s32[]{:S(2)}) async-start(), calls=%async_computation.5 | async-start | bytes 5242880
  475.8 9.9 %copy-start.115 = (f32[128]{0:T(128)S(1)}, f32[128]{0:T(128)}, u32[]{:S(2)}) copy-start(f32[128]{0:T(128)} %get-tuple-element.267) | copy-start | bytes 1540
  476.9 7.1 copy-start.58
  476.9 8.8 %copy-start.67 = (f32[128,2048]{1,0:T(8,128)S(1)}, f32[128,2048]{1,0:T(8,128)}, u32[]{:S(2)}) copy-start(f32[128,2048]{1,0:T(8,128)} %copy-done.66) | copy-start | bytes 3145732
  476.9 8.8 %copy-start.72 = (f32[128,2048]{1,0:T(8,128)S(1)}, f32[128,2048]{1,0:T(8,128)}, u32[]{:S(2)}) copy-start(f32[128,2048]{1,0:T(8,128)} %get-tuple-element.180) | copy-start | bytes 3145732
  492.5 45.1 %copy-start.70 = (bf16[4,256,4,128]{1,3,0,2:T(8,128)(2,1)S(1)}, bf16[4,256,4,128]{1,3,0,2:T(8,128)(2,1)}, u32[]{:S(2)}) copy-start(bf16[4,256,4,128]{1,3,0,2:T(8,128)(2,1)} %copy-done.69) | copy-start | bytes 3145732
  537.5 28.1 %copy-start.79 = (bf16[320,512]{1,0:T(8,128)(2,1)}, bf16[320,512]{1,0:T(8,128)(2,1)S(1)}, u32[]{:S(2)}) copy-start(bf16[320,512]{1,0:T(8,128)(2,1)S(1)} %convert_element_type.238) | copy-start | bytes 983044
  537.5 28.1 %copy-start.83 = (bf16[128,512]{1,0:T(8,128)(2,1)}, bf16[128,512]{1,0:T(8,128)(2,1)S(1)}, u32[]{:S(2)}) copy-start(bf16[128,512]{1,0:T(8,128)(2,1)S(1)} %slice.302) | copy-start | bytes 393220
  567.9 3.4 copy-start.53
  569.1 4.6 copy-start.37
  576.4 43.2 %copy-start.100 = (f32[256]{0:T(256)S(1)}, f32[256]{0:T(256)}, u32[]{:S(2)}) copy-start(f32[256]{0:T(256)} %get-tuple-element.312) | copy-start | bytes 3076
  576.8 44.1 %copy-start.104 = (f32[256]{0:T(256)S(1)}, f32[256]{0:T(256)}, u32[]{:S(2)}) copy-start(f32[256]{0:T(256)} %get-tuple-element.311) | copy-start | bytes 3076
  625.0 63.6 %copy-start.9 = (bf16[1,2,2048,256]{3,2,1,0:T(8,128)(2,1)S(1)}, bf16[1,2,2048,256]{3,2,1,0:T(8,128)(2,1)}, u32[]{:S(2)}) copy-start(bf16[1,2,2048,256]{3,2,1,0:T(8,128)(2,1)} %reduce-scatter.7.cloned.1.call-done) | copy-start | bytes 6291460
  687.7 5.6 copy-start.26
  696.0 3.6 copy-start.118
  709.5 40.3 %copy-start.105 = (f32[512]{0:T(512)S(1)}, f32[512]{0:T(512)}, u32[]{:S(2)}) copy-start(f32[512]{0:T(512)} %get-tuple-element.263) | copy-start | bytes 6148
  709.5 40.3 %copy-start.106 = (f32[512]{0:T(512)S(1)}, f32[512]{0:T(512)}, u32[]{:S(2)}) copy-start(f32[512]{0:T(512)} %get-tuple-element.264) | copy-start | bytes 6148
  747.0 6.1 copy-start.12
  747.0 6.1 copy-start.13
  747.0 6.1 copy-start.20
  749.9 3.3 copy-start.95
  749.9 3.3 copy-start.96
  749.9 3.3 copy-start.97
  749.9 3.3 copy-start.98
  749.9 3.4 copy-start.71
  749.9 7.2 copy-start.117
  771.5 4.0 copy-start.29
  775.5 22.8 %copy-start.85 = (bf16[512,512]{1,0:T(8,128)(2,1)S(1)}, bf16[512,512]{1,0:T(8,128)(2,1)}, u32[]{:S(2)}) copy-start(bf16[512,512]{1,0:T(8,128)(2,1)} %get-tuple-element.370) | copy-start | bytes 1572868
  775.5 23.5 %copy-start.1 = (s32[4,2]{0,1:T(2,128)S(1)}, s32[4,2]{0,1:T(2,128)}, u32[]{:S(2)}) copy-start(s32[4,2]{0,1:T(2,128)} %param.44) | copy-start | bytes 100
  (76 other events, 118.4 us)
Sparse Core Ops, SparseCore 0:
  71.2 93.6 all-gather.4
  232.0 51.0 all-gather.6
  473.3 84.3 reduce-scatter.6
  565.8 51.3 reduce-scatter.8

commit v7 on v6

--- a/solution.py
+++ b/solution.py
@@ -1,3 +1,5 @@
+import functools
+
 import jax
 import jax.numpy as jnp
 from jax import lax
@@ -746,27 +748,253 @@
             item.finish()
 
 
-def transfers(items, ident, micros, mebibytes=16):
+def transfers(items, ident, micros, mebibytes=16, work=None, arrays=(), shapes=()):
     bundle = Bundle(items)
-    number = bundle.number
+    number, given, made = bundle.number, len(arrays), len(shapes)
 
     def kernel(*refs):
-        bundle.bind(refs[:number], refs[number : 2 * number], refs[2 * number :])
+        inputs, refs = refs[:given], refs[given:]
+        x_refs, refs = refs[:number], refs[number:]
+        outputs, refs = refs[:made], refs[made:]
+        bundle.bind(x_refs, refs[:number], refs[number:])
         bundle.greet()
         bundle.start()
+        if work:
+            work(inputs, outputs)
         for k in range(1, bundle.sizes[0]):
             bundle.step(k)
         bundle.finish()
 
+    vmem = pl.BlockSpec(memory_space=pltpu.VMEM)
     return pl.pallas_call(
         kernel,
-        out_shape=bundle.shapes,
-        in_specs=bundle.specs,
-        out_specs=bundle.specs,
+        out_shape=list(shapes) + bundle.shapes,
+        in_specs=[vmem] * given + bundle.specs,
+        out_specs=[vmem] * made + bundle.specs,
         scratch_shapes=bundle.scratch,
         compiler_params=params(ident, mebibytes),
         cost_estimate=cost(micros),
-    )(*bundle.sources)
+    )(*arrays, *bundle.sources)
+
+
+def local(function, shapes, *arrays, mebibytes=60):
+    def kernel(*refs):
+        results = function(*[ref[...] for ref in refs[: len(arrays)]])
+        for ref, value in zip(refs[len(arrays) :], results):
+            ref[...] = value.astype(ref.dtype)
+
+    vmem = pl.BlockSpec(memory_space=pltpu.VMEM)
+    return pl.pallas_call(
+        kernel,
+        out_shape=[jax.ShapeDtypeStruct(shape, kind) for shape, kind in shapes],
+        in_specs=[vmem] * len(arrays),
+        out_specs=[vmem] * len(shapes),
+        compiler_params=pltpu.CompilerParams(vmem_limit_bytes=mebibytes * 2**20),
+        cost_estimate=cost(5),
+    )(*arrays)
+
+
+def norm_back(values_in, gain, grad_out):
+    scale = lax.rsqrt(jnp.mean(values_in * values_in, axis=-1, keepdims=True) + EPS)
+    weighted = grad_out * gain
+    inner = jnp.mean(weighted * values_in, axis=-1, keepdims=True)
+    return (
+        scale * weighted - values_in * (scale * scale * scale) * inner,
+        jnp.sum(grad_out * values_in * scale, axis=0, keepdims=True),
+    )
+
+
+def mix(acts, projected, gains, left_t, right_w):
+    inputs = acts.astype(FULL)
+    hidden, _ = whole_norm(inputs, gains[0:1])
+    hidden_low = hidden.astype(LOW)
+    middle = against(hidden_low, left_t).astype(LOW)
+    right_raw = flat_dot(middle, right_w)
+    right_n, _ = whole_norm(right_raw, gains[1:2])
+    proj_n, _ = whole_norm(projected, gains[2:3])
+    mixture = ((inputs + proj_n) + (hidden + right_n)) * HALF_ROOT
+    ffn_n, _ = whole_norm(mixture, gains[3:4])
+    return hidden_low, middle, right_raw, mixture, ffn_n
+
+
+def per_layer_both(mixture, down_raw, gains, extras, pergate_t, perproj_w, upstream):
+    extras, upstream = extras.astype(FULL), upstream.astype(FULL)
+    down_n, _ = whole_norm(down_raw, gains[4:5])
+    block_out = mixture + down_n
+    out_low = block_out.astype(LOW)
+    pgate = against(out_low, pergate_t)
+    curve, slope = gelu_of(pgate)
+    pact = (curve * extras).astype(LOW)
+    perproj = flat_dot(pact, perproj_w)
+    perproj_n, _ = whole_norm(perproj, gains[5:6])
+    result = block_out + perproj_n
+    d_perproj, gain_five = norm_back(perproj, gains[5:6], upstream)
+    d_perproj = d_perproj.astype(LOW)
+    d_pact = against(d_perproj, perproj_w)
+    d_pgate = (d_pact * extras * slope).astype(LOW)
+    d_out = upstream + flat_dot(d_pgate, pergate_t)
+    d_down, gain_four = norm_back(down_raw, gains[4:5], d_out)
+    return (
+        result,
+        d_out,
+        d_down,
+        inner_rows(pact, d_perproj),
+        inner_rows(d_pgate, out_low),
+        gain_four,
+        gain_five,
+    )
+
+
+def mix_back(
+    d_out, d_ffn, mixture, projected, right_raw, gains, acts, left_t, right_w, hidden_low, middle, dw_pergate, dw_perproj
+):
+    d_mix, gain_three = norm_back(mixture, gains[3:4], d_ffn)
+    d_half = (d_out + d_mix) * HALF_ROOT
+    d_proj, gain_two = norm_back(projected, gains[2:3], d_half)
+    d_right, gain_one = norm_back(right_raw, gains[1:2], d_half)
+    d_right = d_right.astype(LOW)
+    dw_right = inner_rows(middle, d_right).astype(LOW)
+    d_middle = against(d_right, right_w).astype(LOW)
+    dw_left = inner_rows(d_middle, hidden_low).astype(LOW)
+    d_hidden = d_half + flat_dot(d_middle, left_t)
+    inner = row_sums(d_hidden * gains[0:1] * acts.astype(FULL))
+    parts = []
+    for core in range(2):
+        for grad in (dw_left, dw_right, dw_pergate, dw_perproj):
+            high = grad.shape[0] // 2
+            parts.append(grad[core * high : (core + 1) * high])
+    return d_proj, d_half, d_middle, jnp.concatenate(parts, axis=0), inner, gain_one, gain_two, gain_three
+
+
+def row_sums(values_in):
+    ones = jnp.ones((8, values_in.shape[1]), FULL)
+    return lax.dot_general(
+        ones,
+        values_in,
+        (((1,), (1,)), ((), ())),
+        precision=lax.Precision.HIGHEST,
+        preferred_element_type=FULL,
+    )
+
+
+def shard_parts(sums, extents):
+    out_cols, data = 128, sums.shape[1] // 128
+    parts = []
+    for at in range(data):
+        start = 0
+        for rows, by_rows in extents:
+            if by_rows:
+                high = rows // data
+                cut = sums[start + at * high : start + (at + 1) * high]
+                parts += [cut[:, k * out_cols : (k + 1) * out_cols] for k in range(data)]
+            else:
+                parts.append(sums[start : start + rows, at * out_cols : (at + 1) * out_cols])
+            start += rows
+    return jnp.concatenate(parts, axis=0)
+
+
+def key_value_ends(hidden, d_key, d_value, qkv_w, d_hidden, acts, gain, sums, extents):
+    first = lax.axis_index("col") == 0
+    key_w = jnp.where(first, qkv_w[0, :, HEAD_WIDTH:], qkv_w[1, :, HEAD_WIDTH:])
+    value_w = jnp.where(first, qkv_w[2, :, HEAD_WIDTH:], qkv_w[3, :, HEAD_WIDTH:])
+    d_hidden = d_hidden + against(d_key, key_w) + against(d_value, value_w)
+    return (
+        jnp.concatenate([inner_rows(hidden, d_key), inner_rows(hidden, d_value)], axis=0),
+        d_hidden,
+        row_sums(d_hidden * gain[0:1] * acts.astype(FULL)),
+        shard_parts(sums, extents),
+    )
+
+
+def input_ends(pair, half, middle, left_t, acts, scale, gains, inner, inner_share, grads, gateup_squares, gain_grads, dg_query, dg_key, top):
+    half_tok, wide = acts.shape
+    rows_n = inner.shape[1]
+    width = gain_grads[0].shape[1]
+    lanes = width // 128
+    head_rows = (QUERY_HEADS + 1) * HEAD_WIDTH // 128
+    sum_rows = 6 * lanes + head_rows
+    high = -(-(sum_rows + 1) // 8) * 8 + 8
+    given = (pair, half, middle, left_t, acts, scale, gains, inner, inner_share, gateup_squares, dg_query, dg_key, top)
+    given += tuple(gain_grads) + tuple(grads)
+
+    def kernel(*refs):
+        pair, half, middle, left_t, acts, scale, gains, inner, inner_share, gateup_squares, dg_query, dg_key, top = refs[:13]
+        gain_grads, grads = refs[13:18], refs[18:23]
+        out_ref, small_ref = refs[23:]
+        me, column = lax.axis_index("row"), lax.axis_index("col")
+        total = None
+        for core in range(2):
+            for row in range(rows_n):
+                part = jnp.where(
+                    column == 0, inner[core, row, :, :half_tok], inner[core, row, :, half_tok:]
+                )
+                total = part if total is None else total + part
+        shares = jnp.concatenate(
+            [jnp.where(column == 0, inner_share[0, row], inner_share[1, row]) for row in range(rows_n)],
+            axis=1,
+        )
+        mean = ((total + shares) / MODEL_WIDTH).T[:, :1]
+        inputs = acts[...].astype(FULL)
+        factor = scale[:, :1]
+        gain = gains[0:1]
+        left = left_t[:, pl.ds(pl.multiple_of(me * wide, wide), wide)]
+        d_hidden = (
+            pair[0].astype(FULL) + pair[1].astype(FULL) + half[...].astype(FULL) + flat_dot(middle[...], left)
+        )
+        out_ref[...] = (
+            half[...].astype(FULL)
+            + factor * (d_hidden * gain)
+            - inputs * (factor * factor * factor) * mean
+        ).astype(LOW)
+        small_ref[...] = jnp.zeros(small_ref.shape, FULL)
+        gain_zero = jnp.sum(d_hidden * inputs * factor, axis=0, keepdims=True)
+        for k in range(wide // 128):
+            small_ref[pl.ds(me * (wide // 128) + k, 1)] = gain_zero[:, k * 128 : (k + 1) * 128]
+        for at, grad in enumerate(gain_grads):
+            for k in range(lanes):
+                small_ref[(at + 1) * lanes + k : (at + 1) * lanes + k + 1] = grad[:, k * 128 : (k + 1) * 128]
+        head = column * rows_n + me
+        for k in range(HEAD_WIDTH // 128):
+            cut = slice(k * 128, (k + 1) * 128)
+            small_ref[pl.ds(6 * lanes + head * (HEAD_WIDTH // 128) + k, 1)] = dg_query[:, cut]
+            last = 6 * lanes + QUERY_HEADS * (HEAD_WIDTH // 128) + k
+            small_ref[last : last + 1] = dg_key[:, cut]
+        squares = jnp.zeros((1, 128), FULL)
+        first = jnp.where(column == 0, 1.0, 0.0)
+        for grad, weight in zip(grads, (1.0, first, 1.0, 1.0, 1.0)):
+            values = grad[...].astype(FULL).reshape(-1, grad.shape[-1])
+            line = jnp.sum(values * values, axis=0, keepdims=True)
+            for cut in range(0, values.shape[1], 128):
+                squares = squares + weight * line[:, cut : cut + 128]
+        line = jnp.sum(gateup_squares[...], axis=0, keepdims=True)
+        for cut in range(0, line.shape[1], 128):
+            squares = squares + line[:, cut : cut + 128]
+        small_ref[sum_rows : sum_rows + 1] = jnp.broadcast_to(
+            jnp.sum(squares, axis=1, keepdims=True), (1, 128)
+        )
+        places = lax.broadcasted_iota(jnp.int32, (8, 128), 1)
+        small_ref[high - 8 :] = jnp.where(places == head, top[...], NEGATIVE)
+
+    vmem = pl.BlockSpec(memory_space=pltpu.VMEM)
+    return pl.pallas_call(
+        kernel,
+        out_shape=[
+            jax.ShapeDtypeStruct((half_tok, wide), LOW),
+            jax.ShapeDtypeStruct((high, 128), FULL),
+        ],
+        in_specs=[vmem] * 23,
+        out_specs=[vmem] * 2,
+        compiler_params=pltpu.CompilerParams(vmem_limit_bytes=24 * 2**20),
+        cost_estimate=cost(3),
+    )(*given)
+
+
+def key_value_back(d_kv, key_raw, value_raw, heads, cos_tab, sin_tab):
+    key_gain = heads[QUERY_HEADS:]
+    quarter = key_raw.shape[0]
+    d_key, dg_key = norm_back(key_raw, key_gain, turn_back(d_kv[:quarter], cos_tab, sin_tab))
+    d_value, _ = norm_back(value_raw, 1.0, d_kv[quarter:])
+    return d_key, d_value, dg_key
 
 
 def shard_total(query_parts, kv_parts, flat_parts, items, ident):
@@ -1003,7 +1231,10 @@
         def _():
             self.to_core(me + k, self.x_ref).wait()
 
-    def visit(self, body, bundle):
+    def reach(self):
+        return jnp.maximum(self.me, self.count - 1 - self.me)
+
+    def visit(self, body, bundle, after=None):
         me, count = self.me, self.count
 
         @pl.loop(0, count)
@@ -1027,6 +1258,8 @@
                     body(source)
                     self.back_core(source).start()
 
+            if after:
+                after(k, k - self.reach() - 1)
             self.give_back(k)
 
     def added(self, target, terms):
@@ -1365,10 +1598,6 @@
             flow.own[source] = total[:share]
             flow.core_out[source] = total[share:].astype(LOW)
 
-        flow.visit(body, bundle)
-        loads[2].wait()
-        loads[3].wait()
-
         def gateup_store(d, which):
             return pltpu.make_async_copy(stage.at[which], dgu_hbm.at[d, which], out_sem.at[which])
 
@@ -1408,9 +1637,22 @@
 
             down_store(d).start()
 
+        def early(k, d):
+            @pl.when(k == count - 1)
+            def _():
+                loads[2].wait()
+                loads[3].wait()
+
+            @pl.when(d >= 0)
+            def _():
+                weights(d)
+
+        flow.visit(body, bundle, early)
+        done = count - 1 - flow.reach()
+
         @pl.loop(0, count - 2)
         def _(t):
-            weights(t)
+            weights(done + t)
             flow.give_back(count + t)
 
         for k in range(2, count):
@@ -1418,7 +1660,9 @@
 
         @pl.loop(count - 2, groups)
         def _(d):
-            weights(d)
+            @pl.when(d + done < groups)
+            def _():
+                weights(d + done)
 
         for which in range(2):
             gateup_store(groups - 1, which).wait()
@@ -1520,7 +1764,8 @@
 
     def kernel(x_ref, *refs):
         sources, refs = refs[: 4 * number], refs[4 * number :]
-        info_ref, outs, refs = refs[0], refs[1 : 1 + 3 * number], refs[1 + 3 * number :]
+        norm_ref, factor_ref = refs[:2]
+        outs, refs = refs[2 : 2 + 3 * number], refs[2 + 3 * number :]
         held, load_sem, store_sem = refs[: 4 * number], refs[4 * number], refs[4 * number + 1]
 
         def rows_of(at):
@@ -1551,8 +1796,8 @@
         tops = x_ref[high - 1 :]
         lanes = lax.broadcasted_iota(jnp.int32, (1, 128), 1)
         group_size = QUERY_HEADS // KEY_VALUE_HEADS
-        info_ref[0:1] = jnp.broadcast_to(norm, (1, 128))
-        info_ref[1:2] = LOGIT_CAP / jnp.maximum(tops, LOGIT_CAP)
+        norm_ref[...] = norm
+        factor_ref[...] = (LOGIT_CAP / jnp.maximum(tops, LOGIT_CAP))[:, :QUERY_HEADS]
 
         def factor(first, count):
             chosen = (lanes >= first) & (lanes < first + count)
@@ -1599,9 +1844,13 @@
     outs = [jax.ShapeDtypeStruct(group[0].shape, FULL) for group in groups for _ in range(3)]
     return pl.pallas_call(
         kernel,
-        out_shape=[jax.ShapeDtypeStruct((8, 128), FULL)] + outs,
+        out_shape=[
+            jax.ShapeDtypeStruct((1, 1), FULL),
+            jax.ShapeDtypeStruct((1, QUERY_HEADS), FULL),
+        ]
+        + outs,
         in_specs=[vmem] + [anywhere] * (4 * number),
-        out_specs=[vmem] + [anywhere] * (3 * number),
+        out_specs=[vmem] * 2 + [anywhere] * (3 * number),
         scratch_shapes=[pltpu.VMEM(array.shape, array.dtype) for array in arrays]
         + [dma((len(cuts), 4)), dma((len(cuts), 3))],
         compiler_params=pltpu.CompilerParams(vmem_limit_bytes=56 * 2**20),
@@ -1613,8 +1862,7 @@
     key_places = lax.broadcasted_iota(jnp.int32, (high, width), 1)
     query_places = at * high + lax.broadcasted_iota(jnp.int32, (high, width), 0)
     seen = key_places <= query_places
-    for piece in range(spans.shape[0] - 1):
-        start = spans[piece + 1]
+    for start in spans[1:]:
         both = (
             (key_places >= start)
             & (key_places < start + IMG)
@@ -1633,131 +1881,197 @@
     return raw_weights / jnp.sum(raw_weights, axis=-1, keepdims=True), peak_row
 
 
-def attention_forward_head(acts, gain, head_w, key_w, value_w, query_gain, key_gain, cos_tab, sin_tab, spans, items, ident):
+def spans_of(lengths_ref, starts_ref):
+    at = lax.axis_index("dp")
+    return [lengths_ref[at]] + [starts_ref[at, piece] for piece in range(starts_ref.shape[1])]
+
+
+def attention_forward_head(acts, gains, head_w, key_w, value_w, heads, cos_tab, sin_tab, extras, lengths, starts, items, ident):
     tokens, width = acts.shape
     step = 256
     bundle = Bundle(items)
     number = bundle.number
-
-    def kernel(spans_ref, x_ref, gain_ref, qw_ref, kw_ref, vw_ref, qg_ref, kg_ref, cos_ref, sin_ref, *refs):
+    rows_n, cols_n = lax.axis_size("row"), lax.axis_size("col")
+    half_tok, wide = tokens // cols_n, width // rows_n
+    share, quarter = half_tok // rows_n, tokens // rows_n
+
+    def kernel(l_ref, s_ref, x_ref, gain_ref, qw_ref, kw_ref, vw_ref, heads_ref, cos_ref, sin_ref, e_ref, *refs):
         x_refs, refs = refs[:number], refs[number:]
-        h_ref, scale_ref, qr_ref, kr_ref, vr_ref, q_ref, k_ref, v_ref, o_ref, top_ref = refs[:10]
-        o_refs, sems = refs[10 : 10 + number], refs[10 + number :]
-        bundle.bind(x_refs, o_refs, sems)
+        hidden_ref, acts_ref, share_ref, scale_ref, qr_ref, kr_ref, vr_ref = refs[:7]
+        q_ref, k_ref, v_ref, o_ref, top_ref, es_ref, oc_ref, os_ref = refs[7:15]
+        o_refs, refs = refs[15 : 15 + number], refs[15 + number :]
+        h_ref, sc_ref, key_ref, value_ref = refs[:4]
+        bundle.bind(x_refs, o_refs, refs[4:])
         bundle.greet()
         bundle.start()
+        me, column = lax.axis_index("row"), lax.axis_index("col")
+        spans = spans_of(l_ref, s_ref)
+        query_gain, key_gain = heads_ref[pl.ds(column * rows_n + me, 1)], heads_ref[QUERY_HEADS:]
 
         def project(at):
             here = pl.ds(pl.multiple_of(at * step, step), step)
             rows = x_ref[here].astype(FULL)
             scale = lax.rsqrt(jnp.mean(rows * rows, axis=-1, keepdims=True) + EPS)
-            scale_ref[here] = jnp.broadcast_to(scale, (step, 128))
-            h_ref[here] = (rows * scale * gain_ref[...]).astype(LOW)
+            sc_ref[here] = jnp.broadcast_to(scale, (step, 128))
+            h_ref[here] = (rows * scale * gain_ref[0:1]).astype(LOW)
             hidden = h_ref[here]
             cos_rows, sin_rows = cos_ref[here], sin_ref[here]
             query = flat_dot(hidden, qw_ref[...])
             qr_ref[here] = query
-            q_ref[here] = turn(whole_norm(query, qg_ref[...])[0], cos_rows, sin_rows).astype(LOW)
+            q_ref[here] = turn(whole_norm(query, query_gain)[0], cos_rows, sin_rows).astype(LOW)
             key = flat_dot(hidden, kw_ref[...])
-            kr_ref[here] = key
-            k_ref[here] = turn(whole_norm(key, kg_ref[...])[0], cos_rows, sin_rows).astype(LOW)
+            key_ref[here] = key
+            k_ref[here] = turn(whole_norm(key, key_gain)[0], cos_rows, sin_rows).astype(LOW)
             value = flat_dot(hidden, vw_ref[...])
-            vr_ref[here] = value
+            value_ref[here] = value
             v_ref[here] = whole_norm(value, 1.0)[0].astype(LOW)
 
         def attend(at):
             here = pl.ds(pl.multiple_of(at * step, step), step)
-            allowed = allowed_block(at, step, tokens, spans_ref)
+            allowed = allowed_block(at, step, tokens, spans)
             probs, peak_row = softmax_block(q_ref[here], k_ref[...], allowed)
             o_ref[here] = flat_dot(probs.astype(LOW), v_ref[...]).astype(LOW)
             top_ref[...] = jnp.maximum(top_ref[...], jnp.max(peak_row))
 
         top_ref[...] = jnp.full(top_ref.shape, NEGATIVE, FULL)
-        pl.loop(0, tokens // step)(project)
+        blocks = tokens // step
+        half = max(blocks // 2, 1)
+        pl.loop(0, half)(project)
         bundle.step(1)
-        pl.loop(0, tokens // step)(attend)
-        for k in range(2, bundle.sizes[0]):
+        pl.loop(half, blocks)(project)
+        bundle.step(2)
+        pl.loop(0, half)(attend)
+        for k in range(3, bundle.sizes[0]):
             bundle.step(k)
+        pl.loop(half, blocks)(attend)
+        columns = pl.ds(pl.multiple_of(me * wide, wide), wide)
+
+        @pl.loop(0, blocks)
+        def _(at):
+            here = pl.ds(pl.multiple_of(at * step, step), step)
+            hidden_ref[here] = h_ref[here, columns]
+            acts_ref[here] = x_ref[here, columns]
+
+        mine = pl.ds(pl.multiple_of(column * half_tok + me * share, share), share)
+        share_ref[...] = x_ref[mine]
+        es_ref[...] = e_ref[mine]
+        scale_ref[...] = sc_ref[pl.ds(pl.multiple_of(column * half_tok, half_tok), half_tok)]
+        fourth = pl.ds(pl.multiple_of(me * quarter, quarter), quarter)
+        kr_ref[...] = key_ref[fourth]
+        vr_ref[...] = value_ref[fourth]
+        oc_ref[...] = cos_ref[fourth]
+        os_ref[...] = sin_ref[fourth]
         bundle.finish()
 
     vmem = pl.BlockSpec(memory_space=pltpu.VMEM)
-    low = jax.ShapeDtypeStruct((tokens, HEAD_WIDTH), LOW)
-    full = jax.ShapeDtypeStruct((tokens, HEAD_WIDTH), FULL)
+    smem = pl.BlockSpec(memory_space=pltpu.SMEM)
+
+    def low(*shape):
+        return jax.ShapeDtypeStruct(shape, LOW)
+
+    def full(*shape):
+        return jax.ShapeDtypeStruct(shape, FULL)
+
     return pl.pallas_call(
         kernel,
         out_shape=[
-            jax.ShapeDtypeStruct((tokens, width), LOW),
-            jax.ShapeDtypeStruct((tokens, 128), FULL),
-            full,
-            full,
-            full,
-            low,
-            low,
-            low,
-            low,
-            jax.ShapeDtypeStruct((8, 128), FULL),
+            low(tokens, wide),
+            low(tokens, wide),
+            low(share, width),
+            full(half_tok, 128),
+            full(tokens, HEAD_WIDTH),
+            full(quarter, HEAD_WIDTH),
+            full(quarter, HEAD_WIDTH),
+            low(tokens, HEAD_WIDTH),
+            low(tokens, HEAD_WIDTH),
+            low(tokens, HEAD_WIDTH),
+            low(tokens, HEAD_WIDTH),
+            full(8, 128),
+            low(share, PLD),
+            full(quarter, HEAD_WIDTH // 2),
+            full(quarter, HEAD_WIDTH // 2),
         ]
         + bundle.shapes,
-        in_specs=[pl.BlockSpec(memory_space=pltpu.SMEM)] + [vmem] * 9 + bundle.specs,
-        out_specs=[vmem] * 10 + bundle.specs,
-        scratch_shapes=bundle.scratch,
-        compiler_params=params(ident),
+        in_specs=[smem, smem] + [vmem] * 9 + bundle.specs,
+        out_specs=[vmem] * 15 + bundle.specs,
+        scratch_shapes=[
+            pltpu.VMEM((tokens, width), LOW),
+            pltpu.VMEM((tokens, 128), FULL),
+            pltpu.VMEM((tokens, HEAD_WIDTH), FULL),
+            pltpu.VMEM((tokens, HEAD_WIDTH), FULL),
+        ]
+        + bundle.scratch,
+        compiler_params=params(ident, 60),
         cost_estimate=cost(40),
-    )(spans, acts, gain, head_w, key_w, value_w, query_gain, key_gain, cos_tab, sin_tab, *bundle.sources)
-
-
-def head_backward(queries, keys, values, grads, spans, items, ident):
+    )(lengths, starts, acts, gains, head_w, key_w, value_w, heads, cos_tab, sin_tab, extras, *bundle.sources)
+
+
+def head_backward(queries, keys, values, attended, grads, attend_w, query_raw, heads, cos_tab, sin_tab, lengths, starts, items, ident):
     rows = queries.shape[0]
     step = min(256, rows)
-
     bundle = Bundle(items)
     number = bundle.number
-
-    def kernel(spans_ref, q_ref, k_ref, v_ref, g_ref, *refs):
+    devices = lax.axis_size("row")
+    quarter = rows // devices
+
+    def kernel(l_ref, s_ref, q_ref, k_ref, v_ref, a_ref, g_ref, w_ref, r_ref, heads_ref, cos_ref, sin_ref, *refs):
         x_refs, refs = refs[:number], refs[number:]
-        dq_ref, dk_ref, dv_ref = refs[:3]
-        bundle.bind(x_refs, refs[3 : 3 + number], refs[3 + number :])
+        dq_ref, kv_ref, dg_ref, dw_ref = refs[:4]
+        o_refs, refs = refs[4 : 4 + number], refs[4 + number :]
+        dk_ref, dv_ref = refs[:2]
+        bundle.bind(x_refs, o_refs, refs[2:])
         bundle.greet()
         bundle.start()
+        spans = spans_of(l_ref, s_ref)
+        gain = heads_ref[pl.ds(lax.axis_index("col") * devices + lax.axis_index("row"), 1)]
         dk_ref[...] = jnp.zeros(dk_ref.shape, FULL)
         dv_ref[...] = jnp.zeros(dv_ref.shape, FULL)
-
-        blocks = rows // step
-        ahead = min(blocks, bundle.sizes[0])
-
-        @pl.loop(0, blocks)
+        dg_ref[...] = jnp.zeros(dg_ref.shape, FULL)
+
+        @pl.loop(0, rows // step)
         def _(at):
-            @pl.when((at > 0) & (at < ahead))
-            def _():
-                bundle.step(at)
-
             here = pl.ds(pl.multiple_of(at * step, step), step)
-            allowed = allowed_block(at, step, keys.shape[0], spans_ref)
-            block_rows, grad_rows = q_ref[here], g_ref[here]
+            allowed = allowed_block(at, step, keys.shape[0], spans)
+            block_rows, grad_rows = q_ref[here], against(g_ref[here], w_ref[...]).astype(LOW)
             probs, _ = softmax_block(block_rows, k_ref[...], allowed)
             grad_probs = against(grad_rows, v_ref[...])
             delta_row = jnp.sum(probs * grad_probs, axis=-1, keepdims=True)
             grad_scores = (probs * (grad_probs - delta_row)).astype(LOW)
-            dq_ref[here] = flat_dot(grad_scores, k_ref[...])
+            d_query = turn_back(flat_dot(grad_scores, k_ref[...]), cos_ref[here], sin_ref[here])
+            d_query, d_gain = norm_back(r_ref[here], gain, d_query)
+            dq_ref[here] = d_query.astype(LOW)
+            dg_ref[...] += d_gain
             dk_ref[...] += inner_rows(grad_scores, block_rows)
             dv_ref[...] += inner_rows(probs.astype(LOW), grad_rows)
 
-        for k in range(ahead, bundle.sizes[0]):
+        for device in range(devices):
+            cut = slice(device * quarter, (device + 1) * quarter)
+            kv_ref[device, :quarter] = dk_ref[cut].astype(LOW)
+            kv_ref[device, quarter:] = dv_ref[cut].astype(LOW)
+        for cut in range(0, grads.shape[1], 512):
+            dw_ref[:, cut : cut + 512] = inner_rows(a_ref[...], g_ref[:, cut : cut + 512]).astype(LOW)
+        for k in range(1, bundle.sizes[0]):
             bundle.step(k)
         bundle.finish()
 
     vmem = pl.BlockSpec(memory_space=pltpu.VMEM)
     return pl.pallas_call(
         kernel,
-        out_shape=[jax.ShapeDtypeStruct(queries.shape, FULL)]
-        + [jax.ShapeDtypeStruct(keys.shape, FULL)] * 2
+        out_shape=[
+            jax.ShapeDtypeStruct(queries.shape, LOW),
+            jax.ShapeDtypeStruct((devices, 2 * quarter, HEAD_WIDTH), LOW),
+            jax.ShapeDtypeStruct((1, HEAD_WIDTH), FULL),
+            jax.ShapeDtypeStruct((HEAD_WIDTH, grads.shape[1]), LOW),
+        ]
         + bundle.shapes,
-        in_specs=[pl.BlockSpec(memory_space=pltpu.SMEM)] + [vmem] * 4 + bundle.specs,
-        out_specs=[vmem] * 3 + bundle.specs,
-        scratch_shapes=bundle.scratch,
-        compiler_params=params(ident),
+        in_specs=[pl.BlockSpec(memory_space=pltpu.SMEM)] * 2 + [vmem] * 10 + bundle.specs,
+        out_specs=[vmem] * 4 + bundle.specs,
+        scratch_shapes=[pltpu.VMEM(keys.shape, FULL)] * 2 + bundle.scratch,
+        compiler_params=params(ident, 60),
         cost_estimate=cost(25),
-    )(spans, queries, keys, values, grads, *bundle.sources)
+    )(
+        lengths, starts, queries, keys, values, attended, grads, attend_w, query_raw, heads, cos_tab, sin_tab, *bundle.sources
+    )
 
 
 def whole_norm(values_in, gain_vec):
@@ -1904,12 +2218,15 @@
         60,
     )
     gateup_all = lax.all_gather(gateup_own, "dp")
-    query_w = qkv_w[:, :, :HEAD_WIDTH]
-    kv_w = qkv_w[:, :, HEAD_WIDTH:]
-    key_w = lax.dynamic_index_in_dim(kv_w, column, 0, False)
-    value_w = lax.dynamic_index_in_dim(kv_w, KEY_VALUE_HEADS + column, 0, False)
+
+    def lower(inputs, outputs):
+        @pl.loop(0, inputs[0].shape[0] // 256)
+        def _(at):
+            rows = pl.ds(pl.multiple_of(at * 256, 256), 256)
+            outputs[0][rows] = inputs[0][rows].astype(LOW)
+
     last = pl.ds(HEAD_WIDTH, HEAD_WIDTH)
-    whole_acts, whole_key, whole_value, head_w, gains, extras, attend_all = transfers(
+    down_low, whole_acts, whole_key, whole_value, head_w, gains, extras, attend_all = transfers(
         [
             along(activations),
             Line(
@@ -1949,77 +2266,65 @@
         ],
         2,
         95,
+        60,
+        lower,
+        (w_down,),
+        [jax.ShapeDtypeStruct(w_down.shape, LOW)],
     )
     attend_w = (
         attend_all.reshape(data_n, HEAD_WIDTH, rows_n, out_cols)
         .transpose(1, 2, 0, 3)
         .reshape(HEAD_WIDTH, width)
     )
-    token_at = column * half_tok + me * share
-    extras = lax.dynamic_slice_in_dim(extras, token_at, share, 0).astype(FULL)
-    length = lax.dynamic_index_in_dim(lengths, data_at, 0, keepdims=True)
-    piece_starts = lax.dynamic_index_in_dim(starts, data_at, 0, keepdims=False)
-    spans = jnp.concatenate([length, piece_starts])
-
-    query_gain = lax.dynamic_index_in_dim(w_heads, column * rows_n + me, 0, True)
-    key_gain = w_heads[QUERY_HEADS:]
     all_cos, all_sin = rope_tables(jnp.arange(tokens, dtype=jnp.int32), HEAD_WIDTH)
-    own_cos = lax.dynamic_slice_in_dim(all_cos, me * quarter, quarter, 0)
-    own_sin = lax.dynamic_slice_in_dim(all_sin, me * quarter, quarter, 0)
     (
-        whole_hidden,
-        whole_scale,
+        spread_h,
+        own_acts,
+        acts_share,
+        scale_here,
         query_raw,
-        all_key_raw,
-        all_value_raw,
+        key_raw,
+        value_raw,
         queries,
         keys,
         values,
         attended,
         top,
-        down_own,
+        extras,
+        own_cos,
+        own_sin,
         left_t,
         right_w,
+        down_own,
     ) = attention_forward_head(
         whole_acts,
-        gains[:1],
+        gains,
         head_w,
         whole_key,
         whole_value,
-        query_gain,
-        key_gain,
+        w_heads,
         all_cos,
         all_sin,
-        spans,
+        extras,
+        lengths,
+        starts,
         [
+            along(left_t.astype(LOW)),
+            along(right_w),
             Swap(
-                w_down.astype(LOW).reshape(data_n, rows_n, ff_part, out_cols),
+                down_low.reshape(data_n, rows_n, ff_part, out_cols),
                 (data_n, ff_part, rows_n * out_cols),
                 lambda ref, q: ref.at[:, q],
                 lambda ref, at: ref.at[:, :, columns_of(at, out_cols)],
             ),
-            along(left_t.astype(LOW)),
-            along(right_w),
         ],
         3,
     )
     down_own, gateup_all = lax.optimization_barrier((down_own, gateup_all))
     down_all = lax.all_gather(down_own, "dp").reshape(data_n, data_n * ff_part, -1)
-    inputs = lax.dynamic_slice_in_dim(whole_acts, token_at, share, 0).astype(FULL)
-    key_raw = lax.dynamic_slice_in_dim(all_key_raw, me * quarter, quarter, 0)
-    value_raw = lax.dynamic_slice_in_dim(all_value_raw, me * quarter, quarter, 0)
-    _, query_scale = whole_norm(query_raw, query_gain)
-    _, key_scale = whole_norm(key_raw, key_gain)
-    _, value_scale = whole_norm(value_raw, 1.0)
-
     def shares(parts):
         return parts.astype(LOW).reshape(cols_n, rows_n, share, width)
 
-    hidden, _ = whole_norm(inputs, gains[0])
-    hidden_low = hidden.astype(LOW)
-    middle = against(hidden_low, left_t).astype(LOW)
-    right_raw = flat_dot(middle, right_w)
-    right_n, scale_r = whole_norm(right_raw, gains[1])
     projected, pergate_t, perproj_w = transfers(
         [
             Reduce(
@@ -2030,13 +2335,21 @@
         ],
         5,
         45,
-        30,
-    )
-    proj_n, scale_p = whole_norm(projected, gains[2])
-    mixture = ((inputs + proj_n) + (hidden + right_n)) * HALF_ROOT
-    ffn_n, scale_f = whole_norm(mixture, gains[3])
+        60,
+    )
+    wide_low, wide_full = ((share, width), LOW), ((share, width), FULL)
+    line = ((1, width), FULL)
+    hidden_low, middle, right_raw, mixture, ffn_in = local(
+        mix,
+        [wide_low, ((share, RANK), LOW), wide_full, wide_full, wide_low],
+        acts_share,
+        projected,
+        gains,
+        left_t,
+        right_w,
+    )
     down_raw, spread_ft, act_t, gate_raw, up_raw, upstream = ffn_forward(
-        ffn_n.astype(LOW),
+        ffn_in,
         gateup_all,
         down_all,
         [
@@ -2045,67 +2358,52 @@
                 (share, width),
                 lambda ref, q: ref.at[columns_of(q, share)],
                 lambda ref, at: ref.at[:, columns_of(at, width_a)],
-            ),
+            )
         ],
         6,
     )
-    upstream = upstream.astype(FULL)
-    down_n, scale_d = whole_norm(down_raw, gains[4])
-    block_out = mixture + down_n
-    out_low = block_out.astype(LOW)
-    pgate = against(out_low, pergate_t)
-    pact = (jax.nn.gelu(pgate, approximate=True) * extras).astype(LOW)
-    perproj = flat_dot(pact, perproj_w)
-    perproj_n, scale_pp = whole_norm(perproj, gains[5])
-    result = (block_out + perproj_n).astype(LOW)
-
-    gain_grads = [None] * 6
-    d_perproj, gain_grads[5] = whole_norm_backward(perproj, scale_pp, gains[5], upstream)
-    d_perproj = d_perproj.astype(LOW)
-    dw_perproj = inner_rows(pact, d_perproj)
-    d_pact = against(d_perproj, perproj_w)
-    _, pullback = jax.vjp(lambda v: jax.nn.gelu(v, approximate=True), pgate)
-    (d_pgate,) = pullback(d_pact * extras)
-    d_pgate = d_pgate.astype(LOW)
-    dw_pergate = inner_rows(d_pgate, out_low)
-    d_out = upstream + flat_dot(d_pgate, pergate_t)
-    d_down, gain_grads[4] = whole_norm_backward(down_raw, scale_d, gains[4], d_out)
-    d_ffn, dw_gateup, dw_down, result = ffn_backward(
-        d_down.astype(LOW),
-        gateup_all,
-        down_all,
-        spread_ft,
-        act_t,
-        gate_raw,
-        up_raw,
+    result, d_out, d_down, dw_perproj, dw_pergate, gain_four, gain_five = local(
+        per_layer_both,
+        [wide_low, wide_full, wide_low, ((PLD, width), LOW), ((PLD, width), LOW), line, line],
+        mixture,
+        down_raw,
+        gains,
+        extras,
+        pergate_t,
+        perproj_w,
+        upstream,
+    )
+    d_ffn, dw_gateup, dw_down = ffn_backward(
+        d_down, gateup_all, down_all, spread_ft, act_t, gate_raw, up_raw, [], 8
+    )
+    g_gateup = lax.psum_scatter(dw_gateup, "dp", scatter_dimension=0)
+    d_proj, d_half, d_middle, small_parts, inner_share, gain_one, gain_two, gain_three = local(
+        mix_back,
         [
-            Swap(
-                result,
-                (half_tok, width_a),
-                lambda ref, q: ref.at[:, columns_of(q, width_a)],
-                lambda ref, at: ref.at[columns_of(at, share)],
-            )
+            wide_low,
+            wide_low,
+            ((share, RANK), LOW),
+            ((2 * (RANK + PLD), width), LOW),
+            ((8, share), FULL),
+            line,
+            line,
+            line,
         ],
-        8,
-    )
-    g_gateup = lax.psum_scatter(dw_gateup, "dp", scatter_dimension=0)
-    d_mix, gain_grads[3] = whole_norm_backward(mixture, scale_f, gains[3], d_ffn)
-    d_half = (d_out + d_mix) * HALF_ROOT
-    d_proj, gain_grads[2] = whole_norm_backward(projected, scale_p, gains[2], d_half)
-    d_right, gain_grads[1] = whole_norm_backward(right_raw, scale_r, gains[1], d_half)
-    d_right = d_right.astype(LOW)
-    dw_right = inner_rows(middle, d_right)
-    d_middle = against(d_right, right_w).astype(LOW)
-    dw_left = inner_rows(d_middle, hidden_low)
-    d_hidden_share = d_half + flat_dot(d_middle, left_t)
-    inner_share = jnp.sum(d_hidden_share * gains[0] * inputs, axis=1)
-    small_parts = jnp.concatenate(
-        [
-            grad.astype(LOW).reshape(cols_n, -1, width)
-            for grad in (dw_left, dw_right, dw_pergate, dw_perproj)
-        ],
-        axis=1,
-    )
+        d_out,
+        d_ffn,
+        mixture,
+        projected,
+        right_raw,
+        gains,
+        acts_share,
+        left_t,
+        right_w,
+        hidden_low,
+        middle,
+        dw_pergate,
+        dw_perproj,
+    )
+    small_parts = small_parts.reshape(cols_n, -1, width)
     spread_p, small_parts = transfers(
         [
             Line(
@@ -2122,70 +2420,91 @@
         ],
         10,
         50,
-        30,
+        60,
     )
     spread_p = spread_p.reshape(tokens, width)
-    d_attended = against(spread_p, attend_w).astype(LOW)
-    dw_attend = inner_rows(attended, spread_p).astype(LOW)
-    d_queries, d_keys, d_values, half_here, middle_here = head_backward(
+    d_q_raw, kv_parts, dg_query, dw_attend, middle_here, half_here, result = head_backward(
         queries,
         keys,
         values,
-        d_attended,
-        spans,
+        attended,
+        spread_p,
+        attend_w,
+        query_raw,
+        w_heads,
+        all_cos,
+        all_sin,
+        lengths,
+        starts,
         [
+            Line(
+                d_middle, (half_tok, d_middle.shape[1]), lambda ref, c, r: ref.at[columns_of(r, share)]
+            )
+        ]
+        + [
             Swap(
-                d_half.astype(LOW),
+                source,
                 (half_tok, width_a),
                 lambda ref, q: ref.at[:, columns_of(q, width_a)],
                 lambda ref, at: ref.at[columns_of(at, share)],
-            ),
-            Line(
-                d_middle, (half_tok, d_middle.shape[1]), lambda ref, c, r: ref.at[columns_of(r, share)]
-            ),
+            )
+            for source in (d_half, result)
         ],
         4,
     )
 
-    small_parts = small_parts.astype(LOW)
-    d_queries, dw_down, g_gateup = lax.optimization_barrier((d_queries, dw_down, g_gateup))
+    d_q_raw, dw_down, g_gateup = lax.optimization_barrier((d_q_raw, dw_down, g_gateup))
     g_down = lax.psum_scatter(
         dw_down.reshape(data_n, data_n, ff_part, -1), "dp", scatter_dimension=0
     )
-    kv_parts = jnp.concatenate(
-        [
-            d_keys.astype(LOW).reshape(rows_n, quarter, HEAD_WIDTH),
-            d_values.astype(LOW).reshape(rows_n, quarter, HEAD_WIDTH),
-        ],
-        axis=1,
-    )
-    d_q_raw, dg_query = whole_norm_backward(
-        query_raw, query_scale, query_gain, turn_back(d_queries, all_cos, all_sin)
-    )
+
     d_q_all, d_kv = transfers(
         [
-            Line(
-                d_q_raw.astype(LOW), (rows_n,) + d_q_raw.shape, lambda ref, c, r: ref.at[r]
-            ),
+            Line(d_q_raw, (rows_n,) + d_q_raw.shape, lambda ref, c, r: ref.at[r]),
             Reduce(kv_parts, kv_parts.shape[1:], lambda ref, q: ref.at[q], False),
         ],
         11,
         45,
-        30,
-    )
-    d_k_raw, dg_key = whole_norm_backward(
-        key_raw, key_scale, key_gain, turn_back(d_kv[:quarter], own_cos, own_sin)
-    )
-    d_v_raw, _ = whole_norm_backward(value_raw, value_scale, 1.0, d_kv[quarter:])
-    d_raw = jnp.stack([d_k_raw, d_v_raw]).astype(LOW)
-    gateup_squares = jnp.sum(jnp.square(g_gateup.astype(FULL)))
-    d_kv_all, g_gateup, g_attend = transfers(
+        60,
+    )
+    d_k_raw, d_v_raw, dg_key = local(
+        key_value_back,
+        [((quarter, HEAD_WIDTH), LOW), ((quarter, HEAD_WIDTH), LOW), ((1, HEAD_WIDTH), FULL)],
+        d_kv,
+        key_raw,
+        value_raw,
+        w_heads,
+        own_cos,
+        own_sin,
+        mebibytes=16,
+    )
+
+    def query_work(inputs, outputs):
+        h_ref, dq_ref, qw_ref, g_ref = inputs
+        dw_ref, dh_ref, sq_ref = outputs
+        hidden = h_ref[...]
+        for k in range(heads_here):
+            dw_ref[k] = inner_rows(hidden, dq_ref[k]).astype(LOW)
+        total = against(dq_ref[0], qw_ref[0, :, :HEAD_WIDTH])
+        for k in range(1, heads_here):
+            total = total + against(dq_ref[k], qw_ref[k, :, :HEAD_WIDTH])
+        dh_ref[...] = total
+        sq_ref[...] = jnp.zeros(sq_ref.shape, FULL)
+        for which in range(2):
+
+            @pl.loop(0, width // 128)
+            def _(at):
+                rows = g_ref[which, pl.ds(pl.multiple_of(at * 128, 128), 128)].astype(FULL)
+                sq_ref[...] += jnp.sum((rows * rows).reshape(16, 8, ff_part), axis=0)
+
+    dw_query, d_hidden, gateup_squares, d_k_all, d_v_all, g_gateup, g_attend = transfers(
         [
             Line(
-                d_raw,
-                (2, tokens, HEAD_WIDTH),
-                lambda ref, c, r: ref.at[:, columns_of(r, quarter)],
-            ),
+                d_raw, (tokens, HEAD_WIDTH), lambda ref, c, r: ref.at[columns_of(r, quarter)]
+            )
+            for d_raw in (d_k_raw, d_v_raw)
+        ]
+        + [
             Swap(
                 g_gateup,
                 w_gateup.shape,
@@ -2195,69 +2514,71 @@
             ShardSum(dw_attend, out_cols),
         ],
         12,
-        100,
-    )
-    d_k_all, d_v_all = d_kv_all[0], d_kv_all[1]
-    d_hidden = against(d_k_all, key_w) + against(d_v_all, value_w)
-    for k in range(heads_here):
-        d_hidden = d_hidden + against(d_q_all[k], query_w[k])
-    acts = activations.astype(FULL)
-    gains_here = lax.dynamic_slice_in_dim(w_gains, 0, 1, 0)[0]
-    scale_here = lax.dynamic_slice_in_dim(whole_scale[:, :1], column * half_tok, half_tok, 0)
-    own_acts = lax.dynamic_slice_in_dim(whole_acts, me * width_a, width_a, 1).astype(FULL)
-    inner = jnp.sum(d_hidden * gains_here * own_acts, axis=1)
-    inner = lax.dynamic_update_slice_in_dim(
-        inner, lax.dynamic_slice_in_dim(inner, token_at, share, 0) + inner_share, token_at, 0
-    ).reshape(-1, 128)
-
-    spread_h = lax.dynamic_slice_in_dim(whole_hidden, me * width_a, width_a, 1)
-    dw_query = jnp.stack([inner_rows(spread_h, d_q_all[k]).astype(LOW) for k in range(heads_here)])
-    dw_kv = jnp.stack(
-        [inner_rows(spread_h, d_k_all).astype(LOW), inner_rows(spread_h, d_v_all).astype(LOW)]
-    )
-    cuts = []
-    start = 0
-    for rows, by_rows in (
+        65,
+        40,
+        query_work,
+        (spread_h, d_q_all, qkv_w, g_gateup),
+        [
+            jax.ShapeDtypeStruct((heads_here, width_a, HEAD_WIDTH), LOW),
+            jax.ShapeDtypeStruct((tokens, width_a), FULL),
+            jax.ShapeDtypeStruct((8, ff_part), FULL),
+        ],
+    )
+    extents = (
         (data_n * left_cols, True),
         (right_rows, False),
         (data_n * gate_cols, True),
         (proj_rows, False),
-    ):
-        cut = small_parts[start : start + rows]
-        start += rows
-        if by_rows:
-            cut = cut.reshape(data_n, -1, width_a)
-            cut = [cut[:, :, k * out_cols : (k + 1) * out_cols] for k in range(data_n)]
-            cuts.append(jnp.concatenate(cut, axis=1))
-        else:
-            cuts.append(jnp.stack([cut[:, k * out_cols : (k + 1) * out_cols] for k in range(data_n)]))
-    squares = gateup_squares
-    for gradient in (g_attend, g_down):
-        squares = squares + jnp.sum(jnp.square(gradient.astype(FULL)))
-    g_query, g_keyval, flat_grads, g_down, g_attend, d_hidden, inner = shard_total(
+    )
+    flat_rows = sum(rows for rows, _ in extents)
+    dw_kv, d_hidden, inner, flat_parts = local(
+        functools.partial(key_value_ends, extents=extents),
+        [
+            ((2 * width_a, HEAD_WIDTH), LOW),
+            ((tokens, width_a), LOW),
+            ((8, tokens), FULL),
+            ((data_n * flat_rows, out_cols), LOW),
+        ],
+        spread_h,
+        d_k_all,
+        d_v_all,
+        qkv_w,
+        d_hidden,
+        own_acts,
+        w_gains,
+        small_parts,
+        mebibytes=24,
+    )
+    dw_kv = dw_kv.reshape(2, width_a, HEAD_WIDTH)
+    down_sums = g_down
+    g_query, g_keyval, flat_grads, inner, inner_share, d_hidden, g_attend, g_down = shard_total(
         dw_query,
         dw_kv,
-        jnp.concatenate(cuts, axis=1),
+        flat_parts.reshape(data_n, flat_rows, out_cols),
         [
+            Line(inner, (cols_n, rows_n) + inner.shape, lambda ref, c, r: ref.at[c, r], True),
+            Line(
+                inner_share,
+                (cols_n, rows_n) + inner_share.shape,
+                lambda ref, c, r: ref.at[c, r],
+                True,
+            ),
+            Pair(d_hidden.reshape(cols_n, half_tok, width_a)),
+            Swap(
+                g_attend,
+                (rows_n, HEAD_WIDTH, out_cols),
+                lambda ref, q: ref.at[:, columns_of(q, out_cols)],
+                lambda ref, at: ref.at[at],
+            ),
             Swap(
                 g_down,
                 (data_n, rows_n, ff_part, out_cols),
                 lambda ref, q: ref.at[:, :, columns_of(q, out_cols)],
                 lambda ref, at: ref.at[:, at],
             ),
-            Swap(
-                g_attend,
-                (rows_n, HEAD_WIDTH, out_cols),
-                lambda ref, q: ref.at[:, columns_of(q, out_cols)],
-                lambda ref, at: ref.at[at],
-            ),
-            Pair(d_hidden.astype(LOW).reshape(cols_n, half_tok, width_a)),
-            Line(inner, (cols_n, rows_n) + inner.shape, lambda ref, c, r: ref.at[c, r], True),
         ],
         13,
     )
-    squares = squares + jnp.where(column == 0, jnp.sum(g_keyval * g_keyval), 0.0)
-    squares = squares + jnp.sum(g_query * g_query) + jnp.sum(flat_grads * flat_grads)
     g_down = g_down.reshape(w_down.shape)
     g_attend = g_attend.reshape(w_attend.shape)
     small_grads = []
@@ -2273,45 +2594,25 @@
         small_grads.append(cut)
     g_left, g_right, g_pergate, g_perproj = small_grads
 
-    inner = jnp.sum(inner, axis=(0, 1)).reshape(cols_n, half_tok) / MODEL_WIDTH
-    inner = lax.dynamic_index_in_dim(inner, column, 0, False)[:, None]
-    half_here = half_here.astype(FULL)
-    own_left = lax.dynamic_slice_in_dim(left_t, me * width_a, width_a, 1)
-    d_hidden = d_hidden[0].astype(FULL) + d_hidden[1].astype(FULL) + half_here
-    d_hidden = d_hidden + flat_dot(middle_here, own_left)
-    grad_input = (
-        half_here
-        + scale_here * d_hidden * gains_here
-        - acts * (scale_here * scale_here * scale_here) * inner
-    ).astype(LOW)
-    gain_zero = jnp.sum(d_hidden * acts * scale_here, axis=0)
-
-    gain_full = jnp.stack(
-        [
-            lax.dynamic_update_slice_in_dim(
-                jnp.zeros((width,), FULL), gain_zero, me * width_a, 0
-            )
-        ]
-        + gain_grads[1:]
-    )
-    head_full = lax.dynamic_update_slice_in_dim(
-        jnp.zeros((QUERY_HEADS + 1, HEAD_WIDTH), FULL), dg_query[None], column * rows_n + me, 0
-    )
-    head_full = head_full.at[QUERY_HEADS].add(dg_key)
-    logit_row = lax.dynamic_update_slice_in_dim(
-        jnp.full((128,), NEGATIVE, FULL), top[0, :1], column * rows_n + me, 0
-    )
-    gain_rows = gain_full.size // 128
-    head_rows = head_full.size // 128
-    pad_rows = -(gain_rows + head_rows) % 8
-    small = jnp.concatenate(
-        [
-            gain_full.reshape(-1, 128),
-            head_full.reshape(-1, 128),
-            jnp.broadcast_to(squares, (pad_rows, 128)),
-            jnp.broadcast_to(logit_row[None], (8, 128)),
-        ]
-    )
+    grad_input, small = input_ends(
+        d_hidden,
+        half_here,
+        middle_here,
+        left_t,
+        activations,
+        scale_here,
+        w_gains,
+        inner,
+        inner_share,
+        (g_query, g_keyval, flat_grads, g_attend, down_sums),
+        gateup_squares,
+        (gain_one, gain_two, gain_three, gain_four, gain_five),
+        dg_query,
+        dg_key,
+        top,
+    )
+    gain_rows = 6 * width // 128
+    head_rows = (QUERY_HEADS + 1) * HEAD_WIDTH // 128
     small = last_sums(small, 15)
     gain_sum = small[:gain_rows].reshape(6, width)
     head_sum = small[gain_rows : gain_rows + head_rows].reshape(QUERY_HEADS + 1, HEAD_WIDTH)
@@ -2351,9 +2652,9 @@
             ((w_heads, m_heads, v_heads, head_sum), kept, (HEAD_RATE, 0.0, None)),
         )
     ]
-    info, *stepped = adam_all(small, gain_rows + head_rows, groups)
-    grad_norm = info[0, 0]
-    scale_factors = info[1, :QUERY_HEADS]
+    grad_norm, scale_factors, *stepped = adam_all(small, gain_rows + head_rows, groups)
+    grad_norm = grad_norm.reshape(())
+    scale_factors = scale_factors.reshape(-1)
     gateup, down, query, keyval, attend, left, right, pergate, perproj, gain, head = (
         stepped[3 * k : 3 * k + 3] for k in range(11)
     )

time: 815 us -> 758 us (0.930)
  other arithmetic: 47.8 us -> 7.66 us
  Pallas kernels: 659 us -> 692 us
  matrix products: 33 us -> 3.27 us
  local copies, waits for them, and re-layouts: 45.9 us -> 32.2 us
    pallas_call x9 -> x15, Pallas kernels: 436 us -> 473 us  [the longest x6 350 us: transfers(): pl.pallas_call(kernel, out_shape=list(shapes) + bundle.shapes, in_specs=[...]
    dot_general x22 -> x0, matrix products: 24.6 us -> none  [the longest x11 13.2 us: inner_rows(): lax.dot_general(left_mat, right_mat, (((0,), (0,)), ((), ())), preferred_...]
    reduce_sum x18 -> x0, other arithmetic: 19.6 us -> none  [the longest x6 7.18 us: whole_norm(): jnp.mean(values_in * values_in, axis=-1, keepdims=True) + EPS]
    unnamed x249 -> x124, local copies, waits for them, and re-layouts: 33.4 us -> 27.1 us
  transfers between devices with their start and end apart: 4 -> 4, of which waited for: 0 -> 0; matrix products, arithmetic and copies ran while one was open for 8% -> 1% of each run, Pallas kernels for 44% -> 51%
where the time goes in v7:
time: 758 us; the launch traced here: 751 us
  Pallas kernels  692 us (91%)
  local copies, waits for them, and re-layouts  32.2 us (4%)
  between operations  14.7 us (2%)
  other arithmetic  7.66 us (1%)
    pallas_call x6, Pallas kernels, transfers(): pl.pallas_call(kernel, out_shape=list(shapes) + bundle.shapes, in_specs=[...  350 us
    pallas_call x1, Pallas kernels, ffn_forward(): pl.pallas_call(kernel, out_shape=[jax.ShapeDtypeStruct((share, width), FU...  86.7 us
    pallas_call x1, Pallas kernels, ffn_backward(): pl.pallas_call(kernel, out_shape=[jax.ShapeDtypeStruct((share, width), FU...  83.9 us
    pallas_call x1, Pallas kernels, attention_forward_head(): pl.pallas_call(kernel, out_shape=[low(tokens, wide), low(tokens, wide), l...  43.8 us
    pallas_call x1, Pallas kernels, shard_total(): pl.pallas_call(kernel, out_shape=[jax.ShapeDtypeStruct(shape, FULL) for s...  35 us
    pallas_call x1, Pallas kernels, head_backward(): pl.pallas_call(kernel, out_shape=[jax.ShapeDtypeStruct(queries.shape, LOW...  34.4 us
    unnamed x124, local copies, waits for them, and re-layouts  27.1 us
    pallas_call x5, Pallas kernels, local(): pl.pallas_call(kernel, out_shape=[jax.ShapeDtypeStruct(shape, kind) for s...  23.1 us
  transfers between devices with their start and end apart: 4, of which 0 were waited for; matrix products, arithmetic and copies ran while one was open for 1% of the time, Pallas kernels for 51%

profile of v7, /device:TPU:0, one launch (start us, length us, event | category | flops | bytes accessed | tf_op | source)
XLA Modules:
  0.0 750.7 jit_solution(18036748409657699350)
XLA Ops:
  7.3 2.6 convert_element_type.48.refs_0_
  10.2 57.5 %shard_map.645 = (bf16[2,2048,256]{2,1,0:T(8,128)(2,1)}, bf16[256,512]{1,0:T(8,128)(2,1)S(1)}, bf16[4,512,512]{2,1,0:T(8,128)(2,1)S(1)}, f32[32,512]{1,0:T(8,128...) custom-call(bf16[2,512,1024]{2,1,0:T(8,128)(2,1)S(1)} %convert_element_type.48.refs_0, ...), custom_call_target="tpu_custom_call" | custom-call | bytes 180000000 | tf_op jit(solution)/shard_map/pallas_call | solution.py:769
  67.7 1.3 copy-done
  69.0 0.7 copy-done.28
  73.0 98.7 %shard_map.646 = (bf16[4096,128]{1,0:T(8,128)(2,1)}, bf16[1024,2048]{1,0:T(8,128)(2,1)}, bf16[2048,256]{1,0:T(8,128)(2,1)}, bf16[2048,256]{1,0:T(8,128)(2,1)}, b...) custom-call(f32[4096,128]{1,0:T(8,128)} %refs_4_.3, ...), custom_call_target="tpu_custom_call" | custom-call | bytes 285000000 | tf_op jit(solution)/shard_map/pallas_call | solution.py:769
  171.8 3.1 multiply_sine_fusion
  174.8 43.8 %shard_map.647 = (bf16[1024,512]{1,0:T(8,128)(2,1)}, bf16[1024,512]{1,0:T(8,128)(2,1)}, bf16[128,2048]{1,0:T(8,128)(2,1)}, f32[512,128]{1,0:T(8,128)}, f32[1024,...) custom-call(s32[4]{0:T(128)} %l_ref.3, ...), custom_call_target="tpu_custom_call" | custom-call | bytes 120000000 | tf_op jit(solution)/shard_map/pallas_call | solution.py:1975
  219.5 1.4 copy.82
  220.9 0.8 reshape.163.w_ref
  221.7 3.3 convolution_convert_fusion
  225.0 44.4 %shard_map.648 = (f32[128,2048]{1,0:T(8,128)}, bf16[256,2048]{1,0:T(8,128)(2,1)}, bf16[256,2048]{1,0:T(8,128)(2,1)}) custom-call(bf16[2,4,128,2048]{3,2,1,0:T(8,128)(2,1)} %bitcast.57, bf16[128,512]{1,0:T(8,128)(2,1)} %copy-done.32, bf16[128,512]{1,0:T(8,128)(2,1)} %copy-done.33), custom_call_target="tpu_custom_call" | custom-call | bytes 135000000 | tf_op jit(solution)/shard_map/pallas_call | solution.py:769
  269.5 4.1 shard_map.649
  273.6 86.7 %shard_map.650 = (f32[128,2048]{1,0:T(8,128)}, bf16[2048,1024]{1,0:T(8,128)(2,1)}, bf16[1024,1024]{1,0:T(8,128)(2,1)}, f32[4,256,1024]{2,1,0:T(8,128)}, f32[4,25...) custom-call(bf16[128,2048]{1,0:T(8,128)(2,1)} %get-tuple-element.200.x_ref, bf16[4,2,2048,256]{3,2,1,0:T(8,128)(2,1)} %bitcast.55, ...), custom_call_target="tpu_custom_call" | custom-call | bytes 240000000 | tf_op jit(solution)/shard_map/pallas_call | solution.py:1484
  360.3 7.0 shard_map.651
  367.3 83.9 %shard_map.652 = (f32[128,2048]{1,0:T(8,128)}, bf16[4,2,2048,256]{3,2,1,0:T(8,128)(2,1)}, bf16[4,1024,512]{2,1,0:T(8,128)(2,1)}) custom-call(bf16[128,2048]{1,0:T(8,128)(2,1)} %get-tuple-element.211.x_ref, bf16[4,2,2048,256]{3,2,1,0:T(8,128)(2,1)} %bitcast.56, bf16[4,1024,512]{2,1,0:T(8,128)(2,1)} %bitcast.60, bf16[2048,1024]{1,0:T(8,128)(2,1)} %get-tuple-element.212.xt_hbm, ...), custom_call_target="tpu_custom_call" | custom-call | bytes 270000000 | tf_op jit(solution)/shard_map/pallas_call | solution.py:1676
  451.3 8.8 %shard_map.653 = (bf16[128,2048]{1,0:T(8,128)(2,1)}, bf16[128,2048]{1,0:T(8,128)(2,1)}, bf16[128,64]{1,0:T(8,128)(2,1)}, bf16[640,2048]{1,0:T(8,128)(2,1)}, f32[...) custom-call(f32[128,2048]{1,0:T(8,128)} %get-tuple-element.210.refs_0_, ...), custom_call_target="tpu_custom_call" | custom-call | bytes 15000000 | tf_op jit(solution)/shard_map/pallas_call | solution.py:787
  460.0 45.6 %shard_map.654 = (bf16[2,4,128,2048]{3,2,1,0:T(8,128)(2,1)}, f32[320,512]{1,0:T(8,128)}) custom-call(bf16[128,2048]{1,0:T(8,128)(2,1)} %get-tuple-element.222.refs_0_, bf16[2,320,2048]{2,1,0:T(8,128)(2,1)} %bitcast.68), custom_call_target="tpu_custom_call" | custom-call | bytes 150000000 | tf_op jit(solution)/shard_map/pallas_call | solution.py:769
  505.7 34.4 %shard_map.655 = (bf16[1024,256]{1,0:T(8,128)(2,1)}, bf16[4,512,256]{2,1,0:T(8,128)(2,1)}, f32[1,256]{1,0:T(1,128)}, bf16[256,2048]{1,0:T(8,128)(2,1)}, bf16[512...) custom-call(s32[4]{0:T(128)} %l_ref.3, s32[4,2]{1,0:T(4,128)} %copy.80.s_ref, ...), custom_call_target="tpu_custom_call" | custom-call | bytes 75000000 | tf_op jit(solution)/shard_map/pallas_call | solution.py:2058
  540.1 42.2 %shard_map.656 = (bf16[4,1024,256]{2,1,0:T(8,128)(2,1)}, f32[512,256]{1,0:T(8,128)}) custom-call(bf16[1024,256]{1,0:T(8,128)(2,1)} %get-tuple-element.234.refs_0_, bf16[4,512,256]{2,1,0:T(8,128)(2,1)} %get-tuple-element.235.refs_1_), custom_call_target="tpu_custom_call" | custom-call | bytes 135000000 | tf_op jit(solution)/shard_map/pallas_call | solution.py:769
  582.4 1.0 copy-done.22
  583.4 1.0 copy-done.30
  584.4 0.9 copy-done.34
  585.3 0.9 copy-done.35
  586.5 1.6 copy-done.9
  588.1 1.2 copy-done.16
  589.3 61.1 %shard_map.658 = (bf16[4,512,256]{2,1,0:T(8,128)(2,1)S(1)}, f32[1024,512]{1,0:T(8,128)S(1)}, f32[8,256]{1,0:T(8,128)S(1)}, bf16[1024,256]{1,0:T(8,128)(2,1)S(1)}...) custom-call(bf16[1024,512]{1,0:T(8,128)(2,1)S(1)} %copy-done.3, ...), custom_call_target="tpu_custom_call" | custom-call | bytes 195000000 | tf_op jit(solution)/shard_map/pallas_call | solution.py:769
  650.5 1.3 copy-done.7
  651.7 1.0 copy-done.13
  652.7 0.7 copy-done.26
  654.1 3.0 shard_map.659
  657.0 1.0 copy-done.15
  658.0 0.8 copy-done.20
  658.8 1.3 copy-done.14
  660.2 1.0 copy-done.21
  661.2 0.9 copy-done.27
  662.2 0.7 copy-done.45
  662.9 35.0 %shard_map.660 = (f32[512,256]{1,0:T(8,128)S(1)}, f32[512,256]{1,0:T(8,128)S(1)}, f32[320,128]{1,0:T(8,128)S(1)}, f32[2,4,8,1024]{3,2,1,0:T(8,128)S(1)}, f32[2,4...) custom-call(bf16[4,512,256]{2,1,0:T(8,128)(2,1)S(1)} %copy-done.14, ...), custom_call_target="tpu_custom_call" | custom-call | bytes 120000000 | tf_op jit(solution)/shard_map/pallas_call | solution.py:1083
  697.9 0.7 fusion
  698.6 1.0 copy-done.19
  699.7 0.9 copy-done.25
  700.6 0.9 copy-done.31
  701.5 0.7 copy-done.42
  702.9 0.7 copy-done.47
  703.6 0.7 copy-done.49
  704.3 1.9 shard_map.661
  706.1 13.3 %shard_map.662.x_ref = f32[128,128]{1,0:T(8,128)S(1)} custom-call(f32[128,128]{1,0:T(8,128)S(1)} %get-tuple-element.279.x_ref), custom_call_target="tpu_custom_call" | custom-call | bytes 42000000 | tf_op jit(solution)/shard_map/pallas_call | solution.py:1744
  722.5 20.6 %shard_map.663 = (f32[1,1]{1,0:T(1,128)}, f32[1,8]{1,0:T(1,128)}, f32[1024,1024]{1,0:T(8,128)}, f32[1024,1024]{1,0:T(8,128)}, f32[1024,1024]{1,0:T(8,128)}, /*in...) custom-call(f32[128,128]{1,0:T(8,128)} %copy-done.18, ...), custom_call_target="tpu_custom_call" | custom-call | bytes 75000000 | tf_op jit(solution)/shard_map/pallas_call | solution.py:1845
  743.2 0.8 copy.84
  (133 shorter events, 9.2 us)
Async XLA Ops:
  7.2 2.8 copy-start.54
  7.2 2.8 copy-start.53
  7.2 2.8 copy-start.52
  7.3 2.9 copy-start.57
  7.3 2.9 copy-start.58
  7.3 2.9 copy-start.59
  7.3 2.9 copy-start.36
  7.3 211.4 %all-gather.5.cloned.1.call-start = ((), (), s32[]{:S(2)}) async-start(), calls=%async_computation.2 | async-start | bytes 10485760 | tf_op jit(solution)/shard_map/all_gather | solution.py:2220
  10.0 62.3 %copy-start.60 = (s32[4,2]{0,1:T(2,128)S(1)}, s32[4,2]{0,1:T(2,128)}, u32[]{:S(2)}) copy-start(s32[4,2]{0,1:T(2,128)} %param.42) | copy-start | bytes 100
  67.7 1.3 copy-start
  71.7 201.9 %all-gather.7.cloned.1.call-start = ((), (), s32[]{:S(2)}) async-start(), calls=%async_computation.3 | async-start | bytes 5242880 | tf_op jit(solution)/shard_map/all_gather | solution.py:2324
  174.8 44.4 %copy-start.55 = (bf16[4,256,512]{2,1,0:T(8,128)(2,1)S(1)}, bf16[4,256,512]{2,1,0:T(8,128)(2,1)}, u32[]{:S(2)}) copy-start(bf16[4,256,512]{2,1,0:T(8,128)(2,1)} %get-tuple-element.193) | copy-start | bytes 3145732
  218.6 3.1 copy-start.51
  218.7 321.4 %reduce-scatter.7.cloned.1.call-start = ((), (), s32[]{:S(2)}) async-start(), calls=%async_computation.4 | async-start | bytes 10485760
  221.7 47.7 %copy-start.50 = (bf16[256,2048]{1,0:T(8,128)(2,1)}, bf16[256,2048]{1,0:T(8,128)(2,1)S(1)}, u32[]{:S(2)}) copy-start(bf16[256,2048]{1,0:T(8,128)(2,1)S(1)} %reshape.163.w_ref) | copy-start | bytes 3145732
  451.2 207.6 %reduce-scatter.9.cloned.1.call-start = ((), (), s32[]{:S(2)}) async-start(), calls=%async_computation.5 | async-start | bytes 5242880
  540.0 42.3 %copy-start.24 = (f32[9,256]{1,0:T(8,128)S(1)}, f32[9,256]{1,0:T(8,128)}, u32[]{:S(2)}) copy-start(f32[9,256]{1,0:T(8,128)} %refs_40_.1) | copy-start | bytes 27652
  540.1 42.3 %copy-start.29 = (f32[256,256]{1,0:T(8,128)S(1)}, f32[256,256]{1,0:T(8,128)}, u32[]{:S(2)}) copy-start(f32[256,256]{1,0:T(8,128)} %get-tuple-element.239.refs_1_) | copy-start | bytes 786436
  540.1 46.4 %copy-start.1 = (bf16[4,512,512]{2,1,0:T(8,128)(2,1)S(1)}, bf16[4,512,512]{2,1,0:T(8,128)(2,1)}, u32[]{:S(2)}) copy-start(bf16[4,512,512]{2,1,0:T(8,128)(2,1)} %copy-done) | copy-start | bytes 6291460
  540.1 46.4 %copy-start.3 = (bf16[1024,512]{1,0:T(8,128)(2,1)S(1)}, bf16[1024,512]{1,0:T(8,128)(2,1)}, u32[]{:S(2)}) copy-start(bf16[1024,512]{1,0:T(8,128)(2,1)} %get-tuple-element.230.refs_0_) | copy-start | bytes 3145732
  582.4 1.0 copy-start.22
  583.4 1.0 copy-start.30
  586.5 64.0 %copy-start.48 = (f32[1,256]{1,0:T(1,128)}, f32[1,256]{1,0:T(1,128)S(1)}, u32[]{:S(2)}) copy-start(f32[1,256]{1,0:T(1,128)S(1)} %get-tuple-element.267.refs_11_) | copy-start | bytes 3076
  586.5 1.6 copy-start.9
  588.1 1.2 copy-start.16
  589.3 64.7 %copy-start.12 = (bf16[1024,512]{1,0:T(8,128)(2,1)S(1)}, bf16[1024,512]{1,0:T(8,128)(2,1)}, u32[]{:S(2)}) copy-start(bf16[1024,512]{1,0:T(8,128)(2,1)} %get-tuple-element.250.refs_5_) | copy-start | bytes 3145732
  589.3 64.7 %copy-start.17 = (f32[320,512]{1,0:T(8,128)S(1)}, f32[320,512]{1,0:T(8,128)}, u32[]{:S(2)}) copy-start(f32[320,512]{1,0:T(8,128)} %get-tuple-element.251.refs_7_) | copy-start | bytes 1966084
  589.3 64.7 %copy-start.23 = (f32[6,512]{1,0:T(8,128)S(1)}, f32[6,512]{1,0:T(8,128)}, u32[]{:S(2)}) copy-start(f32[6,512]{1,0:T(8,128)} %refs_36_.1) | copy-start | bytes 36868
  650.4 1.3 copy-start.7
  651.7 1.0 copy-start.13
  654.0 44.6 %copy-start.38 = (f32[1,2048]{1,0:T(1,128)S(1)}, f32[1,2048]{1,0:T(1,128)}, u32[]{:S(2)}) copy-start(f32[1,2048]{1,0:T(1,128)} %get-tuple-element.272.refs_16_) | copy-start | bytes 24580
  654.0 44.5 %copy-start.39 = (f32[1,2048]{1,0:T(1,128)S(1)}, f32[1,2048]{1,0:T(1,128)}, u32[]{:S(2)}) copy-start(f32[1,2048]{1,0:T(1,128)} %get-tuple-element.273.refs_17_) | copy-start | bytes 24580
  654.0 44.5 %copy-start.40 = (f32[1,2048]{1,0:T(1,128)S(1)}, f32[1,2048]{1,0:T(1,128)}, u32[]{:S(2)}) copy-start(f32[1,2048]{1,0:T(1,128)} %get-tuple-element.269.refs_13_) | copy-start | bytes 24580
  654.1 44.5 %copy-start.41 = (f32[1,2048]{1,0:T(1,128)S(1)}, f32[1,2048]{1,0:T(1,128)}, u32[]{:S(2)}) copy-start(f32[1,2048]{1,0:T(1,128)} %get-tuple-element.270.refs_14_) | copy-start | bytes 24580
  657.0 1.0 copy-start.15
  658.8 39.8 %copy-start.4 = (bf16[64,2048]{1,0:T(8,128)(2,1)S(1)}, bf16[64,2048]{1,0:T(8,128)(2,1)}, u32[]{:S(2)}) copy-start(bf16[64,2048]{1,0:T(8,128)(2,1)} %get-tuple-element.197.refs_3_.refs_7_) | copy-start | bytes 786436
  658.8 39.8 %copy-start.8 = (bf16[512,512]{1,0:T(8,128)(2,1)S(1)}, bf16[512,512]{1,0:T(8,128)(2,1)}, u32[]{:S(2)}) copy-start(bf16[512,512]{1,0:T(8,128)(2,1)} %refs_4_.2) | copy-start | bytes 1572868
  658.8 39.8 %copy-start.2 = (bf16[1,4,256,512]{3,2,1,0:T(8,128)(2,1)S(1)}, bf16[1,4,256,512]{3,2,1,0:T(8,128)(2,1)}, u32[]{:S(2)}) copy-start(bf16[1,4,256,512]{3,2,1,0:T(8,128)(2,1)} %reduce-scatter.9.cloned.1.call-done) | copy-start | bytes 3145732
  658.8 1.4 copy-start.14
  660.2 1.0 copy-start.21
  662.9 35.8 %copy-start.44 = (f32[8,256]{1,0:T(8,128)S(1)}, f32[8,256]{1,0:T(8,128)}, u32[]{:S(2)}) copy-start(f32[8,256]{1,0:T(8,128)} %copy-done.43) | copy-start | bytes 24580
  697.8 8.3 %copy-start.10 = (bf16[4,4,256,128]{3,2,1,0:T(8,128)(2,1)}, bf16[4,4,256,128]{3,2,1,0:T(8,128)(2,1)S(1)}, u32[]{:S(2)}) copy-start(bf16[4,4,256,128]{3,2,1,0:T(8,128)(2,1)S(1)} %get-tuple-element.281) | copy-start | bytes 3145732
  697.8 24.7 %copy-start.5 = (f32[512,256]{1,0:T(8,128)}, f32[512,256]{1,0:T(8,128)S(1)}, u32[]{:S(2)}) copy-start(f32[512,256]{1,0:T(8,128)S(1)} %get-tuple-element.274.refs_18_.refs_11_) | copy-start | bytes 1572868
  697.9 24.7 %copy-start.6 = (f32[512,256]{1,0:T(8,128)}, f32[512,256]{1,0:T(8,128)S(1)}, u32[]{:S(2)}) copy-start(f32[512,256]{1,0:T(8,128)S(1)} %get-tuple-element.275.refs_19_.refs_15_) | copy-start | bytes 1572868
  697.9 24.7 %copy-start.11 = (bf16[4,256,128]{2,1,0:T(8,128)(2,1)}, bf16[4,256,128]{2,1,0:T(8,128)(2,1)S(1)}, u32[]{:S(2)}) copy-start(bf16[4,256,128]{2,1,0:T(8,128)(2,1)S(1)} %get-tuple-element.277) | copy-start | bytes 786436
  698.6 1.0 copy-start.19
  719.4 3.1 copy-start.18
  722.5 20.6 %copy-start.56 = (bf16[512,512]{1,0:T(8,128)(2,1)S(1)}, bf16[512,512]{1,0:T(8,128)(2,1)}, u32[]{:S(2)}) copy-start(bf16[512,512]{1,0:T(8,128)(2,1)} %get-tuple-element.365) | copy-start | bytes 1572868
  (17 other events, 12.7 us)
Sparse Core Ops, SparseCore 0:
  71.8 91.3 all-gather.4
  218.8 51.2 all-gather.6
  451.3 84.5 reduce-scatter.6
  540.3 53.5 reduce-scatter.8

commit v8 on v7

--- a/solution.py
+++ b/solution.py
@@ -1393,17 +1393,18 @@
     return values_in * half, slope
 
 
-def ffn_forward(block, gateup, down, items, ident):
+def ffn_forward(block, gateup, downs, items, ident):
     count = lax.axis_size("row")
     share, width = block.shape
     groups, _, _, part = gateup.shape
     hidden = groups * part
-    out_cols = down.shape[2] // count
+    down_shape = (groups, hidden, downs[0].shape[2])
+    out_cols = down_shape[2] // count
     rows = 2 * share
     bundle = Bundle(items)
     number = bundle.number
 
-    def kernel(x_ref, gw_hbm, dw_hbm, *refs):
+    def kernel(x_ref, gw_hbm, dw_one, dw_two, *refs):
         x_refs, refs = refs[:number], refs[number:]
         o_ref, xt_hbm, at_hbm, g_hbm, u_hbm = refs[:5]
         o_refs, scratch = refs[5 : 5 + number], refs[5 + number :]
@@ -1412,13 +1413,18 @@
         gw_sem, dw_sem, xt_sem, at_sem, g_sem, u_sem = scratch[26:32]
         bundle.bind(x_refs, o_refs, scratch[32:])
         gw_load = pltpu.make_async_copy(gw_hbm, gw, gw_sem)
-        dw_load = pltpu.make_async_copy(dw_hbm, dw, dw_sem)
+        dw_loads = [
+            pltpu.make_async_copy(source, dw.at[:, pl.ds(k * hidden // 2, hidden // 2)], dw_sem.at[k])
+            for k, source in enumerate((dw_one, dw_two))
+        ]
         gw_load.start()
-        dw_load.start()
+        for dw_load in dw_loads:
+            dw_load.start()
         bundle.greet(False, True)
         flow.start()
         gw_load.wait()
-        dw_load.wait()
+        for dw_load in dw_loads:
+            dw_load.wait()
 
         def stores(source):
             return (
@@ -1491,38 +1497,39 @@
             jax.ShapeDtypeStruct((count, rows, hidden), FULL),
         ]
         + bundle.shapes,
-        in_specs=[vmem, anywhere, anywhere] + bundle.specs,
+        in_specs=[vmem] + [anywhere] * 3 + bundle.specs,
         out_specs=[vmem] + [anywhere] * 4 + bundle.specs,
         scratch_shapes=buffers
         + sems
         + [
             pltpu.VMEM(gateup.shape, LOW),
-            pltpu.VMEM(down.shape, LOW),
+            pltpu.VMEM(down_shape, LOW),
             pltpu.VMEM((width, tokens), LOW),
             pltpu.VMEM((hidden, tokens), LOW),
             pltpu.VMEM((count, rows, hidden), LOW),
             pltpu.VMEM((count, rows, hidden), FULL),
             pltpu.VMEM((count, rows, hidden), FULL),
         ]
-        + [dma, dma, dma, dma, dma((count,)), dma((count,))]
+        + [dma, dma((2,)), dma, dma, dma((count,)), dma((count,))]
         + bundle.scratch,
         compiler_params=params(ident, 60),
         cost_estimate=cost(80),
-    )(block, gateup, down, *bundle.sources)
-
-
-def ffn_backward(block, gateup, down, xt, at, gate, up, items, ident):
+    )(block, gateup, *downs, *bundle.sources)
+
+
+def ffn_backward(block, gateup, downs, xt, at, gate, up, items, ident):
     count = lax.axis_size("row")
     share, width = block.shape
     groups, _, _, part = gateup.shape
     hidden = groups * part
-    out_cols = down.shape[2] // count
+    down_shape = (groups, hidden, downs[0].shape[2])
+    out_cols = down_shape[2] // count
     rows = 2 * share
     tokens = count * rows
     bundle = Bundle(items)
     number = bundle.number
 
-    def kernel(x_ref, gw_hbm, dw_hbm, xt_hbm, at_hbm, g_hbm, u_hbm, *refs):
+    def kernel(x_ref, gw_hbm, dw_one, dw_two, xt_hbm, at_hbm, g_hbm, u_hbm, *refs):
         x_refs, refs = refs[:number], refs[number:]
         o_ref, dgu_hbm, ddn_hbm = refs[:3]
         o_refs, scratch = refs[3 : 3 + number], refs[3 + number :]
@@ -1533,7 +1540,13 @@
         loads = [
             pltpu.make_async_copy(source, target, load_sems.at[k])
             for k, (source, target) in enumerate(
-                [(dw_hbm, dw), (gw_hbm, gw), (xt_hbm, xt_own), (at_hbm, at_own)]
+                [
+                    (dw_one, dw.at[:, pl.ds(0, hidden // 2)]),
+                    (dw_two, dw.at[:, pl.ds(hidden // 2, hidden // 2)]),
+                    (gw_hbm, gw),
+                    (xt_hbm, xt_own),
+                    (at_hbm, at_own),
+                ]
             )
         ]
 
@@ -1543,7 +1556,7 @@
                 pltpu.make_async_copy(u_hbm.at[source], up_own.at[source], u_sem.at[source]),
             )
 
-        for load in loads[:2]:
+        for load in loads[:3]:
             load.start()
 
         @pl.loop(0, count)
@@ -1551,12 +1564,12 @@
             for copy in fetches(source):
                 copy.start()
 
-        for load in loads[2:]:
+        for load in loads[3:]:
             load.start()
         bundle.greet(False, True)
         flow.start()
-        loads[0].wait()
-        loads[1].wait()
+        for load in loads[:3]:
+            load.wait()
 
         def columns_of(s, d):
             return pl.ds(pl.multiple_of((s * groups + d) * out_cols, out_cols), out_cols)
@@ -1640,8 +1653,8 @@
         def early(k, d):
             @pl.when(k == count - 1)
             def _():
-                loads[2].wait()
                 loads[3].wait()
+                loads[4].wait()
 
             @pl.when(d >= 0)
             def _():
@@ -1678,16 +1691,16 @@
         out_shape=[
             jax.ShapeDtypeStruct((share, width), FULL),
             jax.ShapeDtypeStruct(gateup.shape, LOW),
-            jax.ShapeDtypeStruct(down.shape, LOW),
+            jax.ShapeDtypeStruct(down_shape, LOW),
         ]
         + bundle.shapes,
-        in_specs=[vmem] + [anywhere] * 6 + bundle.specs,
+        in_specs=[vmem] + [anywhere] * 7 + bundle.specs,
         out_specs=[vmem, anywhere, anywhere] + bundle.specs,
         scratch_shapes=buffers
         + sems
         + [
             pltpu.VMEM(gateup.shape, LOW),
-            pltpu.VMEM(down.shape, LOW),
+            pltpu.VMEM(down_shape, LOW),
             pltpu.VMEM((width, tokens), LOW),
             pltpu.VMEM((hidden, tokens), LOW),
             pltpu.VMEM((count, rows, hidden), FULL),
@@ -1698,11 +1711,11 @@
             pltpu.VMEM((2, width, part), LOW),
             pltpu.VMEM((hidden, count * out_cols), LOW),
         ]
-        + [dma((4,)), dma((count,)), dma((count,)), dma((2,)), dma]
+        + [dma((5,)), dma((count,)), dma((count,)), dma((2,)), dma]
         + bundle.scratch,
         compiler_params=params(ident, 62),
         cost_estimate=cost(90),
-    )(block, gateup, down, xt, at, gate, up, *bundle.sources)
+    )(block, gateup, *downs, xt, at, gate, up, *bundle.sources)
 
 
 def last_sums(small, ident):
@@ -1886,7 +1899,7 @@
     return [lengths_ref[at]] + [starts_ref[at, piece] for piece in range(starts_ref.shape[1])]
 
 
-def attention_forward_head(acts, gains, head_w, key_w, value_w, heads, cos_tab, sin_tab, extras, lengths, starts, items, ident):
+def attention_forward_head(acts, gains, head_w, key_w, value_w, attend_w, heads, cos_tab, sin_tab, extras, lengths, starts, items, ident):
     tokens, width = acts.shape
     step = 256
     bundle = Bundle(items)
@@ -1894,12 +1907,13 @@
     rows_n, cols_n = lax.axis_size("row"), lax.axis_size("col")
     half_tok, wide = tokens // cols_n, width // rows_n
     share, quarter = half_tok // rows_n, tokens // rows_n
-
-    def kernel(l_ref, s_ref, x_ref, gain_ref, qw_ref, kw_ref, vw_ref, heads_ref, cos_ref, sin_ref, e_ref, *refs):
+    groups, out_cols = attend_w.shape[0], attend_w.shape[2] // rows_n
+
+    def kernel(l_ref, s_ref, x_ref, gain_ref, qw_ref, kw_ref, vw_ref, aw_ref, heads_ref, cos_ref, sin_ref, e_ref, *refs):
         x_refs, refs = refs[:number], refs[number:]
         hidden_ref, acts_ref, share_ref, scale_ref, qr_ref, kr_ref, vr_ref = refs[:7]
-        q_ref, k_ref, v_ref, o_ref, top_ref, es_ref, oc_ref, os_ref = refs[7:15]
-        o_refs, refs = refs[15 : 15 + number], refs[15 + number :]
+        q_ref, k_ref, v_ref, o_ref, top_ref, es_ref, oc_ref, os_ref, p_ref = refs[7:16]
+        o_refs, refs = refs[16 : 16 + number], refs[16 + number :]
         h_ref, sc_ref, key_ref, value_ref = refs[:4]
         bundle.bind(x_refs, o_refs, refs[4:])
         bundle.greet()
@@ -1930,7 +1944,13 @@
             here = pl.ds(pl.multiple_of(at * step, step), step)
             allowed = allowed_block(at, step, tokens, spans)
             probs, peak_row = softmax_block(q_ref[here], k_ref[...], allowed)
-            o_ref[here] = flat_dot(probs.astype(LOW), v_ref[...]).astype(LOW)
+            outputs = flat_dot(probs.astype(LOW), v_ref[...]).astype(LOW)
+            o_ref[here] = outputs
+            for d in range(groups):
+                part = flat_dot(outputs, aw_ref[d])
+                for s in range(rows_n):
+                    cut = slice((s * groups + d) * out_cols, (s * groups + d + 1) * out_cols)
+                    p_ref[here, cut] = part[:, s * out_cols : (s + 1) * out_cols].astype(LOW)
             top_ref[...] = jnp.maximum(top_ref[...], jnp.max(peak_row))
 
         top_ref[...] = jnp.full(top_ref.shape, NEGATIVE, FULL)
@@ -1990,10 +2010,11 @@
             low(share, PLD),
             full(quarter, HEAD_WIDTH // 2),
             full(quarter, HEAD_WIDTH // 2),
+            low(tokens, width),
         ]
         + bundle.shapes,
-        in_specs=[smem, smem] + [vmem] * 9 + bundle.specs,
-        out_specs=[vmem] * 15 + bundle.specs,
+        in_specs=[smem, smem] + [vmem] * 10 + bundle.specs,
+        out_specs=[vmem] * 16 + bundle.specs,
         scratch_shapes=[
             pltpu.VMEM((tokens, width), LOW),
             pltpu.VMEM((tokens, 128), FULL),
@@ -2003,7 +2024,9 @@
         + bundle.scratch,
         compiler_params=params(ident, 60),
         cost_estimate=cost(40),
-    )(lengths, starts, acts, gains, head_w, key_w, value_w, heads, cos_tab, sin_tab, extras, *bundle.sources)
+    )(
+        lengths, starts, acts, gains, head_w, key_w, value_w, attend_w, heads, cos_tab, sin_tab, extras, *bundle.sources
+    )
 
 
 def head_backward(queries, keys, values, attended, grads, attend_w, query_raw, heads, cos_tab, sin_tab, lengths, starts, items, ident):
@@ -2013,6 +2036,7 @@
     number = bundle.number
     devices = lax.axis_size("row")
     quarter = rows // devices
+    groups, out_cols = attend_w.shape[0], attend_w.shape[2] // devices
 
     def kernel(l_ref, s_ref, q_ref, k_ref, v_ref, a_ref, g_ref, w_ref, r_ref, heads_ref, cos_ref, sin_ref, *refs):
         x_refs, refs = refs[:number], refs[number:]
@@ -2032,7 +2056,18 @@
         def _(at):
             here = pl.ds(pl.multiple_of(at * step, step), step)
             allowed = allowed_block(at, step, keys.shape[0], spans)
-            block_rows, grad_rows = q_ref[here], against(g_ref[here], w_ref[...]).astype(LOW)
+            block_rows, grad_rows = q_ref[here], None
+            for d in range(groups):
+                cut = jnp.concatenate(
+                    [
+                        g_ref[here, (s * groups + d) * out_cols : (s * groups + d + 1) * out_cols]
+                        for s in range(devices)
+                    ],
+                    axis=1,
+                )
+                term = against(cut, w_ref[d])
+                grad_rows = term if grad_rows is None else grad_rows + term
+            grad_rows = grad_rows.astype(LOW)
             probs, _ = softmax_block(block_rows, k_ref[...], allowed)
             grad_probs = against(grad_rows, v_ref[...])
             delta_row = jnp.sum(probs * grad_probs, axis=-1, keepdims=True)
@@ -2188,7 +2223,13 @@
             True,
         )
 
-    gateup_own, attend_own, qkv_w, left_t, right_w, pergate_t, perproj_w = transfers(
+    def lower(inputs, outputs):
+        @pl.loop(0, inputs[0].shape[0] // 256)
+        def _(at):
+            rows = pl.ds(pl.multiple_of(at * 256, 256), 256)
+            outputs[0][rows] = inputs[0][rows].astype(LOW)
+
+    down_low, gateup_own, attend_own, qkv_w, left_t, right_w, pergate_t, perproj_w = transfers(
         [
             Swap(
                 w_gateup.astype(LOW),
@@ -2216,17 +2257,24 @@
         ],
         1,
         60,
-    )
+        16,
+        lower,
+        (w_down,),
+        [jax.ShapeDtypeStruct(w_down.shape, LOW)],
+    )
+    down_low = down_low.reshape(data_n, rows_n, ff_part, out_cols)
+
+    def down_half(k):
+        return Swap(
+            down_low[k * data_n // 2 : (k + 1) * data_n // 2],
+            (data_n // 2, ff_part, rows_n * out_cols),
+            lambda ref, q: ref.at[:, q],
+            lambda ref, at: ref.at[:, :, columns_of(at, out_cols)],
+        )
+
     gateup_all = lax.all_gather(gateup_own, "dp")
-
-    def lower(inputs, outputs):
-        @pl.loop(0, inputs[0].shape[0] // 256)
-        def _(at):
-            rows = pl.ds(pl.multiple_of(at * 256, 256), 256)
-            outputs[0][rows] = inputs[0][rows].astype(LOW)
-
     last = pl.ds(HEAD_WIDTH, HEAD_WIDTH)
-    down_low, whole_acts, whole_key, whole_value, head_w, gains, extras, attend_all = transfers(
+    whole_acts, whole_key, whole_value, head_w, gains, extras, attend_all, down_one = transfers(
         [
             along(activations),
             Line(
@@ -2263,19 +2311,14 @@
                 lambda ref, at: ref.at[at],
                 "dp",
             ),
+            down_half(0),
         ],
         2,
-        95,
+        105,
         60,
-        lower,
-        (w_down,),
-        [jax.ShapeDtypeStruct(w_down.shape, LOW)],
-    )
-    attend_w = (
-        attend_all.reshape(data_n, HEAD_WIDTH, rows_n, out_cols)
-        .transpose(1, 2, 0, 3)
-        .reshape(HEAD_WIDTH, width)
-    )
+    )
+    down_one, gateup_all = lax.optimization_barrier((down_one, gateup_all))
+    down_one = lax.all_gather(down_one, "dp").reshape(data_n, data_n * ff_part // 2, -1)
     all_cos, all_sin = rope_tables(jnp.arange(tokens, dtype=jnp.int32), HEAD_WIDTH)
     (
         spread_h,
@@ -2293,15 +2336,17 @@
         extras,
         own_cos,
         own_sin,
+        projected,
         left_t,
         right_w,
-        down_own,
+        down_two,
     ) = attention_forward_head(
         whole_acts,
         gains,
         head_w,
         whole_key,
         whole_value,
+        attend_all,
         w_heads,
         all_cos,
         all_sin,
@@ -2311,24 +2356,19 @@
         [
             along(left_t.astype(LOW)),
             along(right_w),
-            Swap(
-                down_low.reshape(data_n, rows_n, ff_part, out_cols),
-                (data_n, ff_part, rows_n * out_cols),
-                lambda ref, q: ref.at[:, q],
-                lambda ref, at: ref.at[:, :, columns_of(at, out_cols)],
-            ),
+            down_half(1),
         ],
         3,
     )
-    down_own, gateup_all = lax.optimization_barrier((down_own, gateup_all))
-    down_all = lax.all_gather(down_own, "dp").reshape(data_n, data_n * ff_part, -1)
-    def shares(parts):
-        return parts.astype(LOW).reshape(cols_n, rows_n, share, width)
-
+    down_two, down_one = lax.optimization_barrier((down_two, down_one))
+    down_two = lax.all_gather(down_two, "dp").reshape(data_n, data_n * ff_part // 2, -1)
+    down_all = (down_one, down_two)
     projected, pergate_t, perproj_w = transfers(
         [
             Reduce(
-                shares(flat_dot(attended, attend_w)), (share, width), lambda ref, q: ref.at[q]
+                projected.reshape(cols_n, rows_n, share, width),
+                (share, width),
+                lambda ref, q: ref.at[q],
             ),
             along(pergate_t),
             along(perproj_w),
@@ -2429,7 +2469,7 @@
         values,
         attended,
         spread_p,
-        attend_w,
+        attend_all,
         query_raw,
         w_heads,
         all_cos,

time: 758 us -> 754 us (level)
    pallas_call x1, Pallas kernels: 43.8 us -> 35.1 us  [attention_forward_head(): pl.pallas_call(kernel, out_shape=[low(tokens, wide), low(tokens, wide), l...]
    unnamed x124 -> x120, local copies, waits for them, and re-layouts: 27.1 us -> 28.4 us
  transfers between devices with their start and end apart: 4 -> 5, of which waited for: 0 -> 0; matrix products, arithmetic and copies ran while one was open for 1% -> 1% of each run, Pallas kernels for 51% -> 52%
where the time goes in v8:
time: 754 us; the launch traced here: 745 us
  Pallas kernels  690 us (92%)
  local copies, waits for them, and re-layouts  32 us (4%)
  between operations  14.9 us (2%)
  other arithmetic  7.68 us (1%)
    pallas_call x6, Pallas kernels, transfers(): pl.pallas_call(kernel, out_shape=list(shapes) + bundle.shapes, in_specs=[...  356 us
    pallas_call x1, Pallas kernels, ffn_forward(): pl.pallas_call(kernel, out_shape=[jax.ShapeDtypeStruct((share, width), FU...  86.7 us
    pallas_call x1, Pallas kernels, ffn_backward(): pl.pallas_call(kernel, out_shape=[jax.ShapeDtypeStruct((share, width), FU...  83.9 us
    pallas_call x1, Pallas kernels, attention_forward_head(): pl.pallas_call(kernel, out_shape=[low(tokens, wide), low(tokens, wide), l...  35.1 us
    pallas_call x1, Pallas kernels, shard_total(): pl.pallas_call(kernel, out_shape=[jax.ShapeDtypeStruct(shape, FULL) for s...  35 us
    pallas_call x1, Pallas kernels, head_backward(): pl.pallas_call(kernel, out_shape=[jax.ShapeDtypeStruct(queries.shape, LOW...  34.4 us
    unnamed x120, local copies, waits for them, and re-layouts  28.4 us
    pallas_call x5, Pallas kernels, local(): pl.pallas_call(kernel, out_shape=[jax.ShapeDtypeStruct(shape, kind) for s...  23 us
  transfers between devices with their start and end apart: 5, of which 0 were waited for; matrix products, arithmetic and copies ran while one was open for 1% of the time, Pallas kernels for 52%

profile of v8, /device:TPU:0, one launch (start us, length us, event | category | flops | bytes accessed | tf_op | source)
XLA Modules:
  0.0 745.2 jit_solution(4077116214277567202)
XLA Ops:
  7.3 2.6 convert_element_type.45.refs_1_
  10.2 1.3 copy-done.2
  11.6 57.4 %shard_map.645 = (bf16[4096,128]{1,0:T(8,128)(2,1)S(1)}, bf16[2,2048,256]{2,1,0:T(8,128)(2,1)}, bf16[256,512]{1,0:T(8,128)(2,1)S(1)}, bf16[4,512,512]{2,1,0:T(8,...) custom-call(f32[4096,128]{1,0:T(8,128)S(1)} %copy-done.2, ...), custom_call_target="tpu_custom_call" | custom-call | bytes 180000000 | tf_op jit(solution)/shard_map/pallas_call | solution.py:769
  69.0 1.3 copy-done
  70.3 0.7 copy-done.31
  73.0 1.0 fusion
  74.0 104.6 %shard_map.646 = (bf16[1024,2048]{1,0:T(8,128)(2,1)}, bf16[2048,256]{1,0:T(8,128)(2,1)}, bf16[2048,256]{1,0:T(8,128)(2,1)}, bf16[2048,256]{1,0:T(8,128)(2,1)}, f...) custom-call(bf16[512,512]{1,0:T(8,128)(2,1)} %refs_4_.4, ...), custom_call_target="tpu_custom_call" | custom-call | bytes 315000000 | tf_op jit(solution)/shard_map/pallas_call | solution.py:769
  179.4 0.7 copy.78.s_ref
  180.1 3.0 multiply_sine_fusion
  183.1 35.1 %shard_map.647 = (bf16[1024,512]{1,0:T(8,128)(2,1)}, bf16[1024,512]{1,0:T(8,128)(2,1)}, bf16[128,2048]{1,0:T(8,128)(2,1)}, f32[512,128]{1,0:T(8,128)}, f32[1024,...) custom-call(s32[4]{0:T(128)} %l_ref.3, ...), custom_call_target="tpu_custom_call" | custom-call | bytes 120000000 | tf_op jit(solution)/shard_map/pallas_call | solution.py:1995
  218.3 45.2 %shard_map.648 = (f32[128,2048]{1,0:T(8,128)}, bf16[256,2048]{1,0:T(8,128)(2,1)}, bf16[256,2048]{1,0:T(8,128)(2,1)}) custom-call(bf16[2,4,128,2048]{3,2,1,0:T(8,128)(2,1)} %bitcast.64, bf16[128,512]{1,0:T(8,128)(2,1)} %copy-done.33, bf16[128,512]{1,0:T(8,128)(2,1)} %copy-done.34), custom_call_target="tpu_custom_call" | custom-call | bytes 135000000 | tf_op jit(solution)/shard_map/pallas_call | solution.py:769
  263.6 4.1 shard_map.649
  267.7 86.7 %shard_map.650 = (f32[128,2048]{1,0:T(8,128)}, bf16[2048,1024]{1,0:T(8,128)(2,1)}, bf16[1024,1024]{1,0:T(8,128)(2,1)}, f32[4,256,1024]{2,1,0:T(8,128)}, f32[4,25...) custom-call(bf16[128,2048]{1,0:T(8,128)(2,1)} %get-tuple-element.205.x_ref, bf16[4,2,2048,256]{3,2,1,0:T(8,128)(2,1)} %bitcast.52, ...), custom_call_target="tpu_custom_call" | custom-call | bytes 240000000 | tf_op jit(solution)/shard_map/pallas_call | solution.py:1490
  354.4 6.9 shard_map.651
  361.4 83.9 %shard_map.652 = (f32[128,2048]{1,0:T(8,128)}, bf16[4,2,2048,256]{3,2,1,0:T(8,128)(2,1)}, bf16[4,1024,512]{2,1,0:T(8,128)(2,1)}) custom-call(bf16[128,2048]{1,0:T(8,128)(2,1)} %get-tuple-element.219.x_ref, bf16[4,2,2048,256]{3,2,1,0:T(8,128)(2,1)} %bitcast.53, bf16[4,512,512]{2,1,0:T(8,128)(2,1)} %bitcast.58, bf16[4,512,512]{2,1,0:T(8,128)(2,1)} %bitcast.60, ...), custom_call_target="tpu_custom_call" | custom-call | bytes 270000000 | tf_op jit(solution)/shard_map/pallas_call | solution.py:1689
  445.4 8.8 %shard_map.653 = (bf16[128,2048]{1,0:T(8,128)(2,1)}, bf16[128,2048]{1,0:T(8,128)(2,1)}, bf16[128,64]{1,0:T(8,128)(2,1)}, bf16[640,2048]{1,0:T(8,128)(2,1)}, f32[...) custom-call(f32[128,2048]{1,0:T(8,128)} %get-tuple-element.218.refs_0_, ...), custom_call_target="tpu_custom_call" | custom-call | bytes 15000000 | tf_op jit(solution)/shard_map/pallas_call | solution.py:787
  454.2 45.6 %shard_map.654 = (bf16[2,4,128,2048]{3,2,1,0:T(8,128)(2,1)}, f32[320,512]{1,0:T(8,128)}) custom-call(bf16[128,2048]{1,0:T(8,128)(2,1)} %get-tuple-element.230.refs_0_, bf16[2,320,2048]{2,1,0:T(8,128)(2,1)} %bitcast.66), custom_call_target="tpu_custom_call" | custom-call | bytes 150000000 | tf_op jit(solution)/shard_map/pallas_call | solution.py:769
  499.8 34.4 %shard_map.655 = (bf16[1024,256]{1,0:T(8,128)(2,1)}, bf16[4,512,256]{2,1,0:T(8,128)(2,1)}, f32[1,256]{1,0:T(1,128)}, bf16[256,2048]{1,0:T(8,128)(2,1)}, bf16[512...) custom-call(s32[4]{0:T(128)} %l_ref.3, s32[4,2]{1,0:T(4,128)} %copy.78.s_ref, ...), custom_call_target="tpu_custom_call" | custom-call | bytes 75000000 | tf_op jit(solution)/shard_map/pallas_call | solution.py:2093
  534.3 42.1 %shard_map.656 = (bf16[4,1024,256]{2,1,0:T(8,128)(2,1)}, f32[512,256]{1,0:T(8,128)}) custom-call(bf16[1024,256]{1,0:T(8,128)(2,1)} %get-tuple-element.242.refs_0_, bf16[4,512,256]{2,1,0:T(8,128)(2,1)} %get-tuple-element.243.refs_1_), custom_call_target="tpu_custom_call" | custom-call | bytes 135000000 | tf_op jit(solution)/shard_map/pallas_call | solution.py:769
  576.4 1.0 copy-done.23
  577.5 1.0 copy-done.30
  578.4 0.9 copy-done.35
  579.3 0.9 copy-done.36
  580.5 1.6 copy-done.9
  582.1 1.2 copy-done.17
  583.4 61.0 %shard_map.658 = (bf16[4,512,256]{2,1,0:T(8,128)(2,1)S(1)}, f32[1024,512]{1,0:T(8,128)S(1)}, f32[8,256]{1,0:T(8,128)S(1)}, bf16[1024,256]{1,0:T(8,128)(2,1)S(1)}...) custom-call(bf16[1024,512]{1,0:T(8,128)(2,1)S(1)} %copy-done.4, ...), custom_call_target="tpu_custom_call" | custom-call | bytes 195000000 | tf_op jit(solution)/shard_map/pallas_call | solution.py:769
  644.4 1.3 copy-done.8
  645.7 1.0 copy-done.14
  646.6 0.7 copy-done.27
  648.0 2.9 shard_map.659
  650.9 1.0 copy-done.16
  651.9 0.8 copy-done.21
  652.7 1.3 copy-done.15
  654.0 1.0 copy-done.22
  655.1 0.9 copy-done.28
  656.0 0.7 copy-done.46
  656.7 35.0 %shard_map.660 = (f32[512,256]{1,0:T(8,128)S(1)}, f32[512,256]{1,0:T(8,128)S(1)}, f32[320,128]{1,0:T(8,128)S(1)}, f32[2,4,8,1024]{3,2,1,0:T(8,128)S(1)}, f32[2,4...) custom-call(bf16[4,512,256]{2,1,0:T(8,128)(2,1)S(1)} %copy-done.15, ...), custom_call_target="tpu_custom_call" | custom-call | bytes 120000000 | tf_op jit(solution)/shard_map/pallas_call | solution.py:1083
  691.7 0.7 fusion.1
  692.5 1.1 copy-done.20
  693.5 0.9 copy-done.26
  694.5 0.9 copy-done.32
  695.4 0.7 copy-done.43
  696.1 0.7 copy-done.47
  697.4 0.7 copy-done.50
  698.0 1.8 shard_map.661
  699.9 13.9 %shard_map.662.x_ref = f32[128,128]{1,0:T(8,128)S(1)} custom-call(f32[128,128]{1,0:T(8,128)S(1)} %get-tuple-element.287.x_ref), custom_call_target="tpu_custom_call" | custom-call | bytes 42000000 | tf_op jit(solution)/shard_map/pallas_call | solution.py:1757
  717.0 20.4 %shard_map.663 = (f32[1,1]{1,0:T(1,128)}, f32[1,8]{1,0:T(1,128)}, f32[1024,1024]{1,0:T(8,128)}, f32[1024,1024]{1,0:T(8,128)}, f32[1024,1024]{1,0:T(8,128)}, /*in...) custom-call(f32[128,128]{1,0:T(8,128)} %copy-done.19, ...), custom_call_target="tpu_custom_call" | custom-call | bytes 75000000 | tf_op jit(solution)/shard_map/pallas_call | solution.py:1858
  737.4 0.8 copy.80
  (129 shorter events, 7.8 us)
Async XLA Ops:
  7.2 2.7 copy-start.53
  7.2 2.8 copy-start.52
  7.2 2.8 copy-start.51
  7.3 2.9 copy-start.55
  7.3 2.9 copy-start.56
  7.3 2.9 copy-start.57
  7.3 171.4 %all-gather.7.cloned.1.call-start = ((), (), s32[]{:S(2)}) async-start(), calls=%async_computation.2 | async-start | bytes 10485760 | tf_op jit(solution)/shard_map/all_gather | solution.py:2275
  10.0 1.6 copy-start.2
  10.0 1.6 copy-start.37
  69.0 1.3 copy-start
  72.9 145.3 %all-gather.9.cloned.1.call-start = ((), (), s32[]{:S(2)}) async-start(), calls=%async_computation.3 | async-start | bytes 2621440 | tf_op jit(solution)/shard_map/all_gather | solution.py:2321
  74.0 105.4 %copy-start.58 = (s32[4,2]{0,1:T(2,128)S(1)}, s32[4,2]{0,1:T(2,128)}, u32[]{:S(2)}) copy-start(s32[4,2]{0,1:T(2,128)} %param.42) | copy-start | bytes 100
  178.7 89.0 %all-gather.11.cloned.1.call-start = ((), (), s32[]{:S(2)}) async-start(), calls=%async_computation.4 | async-start | bytes 2621440 | tf_op jit(solution)/shard_map/all_gather | solution.py:2364
  218.3 315.9 %reduce-scatter.7.cloned.1.call-start = ((), (), s32[]{:S(2)}) async-start(), calls=%async_computation.5 | async-start | bytes 10485760
  445.4 207.3 %reduce-scatter.9.cloned.1.call-start = ((), (), s32[]{:S(2)}) async-start(), calls=%async_computation.6 | async-start | bytes 5242880
  534.2 42.2 %copy-start.25 = (f32[9,256]{1,0:T(8,128)S(1)}, f32[9,256]{1,0:T(8,128)}, u32[]{:S(2)}) copy-start(f32[9,256]{1,0:T(8,128)} %refs_40_.1) | copy-start | bytes 27652
  534.2 42.2 %copy-start.29 = (f32[256,256]{1,0:T(8,128)S(1)}, f32[256,256]{1,0:T(8,128)}, u32[]{:S(2)}) copy-start(f32[256,256]{1,0:T(8,128)} %get-tuple-element.247.refs_1_) | copy-start | bytes 786436
  534.2 46.3 %copy-start.1 = (bf16[4,512,512]{2,1,0:T(8,128)(2,1)S(1)}, bf16[4,512,512]{2,1,0:T(8,128)(2,1)}, u32[]{:S(2)}) copy-start(bf16[4,512,512]{2,1,0:T(8,128)(2,1)} %copy-done) | copy-start | bytes 6291460
  534.2 46.3 %copy-start.4 = (bf16[1024,512]{1,0:T(8,128)(2,1)S(1)}, bf16[1024,512]{1,0:T(8,128)(2,1)}, u32[]{:S(2)}) copy-start(bf16[1024,512]{1,0:T(8,128)(2,1)} %get-tuple-element.238.refs_0_) | copy-start | bytes 3145732
  576.4 1.0 copy-start.23
  577.5 1.0 copy-start.30
  580.5 63.9 %copy-start.49 = (f32[1,256]{1,0:T(1,128)}, f32[1,256]{1,0:T(1,128)S(1)}, u32[]{:S(2)}) copy-start(f32[1,256]{1,0:T(1,128)S(1)} %get-tuple-element.275.refs_11_) | copy-start | bytes 3076
  580.5 1.6 copy-start.9
  582.1 1.2 copy-start.17
  583.3 64.6 %copy-start.13 = (bf16[1024,512]{1,0:T(8,128)(2,1)S(1)}, bf16[1024,512]{1,0:T(8,128)(2,1)}, u32[]{:S(2)}) copy-start(bf16[1024,512]{1,0:T(8,128)(2,1)} %get-tuple-element.258.refs_5_) | copy-start | bytes 3145732
  583.3 64.6 %copy-start.18 = (f32[320,512]{1,0:T(8,128)S(1)}, f32[320,512]{1,0:T(8,128)}, u32[]{:S(2)}) copy-start(f32[320,512]{1,0:T(8,128)} %get-tuple-element.259.refs_7_) | copy-start | bytes 1966084
  583.3 64.6 %copy-start.24 = (f32[6,512]{1,0:T(8,128)S(1)}, f32[6,512]{1,0:T(8,128)}, u32[]{:S(2)}) copy-start(f32[6,512]{1,0:T(8,128)} %refs_36_.1) | copy-start | bytes 36868
  644.4 1.3 copy-start.8
  645.7 1.0 copy-start.14
  647.9 44.4 %copy-start.39 = (f32[1,2048]{1,0:T(1,128)S(1)}, f32[1,2048]{1,0:T(1,128)}, u32[]{:S(2)}) copy-start(f32[1,2048]{1,0:T(1,128)} %get-tuple-element.280.refs_16_) | copy-start | bytes 24580
  648.0 44.4 %copy-start.40 = (f32[1,2048]{1,0:T(1,128)S(1)}, f32[1,2048]{1,0:T(1,128)}, u32[]{:S(2)}) copy-start(f32[1,2048]{1,0:T(1,128)} %get-tuple-element.281.refs_17_) | copy-start | bytes 24580
  648.0 44.4 %copy-start.41 = (f32[1,2048]{1,0:T(1,128)S(1)}, f32[1,2048]{1,0:T(1,128)}, u32[]{:S(2)}) copy-start(f32[1,2048]{1,0:T(1,128)} %get-tuple-element.277.refs_13_) | copy-start | bytes 24580
  648.0 44.4 %copy-start.42 = (f32[1,2048]{1,0:T(1,128)S(1)}, f32[1,2048]{1,0:T(1,128)}, u32[]{:S(2)}) copy-start(f32[1,2048]{1,0:T(1,128)} %get-tuple-element.278.refs_14_) | copy-start | bytes 24580
  650.9 1.0 copy-start.16
  652.7 39.8 %copy-start.5 = (bf16[64,2048]{1,0:T(8,128)(2,1)S(1)}, bf16[64,2048]{1,0:T(8,128)(2,1)}, u32[]{:S(2)}) copy-start(bf16[64,2048]{1,0:T(8,128)(2,1)} %get-tuple-element.202.refs_3_.refs_7_) | copy-start | bytes 786436
  652.7 39.8 %copy-start.10 = (bf16[512,512]{1,0:T(8,128)(2,1)S(1)}, bf16[512,512]{1,0:T(8,128)(2,1)}, u32[]{:S(2)}) copy-start(bf16[512,512]{1,0:T(8,128)(2,1)} %refs_4_.4) | copy-start | bytes 1572868
  652.7 39.8 %copy-start.3 = (bf16[1,4,256,512]{3,2,1,0:T(8,128)(2,1)S(1)}, bf16[1,4,256,512]{3,2,1,0:T(8,128)(2,1)}, u32[]{:S(2)}) copy-start(bf16[1,4,256,512]{3,2,1,0:T(8,128)(2,1)} %reduce-scatter.9.cloned.1.call-done) | copy-start | bytes 3145732
  652.7 1.4 copy-start.15
  654.0 1.0 copy-start.22
  655.1 0.9 copy-start.28
  656.7 35.7 %copy-start.45 = (f32[8,256]{1,0:T(8,128)S(1)}, f32[8,256]{1,0:T(8,128)}, u32[]{:S(2)}) copy-start(f32[8,256]{1,0:T(8,128)} %copy-done.44) | copy-start | bytes 24580
  691.7 8.2 %copy-start.6 = (f32[512,256]{1,0:T(8,128)}, f32[512,256]{1,0:T(8,128)S(1)}, u32[]{:S(2)}) copy-start(f32[512,256]{1,0:T(8,128)S(1)} %get-tuple-element.282.refs_18_.refs_11_) | copy-start | bytes 1572868
  691.7 8.2 %copy-start.7 = (f32[512,256]{1,0:T(8,128)}, f32[512,256]{1,0:T(8,128)S(1)}, u32[]{:S(2)}) copy-start(f32[512,256]{1,0:T(8,128)S(1)} %get-tuple-element.283.refs_19_.refs_15_) | copy-start | bytes 1572868
  691.7 8.2 %copy-start.11 = (bf16[4,4,256,128]{3,2,1,0:T(8,128)(2,1)}, bf16[4,4,256,128]{3,2,1,0:T(8,128)(2,1)S(1)}, u32[]{:S(2)}) copy-start(bf16[4,4,256,128]{3,2,1,0:T(8,128)(2,1)S(1)} %get-tuple-element.289) | copy-start | bytes 3145732
  691.7 8.2 %copy-start.12 = (bf16[4,256,128]{2,1,0:T(8,128)(2,1)}, bf16[4,256,128]{2,1,0:T(8,128)(2,1)S(1)}, u32[]{:S(2)}) copy-start(bf16[4,256,128]{2,1,0:T(8,128)(2,1)S(1)} %get-tuple-element.285) | copy-start | bytes 786436
  692.5 1.1 copy-start.20
  713.8 3.1 copy-start.19
  717.0 20.5 %copy-start.54 = (bf16[512,512]{1,0:T(8,128)(2,1)S(1)}, bf16[512,512]{1,0:T(8,128)(2,1)}, u32[]{:S(2)}) copy-start(bf16[512,512]{1,0:T(8,128)(2,1)} %get-tuple-element.375) | copy-start | bytes 1572868
  (16 other events, 11.7 us)
Sparse Core Ops, SparseCore 0:
  73.1 89.8 all-gather.6
  178.8 33.5 all-gather.8
  218.4 34.2 all-gather.10
  445.5 84.1 reduce-scatter.6
  534.4 52.7 reduce-scatter.8

commit v9 on v8

--- a/solution.py
+++ b/solution.py
@@ -2340,6 +2340,7 @@
         left_t,
         right_w,
         down_two,
+        upstream,
     ) = attention_forward_head(
         whole_acts,
         gains,
@@ -2357,6 +2358,12 @@
             along(left_t.astype(LOW)),
             along(right_w),
             down_half(1),
+            Swap(
+                cotangent,
+                (share, width),
+                lambda ref, q: ref.at[columns_of(q, share)],
+                lambda ref, at: ref.at[:, columns_of(at, width_a)],
+            ),
         ],
         3,
     )
@@ -2388,18 +2395,11 @@
         left_t,
         right_w,
     )
-    down_raw, spread_ft, act_t, gate_raw, up_raw, upstream = ffn_forward(
+    down_raw, spread_ft, act_t, gate_raw, up_raw = ffn_forward(
         ffn_in,
         gateup_all,
         down_all,
-        [
-            Swap(
-                cotangent,
-                (share, width),
-                lambda ref, q: ref.at[columns_of(q, share)],
-                lambda ref, at: ref.at[:, columns_of(at, width_a)],
-            )
-        ],
+        [],
         6,
     )
     result, d_out, d_down, dw_perproj, dw_pergate, gain_four, gain_five = local(

time: 754 us -> 758 us (level)
    pallas_call x1, Pallas kernels: 35.1 us -> 46.4 us  [attention_forward_head(): pl.pallas_call(kernel, out_shape=[low(tokens, wide), low(tokens, wide), l...]
  transfers between devices with their start and end apart: 5 -> 5, of which waited for: 0 -> 0; matrix products, arithmetic and copies ran while one was open for 1% -> 1% of each run, Pallas kernels for 52% -> 53%
where the time goes in v9:
time: 758 us; the launch traced here: 749 us
  Pallas kernels  695 us (92%)
  local copies, waits for them, and re-layouts  32 us (4%)
  between operations  14.9 us (2%)
  other arithmetic  7.65 us (1%)
    pallas_call x6, Pallas kernels, transfers(): pl.pallas_call(kernel, out_shape=list(shapes) + bundle.shapes, in_specs=[...  356 us
    pallas_call x1, Pallas kernels, ffn_backward(): pl.pallas_call(kernel, out_shape=[jax.ShapeDtypeStruct((share, width), FU...  83.9 us
    pallas_call x1, Pallas kernels, ffn_forward(): pl.pallas_call(kernel, out_shape=[jax.ShapeDtypeStruct((share, width), FU...  79.8 us
    pallas_call x1, Pallas kernels, attention_forward_head(): pl.pallas_call(kernel, out_shape=[low(tokens, wide), low(tokens, wide), l...  46.4 us
    pallas_call x1, Pallas kernels, shard_total(): pl.pallas_call(kernel, out_shape=[jax.ShapeDtypeStruct(shape, FULL) for s...  35 us
    pallas_call x1, Pallas kernels, head_backward(): pl.pallas_call(kernel, out_shape=[jax.ShapeDtypeStruct(queries.shape, LOW...  34.3 us
    unnamed x120, local copies, waits for them, and re-layouts  28.4 us
    pallas_call x5, Pallas kernels, local(): pl.pallas_call(kernel, out_shape=[jax.ShapeDtypeStruct(shape, kind) for s...  23 us
  transfers between devices with their start and end apart: 5, of which 0 were waited for; matrix products, arithmetic and copies ran while one was open for 1% of the time, Pallas kernels for 53%

profile of v9, /device:TPU:0, one launch (start us, length us, event | category | flops | bytes accessed | tf_op | source)
XLA Modules:
  0.0 749.5 jit_solution(14233410787515833449)
XLA Ops:
  7.3 2.6 convert_element_type.45.refs_1_
  10.2 1.3 copy-done.2
  11.6 57.4 %shard_map.645 = (bf16[4096,128]{1,0:T(8,128)(2,1)S(1)}, bf16[2,2048,256]{2,1,0:T(8,128)(2,1)}, bf16[256,512]{1,0:T(8,128)(2,1)S(1)}, bf16[4,512,512]{2,1,0:T(8,...) custom-call(f32[4096,128]{1,0:T(8,128)S(1)} %copy-done.2, ...), custom_call_target="tpu_custom_call" | custom-call | bytes 180000000 | tf_op jit(solution)/shard_map/pallas_call | solution.py:769
  69.0 1.3 copy-done
  70.3 0.7 copy-done.31
  73.0 1.0 fusion
  74.0 104.6 %shard_map.646 = (bf16[1024,2048]{1,0:T(8,128)(2,1)}, bf16[2048,256]{1,0:T(8,128)(2,1)}, bf16[2048,256]{1,0:T(8,128)(2,1)}, bf16[2048,256]{1,0:T(8,128)(2,1)}, f...) custom-call(bf16[512,512]{1,0:T(8,128)(2,1)} %refs_4_.4, ...), custom_call_target="tpu_custom_call" | custom-call | bytes 315000000 | tf_op jit(solution)/shard_map/pallas_call | solution.py:769
  179.4 0.7 copy.78.s_ref
  180.1 3.0 multiply_sine_fusion
  183.1 46.4 %shard_map.647 = (bf16[1024,512]{1,0:T(8,128)(2,1)}, bf16[1024,512]{1,0:T(8,128)(2,1)}, bf16[128,2048]{1,0:T(8,128)(2,1)}, f32[512,128]{1,0:T(8,128)}, f32[1024,...) custom-call(s32[4]{0:T(128)} %l_ref.3, ...), custom_call_target="tpu_custom_call" | custom-call | bytes 120000000 | tf_op jit(solution)/shard_map/pallas_call | solution.py:1995
  229.6 45.1 %shard_map.648 = (f32[128,2048]{1,0:T(8,128)}, bf16[256,2048]{1,0:T(8,128)(2,1)}, bf16[256,2048]{1,0:T(8,128)(2,1)}) custom-call(bf16[2,4,128,2048]{3,2,1,0:T(8,128)(2,1)} %bitcast.64, bf16[128,512]{1,0:T(8,128)(2,1)} %copy-done.33, bf16[128,512]{1,0:T(8,128)(2,1)} %copy-done.34), custom_call_target="tpu_custom_call" | custom-call | bytes 135000000 | tf_op jit(solution)/shard_map/pallas_call | solution.py:769
  274.7 4.1 shard_map.649
  278.8 79.8 %shard_map.650 = (f32[128,2048]{1,0:T(8,128)}, bf16[2048,1024]{1,0:T(8,128)(2,1)}, bf16[1024,1024]{1,0:T(8,128)(2,1)}, f32[4,256,1024]{2,1,0:T(8,128)}, f32[4,256,1024]{2,1,0:T(8,128)}) custom-call(bf16[128,2048]{1,0:T(8,128)(2,1)} %get-tuple-element.205.x_ref, bf16[4,2,2048,256]{3,2,1,0:T(8,128)(2,1)} %bitcast.52, bf16[4,512,512]{2,1,0:T(8,128)(2,1)} %bitcast.57, ...), custom_call_target="tpu_custom_call" | custom-call | bytes 240000000 | tf_op jit(solution)/shard_map/pallas_call | solution.py:1490
  358.7 6.9 shard_map.651
  365.6 83.9 %shard_map.652 = (f32[128,2048]{1,0:T(8,128)}, bf16[4,2,2048,256]{3,2,1,0:T(8,128)(2,1)}, bf16[4,1024,512]{2,1,0:T(8,128)(2,1)}) custom-call(bf16[128,2048]{1,0:T(8,128)(2,1)} %get-tuple-element.219.x_ref, bf16[4,2,2048,256]{3,2,1,0:T(8,128)(2,1)} %bitcast.53, bf16[4,512,512]{2,1,0:T(8,128)(2,1)} %bitcast.58, bf16[4,512,512]{2,1,0:T(8,128)(2,1)} %bitcast.60, ...), custom_call_target="tpu_custom_call" | custom-call | bytes 270000000 | tf_op jit(solution)/shard_map/pallas_call | solution.py:1689
  449.6 8.8 %shard_map.653 = (bf16[128,2048]{1,0:T(8,128)(2,1)}, bf16[128,2048]{1,0:T(8,128)(2,1)}, bf16[128,64]{1,0:T(8,128)(2,1)}, bf16[640,2048]{1,0:T(8,128)(2,1)}, f32[...) custom-call(f32[128,2048]{1,0:T(8,128)} %get-tuple-element.218.refs_0_, ...), custom_call_target="tpu_custom_call" | custom-call | bytes 15000000 | tf_op jit(solution)/shard_map/pallas_call | solution.py:787
  458.4 45.6 %shard_map.654 = (bf16[2,4,128,2048]{3,2,1,0:T(8,128)(2,1)}, f32[320,512]{1,0:T(8,128)}) custom-call(bf16[128,2048]{1,0:T(8,128)(2,1)} %get-tuple-element.230.refs_0_, bf16[2,320,2048]{2,1,0:T(8,128)(2,1)} %bitcast.66), custom_call_target="tpu_custom_call" | custom-call | bytes 150000000 | tf_op jit(solution)/shard_map/pallas_call | solution.py:769
  504.1 34.3 %shard_map.655 = (bf16[1024,256]{1,0:T(8,128)(2,1)}, bf16[4,512,256]{2,1,0:T(8,128)(2,1)}, f32[1,256]{1,0:T(1,128)}, bf16[256,2048]{1,0:T(8,128)(2,1)}, bf16[512...) custom-call(s32[4]{0:T(128)} %l_ref.3, s32[4,2]{1,0:T(4,128)} %copy.78.s_ref, ...), custom_call_target="tpu_custom_call" | custom-call | bytes 75000000 | tf_op jit(solution)/shard_map/pallas_call | solution.py:2093
  538.5 42.1 %shard_map.656 = (bf16[4,1024,256]{2,1,0:T(8,128)(2,1)}, f32[512,256]{1,0:T(8,128)}) custom-call(bf16[1024,256]{1,0:T(8,128)(2,1)} %get-tuple-element.242.refs_0_, bf16[4,512,256]{2,1,0:T(8,128)(2,1)} %get-tuple-element.243.refs_1_), custom_call_target="tpu_custom_call" | custom-call | bytes 135000000 | tf_op jit(solution)/shard_map/pallas_call | solution.py:769
  580.6 1.0 copy-done.23
  581.7 1.0 copy-done.30
  582.6 0.9 copy-done.35
  583.5 0.9 copy-done.36
  584.7 1.6 copy-done.9
  586.3 1.2 copy-done.17
  587.6 61.0 %shard_map.658 = (bf16[4,512,256]{2,1,0:T(8,128)(2,1)S(1)}, f32[1024,512]{1,0:T(8,128)S(1)}, f32[8,256]{1,0:T(8,128)S(1)}, bf16[1024,256]{1,0:T(8,128)(2,1)S(1)}...) custom-call(bf16[1024,512]{1,0:T(8,128)(2,1)S(1)} %copy-done.4, ...), custom_call_target="tpu_custom_call" | custom-call | bytes 195000000 | tf_op jit(solution)/shard_map/pallas_call | solution.py:769
  648.6 1.3 copy-done.8
  649.9 1.0 copy-done.14
  650.8 0.7 copy-done.27
  652.2 2.9 shard_map.659
  655.1 1.0 copy-done.16
  656.1 0.8 copy-done.21
  656.9 1.3 copy-done.15
  658.2 1.0 copy-done.22
  659.3 0.9 copy-done.28
  660.2 0.7 copy-done.46
  660.9 35.0 %shard_map.660 = (f32[512,256]{1,0:T(8,128)S(1)}, f32[512,256]{1,0:T(8,128)S(1)}, f32[320,128]{1,0:T(8,128)S(1)}, f32[2,4,8,1024]{3,2,1,0:T(8,128)S(1)}, f32[2,4...) custom-call(bf16[4,512,256]{2,1,0:T(8,128)(2,1)S(1)} %copy-done.15, ...), custom_call_target="tpu_custom_call" | custom-call | bytes 120000000 | tf_op jit(solution)/shard_map/pallas_call | solution.py:1083
  695.9 0.7 fusion.1
  696.7 1.1 copy-done.20
  697.7 0.9 copy-done.26
  698.7 0.9 copy-done.32
  699.6 0.7 copy-done.43
  700.3 0.7 copy-done.47
  701.6 0.7 copy-done.50
  702.2 1.9 shard_map.661
  704.1 14.0 %shard_map.662.x_ref = f32[128,128]{1,0:T(8,128)S(1)} custom-call(f32[128,128]{1,0:T(8,128)S(1)} %get-tuple-element.287.x_ref), custom_call_target="tpu_custom_call" | custom-call | bytes 42000000 | tf_op jit(solution)/shard_map/pallas_call | solution.py:1757
  721.2 20.4 %shard_map.663 = (f32[1,1]{1,0:T(1,128)}, f32[1,8]{1,0:T(1,128)}, f32[1024,1024]{1,0:T(8,128)}, f32[1024,1024]{1,0:T(8,128)}, f32[1024,1024]{1,0:T(8,128)}, /*in...) custom-call(f32[128,128]{1,0:T(8,128)} %copy-done.19, ...), custom_call_target="tpu_custom_call" | custom-call | bytes 75000000 | tf_op jit(solution)/shard_map/pallas_call | solution.py:1858
  741.7 0.8 copy.80
  (129 shorter events, 7.8 us)
Async XLA Ops:
  7.2 2.7 copy-start.53
  7.2 2.8 copy-start.52
  7.2 2.8 copy-start.51
  7.3 2.9 copy-start.55
  7.3 2.9 copy-start.56
  7.3 2.9 copy-start.57
  7.3 171.4 %all-gather.7.cloned.1.call-start = ((), (), s32[]{:S(2)}) async-start(), calls=%async_computation.2 | async-start | bytes 10485760 | tf_op jit(solution)/shard_map/all_gather | solution.py:2275
  10.0 1.6 copy-start.2
  10.0 1.6 copy-start.37
  69.0 1.3 copy-start
  72.9 156.6 %all-gather.9.cloned.1.call-start = ((), (), s32[]{:S(2)}) async-start(), calls=%async_computation.3 | async-start | bytes 2621440 | tf_op jit(solution)/shard_map/all_gather | solution.py:2321
  74.0 105.4 %copy-start.58 = (s32[4,2]{0,1:T(2,128)S(1)}, s32[4,2]{0,1:T(2,128)}, u32[]{:S(2)}) copy-start(s32[4,2]{0,1:T(2,128)} %param.42) | copy-start | bytes 100
  178.7 100.1 %all-gather.11.cloned.1.call-start = ((), (), s32[]{:S(2)}) async-start(), calls=%async_computation.4 | async-start | bytes 2621440 | tf_op jit(solution)/shard_map/all_gather | solution.py:2371
  229.5 308.9 %reduce-scatter.7.cloned.1.call-start = ((), (), s32[]{:S(2)}) async-start(), calls=%async_computation.5 | async-start | bytes 10485760
  449.6 207.3 %reduce-scatter.9.cloned.1.call-start = ((), (), s32[]{:S(2)}) async-start(), calls=%async_computation.6 | async-start | bytes 5242880
  538.4 42.2 %copy-start.25 = (f32[9,256]{1,0:T(8,128)S(1)}, f32[9,256]{1,0:T(8,128)}, u32[]{:S(2)}) copy-start(f32[9,256]{1,0:T(8,128)} %refs_40_.1) | copy-start | bytes 27652
  538.4 42.2 %copy-start.29 = (f32[256,256]{1,0:T(8,128)S(1)}, f32[256,256]{1,0:T(8,128)}, u32[]{:S(2)}) copy-start(f32[256,256]{1,0:T(8,128)} %get-tuple-element.247.refs_1_) | copy-start | bytes 786436
  538.5 46.2 %copy-start.1 = (bf16[4,512,512]{2,1,0:T(8,128)(2,1)S(1)}, bf16[4,512,512]{2,1,0:T(8,128)(2,1)}, u32[]{:S(2)}) copy-start(bf16[4,512,512]{2,1,0:T(8,128)(2,1)} %copy-done) | copy-start | bytes 6291460
  538.5 46.2 %copy-start.4 = (bf16[1024,512]{1,0:T(8,128)(2,1)S(1)}, bf16[1024,512]{1,0:T(8,128)(2,1)}, u32[]{:S(2)}) copy-start(bf16[1024,512]{1,0:T(8,128)(2,1)} %get-tuple-element.238.refs_0_) | copy-start | bytes 3145732
  580.6 1.0 copy-start.23
  581.7 1.0 copy-start.30
  584.7 63.9 %copy-start.49 = (f32[1,256]{1,0:T(1,128)}, f32[1,256]{1,0:T(1,128)S(1)}, u32[]{:S(2)}) copy-start(f32[1,256]{1,0:T(1,128)S(1)} %get-tuple-element.275.refs_11_) | copy-start | bytes 3076
  584.7 1.6 copy-start.9
  586.3 1.2 copy-start.17
  587.5 64.6 %copy-start.13 = (bf16[1024,512]{1,0:T(8,128)(2,1)S(1)}, bf16[1024,512]{1,0:T(8,128)(2,1)}, u32[]{:S(2)}) copy-start(bf16[1024,512]{1,0:T(8,128)(2,1)} %get-tuple-element.258.refs_5_) | copy-start | bytes 3145732
  587.5 64.6 %copy-start.18 = (f32[320,512]{1,0:T(8,128)S(1)}, f32[320,512]{1,0:T(8,128)}, u32[]{:S(2)}) copy-start(f32[320,512]{1,0:T(8,128)} %get-tuple-element.259.refs_7_) | copy-start | bytes 1966084
  587.6 64.6 %copy-start.24 = (f32[6,512]{1,0:T(8,128)S(1)}, f32[6,512]{1,0:T(8,128)}, u32[]{:S(2)}) copy-start(f32[6,512]{1,0:T(8,128)} %refs_36_.1) | copy-start | bytes 36868
  648.6 1.3 copy-start.8
  649.9 1.0 copy-start.14
  652.2 44.4 %copy-start.39 = (f32[1,2048]{1,0:T(1,128)S(1)}, f32[1,2048]{1,0:T(1,128)}, u32[]{:S(2)}) copy-start(f32[1,2048]{1,0:T(1,128)} %get-tuple-element.280.refs_16_) | copy-start | bytes 24580
  652.2 44.4 %copy-start.40 = (f32[1,2048]{1,0:T(1,128)S(1)}, f32[1,2048]{1,0:T(1,128)}, u32[]{:S(2)}) copy-start(f32[1,2048]{1,0:T(1,128)} %get-tuple-element.281.refs_17_) | copy-start | bytes 24580
  652.2 44.4 %copy-start.41 = (f32[1,2048]{1,0:T(1,128)S(1)}, f32[1,2048]{1,0:T(1,128)}, u32[]{:S(2)}) copy-start(f32[1,2048]{1,0:T(1,128)} %get-tuple-element.277.refs_13_) | copy-start | bytes 24580
  652.2 44.4 %copy-start.42 = (f32[1,2048]{1,0:T(1,128)S(1)}, f32[1,2048]{1,0:T(1,128)}, u32[]{:S(2)}) copy-start(f32[1,2048]{1,0:T(1,128)} %get-tuple-element.278.refs_14_) | copy-start | bytes 24580
  655.1 1.0 copy-start.16
  656.9 39.8 %copy-start.5 = (bf16[64,2048]{1,0:T(8,128)(2,1)S(1)}, bf16[64,2048]{1,0:T(8,128)(2,1)}, u32[]{:S(2)}) copy-start(bf16[64,2048]{1,0:T(8,128)(2,1)} %get-tuple-element.202.refs_3_.refs_7_) | copy-start | bytes 786436
  656.9 39.8 %copy-start.10 = (bf16[512,512]{1,0:T(8,128)(2,1)S(1)}, bf16[512,512]{1,0:T(8,128)(2,1)}, u32[]{:S(2)}) copy-start(bf16[512,512]{1,0:T(8,128)(2,1)} %refs_4_.4) | copy-start | bytes 1572868
  656.9 39.8 %copy-start.3 = (bf16[1,4,256,512]{3,2,1,0:T(8,128)(2,1)S(1)}, bf16[1,4,256,512]{3,2,1,0:T(8,128)(2,1)}, u32[]{:S(2)}) copy-start(bf16[1,4,256,512]{3,2,1,0:T(8,128)(2,1)} %reduce-scatter.9.cloned.1.call-done) | copy-start | bytes 3145732
  656.9 1.4 copy-start.15
  658.2 1.0 copy-start.22
  659.3 0.9 copy-start.28
  660.9 35.7 %copy-start.45 = (f32[8,256]{1,0:T(8,128)S(1)}, f32[8,256]{1,0:T(8,128)}, u32[]{:S(2)}) copy-start(f32[8,256]{1,0:T(8,128)} %copy-done.44) | copy-start | bytes 24580
  695.9 8.2 %copy-start.6 = (f32[512,256]{1,0:T(8,128)}, f32[512,256]{1,0:T(8,128)S(1)}, u32[]{:S(2)}) copy-start(f32[512,256]{1,0:T(8,128)S(1)} %get-tuple-element.282.refs_18_.refs_11_) | copy-start | bytes 1572868
  695.9 8.2 %copy-start.7 = (f32[512,256]{1,0:T(8,128)}, f32[512,256]{1,0:T(8,128)S(1)}, u32[]{:S(2)}) copy-start(f32[512,256]{1,0:T(8,128)S(1)} %get-tuple-element.283.refs_19_.refs_15_) | copy-start | bytes 1572868
  695.9 8.2 %copy-start.11 = (bf16[4,4,256,128]{3,2,1,0:T(8,128)(2,1)}, bf16[4,4,256,128]{3,2,1,0:T(8,128)(2,1)S(1)}, u32[]{:S(2)}) copy-start(bf16[4,4,256,128]{3,2,1,0:T(8,128)(2,1)S(1)} %get-tuple-element.289) | copy-start | bytes 3145732
  695.9 8.2 %copy-start.12 = (bf16[4,256,128]{2,1,0:T(8,128)(2,1)}, bf16[4,256,128]{2,1,0:T(8,128)(2,1)S(1)}, u32[]{:S(2)}) copy-start(bf16[4,256,128]{2,1,0:T(8,128)(2,1)S(1)} %get-tuple-element.285) | copy-start | bytes 786436
  696.7 1.1 copy-start.20
  718.1 3.1 copy-start.19
  721.2 20.5 %copy-start.54 = (bf16[512,512]{1,0:T(8,128)(2,1)S(1)}, bf16[512,512]{1,0:T(8,128)(2,1)}, u32[]{:S(2)}) copy-start(bf16[512,512]{1,0:T(8,128)(2,1)} %get-tuple-element.375) | copy-start | bytes 1572868
  (16 other events, 11.7 us)
Sparse Core Ops, SparseCore 0:
  73.1 89.8 all-gather.6
  178.8 33.5 all-gather.8
  229.6 34.2 all-gather.10
  449.7 84.1 reduce-scatter.6
  538.6 52.4 reduce-scatter.8
